TPU v7x, 32 devices: a whole 2x2x4 slice. The times are simulated.
32 devices in a mesh: slab: 16 (over z, y, x), tile: 2 (over core).
Axes of the slice: x: 2, y: 2, z: 4, core: 2. Of those that a mesh axis runs over, the one named last changes fastest.
Arguments:
- charges: bfloat16 [64, 8192], P(None, ('slab', 'tile')), may hold values from -6 to 6
- live_count: int32 [32], P(('slab', 'tile')), may hold values from 32 to 256, as said below
- slot_brick: int32 [8192], P(('slab', 'tile')), may hold values from 0 to 4095
- slot_stencil: int32 [8192], P(('slab', 'tile')), may hold values from 0 to 15
- stencils: bfloat16 [16, 64, 512], replicated, may hold values from -0.75 to 0.75
- near_source: int32 [8192, 8], P(('slab', 'tile')), may hold values from 0 to 2303
- near_block: int32 [8192, 8], P(('slab', 'tile')), may hold values from 0 to 15
- near_blocks: bfloat16 [64, 16, 64], replicated, may hold values from -0.25 to 0.25
- kernel_hat: float32 [512, 64, 256], P(('slab', 'tile')), may hold values from 0 to 1, as said below
Outputs:
- potentials: float32 [64, 8192], P(None, ('slab', 'tile'))
Inputs may be any that keep to these rules, and one draw needn't show every extreme that they name: `live_count`: some device has all 256 slots live in every draw. kernel_hat is even: its entry at (kz, kx, ky) equals the one at ((-kz) mod 512, (-kx) mod 64, (-ky) mod 256). It is zero on the plane kz = 256 and at least 0.05 elsewhere.
All inputs are finite; a program needn't handle non-finite values.
Results may differ from a plain program's by a relative error of at most 0.0011.
Values may be sent and summed in bfloat16 or wider, within the bound.
No kernel may reach another device: no remote copies, remote signals or barrier semaphores. Data moves between devices by JAX's collectives and lax.ppermute only.
A program may use at most 64 MiB of HBM per device.

v0:
```python
import math

import jax
import jax.numpy as jnp
from jax import lax
from jax.sharding import PartitionSpec as P

PANELS = 64
POINTS = 512
NY = 256
NZ = 512
KS = 16
KN = 16


slot_block = 128
highest = lax.Precision.HIGHEST


def extended(cells, sides, width):
    for axis, dim in sides:
        count = lax.axis_size(axis)
        head = lax.slice_in_dim(cells, 0, width, axis=dim)
        tail = lax.slice_in_dim(cells, cells.shape[dim] - width, cells.shape[dim], axis=dim)
        cells = jnp.concatenate(
            [
                lax.ppermute(tail, axis, [(i, (i + 1) % count) for i in range(count)]),
                cells,
                lax.ppermute(head, axis, [((i + 1) % count, i) for i in range(count)]),
            ],
            axis=dim,
        )
    return cells


def one_hot_rows(kind_rows, kinds_count, out_type):
    return (kind_rows[None, :] == jnp.arange(kinds_count, dtype=jnp.int32)[:, None]).astype(
        out_type
    )


def spread_rows(values, kind_rows, kinds_count):
    selector = one_hot_rows(kind_rows, kinds_count, values.dtype)
    return (selector[:, None, :] * values[None, :, :]).reshape(
        kinds_count * values.shape[0], values.shape[1]
    )


def footprint_places(bricks, local_y):
    points = jnp.arange(POINTS, dtype=jnp.int32)
    point_x = points // 64
    point_y = points // 8 % 8
    point_z = points % 8
    zbricks = NZ // 4
    brick_y = bricks // zbricks
    brick_z = bricks % zbricks
    return (point_x[:, None] * (local_y + 4) + 4 * brick_y[None, :] + point_y[:, None]) * NZ + (
        4 * brick_z[None, :] - 2 + point_z[:, None]
    ) % NZ


def fold_margins(padded, local_y):
    inner = padded[4:8, 4 : local_y + 4]
    inner = inner.at[0:2].add(padded[0:2, 4 : local_y + 4])
    inner = inner.at[2:4].add(padded[10:12, 4 : local_y + 4])
    inner = inner.at[:, 0:2].add(padded[4:8, 0:2])
    inner = inner.at[:, local_y - 2 : local_y].add(padded[4:8, local_y + 6 : local_y + 8])
    inner = inner.at[0:2, 0:2].add(padded[0:2, 0:2])
    inner = inner.at[0:2, local_y - 2 : local_y].add(padded[0:2, local_y + 6 : local_y + 8])
    inner = inner.at[2:4, 0:2].add(padded[10:12, 0:2])
    inner = inner.at[2:4, local_y - 2 : local_y].add(padded[10:12, local_y + 6 : local_y + 8])
    return inner


def dft_tables(length):
    counter = jnp.arange(length, dtype=jnp.int32)
    angles = (counter[:, None] * counter[None, :] % length).astype(jnp.float32) * (
        2.0 * math.pi / length
    )
    return (jnp.cos(angles), jnp.sin(angles))


def complex_table(length, orient):
    cosine, sine_table = dft_tables(length)
    from_real = jnp.stack([cosine, orient * sine_table], axis=1)
    from_imag = jnp.stack([-orient * sine_table, cosine], axis=1)
    return jnp.stack([from_real, from_imag], axis=0)


def long_dft(paired, dim, orient):
    moved = jnp.moveaxis(paired, dim, -1)
    length = moved.shape[-1]
    first = 1
    for factor in range(1, math.isqrt(length) + 1):
        if length % factor == 0:
            first = factor
    second = length // first
    split = moved.reshape(moved.shape[:-1] + (first, second))
    section = jnp.einsum(
        "s...ab,satc->t...cb", split, complex_table(first, orient), precision=highest
    )
    rows_k = jnp.arange(first, dtype=jnp.int32)
    cols_n = jnp.arange(second, dtype=jnp.int32)
    angles = (rows_k[:, None] * cols_n[None, :] % length).astype(jnp.float32) * (
        2.0 * math.pi / length
    )
    twist_cos = jnp.cos(angles)
    twist_sin = orient * jnp.sin(angles)
    real_part = section[0] * twist_cos - section[1] * twist_sin
    imag_part = section[0] * twist_sin + section[1] * twist_cos
    section = jnp.stack([real_part, imag_part], axis=0)
    final = jnp.einsum(
        "s...cb,sbtd->t...dc", section, complex_table(second, orient), precision=highest
    )
    return jnp.moveaxis(final.reshape(moved.shape), -1, dim)


def regroup(values, leading, trailing):
    shaped = values.reshape(values.shape[:-1] + (leading, trailing, -1))
    return jnp.swapaxes(shaped, -3, -2).reshape(values.shape)


def near_field(charges, near_source, near_block, near_blocks, block_count):
    slot_count = charges.shape[1]
    beside_all = extended(charges[None, None], (("slab", 0), ("tile", 1)), 1)
    source_pool = jnp.transpose(beside_all.reshape(9, PANELS, slot_count), (1, 0, 2)).reshape(
        PANELS, 9 * slot_count
    )
    near_table = near_blocks.reshape(PANELS, KN * PANELS)
    fanout = near_source.shape[1]

    def accumulate(block_index, result):
        offset = block_index * slot_block
        sources = lax.dynamic_slice_in_dim(near_source, offset, slot_block, 0).reshape(-1)
        block_kinds = lax.dynamic_slice_in_dim(near_block, offset, slot_block, 0).reshape(-1)
        gathered = jnp.take(source_pool, sources, axis=1)
        near_sums = jnp.dot(
            near_table, spread_rows(gathered, block_kinds, KN), preferred_element_type=jnp.float32
        )
        return lax.dynamic_update_slice_in_dim(
            result, jnp.sum(near_sums.reshape(PANELS, slot_block, fanout), axis=2), offset, 1
        )

    return lax.fori_loop(0, block_count, accumulate, jnp.zeros((PANELS, slot_count), jnp.float32))


def body(
    charges,
    live_count,
    slot_brick,
    slot_stencil,
    stencils,
    near_source,
    near_block,
    near_blocks,
    kernel_hat,
):
    slot_count = charges.shape[1]
    slab_count = lax.axis_size("slab")
    tile_count = lax.axis_size("tile")
    local_y = NY // tile_count
    slot_lane = jnp.arange(slot_count, dtype=jnp.int32)
    live_slots = live_count[0]
    charges = jnp.where((slot_lane < live_slots)[None, :], charges, jnp.zeros((), charges.dtype))
    block_count = (live_slots + slot_block - 1) // slot_block
    stencil_rows = stencils.reshape(KS * PANELS, POINTS)

    def project(block_index, spread):
        offset = block_index * slot_block
        block_charges = lax.dynamic_slice_in_dim(charges, offset, slot_block, 1)
        block_kinds = lax.dynamic_slice_in_dim(slot_stencil, offset, slot_block, 0)
        bricks = lax.dynamic_slice_in_dim(slot_brick, offset, slot_block, 0)
        footprint = lax.dot_general(
            stencil_rows,
            spread_rows(block_charges, block_kinds, KS),
            (((0,), (0,)), ((), ())),
            preferred_element_type=jnp.float32,
        )
        return spread.at[footprint_places(bricks, local_y).reshape(-1)].add(footprint.reshape(-1))

    spread = lax.fori_loop(
        0, block_count, project, jnp.zeros((8 * (local_y + 4) * NZ,), jnp.float32)
    )
    padded = extended(spread.reshape(8, local_y + 4, NZ), (("slab", 0), ("tile", 1)), 2)
    charge_grid = fold_margins(padded, local_y)
    stacked = jnp.stack([charge_grid, jnp.zeros_like(charge_grid)], axis=0)
    paired = long_dft(stacked, 3, -1.0)
    paired = lax.all_to_all(
        lax.all_to_all(paired, "slab", split_axis=3, concat_axis=1, tiled=True),
        "tile",
        split_axis=3,
        concat_axis=2,
        tiled=True,
    )
    paired = jnp.moveaxis(paired, 3, 1)
    paired = long_dft(paired, 3, -1.0)
    whole_x = paired.shape[2]
    paired = long_dft(paired, 2, -1.0)
    paired = paired * kernel_hat[None]
    paired = long_dft(paired, 2, 1.0)
    paired = long_dft(paired, 3, 1.0)
    paired = jnp.moveaxis(paired, 1, 3)
    paired = lax.all_to_all(
        lax.all_to_all(paired, "slab", split_axis=1, concat_axis=3, tiled=True),
        "tile",
        split_axis=2,
        concat_axis=3,
        tiled=True,
    )
    paired = regroup(paired, tile_count, slab_count)
    potential = long_dft(paired, 3, 1.0)[0] * (1.0 / (whole_x * NY * NZ))
    pulled = extended(potential.astype(jnp.bfloat16), (("slab", 0), ("tile", 1)), 2).reshape(-1)
    near_terms = near_field(charges, near_source, near_block, near_blocks, block_count)

    def sample(block_index, result):
        offset = block_index * slot_block
        block_kinds = lax.dynamic_slice_in_dim(slot_stencil, offset, slot_block, 0)
        bricks = lax.dynamic_slice_in_dim(slot_brick, offset, slot_block, 0)
        samples = pulled[footprint_places(bricks, local_y)]
        stencil_sums = jnp.dot(stencil_rows, samples, preferred_element_type=jnp.float32)
        picked = jnp.sum(
            stencil_sums.reshape(KS, PANELS, slot_block)
            * one_hot_rows(block_kinds, KS, jnp.float32)[:, None, :],
            axis=0,
        )
        summed = picked + lax.dynamic_slice_in_dim(near_terms, offset, slot_block, 1)
        return lax.dynamic_update_slice_in_dim(result, summed, offset, 1)

    result = lax.fori_loop(0, block_count, sample, jnp.zeros((PANELS, slot_count), jnp.float32))
    return jnp.where((slot_lane < live_slots)[None, :], result, 0.0)


def solution(mesh):
    in_specs = (
        P(None, ("slab", "tile")),
        P(("slab", "tile")),
        P(("slab", "tile")),
        P(("slab", "tile")),
        P(),
        P(("slab", "tile"), None),
        P(("slab", "tile"), None),
        P(),
        P(("slab", "tile"), None, None),
    )
    out_specs = P(None, ("slab", "tile"))
    return jax.shard_map(body, mesh=mesh, in_specs=in_specs, out_specs=out_specs, check_vma=False)
```

profile of v0, /device:TPU:10, one launch (start us, length us, event | category | flops | bytes accessed | tf_op | source)
XLA Modules:
  0.0 1801.6 jit_solution(13523290065192148825)
XLA Ops:
  2.3 714.6 %while.44 = (s32[]{:T(128)}, f32[540672]{0:T(1024)S(1)}, s32[]{:T(128)}, s32[256]{0:T(256)}, s32[256]{0:T(256)}, /*index=5*/bf16[64,256]{1,0:T(8,128)(2,1)}, bf1...) while((s32[]{:T(128)}, f32[540672]{0:T(1024)S(1)}, ...), condition=%wide.region_2.3_spmd, body=%wide.region_0.2_spmd.sunk | while | flops 135683328 | bytes 8988367 | solution.py:181
  9.6 350.0 %scatter_fusion = f32[540672]{0:T(1024)S(1)} fusion(f32[540672]{0:T(1024)S(1)} %get-tuple-element.760, s32[65536]{0:T(1024)S(1)} %bitcast.324, f32[65536]{0:T(1024)} %bitcast.325), kind=kCustom, calls=%fused_computation.2.clone.1 | custom fusion | flops 65536 | bytes 1048576 | tf_op jit(solution)/shard_map/while/body/scatter-add | solution.py:179
  366.9 350.0 %scatter_fusion = f32[540672]{0:T(1024)S(1)} fusion(f32[540672]{0:T(1024)S(1)} %get-tuple-element.760, s32[65536]{0:T(1024)S(1)} %bitcast.324, f32[65536]{0:T(1024)} %bitcast.325), kind=kCustom, calls=%fused_computation.2.clone.1 | custom fusion | flops 65536 | bytes 1048576 | tf_op jit(solution)/shard_map/while/body/scatter-add | solution.py:179
  719.9 2.3 copy.191
  722.2 1.9 slice.354
  724.1 2.3 copy.193
  726.4 2.3 collective-permute-start.1
  735.0 2.2 collective-permute-done.1
  739.9 1.9 add_select_fusion.13
  743.9 3.0 fusion.76
  747.4 2.5 fusion.79
  751.1 2.7 copy.201
  753.8 4.6 all-to-all-start
  758.8 2.6 copy.214
  761.6 44.2 %all-to-all-done = f32[2,4,128,512]{2,1,0,3:T(4,128)S(1)} async-done(((f32[2,4,128,512]{2,1,0,3:T(4,128)}), f32[2,4,128,512]{2,1,0,3:T(4,128)S(1)}, u32[]{:S(2)}, u32[]{:S(2)}) %all-to-all-start) | async-done | bytes 2097184 | tf_op jit(solution)/shard_map/all_to_all | solution.py:189
  807.7 5.4 all_to_all.69
  813.1 3.0 copy.206
  816.1 2.9 all_to_all.57
  819.0 2.8 copy.207
  821.8 7.8 fusion.44
  830.8 4.5 fusion.47
  835.4 3.7 copy.210
  839.1 3.0 copy.211
  842.1 2.3 fusion.82
  845.0 2.3 fusion.63
  847.3 2.0 fusion.91
  849.9 2.3 fusion.85
  853.1 2.7 copy.217
  855.8 7.4 fusion.50
  864.5 4.5 fusion.53
  869.0 3.7 copy.222
  872.7 4.2 copy.223
  877.0 6.7 all-to-all-start.2
  885.9 45.1 %all-to-all-done.2 = f32[2,64,256,16]{2,3,0,1:T(8,128)S(1)} async-done(((f32[2,64,256,16]{2,3,0,1:T(8,128)}), f32[2,64,256,16]{2,3,0,1:T(8,128)S(1)}, u32[]{:S(2)}, u32[]{:S(2)}) %all-to-all-start.2) | async-done | bytes 2097184 | tf_op jit(solution)/shard_map/all_to_all | solution.py:204
  932.6 2.2 copy.226
  934.8 5.8 all_to_all.70
  943.2 2.2 copy.229
  947.8 2.5 fusion.88
  950.6 3.1 collective-permute-start.4
  956.6 8.0 collective-permute-done.4
  972.2 10.5 while.45
  972.4 3.2 gather_fusion
  977.7 3.2 gather_fusion
  985.5 3.4 pad_maximum_fusion.5
  988.9 2.1 copy.240
  992.8 808.0 %while.46 = (s32[]{:T(128)}, f32[64,256]{1,0:T(8,128)S(1)}, s32[]{:T(128)}, s32[256]{0:T(256)}, bf16[540672]{0:T(1024)(128)(2,1)S(1)}, /*index=5*/bf16[1024,512]...) while((s32[]{:T(128)}, f32[64,256]{1,0:T(8,128)S(1)}, ...), condition=%wide.region_9.10_spmd, body=%wide.region_7.9_spmd.sunk | while | flops 135814016 | bytes 4228271 | solution.py:229
  993.9 402.1 %gather_fusion.1 = bf16[65536]{0:T(1024)(128)(2,1)S(1)} fusion(bf16[540672]{0:T(1024)(128)(2,1)S(1)} %get-tuple-element.842, s32[65536]{0:T(1024)S(1)} %fusion.220), kind=kCustom, calls=%fused_computation.1.clone.1 | custom fusion | bytes 524288 | tf_op jit(solution)/shard_map/while/body/gather | solution.py:219
  1397.9 402.1 %gather_fusion.1 = bf16[65536]{0:T(1024)(128)(2,1)S(1)} fusion(bf16[540672]{0:T(1024)(128)(2,1)S(1)} %get-tuple-element.842, s32[65536]{0:T(1024)S(1)} %fusion.220), kind=kCustom, calls=%fused_computation.1.clone.1 | custom fusion | bytes 524288 | tf_op jit(solution)/shard_map/while/body/gather | solution.py:219
  (225 shorter events, 70.9 us)
Async XLA Ops:
  0.0 2.3 copy-start
  0.8 1.4 copy-start.12
  9.6 350.0 %copy-start.1 = (bf16[16,64,512]{2,1,0:T(8,128)(2,1)S(1)}, bf16[16,64,512]{2,1,0:T(8,128)(2,1)}, u32[]{:S(2)}) copy-start(bf16[16,64,512]{2,1,0:T(8,128)(2,1)} %get-tuple-element.861) | copy-start | bytes 3145732 | tf_op jit(solution)/shard_map/while
  366.9 350.0 %copy-start.1 = (bf16[16,64,512]{2,1,0:T(8,128)(2,1)S(1)}, bf16[16,64,512]{2,1,0:T(8,128)(2,1)}, u32[]{:S(2)}) copy-start(bf16[16,64,512]{2,1,0:T(8,128)(2,1)} %get-tuple-element.861) | copy-start | bytes 3145732 | tf_op jit(solution)/shard_map/while
  722.2 11.4 collective-permute-start
  726.4 10.8 collective-permute-start.1
  728.7 3.4 copy-start.15
  730.2 4.6 copy-start.2
  738.4 1.3 collective-permute-start.2
  738.5 1.4 collective-permute-start.3
  753.8 52.0 %all-to-all-start = ((f32[2,4,128,512]{2,1,0,3:T(4,128)}), f32[2,4,128,512]{2,1,0,3:T(4,128)S(1)}, u32[]{:S(2)}, u32[]{:S(2)}) async-start(f32[2,4,128,512]{2,1,0,3:T(4,128)} %copy.201), calls=%async_computation | async-start | bytes 4194304 | tf_op jit(solution)/shard_map/all_to_all | solution.py:189
  845.0 2.3 copy-start.4
  877.0 6.7 copy-start.9
  877.0 6.7 copy-start.13
  877.0 54.0 %all-to-all-start.2 = ((f32[2,64,256,16]{2,3,0,1:T(8,128)}), f32[2,64,256,16]{2,3,0,1:T(8,128)S(1)}, u32[]{:S(2)}, u32[]{:S(2)}) async-start(f32[2,64,256,16]{2,3,0,1:T(8,128)} %copy.223), calls=%async_computation.2 | async-start | bytes 4194304 | tf_op jit(solution)/shard_map/all_to_all | solution.py:204
  883.7 70.7 %collective-permute-start.8 = (bf16[1,1,64,256]{3,2,1,0:T(8,128)(2,1)S(1)}, bf16[1,1,64,256]{3,2,1,0:T(8,128)(2,1)S(1)}, u32[]{:S(2)}, u32[]{:S(2)}) collective-permute-start(bf16[1,1,64,256]{3,2,1,0:T(8,128)(2,1)S(1)} %fusion.191), channel_id=1, source_target_pairs={{0,2},{2,4},{4,6},{6,8},{8,10},{10,12},{12,14},{14,16},{16,18},{18... | collective-permute-start | bytes 98312 | tf_op jit(solution)/shard_map/ppermute | solution.py:27
  885.2 69.2 %collective-permute-start.9 = (bf16[1,1,64,256]{3,2,1,0:T(8,128)(2,1)S(1)}, bf16[1,1,64,256]{3,2,1,0:T(8,128)(2,1)S(1)}, u32[]{:S(2)}, u32[]{:S(2)}) collective-permute-start(bf16[1,1,64,256]{3,2,1,0:T(8,128)(2,1)S(1)} %fusion.191), channel_id=1, source_target_pairs={{2,0},{4,2},{6,4},{8,6},{10,8},{12,10},{14,12},{16,14},{18,16},{20... | collective-permute-start | bytes 98312 | tf_op jit(solution)/shard_map/ppermute | solution.py:29
  950.3 4.8 copy-start.8
  950.6 14.0 collective-permute-start.4
  954.4 12.0 collective-permute-start.5
  954.5 1.4 collective-permute-start.10
  954.6 1.4 collective-permute-start.11
  956.6 9.8 copy-start.3
  966.4 1.9 copy-start.5
  968.3 3.9 copy-start.10
  968.3 3.9 copy-start.11
  969.9 12.8 collective-permute-start.6
  971.6 12.5 collective-permute-start.7
  982.7 1.4 copy-start.6
  988.9 3.9 copy-start.7
  988.9 3.9 copy-start.16
  992.8 808.0 %copy-start.14 = (pred[256]{0:T(512)(128)(4,1)S(1)}, pred[256]{0:T(512)(128)(4,1)}, u32[]{:S(2)}) copy-start(pred[256]{0:T(512)(128)(4,1)} %copy-done.12) | copy-start | bytes 772
where the time goes:
time: 1810 us; the launch traced here: 1800 us
  local copies, waits for them, and re-layouts  895 us (49%)
  other arithmetic  723 us (40%)
  waiting for transfers between devices  103 us (6%)
  matrix products  46.9 us (3%)
  starting transfers between devices  20.6 us (1%)
    gather x2, local copies, waits for them, and re-layouts, sample(): samples = pulled[footprint_places(bricks, local_y)]  804 us
    scatter-add x2, other arithmetic, project(): spread.at[footprint_places(bricks, local_y).reshape(-1)]  700 us
    all_to_all x1, waiting for transfers between devices, body(): lax.all_to_all(paired, 'slab', split_axis=1, concat_axis=3, tiled=True)  45.1 us
    all_to_all x1, waiting for transfers between devices, body(): lax.all_to_all(paired, 'slab', split_axis=3, concat_axis=1, tiled=True)  44.2 us
  transfers between devices with their start and end apart: 14, of which 9 were waited for; matrix products, arithmetic and copies ran while one was open for 2% of the time, Pallas kernels for 0%

commit v1 on v0

v1 whole, which is shorter than its diff:
```python
import functools

import jax
import jax.numpy as jnp
import ml_dtypes
import numpy as np
from jax import lax
from jax.experimental import pallas as pl
from jax.experimental.pallas import tpu as pltpu
from jax.sharding import PartitionSpec as P

PANELS = 64
POINTS = 512
NY = 256
NZ = 512
KS = 16
KN = 16
LANES = 128
ZROWS = NZ + 8
UNROLL = 4
F32 = jnp.float32
BF16 = jnp.bfloat16
SMEM = pl.BlockSpec(memory_space=pltpu.SMEM)
VMEM = pl.BlockSpec(memory_space=pltpu.VMEM)
PARAMS = pltpu.CompilerParams(vmem_limit_bytes=48 * 1024 * 1024)


def halves(table):
    high = table.astype(ml_dtypes.bfloat16)
    low = (table - high.astype(np.float64)).astype(ml_dtypes.bfloat16)
    return high, low


def owner_frequencies(slabs, tiles):
    devices = slabs * tiles
    planes = NZ // devices
    owner = np.array([a * tiles + b for b in range(tiles) for a in range(slabs)])
    plane = np.arange(planes // 2)
    return (owner[None, :] * planes + plane[:, None] + (owner[None, :] >= devices // 2)).reshape(-1)


def z_tables(slabs, tiles):
    freq = owner_frequencies(slabs, tiles)
    cell = np.arange(NZ) - 2
    angle = (freq[:, None] * cell[None, :] % NZ) * (2 * np.pi / NZ)
    forward = np.concatenate([np.cos(angle), -np.sin(angle)], axis=0)
    weight = np.where(freq % NZ == 0, 1.0, 2.0)[:, None] / NZ
    inverse = np.concatenate([weight * np.cos(angle), -weight * np.sin(angle)], axis=0).T
    return forward, inverse


def y_tables(cells):
    angle = (np.arange(NY)[:, None] * np.arange(NY)[None, :] % NY) * (2 * np.pi / NY)
    cosine, sine = np.cos(angle), np.sin(angle)
    forward = np.block([[cosine, -sine], [sine, cosine]])
    inverse = np.block([[cosine, sine], [-sine, cosine]]) / cells
    return forward, inverse


def x_tables(length):
    angle = (np.arange(length)[:, None] * np.arange(length)[None, :] % length) * (2 * np.pi / length)
    cosine, sine = np.cos(angle), np.sin(angle)
    forward = np.block([[cosine, sine], [-sine, cosine]])
    inverse = np.block([[cosine, -sine], [sine, cosine]])
    return forward, inverse


def point_order():
    point = np.arange(POINTS)
    target = (point % 8) * 64 + point // 8
    table = np.zeros((POINTS, POINTS), ml_dtypes.bfloat16)
    table[point, target] = 1
    return table


def split(values):
    high = values.astype(BF16)
    return high, (values - high.astype(F32)).astype(BF16)


def dot(a, b):
    return jnp.dot(a, b, preferred_element_type=F32)


def dot3(a, b):
    return dot(a[0], b[0]) + (dot(a[0], b[1]) + dot(a[1], b[0]))


def lane_of(shape):
    return lax.broadcasted_iota(jnp.int32, shape, 1)


def by_kind(values, kinds):
    zero = jnp.zeros_like(values)
    return jnp.concatenate(
        [jnp.where(kinds == kind, values, zero) for kind in range(KS)], axis=0
    )


def footprints(charges_ref, kinds_ref, stk_ref, fp_ref, first, count):
    columns = slice(first, first + count)
    spread = by_kind(charges_ref[:, columns].astype(F32), kinds_ref[0:1, columns]).astype(BF16)
    for pair in range(4):
        part = lax.dot_general(
            spread,
            stk_ref[:, pair * LANES : (pair + 1) * LANES],
            (((0,), (0,)), ((), ())),
            preferred_element_type=F32,
        )
        fp_ref[pl.ds(first * 8 + 2 * pair, count, stride=8), :] = part
        fp_ref[pl.ds(first * 8 + 2 * pair + 1, count, stride=8), :] = pltpu.roll(part, 64, 1)


def scatter_columns(fp_ref, by_ref, bz_ref, grids, edge_ref, first, live, planes, shift_i):
    lane = lane_of((8, LANES))
    in_planes = (lane >= 8 * planes[0]) & (lane < 8 * (planes[-1] + 1))

    def step(index, carry):
        for inner in range(UNROLL):
            column = first + index * UNROLL + inner
            by = by_ref[column]
            row = 4 * bz_ref[column]
            value = fp_ref[pl.ds(pl.multiple_of(column * 8, 8), 8), :]
            begin = 4 * by - 2
            offset = lane - begin
            mask = (offset >= 0) & (offset < 8)
            for plane in planes:
                turned = pltpu.roll(value, (begin - 8 * (plane + shift_i) + 2 * LANES) & (LANES - 1), 1)
                where = pl.ds(row, 8)
                grids[plane][where, :] += jnp.where(mask, turned, 0.0)
            is_first = (by == 0).astype(jnp.int32)
            is_last = (by == NY // 8 - 1).astype(jnp.int32)
            turned = pltpu.roll(value, (2 * LANES - 8 * shift_i - 4 * is_last) & (LANES - 1), 1)
            low = jnp.where(is_first + is_last > 0, 2 * is_last, 8)
            place = (lane & 7) - low
            edge_ref[pl.ds(row, 8), :] += jnp.where(
                in_planes & (place >= 0) & (place < 2), turned, 0.0
            )
        return carry

    lax.fori_loop(0, (live + UNROLL - 1) // UNROLL, step, 0)


def sample_columns(pot_refs, edge_ref, by_ref, bz_ref, sp_ref, first, live, planes, shift_i):
    lane = lane_of((8, LANES))
    point_j = lane & 7

    def step(index, carry):
        for inner in range(UNROLL):
            column = first + index * UNROLL + inner
            by = by_ref[column]
            row = 4 * bz_ref[column]
            begin = 4 * by - 2
            result = jnp.zeros((8, LANES), F32)
            for plane in planes:
                low = 8 * (plane + shift_i)
                turned = pltpu.roll(
                    pot_refs[plane][pl.ds(row, 8), :], (low - begin + 2 * LANES) & (LANES - 1), 1
                )
                result = jnp.where((lane >= low) & (lane < low + 8), turned, result)
            is_first = (by == 0).astype(jnp.int32)
            is_last = (by == NY // 8 - 1).astype(jnp.int32)
            turned = pltpu.roll(
                edge_ref[pl.ds(row, 8), :], (8 * shift_i + 4 * is_last + 2 * LANES) & (LANES - 1), 1
            )
            low = jnp.where(is_first + is_last > 0, 6 * is_last, 8)
            place = point_j - low
            inside = (lane >= 8 * (planes[0] + shift_i)) & (lane < 8 * (planes[-1] + shift_i + 1))
            result = jnp.where(inside & (place >= 0) & (place < 2), turned, result)
            sp_ref[pl.ds(pl.multiple_of(column * 8, 8), 8), :] = result
        return carry

    lax.fori_loop(0, (live + UNROLL - 1) // UNROLL, step, 0)


def far_sums(sp_ref, kinds_ref, stk_ref, first, count):
    lane = lane_of((count, LANES))
    pairs = []
    for pair in range(4):
        even = sp_ref[pl.ds(first * 8 + 2 * pair, count, stride=8), :]
        odd = sp_ref[pl.ds(first * 8 + 2 * pair + 1, count, stride=8), :]
        pairs.append(jnp.where(lane < 64, even, pltpu.roll(odd, 64, 1)).astype(BF16))
    samples = jnp.concatenate(pairs, axis=1)
    sums = lax.dot_general(
        stk_ref[...], samples, (((1,), (1,)), ((), ())), preferred_element_type=F32
    )
    kinds = kinds_ref[0:1, first : first + count]
    result = jnp.zeros((PANELS, count), F32)
    for kind in range(KS):
        result += jnp.where(kinds == kind, sums[kind * PANELS : (kind + 1) * PANELS, :], 0.0)
    return result


def own_kernel(by_ref, bz_ref, live_ref, charges_ref, kinds_ref, stencil_ref, order_ref,
               g0, g1, g2, g3, edge_ref, stk_ref, fp_ref):
    stk_ref[...] = dot(stencil_ref[...], order_ref[...]).astype(BF16)
    for ref in (g0, g1, g2, g3, edge_ref):
        ref[...] = jnp.zeros_like(ref)
    slots = charges_ref.shape[1]
    live = live_ref[0]
    for first in range(0, slots, LANES):
        @pl.when(live > first)
        def _(first=first):
            footprints(charges_ref, kinds_ref, stk_ref, fp_ref, first, LANES)
    scatter_columns(fp_ref, by_ref, bz_ref, (g0, g1, g2, g3), edge_ref, 0, live, (0, 1, 2, 3), 2)


def beside_kernel(by_ref, bz_ref, live_ref, charges_ref, kinds_ref, stk_ref,
                  i0, i1, i2, i3, iedge, g0, g1, g2, g3, out_edge, edge_ref, fp_ref):
    for ref, source in ((g0, i0), (g1, i1), (g2, i2), (g3, i3), (edge_ref, iedge)):
        ref[...] = source[...]
    slots = charges_ref.shape[1] // 2
    for side in range(2):
        live = live_ref[side]
        for first in range(0, slots, LANES):
            @pl.when(live > first)
            def _(first=side * slots + first):
                footprints(charges_ref, kinds_ref, stk_ref, fp_ref, first, LANES)
    for side, planes, shift_i in ((0, (0, 1), 6), (1, (2, 3), -2)):
        scatter_columns(fp_ref, by_ref, bz_ref, (g0, g1, g2, g3), edge_ref,
                        side * slots, live_ref[side], planes, shift_i)
    edge_ref[0:8, :] += edge_ref[NZ:ZROWS, :]
    total = edge_ref[0:LANES, :]
    for block in range(1, 4):
        total += pltpu.roll(edge_ref[block * LANES : (block + 1) * LANES, :], 32 * block, 1)
    out_edge[...] = total


def z_kernel(owners, g0, g1, g2, g3, edge_ref, wh_ref, wl_ref, out_ref):
    lane = lane_of((LANES, LANES))
    at_edge = (lane < 2) | (lane >= LANES - 2)
    parts = NZ // owners
    for plane, grid in enumerate((g0, g1, g2, g3)):
        blocks = []
        for block in range(4):
            turned = pltpu.roll(edge_ref[...], (LANES - 2 - 32 * block - 8 * plane) % LANES, 1)
            blocks.append(
                grid[block * LANES : (block + 1) * LANES, :] + jnp.where(at_edge, turned, 0.0)
            )
        blocks[0] = jnp.concatenate([blocks[0][0:8] + grid[NZ:ZROWS, :], blocks[0][8:]], axis=0)
        values = split(jnp.concatenate(blocks, axis=0))
        result = dot3((wh_ref[...], wl_ref[...]), values)
        for part in range(parts):
            out_ref[pl.ds(plane * parts + part, owners, stride=4 * parts), :] = result[
                part * owners : (part + 1) * owners, :
            ]


def plane_kernel(length, planes, offset_ref, in_ref, hat_ref, yfh, yfl, yih, yil, xfh, xfl, xih, xil,
                 out_ref, ah_ref, al_ref):
    rows = planes * length
    offset = offset_ref[0]
    for part in range(2):
        for tile in range(2):
            block = slice((2 * part + tile) * LANES, (2 * part + tile + 1) * LANES)
            for plane in range(planes):
                values = in_ref[
                    pl.ds(tile * length * 2 * planes + part * planes + plane, length, stride=2 * planes), :
                ]
                high, low = split(values)
                ah_ref[plane * length : (plane + 1) * length, block] = high
                al_ref[plane * length : (plane + 1) * length, block] = low
    along_y = dot3((ah_ref[...], al_ref[...]), (yfh[...], yfl[...]))
    forward = (xfh[...], xfl[...])
    inverse = (xih[...], xil[...])
    for plane in range(planes):
        here = slice(plane * length, (plane + 1) * length)
        values = along_y[here, :]
        values = jnp.concatenate([values[:, :NY], values[:, NY:]], axis=0)
        values = dot3(forward, split(values))
        hat = hat_ref[offset + plane]
        values = values * jnp.concatenate([hat, hat], axis=0)
        values = dot3(inverse, split(values))
        high, low = split(values)
        ah_ref[here, 0:NY] = high[:length]
        ah_ref[here, NY : 2 * NY] = high[length:]
        al_ref[here, 0:NY] = low[:length]
        al_ref[here, NY : 2 * NY] = low[length:]
    result = dot3((ah_ref[...], al_ref[...]), (yih[...], yil[...]))
    for part in range(2):
        for tile in range(2):
            block = slice((2 * part + tile) * LANES, (2 * part + tile + 1) * LANES)
            for plane in range(planes):
                out_ref[
                    pl.ds(tile * length * 2 * planes + part * planes + plane, length, stride=2 * planes), :
                ] = result[plane * length : (plane + 1) * length, block]


def potential_kernel(owners, in_ref, vh_ref, vl_ref, p0, p1, p2, p3, edge_ref):
    parts = NZ // owners
    lane = lane_of((LANES, LANES))
    edge = jnp.zeros((LANES, LANES), F32)
    for plane, pot in enumerate((p0, p1, p2, p3)):
        values = split(jnp.concatenate(
            [in_ref[pl.ds(plane * parts + part, owners, stride=4 * parts), :] for part in range(parts)],
            axis=0,
        ))
        result = dot3((vh_ref[...], vl_ref[...]), values).astype(BF16).astype(F32)
        pot[0:NZ, :] = result
        pot[NZ:ZROWS, :] = result[0:8, :]
        for block in range(4):
            low = 32 * block + 8 * plane
            turned = pltpu.roll(result[block * LANES : (block + 1) * LANES, :], low + 2, 1)
            edge = jnp.where((lane >= low) & (lane < low + 4), turned, edge)
    edge_ref[...] = edge.astype(BF16)


def widen_edge(edge_ref, wide_ref):
    for block in range(4):
        wide_ref[block * LANES : (block + 1) * LANES, :] = pltpu.roll(
            edge_ref[...].astype(F32), (LANES - 32 * block) % LANES, 1
        )
    wide_ref[NZ:ZROWS, :] = wide_ref[0:8, :]


def sample_kernel(sides, by_ref, bz_ref, live_ref, p0, p1, p2, p3, edge_ref, kinds_ref, stk_ref,
                  out_ref, wide_ref, sp_ref):
    widen_edge(edge_ref, wide_ref)
    slots = kinds_ref.shape[1] // len(sides)
    for side, (planes, shift_i) in enumerate(sides):
        live = live_ref[side]
        sample_columns((p0, p1, p2, p3), wide_ref, by_ref, bz_ref, sp_ref,
                       side * slots, live, planes, shift_i)
        for first in range(0, slots, LANES):
            where = slice(side * slots + first, side * slots + first + LANES)

            @pl.when(live > first)
            def _(side=side, first=first, where=where, live=live):
                result = far_sums(sp_ref, kinds_ref, stk_ref, side * slots + first, LANES)
                column = first + lane_of((PANELS, LANES))
                out_ref[:, where] = jnp.where(column < live, result, 0.0)

            @pl.when(live <= first)
            def _(where=where):
                out_ref[:, where] = jnp.zeros((PANELS, LANES), F32)


def near_kernel(live_ref, pool_ref, source_ref, block_ref, table_ref, out_ref):
    live = live_ref[0]
    fanout, slots = source_ref.shape
    total = pool_ref.shape[1]
    for first in range(0, slots, LANES):
        where = slice(first, first + LANES)

        @pl.when(live > first)
        def _(where=where, first=first):
            index = lax.broadcasted_iota(jnp.int32, (total, LANES), 0)
            result = jnp.zeros((PANELS, LANES), F32)
            for j in range(fanout):
                chosen = jnp.where(index == source_ref[j : j + 1, where], 1.0, 0.0).astype(BF16)
                gathered = dot(pool_ref[...], chosen)
                result += dot(
                    table_ref[...], by_kind(gathered, block_ref[j : j + 1, where]).astype(BF16)
                )
            column = first + lane_of((PANELS, LANES))
            out_ref[:, where] = jnp.where(column < live, result, 0.0)

        @pl.when(live <= first)
        def _(where=where):
            out_ref[:, where] = jnp.zeros((PANELS, LANES), F32)


def shape_of(*dims, dtype=F32):
    return jax.ShapeDtypeStruct(dims, dtype)


def body(slabs, tiles, charges, live_count, slot_brick, slot_stencil, stencils, near_source,
         near_block, near_blocks, kernel_hat):
    slots = charges.shape[1]
    owners = slabs * tiles
    planes = kernel_hat.shape[0] // 2
    length = kernel_hat.shape[1]
    parts = NZ // owners
    axes = ("tile", "slab")
    both = ("slab", "tile")

    def moved(values, step, swap):
        pairs = [
            (a * tiles + b, (a + step) % slabs * tiles + (b + swap) % tiles)
            for a in range(slabs)
            for b in range(tiles)
        ]
        return lax.ppermute(values, both, pairs)

    live = live_count[0]
    slot = jnp.arange(slots, dtype=jnp.int32)
    held = jnp.where((slot < live)[None, :], charges, jnp.zeros((), charges.dtype))
    zbricks = NZ // 4
    brick_y = slot_brick // zbricks
    brick_z = slot_brick % zbricks
    facts = jnp.stack([brick_y, brick_z, slot_stencil, jnp.full((slots,), live)], axis=0)
    packed = jnp.concatenate(
        [held, facts.astype(BF16), jnp.zeros((12, slots), BF16)], axis=0
    )
    from_prev = moved(packed, 1, 0)
    from_next = moved(packed, -1, 0)

    grid = shape_of(ZROWS, LANES)
    g = pl.pallas_call(
        own_kernel,
        out_shape=(grid,) * 5 + (shape_of(KS * PANELS, POINTS, dtype=BF16),),
        in_specs=[SMEM] * 3 + [VMEM] * 4,
        out_specs=(VMEM,) * 6,
        scratch_shapes=[pltpu.VMEM((slots * 8, LANES), F32)],
        compiler_params=PARAMS,
        name="own_scatter",
    )(brick_y, brick_z, live_count, held, slot_stencil[None, :],
      stencils.reshape(KS * PANELS, POINTS), jnp.asarray(point_order()))
    grids, stk = g[:5], g[5]

    beside = jnp.concatenate([from_prev, from_next], axis=1)
    facts2 = beside[PANELS : PANELS + 4].astype(jnp.int32)
    by2, bz2, kinds2 = facts2[0], facts2[1], facts2[2:3]
    live2 = jnp.stack([facts2[3, 0], facts2[3, slots]])
    g = pl.pallas_call(
        beside_kernel,
        out_shape=(grid,) * 4 + (shape_of(LANES, LANES),),
        in_specs=[SMEM] * 3 + [VMEM] * 8,
        out_specs=(VMEM,) * 5,
        scratch_shapes=[pltpu.VMEM((ZROWS, LANES), F32), pltpu.VMEM((2 * slots * 8, LANES), F32)],
        compiler_params=PARAMS,
        name="beside_scatter",
    )(by2, bz2, live2, beside[:PANELS], kinds2, stk, *grids)
    edge = moved(g[4], 0, 1)

    forward, inverse = z_tables(slabs, tiles)
    sent = pl.pallas_call(
        functools.partial(z_kernel, owners),
        out_shape=shape_of(owners * 4 * parts, LANES),
        in_specs=[VMEM] * 7,
        out_specs=VMEM,
        compiler_params=PARAMS,
        name="z_forward",
    )(*g[:4], edge, *map(jnp.asarray, halves(forward)))

    def exchanged(values):
        values = values.reshape(owners, 4 * parts, LANES)
        return lax.all_to_all(values, axes, 0, 0, tiled=True).reshape(owners * 4 * parts, LANES)

    got = exchanged(sent)

    swapped = moved(held, 0, 1)
    pool = jnp.concatenate(
        [from_prev[:PANELS], moved(swapped, 1, 0), held, swapped, from_next[:PANELS], moved(swapped, -1, 0)],
        axis=1,
    )
    direction = near_source // slots
    pool_index = (direction // 3 * 2 + (direction % 3 != 1).astype(jnp.int32)) * slots + near_source % slots
    near = pl.pallas_call(
        near_kernel,
        out_shape=shape_of(PANELS, slots),
        in_specs=[SMEM] + [VMEM] * 4,
        out_specs=VMEM,
        compiler_params=PARAMS,
        name="near_field",
    )(live_count, pool, pool_index.T, near_block.T, near_blocks.reshape(PANELS, KN * PANELS))

    me = lax.axis_index("slab") * tiles + lax.axis_index("tile")
    offset = (me >= owners // 2).astype(jnp.int32)[None]
    y_forward, y_inverse = y_tables(length * NY)
    x_forward, x_inverse = x_tables(length)
    tables = [jnp.asarray(t) for pair in map(halves, (y_forward, y_inverse, x_forward, x_inverse)) for t in pair]
    back = pl.pallas_call(
        functools.partial(plane_kernel, length, planes),
        out_shape=shape_of(owners * 4 * parts, LANES),
        in_specs=[SMEM] + [VMEM] * 10,
        out_specs=VMEM,
        scratch_shapes=[pltpu.VMEM((planes * length, 2 * NY), BF16)] * 2,
        compiler_params=PARAMS,
        name="plane_filter",
    )(offset, got, kernel_hat, *tables)
    back = exchanged(back)

    pot = pl.pallas_call(
        functools.partial(potential_kernel, owners),
        out_shape=(grid,) * 4 + (shape_of(LANES, LANES, dtype=BF16),),
        in_specs=[VMEM] * 3,
        out_specs=(VMEM,) * 5,
        compiler_params=PARAMS,
        name="z_inverse",
    )(back, *map(jnp.asarray, halves(inverse)))
    edge = moved(pot[4], 0, 1)

    def sampled(sides, by, bz, counts, kinds, name):
        width = kinds.shape[1]
        return pl.pallas_call(
            functools.partial(sample_kernel, sides),
            out_shape=shape_of(PANELS, width),
            in_specs=[SMEM] * 3 + [VMEM] * 7,
            out_specs=VMEM,
            scratch_shapes=[pltpu.VMEM((ZROWS, LANES), F32), pltpu.VMEM((width * 8, LANES), F32)],
            compiler_params=PARAMS,
            name=name,
        )(by, bz, counts, *pot[:4], edge, kinds, stk)

    others = sampled((((0, 1), 6), ((2, 3), -2)), by2, bz2, live2, kinds2, "beside_sample")
    to_prev = moved(others[:, :slots], -1, 0)
    to_next = moved(others[:, slots:], 1, 0)
    own = sampled((((0, 1, 2, 3), 2),), brick_y, brick_z, live_count, slot_stencil[None, :], "own_sample")
    return own + near + to_prev + to_next


def solution(mesh):
    both = ("slab", "tile")
    in_specs = (
        P(None, both),
        P(both),
        P(both),
        P(both),
        P(),
        P(both, None),
        P(both, None),
        P(),
        P(both, None, None),
    )
    return jax.shard_map(
        functools.partial(body, mesh.shape["slab"], mesh.shape["tile"]),
        mesh=mesh,
        in_specs=in_specs,
        out_specs=P(None, both),
        check_vma=False,
    )
```

time: 1810 us -> 131 us (0.07)
  the two profiles are of different devices: /device:TPU:10 before, /device:TPU:0 now
where the time goes in v1:
time: 131 us
  waiting for transfers between devices  50 us (38%)
  Pallas kernels  42.2 us (32%)
  starting transfers between devices  20.5 us (16%)
  local copies, waits for them, and re-layouts  13.3 us (10%)
  other arithmetic  3.61 us (3%)
    all_to_all x2, waiting for transfers between devices, exchanged(): lax.all_to_all(values, axes, 0, 0, tiled=True)  31 us
    ppermute x9, waiting for transfers between devices, moved(): return lax.ppermute(values, both, pairs)  19 us
    ppermute x9, starting transfers between devices, moved(): return lax.ppermute(values, both, pairs)  15 us
    pallas_call x2, Pallas kernels, sampled(): pl.pallas_call(functools.partial(sample_kernel, sides), out_shape=shape_o...  14.6 us
    pallas_call x1, Pallas kernels, body(): pl.pallas_call(beside_kernel, out_shape=(grid,) * 4 + (shape_of(LANES, LA...  10.7 us
    unnamed x49, local copies, waits for them, and re-layouts  10.6 us
    all_to_all x2, starting transfers between devices, exchanged(): lax.all_to_all(values, axes, 0, 0, tiled=True)  5.57 us
    pallas_call x1, Pallas kernels, body(): pl.pallas_call(own_kernel, out_shape=(grid,) * 5 + (shape_of(KS * PANELS,...  4.79 us
  transfers between devices with their start and end apart: 11, of which 5 were waited for; matrix products, arithmetic and copies ran while one was open for 3% of the time, Pallas kernels for 18%

profile of v1, /device:TPU:0, one launch (start us, length us, event | category | flops | bytes accessed | tf_op | source)
XLA Modules:
  0.0 130.6 jit_solution(13532260183074907783)
XLA Ops:
  0.7 0.7 copy-done.15
  1.4 0.7 copy-done.21
  2.1 0.8 broadcast_select_fusion.charges_ref
  2.9 0.2 concatenate.10
  3.0 3.0 %collective-permute-start = (bf16[80,256]{1,0:T(8,128)(2,1)S(1)}, bf16[80,256]{1,0:T(8,128)(2,1)S(1)}, u32[]{:S(2)}, u32[]{:S(2)}) collective-permute-start(bf16[80,256]{1,0:T(8,128)(2,1)S(1)} %concatenate.10), channel_id=1, source_target_pairs={{0,2},{1,3},{2,4},{3,5},{4,6},{5,7},{6,8},{7,9},{8,10},{9,11},{10,... | collective-permute-start | bytes 122888 | tf_op jit(solution)/shard_map/ppermute | solution.py:383
  6.0 4.1 %collective-permute-start.1 = (bf16[80,256]{1,0:T(8,128)(2,1)S(1)}, bf16[80,256]{1,0:T(8,128)(2,1)S(1)}, u32[]{:S(2)}, u32[]{:S(2)}) collective-permute-start(bf16[80,256]{1,0:T(8,128)(2,1)S(1)} %concatenate.10), channel_id=1, source_target_pairs={{0,30},{1,31},{2,0},{3,1},{4,2},{5,3},{6,4},{7,5},{8,6},{9,7},{10,... | collective-permute-start | bytes 122888 | tf_op jit(solution)/shard_map/ppermute | solution.py:383
  10.1 1.2 copy-done
  11.3 1.0 copy-done.6
  12.3 4.8 %own_scatter.1 = (f32[520,128]{1,0:T(8,128)S(1)}, f32[520,128]{1,0:T(8,128)S(1)}, f32[520,128]{1,0:T(8,128)S(1)}, f32[520,128]{1,0:T(8,128)S(1)}, f32[520,128]{1,0:T(8,128)S(1)}, /*index=5*/bf16[1024,512]{1,0:T(8,128)(2,1)S(1)}) custom-call(s32[256]{0:T(256)S(1)} %get-tuple-element.49.by_ref, s32[256]{0:T(256)S(1)} %get-tuple-element.38.bz_ref, ...), custom_call_target="tpu_custom_call" | custom-call | tf_op jit(solution)/shard_map/own_scatter/pallas_call | solution.py:399
  17.1 0.0 copy-start.19
  17.2 0.6 copy-done.19
  17.8 0.6 copy-done.17
  18.4 0.6 fusion.12
  19.0 1.4 %pad_add_fusion.live_ref = s32[2]{0:T(128)S(1)} fusion(s32[1]{0:T(128)} %bitcast.6, s32[1]{0:T(128)} %bitcast.5), kind=kLoop, calls=%fused_computation.35 | loop fusion | flops 2 | bytes 16 | tf_op jit(solution)/shard_map/stack | solution.py:414
  20.4 10.7 %beside_scatter.1 = (f32[520,128]{1,0:T(8,128)S(1)}, f32[520,128]{1,0:T(8,128)S(1)}, f32[520,128]{1,0:T(8,128)S(1)}, f32[520,128]{1,0:T(8,128)S(1)}, f32[128,128]{1,0:T(8,128)S(1)}) custom-call(s32[512]{0:T(512)S(1)} %bitcast.22, s32[512]{0:T(512)S(1)} %bitcast.20, s32[2]{0:T(128)S(1)} %pad_add_fusion.live_ref, bf16[64,512]{1,0:T(8,128)(2,1)S(1)} %slice.49.charges_ref, ...), custom_call_target="tpu_custom_call" | custom-call | tf_op jit(solution)/shard_map/beside_scatter/pallas_call | solution.py:415
  31.1 0.1 collective-permute-start.2
  31.2 1.2 collective-permute-done.2.edge_ref
  32.4 3.5 %z_forward.1 = f32[2048,128]{1,0:T(8,128)} custom-call(f32[520,128]{1,0:T(8,128)S(1)} %get-tuple-element.27.g0, f32[520,128]{1,0:T(8,128)S(1)} %get-tuple-element.28.g1, f32[520,128]{1,0:T(8,128)S(1)} %get-tuple-element.29.g2, f32[520,128]{1,0:T(8,128)S(1)} %get-tuple-element.30.g3, f32[128,128]{1,0:T(8,128)S(1)} %collective-permute-done.2.edge_ref, ...), custom_call_target="tpu_custom_call" | custom-call | tf_op jit(solution)/shard_map/z_forward/pallas_call | solution.py:427
  35.9 0.0 copy-start.14
  36.0 2.8 %all-to-all-start = ((f32[32,64,128]{2,1,0:T(8,128)}), f32[32,64,128]{2,1,0:T(8,128)S(1)}, u32[]{:S(2)}, u32[]{:S(2)}) async-start(f32[32,64,128]{2,1,0:T(8,128)} %bitcast.8), calls=%async_computation | async-start | bytes 2097152 | tf_op jit(solution)/shard_map/all_to_all | solution.py:438
  38.8 28.1 %all-to-all-done = f32[32,64,128]{2,1,0:T(8,128)S(1)} async-done(((f32[32,64,128]{2,1,0:T(8,128)}), f32[32,64,128]{2,1,0:T(8,128)S(1)}, u32[]{:S(2)}, u32[]{:S(2)}) %all-to-all-start) | async-done | bytes 1048608 | tf_op jit(solution)/shard_map/all_to_all | solution.py:438
  66.9 0.0 copy-start.7
  66.9 1.0 copy-done.7
  67.9 1.0 copy-done.8
  68.9 1.0 copy-done.9
  70.0 1.0 copy-done.10
  71.0 4.5 %plane_filter.1 = f32[2048,128]{1,0:T(8,128)} custom-call(s32[1]{0:T(128)} %bitcast.offset_ref, f32[2048,128]{1,0:T(8,128)S(1)} %bitcast.18, f32[16,64,256]{2,1,0:T(8,128)S(1)} %copy-done.1, bf16[512,512]{1,0:T(8,128)(2,1)S(1)} %copy-done.10, bf16[512,512]{1,0:T(8,128)(2,1)S(1)} %copy-done.9, bf16[512,512]{1,0:T(8,128)(2,1)S(1)} %copy-done.8, ...), custom_call_target="tpu_custom_call" | custom-call | tf_op jit(solution)/shard_map/plane_filter/pallas_call | solution.py:463
  75.5 2.8 %all-to-all-start.1 = ((f32[32,64,128]{2,1,0:T(8,128)}), f32[32,64,128]{2,1,0:T(8,128)S(1)}, u32[]{:S(2)}, u32[]{:S(2)}) async-start(f32[32,64,128]{2,1,0:T(8,128)} %bitcast.10), calls=%async_computation.1 | async-start | bytes 2097152 | tf_op jit(solution)/shard_map/all_to_all | solution.py:438
  78.3 0.0 copy-start.4
  78.3 0.2 collective-permute-start.4
  78.5 1.1 reshape.27.table_ref
  79.7 0.0 collective-permute-done.4
  79.7 5.5 %collective-permute-start.6 = (bf16[64,256]{1,0:T(8,128)(2,1)}, bf16[64,256]{1,0:T(8,128)(2,1)}, u32[]{:S(2)}, u32[]{:S(2)}) collective-permute-start(bf16[64,256]{1,0:T(8,128)(2,1)} %collective-permute-done.4), channel_id=1, source_target_pairs={{0,30},{1,31},{2,0},{3,1},{4,2},{5,3},{6,4},{7,5},{8,6},{9,7},{10,... | collective-permute-start | bytes 98312 | tf_op jit(solution)/shard_map/ppermute | solution.py:383
  85.3 0.8 slice_dynamic-update-slice_fusion.1
  86.0 16.5 %collective-permute-done.5 = bf16[64,256]{1,0:T(8,128)(2,1)S(1)} collective-permute-done((bf16[64,256]{1,0:T(8,128)(2,1)}, bf16[64,256]{1,0:T(8,128)(2,1)S(1)}, u32[]{:S(2)}, u32[]{:S(2)}) %collective-permute-start.5) | collective-permute-done | bytes 32800 | tf_op jit(solution)/shard_map/ppermute | solution.py:383
  102.6 0.8 constant_dynamic-update-slice_fusion.4
  103.3 0.8 constant_dynamic-update-slice_fusion.3
  104.1 3.0 %all-to-all-done.1 = f32[32,64,128]{2,1,0:T(8,128)S(1)} async-done(((f32[32,64,128]{2,1,0:T(8,128)}), f32[32,64,128]{2,1,0:T(8,128)S(1)}, u32[]{:S(2)}, u32[]{:S(2)}) %all-to-all-start.1) | async-done | bytes 1048608 | tf_op jit(solution)/shard_map/all_to_all | solution.py:438
  107.1 2.1 %z_inverse.1 = (f32[520,128]{1,0:T(8,128)S(1)}, f32[520,128]{1,0:T(8,128)S(1)}, f32[520,128]{1,0:T(8,128)S(1)}, f32[520,128]{1,0:T(8,128)S(1)}, bf16[128,128]{1,0:T(8,128)(2,1)S(1)}) custom-call(f32[2048,128]{1,0:T(8,128)S(1)} %bitcast.17, bf16[512,512]{1,0:T(8,128)(2,1)S(1)} %copy-done.5, bf16[512,512]{1,0:T(8,128)(2,1)S(1)} %copy-done.4), custom_call_target="tpu_custom_call" | custom-call | tf_op jit(solution)/shard_map/z_inverse/pallas_call | solution.py:474
  109.2 0.1 collective-permute-start.3
  109.3 1.2 collective-permute-done.3.edge_ref
  110.5 10.4 %beside_sample.1 = f32[64,512]{1,0:T(8,128)S(1)} custom-call(s32[512]{0:T(512)S(1)} %bitcast.23, s32[512]{0:T(512)S(1)} %bitcast.21, s32[2]{0:T(128)S(1)} %pad_add_fusion.live_ref, f32[520,128]{1,0:T(8,128)S(1)} %get-tuple-element.32.p0, f32[520,128]{1,0:T(8,128)S(1)} %get-tuple-element.33.p1, f32[520,128]{1,0:T(8,128)S(1)} %get-tuple-element.34.p2, ...), custom_call_target="tpu_custom_call" | custom-call | tf_op jit(solution)/shard_map/beside_sample/pallas_call | solution.py:486
  120.9 0.1 collective-permute-start.7
  121.0 2.0 %collective-permute-start.8 = (f32[64,256]{1,0:T(8,128)S(1)}, f32[64,256]{1,0:T(8,128)S(1)}, u32[]{:S(2)}, u32[]{:S(2)}) collective-permute-start(f32[64,256]{1,0:T(8,128)S(1)} %get-tuple-element.42), channel_id=1, source_target_pairs={{0,2},{1,3},{2,4},{3,5},{4,6},{5,7},{6,8},{7,9},{8,10},{9,11},{10,... | collective-permute-start | bytes 196616 | tf_op jit(solution)/shard_map/ppermute | solution.py:383
  123.0 0.8 constant_dynamic-update-slice_fusion.2.pool_ref
  123.7 2.0 %near_field.1 = f32[64,256]{1,0:T(8,128)S(1)} custom-call(s32[1]{0:T(128)} %copy.29.live_ref, bf16[64,1536]{1,0:T(8,128)(2,1)S(1)} %constant_dynamic-update-slice_fusion.2.pool_ref, s32[8,256]{1,0:T(8,128)S(1)} %fusion.4.source_ref, s32[8,256]{1,0:T(8,128)S(1)} %bitcast.27, bf16[64,1024]{1,0:T(8,128)(2,1)S(1)} %reshape.27.table_ref), custom_call_target="tpu_custom_call" | custom-call | tf_op jit(solution)/shard_map/near_field/pallas_call | solution.py:449
  125.7 4.2 %own_sample.1 = f32[64,256]{1,0:T(8,128)S(1)} custom-call(s32[256]{0:T(256)S(1)} %get-tuple-element.49.by_ref, s32[256]{0:T(256)S(1)} %get-tuple-element.38.bz_ref, s32[1]{0:T(128)} %copy.29.live_ref, f32[520,128]{1,0:T(8,128)S(1)} %get-tuple-element.32.p0, f32[520,128]{1,0:T(8,128)S(1)} %get-tuple-element.33.p1, f32[520,128]{1,0:T(8,128)S(1)} %get-tuple-element.34.p2, ...), custom_call_target="tpu_custom_call" | custom-call | tf_op jit(solution)/shard_map/own_sample/pallas_call | solution.py:486
  130.0 0.6 add_add_fusion
  (52 shorter events, 0.2 us)
Async XLA Ops:
  0.7 0.7 copy-start.15
  1.4 0.7 copy-start.21
  3.0 14.1 %collective-permute-start = (bf16[80,256]{1,0:T(8,128)(2,1)S(1)}, bf16[80,256]{1,0:T(8,128)(2,1)S(1)}, u32[]{:S(2)}, u32[]{:S(2)}) collective-permute-start(bf16[80,256]{1,0:T(8,128)(2,1)S(1)} %concatenate.10), channel_id=1, source_target_pairs={{0,2},{1,3},{2,4},{3,5},{4,6},{5,7},{6,8},{7,9},{8,10},{9,11},{10,... | collective-permute-start | bytes 122888 | tf_op jit(solution)/shard_map/ppermute | solution.py:383
  6.0 11.8 %collective-permute-start.1 = (bf16[80,256]{1,0:T(8,128)(2,1)S(1)}, bf16[80,256]{1,0:T(8,128)(2,1)S(1)}, u32[]{:S(2)}, u32[]{:S(2)}) collective-permute-start(bf16[80,256]{1,0:T(8,128)(2,1)S(1)} %concatenate.10), channel_id=1, source_target_pairs={{0,30},{1,31},{2,0},{3,1},{4,2},{5,3},{6,4},{7,5},{8,6},{9,7},{10,... | collective-permute-start | bytes 122888 | tf_op jit(solution)/shard_map/ppermute | solution.py:383
  10.1 1.2 copy-start
  11.3 1.0 copy-start.6
  17.1 0.6 copy-start.19
  17.8 0.6 copy-start.17
  20.4 12.0 %copy-start.2 = (bf16[512,512]{1,0:T(8,128)(2,1)S(1)}, bf16[512,512]{1,0:T(8,128)(2,1)}, u32[]{:S(2)}) copy-start(bf16[512,512]{1,0:T(8,128)(2,1)} %constant.111.clone.wl_ref) | copy-start | bytes 1572868
  20.4 12.0 %copy-start.3 = (bf16[512,512]{1,0:T(8,128)(2,1)S(1)}, bf16[512,512]{1,0:T(8,128)(2,1)}, u32[]{:S(2)}) copy-start(bf16[512,512]{1,0:T(8,128)(2,1)} %constant.110.clone.wh_ref) | copy-start | bytes 1572868
  31.1 1.3 %collective-permute-start.2 = (f32[128,128]{1,0:T(8,128)S(1)}, f32[128,128]{1,0:T(8,128)S(1)}, u32[]{:S(2)}, u32[]{:S(2)}) collective-permute-start(f32[128,128]{1,0:T(8,128)S(1)} %get-tuple-element.31), channel_id=1, source_target_pairs={{0,1},{1,0},{2,3},{3,2},{4,5},{5,4},{6,7},{7,6},{8,9},{9,8},{10,11... | collective-permute-start | bytes 196616 | tf_op jit(solution)/shard_map/ppermute | solution.py:383
  35.9 30.9 %copy-start.1 = (f32[16,64,256]{2,1,0:T(8,128)S(1)}, f32[16,64,256]{2,1,0:T(8,128)}, u32[]{:S(2)}) copy-start(f32[16,64,256]{2,1,0:T(8,128)} %hat_ref.1) | copy-start | bytes 3145732
  35.9 30.9 %copy-start.11 = (bf16[128,128]{1,0:T(8,128)(2,1)S(1)}, bf16[128,128]{1,0:T(8,128)(2,1)}, u32[]{:S(2)}) copy-start(bf16[128,128]{1,0:T(8,128)(2,1)} %constant.119.clone.xil) | copy-start | bytes 98308
  35.9 30.9 %copy-start.12 = (bf16[128,128]{1,0:T(8,128)(2,1)S(1)}, bf16[128,128]{1,0:T(8,128)(2,1)}, u32[]{:S(2)}) copy-start(bf16[128,128]{1,0:T(8,128)(2,1)} %constant.118.clone.xih) | copy-start | bytes 98308
  35.9 30.9 %copy-start.13 = (bf16[128,128]{1,0:T(8,128)(2,1)S(1)}, bf16[128,128]{1,0:T(8,128)(2,1)}, u32[]{:S(2)}) copy-start(bf16[128,128]{1,0:T(8,128)(2,1)} %constant.117.clone.xfl) | copy-start | bytes 98308
  35.9 30.9 %copy-start.14 = (bf16[128,128]{1,0:T(8,128)(2,1)S(1)}, bf16[128,128]{1,0:T(8,128)(2,1)}, u32[]{:S(2)}) copy-start(bf16[128,128]{1,0:T(8,128)(2,1)} %constant.116.clone.xfh) | copy-start | bytes 98308
  36.0 30.9 %all-to-all-start = ((f32[32,64,128]{2,1,0:T(8,128)}), f32[32,64,128]{2,1,0:T(8,128)S(1)}, u32[]{:S(2)}, u32[]{:S(2)}) async-start(f32[32,64,128]{2,1,0:T(8,128)} %bitcast.8), calls=%async_computation | async-start | bytes 2097152 | tf_op jit(solution)/shard_map/all_to_all | solution.py:438
  66.9 1.0 copy-start.7
  67.9 1.0 copy-start.8
  68.9 1.0 copy-start.9
  70.0 1.0 copy-start.10
  75.5 3.0 %copy-start.20 = (s32[256,8]{0,1:T(8,128)S(1)}, s32[256,8]{0,1:T(8,128)}, u32[]{:S(2)}) copy-start(s32[256,8]{0,1:T(8,128)} %param.27) | copy-start | bytes 24580
  75.5 31.6 %copy-start.5 = (bf16[512,512]{1,0:T(8,128)(2,1)S(1)}, bf16[512,512]{1,0:T(8,128)(2,1)}, u32[]{:S(2)}) copy-start(bf16[512,512]{1,0:T(8,128)(2,1)} %constant.120.clone.vh_ref) | copy-start | bytes 1572868
  75.5 31.6 %all-to-all-start.1 = ((f32[32,64,128]{2,1,0:T(8,128)}), f32[32,64,128]{2,1,0:T(8,128)S(1)}, u32[]{:S(2)}, u32[]{:S(2)}) async-start(f32[32,64,128]{2,1,0:T(8,128)} %bitcast.10), calls=%async_computation.1 | async-start | bytes 2097152 | tf_op jit(solution)/shard_map/all_to_all | solution.py:438
  78.3 28.8 %copy-start.4 = (bf16[512,512]{1,0:T(8,128)(2,1)S(1)}, bf16[512,512]{1,0:T(8,128)(2,1)}, u32[]{:S(2)}) copy-start(bf16[512,512]{1,0:T(8,128)(2,1)} %constant.121.clone.vl_ref) | copy-start | bytes 1572868
  78.3 1.4 %collective-permute-start.4 = (bf16[64,256]{1,0:T(8,128)(2,1)S(1)}, bf16[64,256]{1,0:T(8,128)(2,1)}, u32[]{:S(2)}, u32[]{:S(2)}) collective-permute-start(bf16[64,256]{1,0:T(8,128)(2,1)S(1)} %broadcast_select_fusion.charges_ref), channel_id=1, source_target_pairs={{0,1},{1,0},{2,3},{3,2},{4,5},{5,4},{6,7},{7,6},{8,9},{9,8},{10,11... | collective-permute-start | bytes 98312 | tf_op jit(solution)/shard_map/ppermute | solution.py:383
  79.7 43.2 %collective-permute-start.6 = (bf16[64,256]{1,0:T(8,128)(2,1)}, bf16[64,256]{1,0:T(8,128)(2,1)}, u32[]{:S(2)}, u32[]{:S(2)}) collective-permute-start(bf16[64,256]{1,0:T(8,128)(2,1)} %collective-permute-done.4), channel_id=1, source_target_pairs={{0,30},{1,31},{2,0},{3,1},{4,2},{5,3},{6,4},{7,5},{8,6},{9,7},{10,... | collective-permute-start | bytes 98312 | tf_op jit(solution)/shard_map/ppermute | solution.py:383
  85.3 17.3 %collective-permute-start.5 = (bf16[64,256]{1,0:T(8,128)(2,1)}, bf16[64,256]{1,0:T(8,128)(2,1)S(1)}, u32[]{:S(2)}, u32[]{:S(2)}) collective-permute-start(bf16[64,256]{1,0:T(8,128)(2,1)} %collective-permute-done.4), channel_id=1, source_target_pairs={{0,2},{1,3},{2,4},{3,5},{4,6},{5,7},{6,8},{7,9},{8,10},{9,11},{10,... | collective-permute-start | bytes 98312 | tf_op jit(solution)/shard_map/ppermute | solution.py:383
  107.1 2.2 %copy-start.18 = (bf16[80,256]{1,0:T(8,128)(2,1)S(1)}, bf16[80,256]{1,0:T(8,128)(2,1)}, u32[]{:S(2)}) copy-start(bf16[80,256]{1,0:T(8,128)(2,1)} %copy-done.17) | copy-start | bytes 122884
  109.2 1.3 collective-permute-start.3
  120.9 9.1 %collective-permute-start.7 = (f32[64,256]{1,0:T(8,128)S(1)}, f32[64,256]{1,0:T(8,128)S(1)}, u32[]{:S(2)}, u32[]{:S(2)}) collective-permute-start(f32[64,256]{1,0:T(8,128)S(1)} %get-tuple-element.41), channel_id=1, source_target_pairs={{0,30},{1,31},{2,0},{3,1},{4,2},{5,3},{6,4},{7,5},{8,6},{9,7},{10,... | collective-permute-start | bytes 196616 | tf_op jit(solution)/shard_map/ppermute | solution.py:383
  120.9 2.8 %copy-start.16 = (s32[256,8]{0,1:T(8,128)S(1)}, s32[256,8]{0,1:T(8,128)}, u32[]{:S(2)}) copy-start(s32[256,8]{0,1:T(8,128)} %param.28) | copy-start | bytes 24580
  121.0 9.0 %collective-permute-start.8 = (f32[64,256]{1,0:T(8,128)S(1)}, f32[64,256]{1,0:T(8,128)S(1)}, u32[]{:S(2)}, u32[]{:S(2)}) collective-permute-start(f32[64,256]{1,0:T(8,128)S(1)} %get-tuple-element.42), channel_id=1, source_target_pairs={{0,2},{1,3},{2,4},{3,5},{4,6},{5,7},{6,8},{7,9},{8,10},{9,11},{10,... | collective-permute-start | bytes 196616 | tf_op jit(solution)/shard_map/ppermute | solution.py:383

commit v2 on v1

v2 whole, which is shorter than its diff:
```python
import functools

import jax
import jax.numpy as jnp
import ml_dtypes
import numpy as np
from jax import lax
from jax.experimental import pallas as pl
from jax.experimental.pallas import tpu as pltpu
from jax.sharding import PartitionSpec as P

PANELS = 64
POINTS = 512
NY = 256
NZ = 512
KS = 16
KN = 16
LANES = 128
ZROWS = NZ + 8
UNROLL = 8
SCALE_ROWS = 8
F32 = jnp.float32
BF16 = jnp.bfloat16
SMEM = pl.BlockSpec(memory_space=pltpu.SMEM)
VMEM = pl.BlockSpec(memory_space=pltpu.VMEM)
PARAMS = pltpu.CompilerParams(vmem_limit_bytes=48 * 1024 * 1024)


def halves(*tables):
    parts = []
    for table in tables:
        high = table.astype(ml_dtypes.bfloat16)
        parts += [high, (table - high.astype(np.float64)).astype(ml_dtypes.bfloat16)]
    return np.concatenate(parts, axis=0)


def owner_frequencies(slabs, tiles):
    devices = slabs * tiles
    planes = NZ // devices
    owner = np.array([a * tiles + b for b in range(tiles) for a in range(slabs)])
    plane = np.arange(planes // 2)
    return (owner[None, :] * planes + plane[:, None] + (owner[None, :] >= devices // 2)).reshape(-1)


def z_tables(slabs, tiles):
    freq = owner_frequencies(slabs, tiles)
    cell = np.arange(NZ) - 2
    angle = (freq[:, None] * cell[None, :] % NZ) * (2 * np.pi / NZ)
    forward = np.concatenate([np.cos(angle), -np.sin(angle)], axis=0)
    weight = np.where(freq % NZ == 0, 1.0, 2.0)[:, None] / NZ
    inverse = np.concatenate([weight * np.cos(angle), -weight * np.sin(angle)], axis=0).T
    return forward, inverse


def y_table():
    angle = (np.arange(NY)[:, None] * np.arange(NY)[None, :] % NY) * (2 * np.pi / NY)
    return np.concatenate([np.cos(angle), np.sin(angle)], axis=1)


def x_tables(slabs):
    length = 4 * slabs
    cell = (np.arange(4)[:, None] + 4 * np.arange(slabs)[None, :]).reshape(-1)
    angle = (np.arange(length)[:, None] * cell[None, :] % length) * (2 * np.pi / length)
    cosine, sine = np.cos(angle), np.sin(angle)
    forward = np.block([[cosine, sine], [-sine, cosine]])
    inverse = np.block([[cosine.T, -sine.T], [sine.T, cosine.T]])
    return forward, inverse


def point_order():
    point = np.arange(POINTS)
    target = (point % 8) * 64 + point // 8
    table = np.zeros((POINTS, POINTS), ml_dtypes.bfloat16)
    table[point, target] = 1
    return table


def split(values):
    high = values.astype(BF16)
    return high, (values - high.astype(F32)).astype(BF16)


def dot(a, b):
    return jnp.dot(a, b, preferred_element_type=F32)


def dot3(a, b):
    return dot(a[0], b[0]) + (dot(a[0], b[1]) + dot(a[1], b[0]))


def lane_of(shape):
    return lax.broadcasted_iota(jnp.int32, shape, 1)


def by_kind(values, kinds):
    zero = jnp.zeros_like(values)
    return jnp.concatenate(
        [jnp.where(kinds == kind, values, zero) for kind in range(KS)], axis=0
    )


def footprints(charges, kinds, stk_ref, fp_ref, first):
    count = charges.shape[1]
    spread = by_kind(charges.astype(F32), kinds).astype(BF16)
    for pair in range(4):
        part = lax.dot_general(
            spread,
            stk_ref[:, pair * LANES : (pair + 1) * LANES],
            (((0,), (0,)), ((), ())),
            preferred_element_type=F32,
        )
        fp_ref[pl.ds(first * 8 + 2 * pair, count, stride=8), :] = part
        fp_ref[pl.ds(first * 8 + 2 * pair + 1, count, stride=8), :] = pltpu.roll(part, 64, 1)


def scatter_columns(fp_ref, place_of, grids, edge_ref, first, live, planes, shift_i):
    lane = lane_of((8, LANES))
    in_planes = (lane >= 8 * planes[0]) & (lane < 8 * (planes[-1] + 1))
    point_j = lane & 7

    def step(index, carry):
        updates = []
        for inner in range(UNROLL):
            column = first + index * UNROLL + inner
            by, bz = place_of(column)
            value = fp_ref[pl.ds(pl.multiple_of(column * 8, 8), 8), :]
            begin = 4 * by - 2
            mask = ((lane - begin) & -8) == 0
            terms = []
            for plane in planes:
                turned = pltpu.roll(value, (begin - 8 * (plane + shift_i)) & (LANES - 1), 1)
                terms.append(jnp.where(mask, turned, 0.0))
            is_last = (by == NY // 8 - 1).astype(jnp.int32)
            low = jnp.where(by == 0, 0, jnp.where(by == NY // 8 - 1, 2, 8))
            turned = pltpu.roll(value, (-8 * shift_i - 4 * is_last) & (LANES - 1), 1)
            mask = in_planes & (((point_j - low) & -2) == 0)
            terms.append(jnp.where(mask, turned, 0.0))
            updates.append((pl.ds(4 * bz, 8), terms))
        refs = [grids[plane] for plane in planes] + [edge_ref]
        for where, terms in updates:
            sums = [ref[where, :] + term for ref, term in zip(refs, terms)]
            for ref, total in zip(refs, sums):
                ref[where, :] = total
        return carry

    lax.fori_loop(0, (live + UNROLL - 1) // UNROLL, step, 0)


def sample_columns(pot_refs, edge_ref, place_of, sp_ref, first, live, planes, shift_i):
    lane = lane_of((8, LANES))
    point_j = lane & 7
    inside = (lane >= 8 * (planes[0] + shift_i)) & (lane < 8 * (planes[-1] + shift_i + 1))

    def step(index, carry):
        results = []
        for inner in range(UNROLL):
            column = first + index * UNROLL + inner
            by, bz = place_of(column)
            where = pl.ds(4 * bz, 8)
            begin = 4 * by - 2
            result = jnp.zeros((8, LANES), F32)
            for plane in planes:
                low = 8 * (plane + shift_i)
                turned = pltpu.roll(pot_refs[plane][where, :], (low - begin) & (LANES - 1), 1)
                result = jnp.where(((lane - low) & -8) == 0, turned, result)
            is_last = (by == NY // 8 - 1).astype(jnp.int32)
            low = jnp.where(by == 0, 0, jnp.where(by == NY // 8 - 1, 6, 8))
            turned = pltpu.roll(edge_ref[where, :], (8 * shift_i + 4 * is_last) & (LANES - 1), 1)
            mask = inside & (((point_j - low) & -2) == 0)
            results.append((pl.ds(pl.multiple_of(column * 8, 8), 8), jnp.where(mask, turned, result)))
        for where, result in results:
            sp_ref[where, :] = result
        return carry

    lax.fori_loop(0, (live + UNROLL - 1) // UNROLL, step, 0)


def far_sums(sp_ref, kinds, stk_ref, first):
    count = kinds.shape[1]
    lane = lane_of((count, LANES))
    pairs = []
    for pair in range(4):
        even = sp_ref[pl.ds(first * 8 + 2 * pair, count, stride=8), :]
        odd = sp_ref[pl.ds(first * 8 + 2 * pair + 1, count, stride=8), :]
        pairs.append(jnp.where(lane < 64, even, pltpu.roll(odd, 64, 1)).astype(BF16))
    samples = jnp.concatenate(pairs, axis=1)
    sums = lax.dot_general(
        stk_ref[...], samples, (((1,), (1,)), ((), ())), preferred_element_type=F32
    )
    result = jnp.zeros((PANELS, count), F32)
    for kind in range(KS):
        result += jnp.where(kinds == kind, sums[kind * PANELS : (kind + 1) * PANELS, :], 0.0)
    return result


def place_in_brick(brick_ref):
    zbricks = NZ // 4

    def place_of(column):
        brick = brick_ref[column]
        return brick // zbricks, brick % zbricks

    return place_of


def place_in_facts(facts_ref):
    return lambda column: (facts_ref[0, column], facts_ref[1, column])


def own_kernel(brick_ref, live_ref, charges_ref, kinds_ref, stencil_ref, order_ref,
               g0, g1, g2, g3, edge_ref, stk_ref, fp_ref):
    stk_ref[...] = dot(stencil_ref[...], order_ref[...]).astype(BF16)
    for ref in (g0, g1, g2, g3, edge_ref):
        ref[...] = jnp.zeros_like(ref)
    slots = charges_ref.shape[1]
    live = live_ref[0]
    for first in range(0, slots, LANES):
        @pl.when(live > first)
        def _(columns=slice(first, first + LANES)):
            footprints(charges_ref[:, columns], kinds_ref[0:1, columns], stk_ref, fp_ref, columns.start)
    scatter_columns(fp_ref, place_in_brick(brick_ref), (g0, g1, g2, g3), edge_ref, 0, live, (0, 1, 2, 3), 2)


def beside_kernel(prev_ref, next_ref, stk_ref, i0, i1, i2, i3, iedge,
                  g0, g1, g2, g3, out_edge, out_facts, edge_ref, fp_ref, facts_ref, sem):
    slots = prev_ref.shape[1]
    for side, source in enumerate((prev_ref, next_ref)):
        facts = source[PANELS : PANELS + 8, :].astype(F32)
        out_facts[:, side * slots : (side + 1) * slots] = facts.astype(jnp.int32)
    copy = pltpu.make_async_copy(out_facts, facts_ref, sem)
    copy.start()
    for ref, source in ((g0, i0), (g1, i1), (g2, i2), (g3, i3), (edge_ref, iedge)):
        ref[...] = source[...]
    copy.wait()
    sides = ((prev_ref, (0, 1), 6), (next_ref, (2, 3), -2))
    for side, (source, planes, shift_i) in enumerate(sides):
        start = side * slots
        live = facts_ref[3, start]
        for first in range(0, slots, LANES):
            @pl.when(live > first)
            def _(source=source, start=start, first=first):
                here = slice(first, first + LANES)
                kinds = out_facts[2:3, start + first : start + first + LANES]
                footprints(source[0:PANELS, here], kinds, stk_ref, fp_ref, start + first)
        scatter_columns(fp_ref, place_in_facts(facts_ref), (g0, g1, g2, g3), edge_ref,
                        start, live, planes, shift_i)
    edge_ref[0:8, :] += edge_ref[NZ:ZROWS, :]
    total = edge_ref[0:LANES, :]
    for block in range(1, 4):
        total += pltpu.roll(edge_ref[block * LANES : (block + 1) * LANES, :], 32 * block, 1)
    out_edge[...] = total


def exponent_of(values):
    top = functools.reduce(jnp.maximum, [jnp.max(jnp.abs(v), axis=0, keepdims=True) for v in values])
    top = jnp.maximum(jnp.max(top, axis=1, keepdims=True), 2.0**-100)
    return jnp.ceil(jnp.log2(top)) - 12.0


def z_kernel(owners, g0, g1, g2, g3, edge_ref, w_ref, out_ref):
    lane = lane_of((LANES, LANES))
    at_edge = (lane < 2) | (lane >= LANES - 2)
    parts = NZ // owners
    stride = 4 * parts + SCALE_ROWS
    results = []
    for plane, grid in enumerate((g0, g1, g2, g3)):
        blocks = []
        for block in range(4):
            turned = pltpu.roll(edge_ref[...], (LANES - 2 - 32 * block - 8 * plane) % LANES, 1)
            blocks.append(
                grid[block * LANES : (block + 1) * LANES, :] + jnp.where(at_edge, turned, 0.0)
            )
        blocks[0] = jnp.concatenate([blocks[0][0:8] + grid[NZ:ZROWS, :], blocks[0][8:]], axis=0)
        values = split(jnp.concatenate(blocks, axis=0))
        results.append(dot3((w_ref[0:NZ, :], w_ref[NZ : 2 * NZ, :]), values))
    exponent = exponent_of(results)
    scale = jnp.exp2(-exponent)
    for plane, result in enumerate(results):
        result = result * scale
        for part in range(parts):
            out_ref[pl.ds(plane * parts + part, owners, stride=stride), :] = result[
                part * owners : (part + 1) * owners, :
            ]
    for row in range(SCALE_ROWS):
        out_ref[pl.ds(4 * parts + row, owners, stride=stride), :] = jnp.broadcast_to(
            exponent, (owners, LANES)
        )


def plane_kernel(slabs, planes, offset_ref, in_ref, hat_ref, y_ref, x_ref, out_ref, ah_ref, al_ref):
    length = 4 * slabs
    rows = planes * length
    parts = 2 * planes
    stride = 4 * parts + SCALE_ROWS
    offset = offset_ref[0]

    def pieces():
        for tile in range(2):
            for part in range(2):
                for xi in range(4):
                    for plane in range(planes):
                        start = tile * slabs * stride + xi * parts + part * planes + plane
                        row = (part * planes + plane) * length + xi * slabs
                        yield tile, part, pl.ds(start, slabs, stride=stride), row

    scales = [
        jnp.exp2(in_ref[pl.ds(tile * slabs * stride + 4 * parts, slabs, stride=stride), :])
        for tile in range(2)
    ]
    for tile, part, where, row in pieces():
        high, low = split(in_ref[where, :] * scales[tile])
        ah_ref[row : row + slabs, tile * LANES : (tile + 1) * LANES] = high
        al_ref[row : row + slabs, tile * LANES : (tile + 1) * LANES] = low
    along_y = (y_ref[0:NY, :], y_ref[NY : 2 * NY, :])
    turned = dot3((ah_ref[...], al_ref[...]), along_y)
    real = turned[:rows, :NY] + turned[rows:, NY:]
    imag = turned[rows:, :NY] - turned[:rows, NY:]
    size = 2 * length
    forward = (x_ref[0:size, :], x_ref[size : 2 * size, :])
    inverse = (x_ref[2 * size : 3 * size, :], x_ref[3 * size : 4 * size, :])
    for plane in range(planes):
        here = slice(plane * length, (plane + 1) * length)
        there = slice(rows + plane * length, rows + (plane + 1) * length)
        values = dot3(forward, split(jnp.concatenate([real[here], imag[here]], axis=0)))
        hat = hat_ref[offset + plane] * (1.0 / (length * NY))
        values = values * jnp.concatenate([hat, hat], axis=0)
        high, low = split(dot3(inverse, split(values)))
        ah_ref[here, :] = high[:length]
        ah_ref[there, :] = high[length:]
        al_ref[here, :] = low[:length]
        al_ref[there, :] = low[length:]
    turned = dot3((ah_ref[...], al_ref[...]), along_y)
    results = (turned[:rows, :NY] - turned[rows:, NY:], turned[rows:, :NY] + turned[:rows, NY:])
    exponent = exponent_of(results)
    scale = jnp.exp2(-exponent)
    results = [result * scale for result in results]
    for tile, part, where, row in pieces():
        row -= part * rows
        out_ref[where, :] = results[part][row : row + slabs, tile * LANES : (tile + 1) * LANES]
    for row in range(SCALE_ROWS):
        out_ref[pl.ds(4 * parts + row, 2 * slabs, stride=stride), :] = jnp.broadcast_to(
            exponent, (2 * slabs, LANES)
        )


def potential_kernel(owners, in_ref, v_ref, p0, p1, p2, p3, edge_ref):
    parts = NZ // owners
    stride = 4 * parts + SCALE_ROWS
    lane = lane_of((LANES, LANES))
    edge = jnp.zeros((LANES, LANES), F32)
    scale = jnp.exp2(in_ref[pl.ds(4 * parts, owners, stride=stride), :])
    for plane, pot in enumerate((p0, p1, p2, p3)):
        values = split(jnp.concatenate(
            [in_ref[pl.ds(plane * parts + part, owners, stride=stride), :] * scale for part in range(parts)],
            axis=0,
        ))
        result = dot3((v_ref[0:NZ, :], v_ref[NZ : 2 * NZ, :]), values).astype(BF16).astype(F32)
        pot[0:NZ, :] = result
        pot[NZ:ZROWS, :] = result[0:8, :]
        for block in range(4):
            low = 32 * block + 8 * plane
            turned = pltpu.roll(result[block * LANES : (block + 1) * LANES, :], low + 2, 1)
            edge = jnp.where((lane >= low) & (lane < low + 4), turned, edge)
    edge_ref[...] = edge.astype(BF16)


def widen_edge(edge_ref, wide_ref):
    for block in range(4):
        wide_ref[block * LANES : (block + 1) * LANES, :] = pltpu.roll(
            edge_ref[...].astype(F32), (LANES - 32 * block) % LANES, 1
        )
    wide_ref[NZ:ZROWS, :] = wide_ref[0:8, :]


def sampled_sums(place_of, pots, wide_ref, kinds, stk_ref, out_ref, sp_ref, start, slots, live, planes, shift_i):
    sample_columns(pots, wide_ref, place_of, sp_ref, start, live, planes, shift_i)
    for first in range(0, slots, LANES):
        where = slice(start + first, start + first + LANES)

        @pl.when(live > first)
        def _(first=first, where=where):
            result = far_sums(sp_ref, kinds[0:1, where], stk_ref, where.start)
            column = first + lane_of((PANELS, LANES))
            out_ref[:, where] = jnp.where(column < live, result, 0.0)

        @pl.when(live <= first)
        def _(where=where):
            out_ref[:, where] = jnp.zeros((PANELS, LANES), F32)


def own_sample_kernel(brick_ref, live_ref, p0, p1, p2, p3, edge_ref, kinds_ref, stk_ref, out_ref, wide_ref, sp_ref):
    widen_edge(edge_ref, wide_ref)
    sampled_sums(place_in_brick(brick_ref), (p0, p1, p2, p3), wide_ref, kinds_ref, stk_ref, out_ref, sp_ref,
                 0, kinds_ref.shape[1], live_ref[0], (0, 1, 2, 3), 2)


def beside_sample_kernel(facts_ref, p0, p1, p2, p3, edge_ref, kinds_ref, stk_ref, out_ref, wide_ref, sp_ref):
    widen_edge(edge_ref, wide_ref)
    slots = kinds_ref.shape[1] // 2
    for side, (planes, shift_i) in enumerate((((0, 1), 6), ((2, 3), -2))):
        sampled_sums(place_in_facts(facts_ref), (p0, p1, p2, p3), wide_ref, kinds_ref.at[2:3, :], stk_ref, out_ref,
                     sp_ref, side * slots, slots, facts_ref[3, side * slots], planes, shift_i)


def near_kernel(live_ref, a0, a1, a2, a3, a4, a5, source_ref, block_ref, table_ref, out_ref):
    live = live_ref[0]
    fanout, slots = source_ref.shape
    pool = jnp.concatenate([ref[0:PANELS, :] for ref in (a0, a1, a2, a3, a4, a5)], axis=1)
    total = pool.shape[1]
    for first in range(0, slots, LANES):
        where = slice(first, first + LANES)

        @pl.when(live > first)
        def _(where=where, first=first):
            index = lax.broadcasted_iota(jnp.int32, (total, LANES), 0)
            result = jnp.zeros((PANELS, LANES), F32)
            for j in range(fanout):
                chosen = jnp.where(index == source_ref[j : j + 1, where], 1.0, 0.0).astype(BF16)
                gathered = dot(pool, chosen)
                result += dot(
                    table_ref[...], by_kind(gathered, block_ref[j : j + 1, where]).astype(BF16)
                )
            column = first + lane_of((PANELS, LANES))
            out_ref[:, where] = jnp.where(column < live, result, 0.0)

        @pl.when(live <= first)
        def _(where=where):
            out_ref[:, where] = jnp.zeros((PANELS, LANES), F32)


def shape_of(*dims, dtype=F32):
    return jax.ShapeDtypeStruct(dims, dtype)


def body(slabs, tiles, charges, live_count, slot_brick, slot_stencil, stencils, near_source,
         near_block, near_blocks, kernel_hat):
    slots = charges.shape[1]
    owners = slabs * tiles
    planes = kernel_hat.shape[0] // 2
    length = kernel_hat.shape[1]
    parts = NZ // owners
    axes = ("tile", "slab")
    both = ("slab", "tile")

    def moved(values, step, swap):
        pairs = [
            (a * tiles + b, (a + step) % slabs * tiles + (b + swap) % tiles)
            for a in range(slabs)
            for b in range(tiles)
        ]
        return lax.ppermute(values, both, pairs)

    live = live_count[0]
    slot = jnp.arange(slots, dtype=jnp.int32)
    held = jnp.where((slot < live)[None, :], charges, jnp.zeros((), charges.dtype))
    zbricks = NZ // 4
    kinds = slot_stencil[None, :]
    facts = jnp.stack(
        [slot_brick // zbricks, slot_brick % zbricks, slot_stencil, jnp.full((slots,), live)], axis=0
    )
    packed = jnp.concatenate(
        [held, facts.astype(BF16), jnp.zeros((12, slots), BF16)], axis=0
    )
    from_prev = moved(packed, 1, 0)
    from_next = moved(packed, -1, 0)
    swapped = moved(held, 0, 1)

    grid = shape_of(ZROWS, LANES)
    g = pl.pallas_call(
        own_kernel,
        out_shape=(grid,) * 5 + (shape_of(KS * PANELS, POINTS, dtype=BF16),),
        in_specs=[SMEM] * 2 + [VMEM] * 4,
        out_specs=(VMEM,) * 6,
        scratch_shapes=[pltpu.VMEM((slots * 8, LANES), F32)],
        compiler_params=PARAMS,
        name="own_scatter",
    )(slot_brick, live_count, held, kinds, stencils.reshape(KS * PANELS, POINTS), jnp.asarray(point_order()))
    grids, stk = g[:5], g[5]

    g = pl.pallas_call(
        beside_kernel,
        out_shape=(grid,) * 4 + (shape_of(LANES, LANES), shape_of(8, 2 * slots, dtype=jnp.int32)),
        in_specs=[VMEM] * 8,
        out_specs=(VMEM,) * 6,
        scratch_shapes=[
            pltpu.VMEM((ZROWS, LANES), F32),
            pltpu.VMEM((2 * slots * 8, LANES), F32),
            pltpu.SMEM((8, 2 * slots), jnp.int32),
            pltpu.SemaphoreType.DMA,
        ],
        compiler_params=PARAMS,
        name="beside_scatter",
    )(from_prev, from_next, stk, *grids)
    facts2 = g[5]
    edge = moved(g[4], 0, 1)

    forward, inverse = z_tables(slabs, tiles)
    rows = owners * (4 * parts + SCALE_ROWS)
    sent = pl.pallas_call(
        functools.partial(z_kernel, owners),
        out_shape=shape_of(rows, LANES),
        in_specs=[VMEM] * 6,
        out_specs=VMEM,
        compiler_params=PARAMS,
        name="z_forward",
    )(*g[:4], edge, jnp.asarray(halves(forward)))

    def exchanged(values):
        values = values.astype(jnp.float16).reshape(owners, 4 * parts + SCALE_ROWS, LANES)
        values = lax.all_to_all(values, axes, 0, 0, tiled=True)
        return values

    def widened(values):
        return values.astype(F32).reshape(rows, LANES)

    got = exchanged(sent)

    pool = [from_prev, moved(swapped, 1, 0), held, swapped, from_next, moved(swapped, -1, 0)]
    direction = near_source // slots
    pool_index = (direction // 3 * 2 + (direction % 3 != 1).astype(jnp.int32)) * slots + near_source % slots
    near = pl.pallas_call(
        near_kernel,
        out_shape=shape_of(PANELS, slots),
        in_specs=[SMEM] + [VMEM] * 9,
        out_specs=VMEM,
        compiler_params=PARAMS,
        name="near_field",
    )(live_count, *pool, pool_index.T, near_block.T, near_blocks.reshape(PANELS, KN * PANELS))

    me = lax.axis_index("slab") * tiles + lax.axis_index("tile")
    offset = (me >= owners // 2).astype(jnp.int32)[None]
    back = pl.pallas_call(
        functools.partial(plane_kernel, slabs, planes),
        out_shape=shape_of(rows, LANES),
        in_specs=[SMEM] + [VMEM] * 4,
        out_specs=VMEM,
        scratch_shapes=[pltpu.VMEM((2 * planes * length, NY), BF16)] * 2,
        compiler_params=PARAMS,
        name="plane_filter",
    )(offset, widened(got), kernel_hat, jnp.asarray(halves(y_table())), jnp.asarray(halves(*x_tables(slabs))))
    back, near = lax.optimization_barrier((exchanged(back), near))

    pot = pl.pallas_call(
        functools.partial(potential_kernel, owners),
        out_shape=(grid,) * 4 + (shape_of(LANES, LANES, dtype=BF16),),
        in_specs=[VMEM] * 2,
        out_specs=(VMEM,) * 5,
        compiler_params=PARAMS,
        name="z_inverse",
    )(widened(back), jnp.asarray(halves(inverse)))
    edge = moved(pot[4], 0, 1)

    def sampling(width):
        return dict(
            out_shape=shape_of(PANELS, width),
            out_specs=VMEM,
            scratch_shapes=[pltpu.VMEM((ZROWS, LANES), F32), pltpu.VMEM((width * 8, LANES), F32)],
            compiler_params=PARAMS,
        )

    others = pl.pallas_call(
        beside_sample_kernel, in_specs=[SMEM] + [VMEM] * 7, name="beside_sample", **sampling(2 * slots)
    )(facts2, *pot[:4], edge, facts2, stk)
    to_prev = moved(others[:, :slots], -1, 0)
    to_next = moved(others[:, slots:], 1, 0)
    own = pl.pallas_call(
        own_sample_kernel, in_specs=[SMEM] * 2 + [VMEM] * 7, name="own_sample", **sampling(slots)
    )(slot_brick, live_count, *pot[:4], edge, kinds, stk)
    return own + near + to_prev + to_next


def solution(mesh):
    both = ("slab", "tile")
    in_specs = (
        P(None, both),
        P(both),
        P(both),
        P(both),
        P(),
        P(both, None),
        P(both, None),
        P(),
        P(both, None, None),
    )
    return jax.shard_map(
        functools.partial(body, mesh.shape["slab"], mesh.shape["tile"]),
        mesh=mesh,
        in_specs=in_specs,
        out_specs=P(None, both),
        check_vma=False,
    )
```

time: 131 us -> 94.6 us (0.72)
  waiting for transfers between devices: 50 us -> 33.5 us
  Pallas kernels: 42.2 us -> 29.5 us
  local copies, waits for them, and re-layouts: 13.3 us -> 4.06 us
    all_to_all x2, waiting for transfers between devices: 31 us -> 18.2 us  [exchanged(): values = lax.all_to_all(values, axes, 0, 0, tiled=True)]
    unnamed x49 -> x28, local copies, waits for them, and re-layouts: 10.6 us -> 3.68 us
    pallas_call x4, Pallas kernels: 22.6 us -> 16.5 us  [the longest x1 5.61 us: body(): pl.pallas_call(functools.partial(plane_kernel, slabs, planes), out_shape=...]
    pallas_call x1, Pallas kernels: 10.7 us -> 4.81 us  [body(): pl.pallas_call(beside_kernel, out_shape=(grid,) * 4 + (shape_of(LANES, LA...]
    ppermute x9, waiting for transfers between devices: 19 us -> 15.2 us  [moved(): return lax.ppermute(values, both, pairs)]
    convert_element_type x1 -> x2, other arithmetic: 0.01 us -> 1.78 us  [exchanged(): values.astype(jnp.float16).reshape(owners, 4 * parts + SCALE_ROWS, LANES)]
  transfers between devices with their start and end apart: 11 -> 11, of which waited for: 5 -> 6; matrix products, arithmetic and copies ran while one was open for 3% -> 0% of each run, Pallas kernels for 18% -> 11%
where the time goes in v2:
time: 94.6 us; the launch traced here: 93.2 us
  waiting for transfers between devices  33.5 us (35%)
  Pallas kernels  29.5 us (31%)
  starting transfers between devices  20.4 us (22%)
  other arithmetic  4.83 us (5%)
  local copies, waits for them, and re-layouts  4.06 us (4%)
  between operations  0.95 us (1%)
    all_to_all x2, waiting for transfers between devices, exchanged(): values = lax.all_to_all(values, axes, 0, 0, tiled=True)  18.2 us
    ppermute x9, waiting for transfers between devices, moved(): return lax.ppermute(values, both, pairs)  15.2 us
    ppermute x9, starting transfers between devices, moved(): return lax.ppermute(values, both, pairs)  15.1 us
    pallas_call x1, Pallas kernels, body(): pl.pallas_call(functools.partial(plane_kernel, slabs, planes), out_shape=...  5.61 us
    all_to_all x2, starting transfers between devices, exchanged(): values = lax.all_to_all(values, axes, 0, 0, tiled=True)  5.35 us
    pallas_call x1, Pallas kernels, body(): pl.pallas_call(beside_sample_kernel, in_specs=[SMEM] + [VMEM] * 7, name='...  4.88 us
    pallas_call x1, Pallas kernels, body(): pl.pallas_call(beside_kernel, out_shape=(grid,) * 4 + (shape_of(LANES, LA...  4.81 us
    pallas_call x1, Pallas kernels, body(): pl.pallas_call(own_kernel, out_shape=(grid,) * 5 + (shape_of(KS * PANELS,...  4.17 us
  transfers between devices with their start and end apart: 11, of which 6 were waited for; matrix products, arithmetic and copies ran while one was open for 0% of the time, Pallas kernels for 11%

profile of v2, /device:TPU:0, one launch (start us, length us, event | category | flops | bytes accessed | tf_op | source)
XLA Modules:
  0.0 93.2 jit_solution(8017740737260750150)
XLA Ops:
  0.7 0.7 convert.20
  1.4 0.7 fusion.8
  2.1 0.8 broadcast_select_fusion.charges_ref.a2
  2.9 0.2 concatenate.4
  3.0 3.0 %collective-permute-start = (bf16[80,256]{1,0:T(8,128)(2,1)S(1)}, bf16[80,256]{1,0:T(8,128)(2,1)S(1)}, u32[]{:S(2)}, u32[]{:S(2)}) collective-permute-start(bf16[80,256]{1,0:T(8,128)(2,1)S(1)} %concatenate.4), channel_id=1, source_target_pairs={{0,2},{1,3},{2,4},{3,5},{4,6},{5,7},{6,8},{7,9},{8,10},{9,11},{10,... | collective-permute-start | bytes 122888 | tf_op jit(solution)/shard_map/ppermute | solution.py:451
  6.0 4.1 %collective-permute-start.1 = (bf16[80,256]{1,0:T(8,128)(2,1)S(1)}, bf16[80,256]{1,0:T(8,128)(2,1)S(1)}, u32[]{:S(2)}, u32[]{:S(2)}) collective-permute-start(bf16[80,256]{1,0:T(8,128)(2,1)S(1)} %concatenate.4), channel_id=1, source_target_pairs={{0,30},{1,31},{2,0},{3,1},{4,2},{5,3},{6,4},{7,5},{8,6},{9,7},{10,... | collective-permute-start | bytes 122888 | tf_op jit(solution)/shard_map/ppermute | solution.py:451
  10.1 1.2 %copy-done.1 = bf16[16,64,512]{2,1,0:T(8,128)(2,1)S(1)} copy-done((bf16[16,64,512]{2,1,0:T(8,128)(2,1)S(1)}, bf16[16,64,512]{2,1,0:T(8,128)(2,1)}, u32[]{:S(2)}) %copy-start.1) | copy-done | bytes 1048600
  11.3 1.0 %copy-done.5 = bf16[512,512]{1,0:T(8,128)(2,1)S(1)} copy-done((bf16[512,512]{1,0:T(8,128)(2,1)S(1)}, bf16[512,512]{1,0:T(8,128)(2,1)}, u32[]{:S(2)}) %copy-start.5) | copy-done | bytes 524312
  12.3 0.7 copy-done.7
  13.0 0.7 copy-done.9
  13.7 4.2 %own_scatter.1 = (f32[520,128]{1,0:T(8,128)S(1)}, f32[520,128]{1,0:T(8,128)S(1)}, f32[520,128]{1,0:T(8,128)S(1)}, f32[520,128]{1,0:T(8,128)S(1)}, f32[520,128]{1,0:T(8,128)S(1)}, /*index=5*/bf16[1024,512]{1,0:T(8,128)(2,1)S(1)}) custom-call(s32[256]{0:T(256)S(1)} %copy-done.7, s32[1]{0:T(128)} %copy.15.live_ref, ...), custom_call_target="tpu_custom_call" | custom-call | tf_op jit(solution)/shard_map/own_scatter/pallas_call | solution.py:469
  17.9 0.0 collective-permute-done.prev_ref.a0
  17.9 0.0 copy-start
  17.9 4.8 %beside_scatter.1 = (f32[520,128]{1,0:T(8,128)S(1)}, f32[520,128]{1,0:T(8,128)S(1)}, f32[520,128]{1,0:T(8,128)S(1)}, f32[520,128]{1,0:T(8,128)S(1)}, f32[128,128]{1,0:T(8,128)S(1)}, /*index=5*/s32[8,512]{1,0:T(8,128)S(1)}) custom-call(bf16[80,256]{1,0:T(8,128)(2,1)S(1)} %collective-permute-done.prev_ref.a0, ...), custom_call_target="tpu_custom_call" | custom-call | tf_op jit(solution)/shard_map/beside_scatter/pallas_call | solution.py:480
  22.7 0.1 collective-permute-start.2
  22.8 1.2 %collective-permute-done.2.edge_ref = f32[128,128]{1,0:T(8,128)S(1)} collective-permute-done((f32[128,128]{1,0:T(8,128)S(1)}, f32[128,128]{1,0:T(8,128)S(1)}, u32[]{:S(2)}, u32[]{:S(2)}) %collective-permute-start.2) | collective-permute-done | bytes 65568 | tf_op jit(solution)/shard_map/ppermute | solution.py:451
  24.0 2.2 %z_forward.1 = f32[2304,128]{1,0:T(8,128)S(1)} custom-call(f32[520,128]{1,0:T(8,128)S(1)} %get-tuple-element.30.g0, f32[520,128]{1,0:T(8,128)S(1)} %get-tuple-element.31.g1, f32[520,128]{1,0:T(8,128)S(1)} %get-tuple-element.32.g2, f32[520,128]{1,0:T(8,128)S(1)} %get-tuple-element.33.g3, f32[128,128]{1,0:T(8,128)S(1)} %collective-permute-done.2.edge_ref, ...), custom_call_target="tpu_custom_call" | custom-call | tf_op jit(solution)/shard_map/z_forward/pallas_call | solution.py:499
  26.2 0.9 convert_element_type.6
  27.1 2.6 %all-to-all-start = ((f16[32,72,128]{2,1,0:T(8,128)(2,1)}), f16[32,72,128]{2,1,0:T(8,128)(2,1)S(1)}, u32[]{:S(2)}, u32[]{:S(2)}) async-start(f16[32,72,128]{2,1,0:T(8,128)(2,1)} %bitcast.4), calls=%async_computation | async-start | bytes 1179648 | tf_op jit(solution)/shard_map/all_to_all | solution.py:510
  29.7 0.0 copy-start.3
  29.8 0.0 copy-start.4
  29.8 0.0 copy-start.6
  29.8 18.2 %all-to-all-done = f16[32,72,128]{2,1,0:T(8,128)(2,1)S(1)} async-done(((f16[32,72,128]{2,1,0:T(8,128)(2,1)}), f16[32,72,128]{2,1,0:T(8,128)(2,1)S(1)}, u32[]{:S(2)}, u32[]{:S(2)}) %all-to-all-start) | async-done | bytes 589856 | tf_op jit(solution)/shard_map/all_to_all | solution.py:510
  48.0 0.1 bitcast_convert_fusion.1.in_ref
  48.1 5.6 %plane_filter.1 = f32[2304,128]{1,0:T(8,128)S(1)} custom-call(s32[1]{0:T(128)} %bitcast.offset_ref, f32[2304,128]{1,0:T(8,128)S(1)} %bitcast_convert_fusion.1.in_ref, f32[16,64,256]{2,1,0:T(8,128)S(1)} %copy-done.3, bf16[512,512]{1,0:T(8,128)(2,1)S(1)} %copy-done.4, bf16[512,128]{1,0:T(8,128)(2,1)S(1)} %copy-done.6), custom_call_target="tpu_custom_call" | custom-call | tf_op jit(solution)/shard_map/plane_filter/pallas_call | solution.py:532
  53.7 0.0 copy-start.13
  53.8 0.0 copy-start.12
  53.8 0.9 convert_element_type.14
  54.7 2.7 %all-to-all-start.1 = ((f16[32,72,128]{2,1,0:T(8,128)(2,1)}), f16[32,72,128]{2,1,0:T(8,128)(2,1)S(1)}, u32[]{:S(2)}, u32[]{:S(2)}) async-start(f16[32,72,128]{2,1,0:T(8,128)(2,1)} %bitcast.6), calls=%async_computation.1 | async-start | bytes 1179648 | tf_op jit(solution)/shard_map/all_to_all | solution.py:510
  57.4 0.2 collective-permute-start.3
  57.6 1.1 %collective-permute-done.3.a3 = bf16[64,256]{1,0:T(8,128)(2,1)S(1)} collective-permute-done((bf16[64,256]{1,0:T(8,128)(2,1)S(1)}, bf16[64,256]{1,0:T(8,128)(2,1)S(1)}, u32[]{:S(2)}, u32[]{:S(2)}) %collective-permute-start.3) | collective-permute-done | bytes 32800 | tf_op jit(solution)/shard_map/ppermute | solution.py:451
  58.7 1.6 %collective-permute-start.4 = (bf16[64,256]{1,0:T(8,128)(2,1)S(1)}, bf16[64,256]{1,0:T(8,128)(2,1)S(1)}, u32[]{:S(2)}, u32[]{:S(2)}) collective-permute-start(bf16[64,256]{1,0:T(8,128)(2,1)S(1)} %collective-permute-done.3.a3), channel_id=1, source_target_pairs={{0,2},{1,3},{2,4},{3,5},{4,6},{5,7},{6,8},{7,9},{8,10},{9,11},{10,... | collective-permute-start | bytes 98312 | tf_op jit(solution)/shard_map/ppermute | solution.py:451
  60.3 4.0 %collective-permute-start.5 = (bf16[64,256]{1,0:T(8,128)(2,1)S(1)}, bf16[64,256]{1,0:T(8,128)(2,1)S(1)}, u32[]{:S(2)}, u32[]{:S(2)}) collective-permute-start(bf16[64,256]{1,0:T(8,128)(2,1)S(1)} %collective-permute-done.3.a3), channel_id=1, source_target_pairs={{0,30},{1,31},{2,0},{3,1},{4,2},{5,3},{6,4},{7,5},{8,6},{9,7},{10,... | collective-permute-start | bytes 98312 | tf_op jit(solution)/shard_map/ppermute | solution.py:451
  64.3 0.2 reshape.31.table_ref
  64.6 0.0 copy-start.2
  64.6 9.6 %collective-permute-done.4.a1 = bf16[64,256]{1,0:T(8,128)(2,1)S(1)} collective-permute-done((bf16[64,256]{1,0:T(8,128)(2,1)S(1)}, bf16[64,256]{1,0:T(8,128)(2,1)S(1)}, u32[]{:S(2)}, u32[]{:S(2)}) %collective-permute-start.4) | collective-permute-done | bytes 32800 | tf_op jit(solution)/shard_map/ppermute | solution.py:451
  74.2 2.1 %near_field.1 = f32[64,256]{1,0:T(8,128)S(1)} custom-call(s32[1]{0:T(128)} %copy.15.live_ref, bf16[80,256]{1,0:T(8,128)(2,1)S(1)} %collective-permute-done.prev_ref.a0, bf16[64,256]{1,0:T(8,128)(2,1)S(1)} %collective-permute-done.4.a1, bf16[64,256]{1,0:T(8,128)(2,1)S(1)} %broadcast_select_fusion.charges_ref.a2, ...), custom_call_target="tpu_custom_call" | custom-call | tf_op jit(solution)/shard_map/near_field/pallas_call | solution.py:521
  76.3 0.0 all-to-all-done.1
  76.3 0.1 bitcast_convert_fusion.in_ref
  76.5 1.9 %z_inverse.1 = (f32[520,128]{1,0:T(8,128)S(1)}, f32[520,128]{1,0:T(8,128)S(1)}, f32[520,128]{1,0:T(8,128)S(1)}, f32[520,128]{1,0:T(8,128)S(1)}, bf16[128,128]{1,0:T(8,128)(2,1)S(1)}) custom-call(f32[2304,128]{1,0:T(8,128)S(1)} %bitcast_convert_fusion.in_ref, bf16[1024,512]{1,0:T(8,128)(2,1)S(1)} %copy-done.2), custom_call_target="tpu_custom_call" | custom-call | tf_op jit(solution)/shard_map/z_inverse/pallas_call | solution.py:543
  78.4 0.1 collective-permute-start.6
  78.5 1.2 %collective-permute-done.6.edge_ref = bf16[128,128]{1,0:T(8,128)(2,1)S(1)} collective-permute-done((bf16[128,128]{1,0:T(8,128)(2,1)S(1)}, bf16[128,128]{1,0:T(8,128)(2,1)S(1)}, u32[]{:S(2)}, u32[]{:S(2)}) %collective-permute-start.6) | collective-permute-done | bytes 32800 | tf_op jit(solution)/shard_map/ppermute | solution.py:451
  79.7 4.9 %beside_sample.1 = f32[64,512]{1,0:T(8,128)S(1)} custom-call(s32[8,512]{1,0:T(8,128)S(1)} %get-tuple-element.42.facts_ref.kinds_ref, f32[520,128]{1,0:T(8,128)S(1)} %get-tuple-element.36.p0, f32[520,128]{1,0:T(8,128)S(1)} %get-tuple-element.37.p1, f32[520,128]{1,0:T(8,128)S(1)} %get-tuple-element.38.p2, f32[520,128]{1,0:T(8,128)S(1)} %get-tuple-element.39.p3, ...), custom_call_target="tpu_custom_call" | custom-call | tf_op jit(solution)/shard_map/beside_sample/pallas_call | solution.py:561
  84.6 0.1 collective-permute-start.7
  84.7 2.0 %collective-permute-start.8 = (f32[64,256]{1,0:T(8,128)S(1)}, f32[64,256]{1,0:T(8,128)S(1)}, u32[]{:S(2)}, u32[]{:S(2)}) collective-permute-start(f32[64,256]{1,0:T(8,128)S(1)} %get-tuple-element.44), channel_id=1, source_target_pairs={{0,2},{1,3},{2,4},{3,5},{4,6},{5,7},{6,8},{7,9},{8,10},{9,11},{10,... | collective-permute-start | bytes 196616 | tf_op jit(solution)/shard_map/ppermute | solution.py:451
  86.7 3.8 %own_sample.1 = f32[64,256]{1,0:T(8,128)S(1)} custom-call(s32[256]{0:T(256)S(1)} %copy-done.8, s32[1]{0:T(128)} %copy.15.live_ref, f32[520,128]{1,0:T(8,128)S(1)} %get-tuple-element.36.p0, f32[520,128]{1,0:T(8,128)S(1)} %get-tuple-element.37.p1, f32[520,128]{1,0:T(8,128)S(1)} %get-tuple-element.38.p2, f32[520,128]{1,0:T(8,128)S(1)} %get-tuple-element.39.p3, ...), custom_call_target="tpu_custom_call" | custom-call | tf_op jit(solution)/shard_map/own_sample/pallas_call | solution.py:566
  90.5 2.1 %collective-permute-done.8 = f32[64,256]{1,0:T(8,128)S(1)} collective-permute-done((f32[64,256]{1,0:T(8,128)S(1)}, f32[64,256]{1,0:T(8,128)S(1)}, u32[]{:S(2)}, u32[]{:S(2)}) %collective-permute-start.8) | collective-permute-done | bytes 65568 | tf_op jit(solution)/shard_map/ppermute | solution.py:451
  92.6 0.6 add_add_fusion
  (27 shorter events, 0.1 us)
Async XLA Ops:
  3.0 14.9 %collective-permute-start = (bf16[80,256]{1,0:T(8,128)(2,1)S(1)}, bf16[80,256]{1,0:T(8,128)(2,1)S(1)}, u32[]{:S(2)}, u32[]{:S(2)}) collective-permute-start(bf16[80,256]{1,0:T(8,128)(2,1)S(1)} %concatenate.4), channel_id=1, source_target_pairs={{0,2},{1,3},{2,4},{3,5},{4,6},{5,7},{6,8},{7,9},{8,10},{9,11},{10,... | collective-permute-start | bytes 122888 | tf_op jit(solution)/shard_map/ppermute | solution.py:451
  6.0 11.9 %collective-permute-start.1 = (bf16[80,256]{1,0:T(8,128)(2,1)S(1)}, bf16[80,256]{1,0:T(8,128)(2,1)S(1)}, u32[]{:S(2)}, u32[]{:S(2)}) collective-permute-start(bf16[80,256]{1,0:T(8,128)(2,1)S(1)} %concatenate.4), channel_id=1, source_target_pairs={{0,30},{1,31},{2,0},{3,1},{4,2},{5,3},{6,4},{7,5},{8,6},{9,7},{10,... | collective-permute-start | bytes 122888 | tf_op jit(solution)/shard_map/ppermute | solution.py:451
  10.1 1.2 %copy-start.1 = (bf16[16,64,512]{2,1,0:T(8,128)(2,1)S(1)}, bf16[16,64,512]{2,1,0:T(8,128)(2,1)}, u32[]{:S(2)}) copy-start(bf16[16,64,512]{2,1,0:T(8,128)(2,1)} %param.18) | copy-start | bytes 3145732
  11.3 1.0 %copy-start.5 = (bf16[512,512]{1,0:T(8,128)(2,1)S(1)}, bf16[512,512]{1,0:T(8,128)(2,1)}, u32[]{:S(2)}) copy-start(bf16[512,512]{1,0:T(8,128)(2,1)} %constant.93.clone.order_ref) | copy-start | bytes 1572868
  12.3 0.7 copy-start.7
  13.0 0.7 copy-start.9
  17.9 6.2 %copy-start = (bf16[1024,512]{1,0:T(8,128)(2,1)S(1)}, bf16[1024,512]{1,0:T(8,128)(2,1)}, u32[]{:S(2)}) copy-start(bf16[1024,512]{1,0:T(8,128)(2,1)} %constant.94.clone.w_ref) | copy-start | bytes 3145732
  22.7 1.3 %collective-permute-start.2 = (f32[128,128]{1,0:T(8,128)S(1)}, f32[128,128]{1,0:T(8,128)S(1)}, u32[]{:S(2)}, u32[]{:S(2)}) collective-permute-start(f32[128,128]{1,0:T(8,128)S(1)} %get-tuple-element.34), channel_id=1, source_target_pairs={{0,1},{1,0},{2,3},{3,2},{4,5},{5,4},{6,7},{7,6},{8,9},{9,8},{10,11... | collective-permute-start | bytes 196616 | tf_op jit(solution)/shard_map/ppermute | solution.py:451
  27.1 20.9 %all-to-all-start = ((f16[32,72,128]{2,1,0:T(8,128)(2,1)}), f16[32,72,128]{2,1,0:T(8,128)(2,1)S(1)}, u32[]{:S(2)}, u32[]{:S(2)}) async-start(f16[32,72,128]{2,1,0:T(8,128)(2,1)} %bitcast.4), calls=%async_computation | async-start | bytes 1179648 | tf_op jit(solution)/shard_map/all_to_all | solution.py:510
  29.7 18.4 %copy-start.3 = (f32[16,64,256]{2,1,0:T(8,128)S(1)}, f32[16,64,256]{2,1,0:T(8,128)}, u32[]{:S(2)}) copy-start(f32[16,64,256]{2,1,0:T(8,128)} %hat_ref.1) | copy-start | bytes 3145732
  29.8 18.4 %copy-start.4 = (bf16[512,512]{1,0:T(8,128)(2,1)S(1)}, bf16[512,512]{1,0:T(8,128)(2,1)}, u32[]{:S(2)}) copy-start(bf16[512,512]{1,0:T(8,128)(2,1)} %constant.95.clone.y_ref) | copy-start | bytes 1572868
  29.8 18.4 %copy-start.6 = (bf16[512,128]{1,0:T(8,128)(2,1)S(1)}, bf16[512,128]{1,0:T(8,128)(2,1)}, u32[]{:S(2)}) copy-start(bf16[512,128]{1,0:T(8,128)(2,1)} %constant.96.clone.x_ref) | copy-start | bytes 393220
  53.7 10.6 %copy-start.13 = (s32[256,8]{0,1:T(8,128)S(1)}, s32[256,8]{0,1:T(8,128)}, u32[]{:S(2)}) copy-start(s32[256,8]{0,1:T(8,128)} %param.19) | copy-start | bytes 24580
  53.8 10.6 %copy-start.12 = (bf16[64,16,64]{2,1,0:T(8,128)(2,1)S(1)}, bf16[64,16,64]{2,1,0:T(8,128)(2,1)}, u32[]{:S(2)}) copy-start(bf16[64,16,64]{2,1,0:T(8,128)(2,1)} %param.21) | copy-start | bytes 393220
  54.7 19.5 %copy-start.11 = (s32[256,8]{0,1:T(8,128)S(1)}, s32[256,8]{0,1:T(8,128)}, u32[]{:S(2)}) copy-start(s32[256,8]{0,1:T(8,128)} %param.20) | copy-start | bytes 24580
  54.7 21.7 %all-to-all-start.1 = ((f16[32,72,128]{2,1,0:T(8,128)(2,1)}), f16[32,72,128]{2,1,0:T(8,128)(2,1)S(1)}, u32[]{:S(2)}, u32[]{:S(2)}) async-start(f16[32,72,128]{2,1,0:T(8,128)(2,1)} %bitcast.6), calls=%async_computation.1 | async-start | bytes 1179648 | tf_op jit(solution)/shard_map/all_to_all | solution.py:510
  57.4 1.3 %collective-permute-start.3 = (bf16[64,256]{1,0:T(8,128)(2,1)S(1)}, bf16[64,256]{1,0:T(8,128)(2,1)S(1)}, u32[]{:S(2)}, u32[]{:S(2)}) collective-permute-start(bf16[64,256]{1,0:T(8,128)(2,1)S(1)} %broadcast_select_fusion.charges_ref.a2), channel_id=1, source_target_pairs={{0,1},{1,0},{2,3},{3,2},{4,5},{5,4},{6,7},{7,6},{8,9},{9,8},{10,11... | collective-permute-start | bytes 98312 | tf_op jit(solution)/shard_map/ppermute | solution.py:451
  58.7 15.5 %collective-permute-start.4 = (bf16[64,256]{1,0:T(8,128)(2,1)S(1)}, bf16[64,256]{1,0:T(8,128)(2,1)S(1)}, u32[]{:S(2)}, u32[]{:S(2)}) collective-permute-start(bf16[64,256]{1,0:T(8,128)(2,1)S(1)} %collective-permute-done.3.a3), channel_id=1, source_target_pairs={{0,2},{1,3},{2,4},{3,5},{4,6},{5,7},{6,8},{7,9},{8,10},{9,11},{10,... | collective-permute-start | bytes 98312 | tf_op jit(solution)/shard_map/ppermute | solution.py:451
  60.3 13.8 %collective-permute-start.5 = (bf16[64,256]{1,0:T(8,128)(2,1)S(1)}, bf16[64,256]{1,0:T(8,128)(2,1)S(1)}, u32[]{:S(2)}, u32[]{:S(2)}) collective-permute-start(bf16[64,256]{1,0:T(8,128)(2,1)S(1)} %collective-permute-done.3.a3), channel_id=1, source_target_pairs={{0,30},{1,31},{2,0},{3,1},{4,2},{5,3},{6,4},{7,5},{8,6},{9,7},{10,... | collective-permute-start | bytes 98312 | tf_op jit(solution)/shard_map/ppermute | solution.py:451
  64.6 11.9 %copy-start.2 = (bf16[1024,512]{1,0:T(8,128)(2,1)S(1)}, bf16[1024,512]{1,0:T(8,128)(2,1)}, u32[]{:S(2)}) copy-start(bf16[1024,512]{1,0:T(8,128)(2,1)} %constant.97.clone.v_ref) | copy-start | bytes 3145732
  78.4 1.3 %collective-permute-start.6 = (bf16[128,128]{1,0:T(8,128)(2,1)S(1)}, bf16[128,128]{1,0:T(8,128)(2,1)S(1)}, u32[]{:S(2)}, u32[]{:S(2)}) collective-permute-start(bf16[128,128]{1,0:T(8,128)(2,1)S(1)} %get-tuple-element.40), channel_id=1, source_target_pairs={{0,1},{1,0},{2,3},{3,2},{4,5},{5,4},{6,7},{7,6},{8,9},{9,8},{10,11... | collective-permute-start | bytes 98312 | tf_op jit(solution)/shard_map/ppermute | solution.py:451
  79.7 7.0 %copy-start.8 = (s32[256]{0:T(256)S(1)}, s32[256]{0:T(256)}, u32[]{:S(2)}) copy-start(s32[256]{0:T(256)} %brick_ref.3) | copy-start | bytes 3076
  79.7 7.0 %copy-start.10 = (s32[256]{0:T(256)S(1)}, s32[256]{0:T(256)}, u32[]{:S(2)}) copy-start(s32[256]{0:T(256)} %param.17) | copy-start | bytes 3076
  84.6 5.9 %collective-permute-start.7 = (f32[64,256]{1,0:T(8,128)S(1)}, f32[64,256]{1,0:T(8,128)S(1)}, u32[]{:S(2)}, u32[]{:S(2)}) collective-permute-start(f32[64,256]{1,0:T(8,128)S(1)} %get-tuple-element.43), channel_id=1, source_target_pairs={{0,30},{1,31},{2,0},{3,1},{4,2},{5,3},{6,4},{7,5},{8,6},{9,7},{10,... | collective-permute-start | bytes 196616 | tf_op jit(solution)/shard_map/ppermute | solution.py:451
  84.7 7.9 %collective-permute-start.8 = (f32[64,256]{1,0:T(8,128)S(1)}, f32[64,256]{1,0:T(8,128)S(1)}, u32[]{:S(2)}, u32[]{:S(2)}) collective-permute-start(f32[64,256]{1,0:T(8,128)S(1)} %get-tuple-element.44), channel_id=1, source_target_pairs={{0,2},{1,3},{2,4},{3,5},{4,6},{5,7},{6,8},{7,9},{8,10},{9,11},{10,... | collective-permute-start | bytes 196616 | tf_op jit(solution)/shard_map/ppermute | solution.py:451

commit v3 on v2

--- a/solution.py
+++ b/solution.py
@@ -17,7 +17,8 @@
 KN = 16
 LANES = 128
 ZROWS = NZ + 8
-UNROLL = 8
+UNROLL = 16
+HALF = NY // 2
 SCALE_ROWS = 8
 F32 = jnp.float32
 BF16 = jnp.bfloat16
@@ -53,8 +54,15 @@
 
 
 def y_table():
-    angle = (np.arange(NY)[:, None] * np.arange(NY)[None, :] % NY) * (2 * np.pi / NY)
-    return np.concatenate([np.cos(angle), np.sin(angle)], axis=1)
+    angle = (np.arange(NY)[:, None] * np.arange(HALF + 1)[None, :] % NY) * (2 * np.pi / NY)
+    return np.concatenate([np.cos(angle[:, :HALF]), np.cos(angle[:, HALF:]), np.sin(angle[:, 1:HALF])], axis=1)
+
+
+def reversal():
+    table = np.zeros((HALF, HALF), ml_dtypes.bfloat16)
+    lane = np.arange(HALF)
+    table[lane, (HALF - lane) % HALF] = 1
+    return table
 
 
 def x_tables(slabs):
@@ -65,14 +73,6 @@
     forward = np.block([[cosine, sine], [-sine, cosine]])
     inverse = np.block([[cosine.T, -sine.T], [sine.T, cosine.T]])
     return forward, inverse
-
-
-def point_order():
-    point = np.arange(POINTS)
-    target = (point % 8) * 64 + point // 8
-    table = np.zeros((POINTS, POINTS), ml_dtypes.bfloat16)
-    table[point, target] = 1
-    return table
 
 
 def split(values):
@@ -113,7 +113,7 @@
         fp_ref[pl.ds(first * 8 + 2 * pair + 1, count, stride=8), :] = pltpu.roll(part, 64, 1)
 
 
-def scatter_columns(fp_ref, place_of, grids, edge_ref, first, live, planes, shift_i):
+def scatter_columns(fp_ref, first, place_of, count, grids, edge_ref, planes, shift_i):
     lane = lane_of((8, LANES))
     in_planes = (lane >= 8 * planes[0]) & (lane < 8 * (planes[-1] + 1))
     point_j = lane & 7
@@ -121,9 +121,9 @@
     def step(index, carry):
         updates = []
         for inner in range(UNROLL):
-            column = first + index * UNROLL + inner
+            column = index * UNROLL + inner
             by, bz = place_of(column)
-            value = fp_ref[pl.ds(pl.multiple_of(column * 8, 8), 8), :]
+            value = fp_ref[pl.ds(pl.multiple_of((first + column) * 8, 8), 8), :]
             begin = 4 * by - 2
             mask = ((lane - begin) & -8) == 0
             terms = []
@@ -143,10 +143,10 @@
                 ref[where, :] = total
         return carry
 
-    lax.fori_loop(0, (live + UNROLL - 1) // UNROLL, step, 0)
-
-
-def sample_columns(pot_refs, edge_ref, place_of, sp_ref, first, live, planes, shift_i):
+    lax.fori_loop(0, lax.shift_right_logical(count + UNROLL - 1, 4), step, 0)
+
+
+def sample_columns(pot_refs, edge_ref, place_of, count, sp_ref, first, planes, shift_i):
     lane = lane_of((8, LANES))
     point_j = lane & 7
     inside = (lane >= 8 * (planes[0] + shift_i)) & (lane < 8 * (planes[-1] + shift_i + 1))
@@ -154,7 +154,7 @@
     def step(index, carry):
         results = []
         for inner in range(UNROLL):
-            column = first + index * UNROLL + inner
+            column = index * UNROLL + inner
             by, bz = place_of(column)
             where = pl.ds(4 * bz, 8)
             begin = 4 * by - 2
@@ -167,12 +167,12 @@
             low = jnp.where(by == 0, 0, jnp.where(by == NY // 8 - 1, 6, 8))
             turned = pltpu.roll(edge_ref[where, :], (8 * shift_i + 4 * is_last) & (LANES - 1), 1)
             mask = inside & (((point_j - low) & -2) == 0)
-            results.append((pl.ds(pl.multiple_of(column * 8, 8), 8), jnp.where(mask, turned, result)))
+            results.append((pl.ds(pl.multiple_of((first + column) * 8, 8), 8), jnp.where(mask, turned, result)))
         for where, result in results:
             sp_ref[where, :] = result
         return carry
 
-    lax.fori_loop(0, (live + UNROLL - 1) // UNROLL, step, 0)
+    lax.fori_loop(0, lax.shift_right_logical(count + UNROLL - 1, 4), step, 0)
 
 
 def far_sums(sp_ref, kinds, stk_ref, first):
@@ -194,56 +194,93 @@
 
 
 def place_in_brick(brick_ref):
-    zbricks = NZ // 4
-
     def place_of(column):
         brick = brick_ref[column]
-        return brick // zbricks, brick % zbricks
+        return lax.shift_right_logical(brick, 7), brick & (NZ // 4 - 1)
 
     return place_of
 
 
-def place_in_facts(facts_ref):
-    return lambda column: (facts_ref[0, column], facts_ref[1, column])
-
-
-def own_kernel(brick_ref, live_ref, charges_ref, kinds_ref, stencil_ref, order_ref,
-               g0, g1, g2, g3, edge_ref, stk_ref, fp_ref):
-    stk_ref[...] = dot(stencil_ref[...], order_ref[...]).astype(BF16)
+def place_in_facts(facts_ref, start):
+    return lambda column: (facts_ref[0, start + column], facts_ref[1, start + column])
+
+
+def pack_kernel(live_ref, charges_ref, brick_ref, stencil_ref, out_ref):
+    slots = charges_ref.shape[1]
+    charges = charges_ref[...].astype(F32)
+    held = jnp.where(lane_of(charges.shape) < live_ref[0], charges, 0.0)
+    row = lax.broadcasted_iota(jnp.int32, (16, slots), 0)
+    brick = jnp.broadcast_to(brick_ref[...], (16, slots))
+    facts = jnp.where(row == 0, lax.shift_right_logical(brick, 7), brick & (NZ // 4 - 1))
+    facts = jnp.where(row == 2, stencil_ref[...], jnp.where(row == 3, live_ref[0], facts))
+    out_ref[...] = jnp.concatenate([held, facts.astype(F32)], axis=0).astype(BF16)
+
+
+def facts_of(packed_ref):
+    return packed_ref[PANELS : PANELS + 8, :].astype(F32).astype(jnp.int32)
+
+
+def own_kernel(brick_ref, live_ref, packed_ref, stencil_ref,
+               g0, g1, g2, g3, edge_ref, stk_ref, fp_ref, rows_ref, sem):
+    copy = pltpu.make_async_copy(stencil_ref, rows_ref, sem)
+    copy.start()
     for ref in (g0, g1, g2, g3, edge_ref):
         ref[...] = jnp.zeros_like(ref)
-    slots = charges_ref.shape[1]
+    shape = (POINTS, POINTS)
+    point = lax.broadcasted_iota(jnp.int32, shape, 0)
+    target = (point & 7) * 64 + lax.shift_right_logical(point, 3)
+    order = jnp.where(lane_of(shape) == target, 1.0, 0.0).astype(BF16)
+    kinds = facts_of(packed_ref)[2:3, :]
+    slots = packed_ref.shape[1]
     live = live_ref[0]
+    copy.wait()
+    stk_ref[...] = dot(rows_ref[...], order).astype(BF16)
+
+    @pl.when(live > LANES)
+    def _():
+        footprints(packed_ref[0:PANELS, :], kinds, stk_ref, fp_ref, 0)
+
+    @pl.when(live <= LANES)
+    def _():
+        footprints(packed_ref[0:PANELS, 0:LANES], kinds[:, 0:LANES], stk_ref, fp_ref, 0)
+
+    scatter_columns(fp_ref, 0, place_in_brick(brick_ref), live, (g0, g1, g2, g3), edge_ref, (0, 1, 2, 3), 2)
+
+
+BESIDE = (((0, 1), 6), ((2, 3), -2))
+
+
+def chunks_beside(facts_ref, slots):
     for first in range(0, slots, LANES):
-        @pl.when(live > first)
-        def _(columns=slice(first, first + LANES)):
-            footprints(charges_ref[:, columns], kinds_ref[0:1, columns], stk_ref, fp_ref, columns.start)
-    scatter_columns(fp_ref, place_in_brick(brick_ref), (g0, g1, g2, g3), edge_ref, 0, live, (0, 1, 2, 3), 2)
+        counts = [jnp.clip(facts_ref[3, side * slots] - first, 0, LANES) for side in range(2)]
+        yield first, counts
+
+
+def both_sides(ref, slots, first):
+    return jnp.concatenate(
+        [ref[:, side * slots + first : side * slots + first + LANES] for side in range(2)], axis=1
+    )
 
 
 def beside_kernel(prev_ref, next_ref, stk_ref, i0, i1, i2, i3, iedge,
-                  g0, g1, g2, g3, out_edge, out_facts, edge_ref, fp_ref, facts_ref, sem):
+                  g0, g1, g2, g3, edge_ref, out_edge, out_facts, fp_ref, facts_ref, sem):
     slots = prev_ref.shape[1]
     for side, source in enumerate((prev_ref, next_ref)):
-        facts = source[PANELS : PANELS + 8, :].astype(F32)
-        out_facts[:, side * slots : (side + 1) * slots] = facts.astype(jnp.int32)
+        out_facts[:, side * slots : (side + 1) * slots] = facts_of(source)
     copy = pltpu.make_async_copy(out_facts, facts_ref, sem)
     copy.start()
-    for ref, source in ((g0, i0), (g1, i1), (g2, i2), (g3, i3), (edge_ref, iedge)):
-        ref[...] = source[...]
     copy.wait()
-    sides = ((prev_ref, (0, 1), 6), (next_ref, (2, 3), -2))
-    for side, (source, planes, shift_i) in enumerate(sides):
-        start = side * slots
-        live = facts_ref[3, start]
-        for first in range(0, slots, LANES):
-            @pl.when(live > first)
-            def _(source=source, start=start, first=first):
-                here = slice(first, first + LANES)
-                kinds = out_facts[2:3, start + first : start + first + LANES]
-                footprints(source[0:PANELS, here], kinds, stk_ref, fp_ref, start + first)
-        scatter_columns(fp_ref, place_in_facts(facts_ref), (g0, g1, g2, g3), edge_ref,
-                        start, live, planes, shift_i)
+    for first, counts in chunks_beside(facts_ref, slots):
+        @pl.when(counts[0] + counts[1] > 0)
+        def _(first=first):
+            here = slice(first, first + LANES)
+            charges = jnp.concatenate([prev_ref[0:PANELS, here], next_ref[0:PANELS, here]], axis=1)
+            kinds = both_sides(out_facts.at[2:3, :], slots, first)
+            footprints(charges, kinds, stk_ref, fp_ref, 2 * first)
+
+        for side, (planes, shift_i) in enumerate(BESIDE):
+            scatter_columns(fp_ref, 2 * first + side * LANES, place_in_facts(facts_ref, side * slots + first),
+                            counts[side], (g0, g1, g2, g3), edge_ref, planes, shift_i)
     edge_ref[0:8, :] += edge_ref[NZ:ZROWS, :]
     total = edge_ref[0:LANES, :]
     for block in range(1, 4):
@@ -287,12 +324,25 @@
         )
 
 
-def plane_kernel(slabs, planes, offset_ref, in_ref, hat_ref, y_ref, x_ref, out_ref, ah_ref, al_ref):
+def hat_kernel(planes, offset_ref, hat_ref, turn_ref, out_ref):
+    length = hat_ref.shape[1]
+    values = jnp.concatenate([hat_ref[offset_ref[0] + plane] for plane in range(planes)], axis=0)
+    values = values * (1.0 / (length * NY))
+    upper = values[:, HALF:]
+    high, low = split(upper)
+    rest = (upper - high.astype(F32) - low.astype(F32)).astype(BF16)
+    turn = turn_ref[...]
+    upper = dot(high, turn) + (dot(low, turn) + dot(rest, turn))
+    for plane in range(planes):
+        here = slice(plane * length, (plane + 1) * length)
+        out_ref[plane] = jnp.concatenate([values[here, :HALF], upper[here, :]], axis=1)
+
+
+def plane_kernel(slabs, planes, in_ref, hat_ref, y_ref, x_ref, out_ref, ah_ref, al_ref):
     length = 4 * slabs
     rows = planes * length
     parts = 2 * planes
     stride = 4 * parts + SCALE_ROWS
-    offset = offset_ref[0]
 
     def pieces():
         for tile in range(2):
@@ -311,10 +361,17 @@
         high, low = split(in_ref[where, :] * scales[tile])
         ah_ref[row : row + slabs, tile * LANES : (tile + 1) * LANES] = high
         al_ref[row : row + slabs, tile * LANES : (tile + 1) * LANES] = low
-    along_y = (y_ref[0:NY, :], y_ref[NY : 2 * NY, :])
-    turned = dot3((ah_ref[...], al_ref[...]), along_y)
-    real = turned[:rows, :NY] + turned[rows:, NY:]
-    imag = turned[rows:, :NY] - turned[:rows, NY:]
+    first_lane = lane_of((rows, HALF)) == 0
+    turned = dot3((ah_ref[...], al_ref[...]), (y_ref[0:NY, :], y_ref[NY : 2 * NY, :]))
+    even = (turned[:rows, :HALF], turned[rows:, :HALF])
+    odd = (turned[:rows, HALF:], turned[rows:, HALF:])
+    zero_odd = [jnp.where(first_lane, 0.0, values) for values in odd]
+    real = jnp.concatenate(
+        [even[0] + zero_odd[1], jnp.where(first_lane, odd[0], even[0] - zero_odd[1])], axis=1
+    )
+    imag = jnp.concatenate(
+        [even[1] - zero_odd[0], jnp.where(first_lane, odd[1], even[1] + zero_odd[0])], axis=1
+    )
     size = 2 * length
     forward = (x_ref[0:size, :], x_ref[size : 2 * size, :])
     inverse = (x_ref[2 * size : 3 * size, :], x_ref[3 * size : 4 * size, :])
@@ -322,15 +379,18 @@
         here = slice(plane * length, (plane + 1) * length)
         there = slice(rows + plane * length, rows + (plane + 1) * length)
         values = dot3(forward, split(jnp.concatenate([real[here], imag[here]], axis=0)))
-        hat = hat_ref[offset + plane] * (1.0 / (length * NY))
-        values = values * jnp.concatenate([hat, hat], axis=0)
-        high, low = split(dot3(inverse, split(values)))
-        ah_ref[here, :] = high[:length]
-        ah_ref[there, :] = high[length:]
-        al_ref[here, :] = low[:length]
-        al_ref[there, :] = low[length:]
-    turned = dot3((ah_ref[...], al_ref[...]), along_y)
-    results = (turned[:rows, :NY] - turned[rows:, NY:], turned[rows:, :NY] + turned[:rows, NY:])
+        values = values * jnp.concatenate([hat_ref[plane], hat_ref[plane]], axis=0)
+        values = dot3(inverse, split(values))
+        low, high = values[:, :HALF], values[:, HALF:]
+        lane = first_lane[:length]
+        even_r = jnp.where(lane, low[:length], low[:length] + high[:length])
+        even_i = jnp.where(lane, low[length:], low[length:] + high[length:])
+        odd_r = jnp.where(lane, high[:length], high[length:] - low[length:])
+        odd_i = jnp.where(lane, high[length:], low[:length] - high[:length])
+        ah_ref[here, :], al_ref[here, :] = split(jnp.concatenate([even_r, odd_r], axis=1))
+        ah_ref[there, :], al_ref[there, :] = split(jnp.concatenate([even_i, odd_i], axis=1))
+    turned = dot3((ah_ref[...], al_ref[...]), (y_ref[2 * NY : 3 * NY, :], y_ref[3 * NY : 4 * NY, :]))
+    results = (turned[:rows], turned[rows:])
     exponent = exponent_of(results)
     scale = jnp.exp2(-exponent)
     results = [result * scale for result in results]
@@ -372,34 +432,47 @@
     wide_ref[NZ:ZROWS, :] = wide_ref[0:8, :]
 
 
-def sampled_sums(place_of, pots, wide_ref, kinds, stk_ref, out_ref, sp_ref, start, slots, live, planes, shift_i):
-    sample_columns(pots, wide_ref, place_of, sp_ref, start, live, planes, shift_i)
-    for first in range(0, slots, LANES):
-        where = slice(start + first, start + first + LANES)
-
-        @pl.when(live > first)
-        def _(first=first, where=where):
-            result = far_sums(sp_ref, kinds[0:1, where], stk_ref, where.start)
-            column = first + lane_of((PANELS, LANES))
-            out_ref[:, where] = jnp.where(column < live, result, 0.0)
-
-        @pl.when(live <= first)
-        def _(where=where):
-            out_ref[:, where] = jnp.zeros((PANELS, LANES), F32)
+def masked(values, live):
+    return jnp.where(lane_of(values.shape) < live, values, 0.0)
 
 
 def own_sample_kernel(brick_ref, live_ref, p0, p1, p2, p3, edge_ref, kinds_ref, stk_ref, out_ref, wide_ref, sp_ref):
     widen_edge(edge_ref, wide_ref)
-    sampled_sums(place_in_brick(brick_ref), (p0, p1, p2, p3), wide_ref, kinds_ref, stk_ref, out_ref, sp_ref,
-                 0, kinds_ref.shape[1], live_ref[0], (0, 1, 2, 3), 2)
-
-
-def beside_sample_kernel(facts_ref, p0, p1, p2, p3, edge_ref, kinds_ref, stk_ref, out_ref, wide_ref, sp_ref):
+    live = live_ref[0]
+    slots = kinds_ref.shape[1]
+    sample_columns((p0, p1, p2, p3), wide_ref, place_in_brick(brick_ref), live, sp_ref, 0, (0, 1, 2, 3), 2)
+
+    @pl.when(live > LANES)
+    def _():
+        out_ref[...] = masked(far_sums(sp_ref, kinds_ref[...], stk_ref, 0), live)
+
+    @pl.when(live <= LANES)
+    def _():
+        out_ref[:, 0:LANES] = masked(far_sums(sp_ref, kinds_ref[:, 0:LANES], stk_ref, 0), live)
+        out_ref[:, LANES:slots] = jnp.zeros((PANELS, slots - LANES), F32)
+
+
+def beside_sample_kernel(facts_ref, p0, p1, p2, p3, edge_ref, kinds_ref, stk_ref, out0, out1, wide_ref, sp_ref):
     widen_edge(edge_ref, wide_ref)
     slots = kinds_ref.shape[1] // 2
-    for side, (planes, shift_i) in enumerate((((0, 1), 6), ((2, 3), -2))):
-        sampled_sums(place_in_facts(facts_ref), (p0, p1, p2, p3), wide_ref, kinds_ref.at[2:3, :], stk_ref, out_ref,
-                     sp_ref, side * slots, slots, facts_ref[3, side * slots], planes, shift_i)
+    outs = (out0, out1)
+    for first, counts in chunks_beside(facts_ref, slots):
+        here = slice(first, first + LANES)
+        for side, (planes, shift_i) in enumerate(BESIDE):
+            sample_columns((p0, p1, p2, p3), wide_ref, place_in_facts(facts_ref, side * slots + first),
+                           counts[side], sp_ref, 2 * first + side * LANES, planes, shift_i)
+
+        @pl.when(counts[0] + counts[1] > 0)
+        def _(first=first, counts=counts, here=here):
+            kinds = both_sides(kinds_ref.at[2:3, :], slots, first)
+            result = far_sums(sp_ref, kinds, stk_ref, 2 * first)
+            for side, out in enumerate(outs):
+                out[:, here] = masked(result[:, side * LANES : (side + 1) * LANES], counts[side])
+
+        @pl.when(counts[0] + counts[1] <= 0)
+        def _(here=here):
+            for out in outs:
+                out[:, here] = jnp.zeros((PANELS, LANES), F32)
 
 
 def near_kernel(live_ref, a0, a1, a2, a3, a4, a5, source_ref, block_ref, table_ref, out_ref):
@@ -450,49 +523,51 @@
         ]
         return lax.ppermute(values, both, pairs)
 
-    live = live_count[0]
-    slot = jnp.arange(slots, dtype=jnp.int32)
-    held = jnp.where((slot < live)[None, :], charges, jnp.zeros((), charges.dtype))
-    zbricks = NZ // 4
     kinds = slot_stencil[None, :]
-    facts = jnp.stack(
-        [slot_brick // zbricks, slot_brick % zbricks, slot_stencil, jnp.full((slots,), live)], axis=0
-    )
-    packed = jnp.concatenate(
-        [held, facts.astype(BF16), jnp.zeros((12, slots), BF16)], axis=0
-    )
+    packed = pl.pallas_call(
+        pack_kernel,
+        out_shape=shape_of(PANELS + 16, slots, dtype=BF16),
+        in_specs=[SMEM] + [VMEM] * 3,
+        out_specs=VMEM,
+        compiler_params=PARAMS,
+        name="pack",
+    )(live_count, charges, slot_brick[None, :], kinds)
     from_prev = moved(packed, 1, 0)
     from_next = moved(packed, -1, 0)
-    swapped = moved(held, 0, 1)
+    swapped = moved(packed, 0, 1)
 
     grid = shape_of(ZROWS, LANES)
     g = pl.pallas_call(
         own_kernel,
         out_shape=(grid,) * 5 + (shape_of(KS * PANELS, POINTS, dtype=BF16),),
-        in_specs=[SMEM] * 2 + [VMEM] * 4,
+        in_specs=[SMEM] * 2 + [VMEM, pl.BlockSpec(memory_space=pl.ANY)],
         out_specs=(VMEM,) * 6,
-        scratch_shapes=[pltpu.VMEM((slots * 8, LANES), F32)],
+        scratch_shapes=[
+            pltpu.VMEM((slots * 8, LANES), F32),
+            pltpu.VMEM((KS * PANELS, POINTS), BF16),
+            pltpu.SemaphoreType.DMA,
+        ],
         compiler_params=PARAMS,
         name="own_scatter",
-    )(slot_brick, live_count, held, kinds, stencils.reshape(KS * PANELS, POINTS), jnp.asarray(point_order()))
+    )(slot_brick, live_count, packed, stencils.reshape(KS * PANELS, POINTS))
     grids, stk = g[:5], g[5]
 
     g = pl.pallas_call(
         beside_kernel,
-        out_shape=(grid,) * 4 + (shape_of(LANES, LANES), shape_of(8, 2 * slots, dtype=jnp.int32)),
+        out_shape=(grid,) * 5 + (shape_of(LANES, LANES), shape_of(8, 2 * slots, dtype=jnp.int32)),
         in_specs=[VMEM] * 8,
-        out_specs=(VMEM,) * 6,
+        out_specs=(VMEM,) * 7,
         scratch_shapes=[
-            pltpu.VMEM((ZROWS, LANES), F32),
             pltpu.VMEM((2 * slots * 8, LANES), F32),
             pltpu.SMEM((8, 2 * slots), jnp.int32),
             pltpu.SemaphoreType.DMA,
         ],
+        input_output_aliases={3: 0, 4: 1, 5: 2, 6: 3, 7: 4},
         compiler_params=PARAMS,
         name="beside_scatter",
     )(from_prev, from_next, stk, *grids)
-    facts2 = g[5]
-    edge = moved(g[4], 0, 1)
+    facts2 = g[6]
+    edge = moved(g[5], 0, 1)
 
     forward, inverse = z_tables(slabs, tiles)
     rows = owners * (4 * parts + SCALE_ROWS)
@@ -513,9 +588,23 @@
     def widened(values):
         return values.astype(F32).reshape(rows, LANES)
 
+    hat, sent = lax.optimization_barrier((kernel_hat, sent))
     got = exchanged(sent)
-
-    pool = [from_prev, moved(swapped, 1, 0), held, swapped, from_next, moved(swapped, -1, 0)]
+    me = lax.axis_index("slab") * tiles + lax.axis_index("tile")
+    offset = (me >= owners // 2).astype(jnp.int32)[None]
+    hat = pl.pallas_call(
+        functools.partial(hat_kernel, planes),
+        out_shape=shape_of(planes, length, NY),
+        in_specs=[SMEM] + [VMEM] * 2,
+        out_specs=VMEM,
+        compiler_params=PARAMS,
+        name="hat_order",
+    )(offset, hat, jnp.asarray(reversal()))
+
+    swapped_prev = moved(swapped, 1, 0)
+    swapped_next = moved(swapped, -1, 0)
+    got, hat, swapped_prev, swapped_next = lax.optimization_barrier((got, hat, swapped_prev, swapped_next))
+    pool = [from_prev, swapped_prev, packed, swapped, from_next, swapped_next]
     direction = near_source // slots
     pool_index = (direction // 3 * 2 + (direction % 3 != 1).astype(jnp.int32)) * slots + near_source % slots
     near = pl.pallas_call(
@@ -527,17 +616,15 @@
         name="near_field",
     )(live_count, *pool, pool_index.T, near_block.T, near_blocks.reshape(PANELS, KN * PANELS))
 
-    me = lax.axis_index("slab") * tiles + lax.axis_index("tile")
-    offset = (me >= owners // 2).astype(jnp.int32)[None]
     back = pl.pallas_call(
         functools.partial(plane_kernel, slabs, planes),
         out_shape=shape_of(rows, LANES),
-        in_specs=[SMEM] + [VMEM] * 4,
+        in_specs=[VMEM] * 4,
         out_specs=VMEM,
         scratch_shapes=[pltpu.VMEM((2 * planes * length, NY), BF16)] * 2,
         compiler_params=PARAMS,
         name="plane_filter",
-    )(offset, widened(got), kernel_hat, jnp.asarray(halves(y_table())), jnp.asarray(halves(*x_tables(slabs))))
+    )(widened(got), hat, jnp.asarray(halves(y_table(), y_table().T)), jnp.asarray(halves(*x_tables(slabs))))
     back, near = lax.optimization_barrier((exchanged(back), near))
 
     pot = pl.pallas_call(
@@ -550,21 +637,29 @@
     )(widened(back), jnp.asarray(halves(inverse)))
     edge = moved(pot[4], 0, 1)
 
-    def sampling(width):
-        return dict(
-            out_shape=shape_of(PANELS, width),
-            out_specs=VMEM,
-            scratch_shapes=[pltpu.VMEM((ZROWS, LANES), F32), pltpu.VMEM((width * 8, LANES), F32)],
-            compiler_params=PARAMS,
-        )
-
+    def sample_scratch(width):
+        return [pltpu.VMEM((ZROWS, LANES), F32), pltpu.VMEM((width * 8, LANES), F32)]
+
+    sums = shape_of(PANELS, slots)
     others = pl.pallas_call(
-        beside_sample_kernel, in_specs=[SMEM] + [VMEM] * 7, name="beside_sample", **sampling(2 * slots)
+        beside_sample_kernel,
+        out_shape=(sums, sums),
+        in_specs=[SMEM] + [VMEM] * 7,
+        out_specs=(VMEM, VMEM),
+        scratch_shapes=sample_scratch(2 * slots),
+        compiler_params=PARAMS,
+        name="beside_sample",
     )(facts2, *pot[:4], edge, facts2, stk)
-    to_prev = moved(others[:, :slots], -1, 0)
-    to_next = moved(others[:, slots:], 1, 0)
+    to_prev = moved(others[0], -1, 0)
+    to_next = moved(others[1], 1, 0)
     own = pl.pallas_call(
-        own_sample_kernel, in_specs=[SMEM] * 2 + [VMEM] * 7, name="own_sample", **sampling(slots)
+        own_sample_kernel,
+        out_shape=sums,
+        in_specs=[SMEM] * 2 + [VMEM] * 7,
+        out_specs=VMEM,
+        scratch_shapes=sample_scratch(slots),
+        compiler_params=PARAMS,
+        name="own_sample",
     )(slot_brick, live_count, *pot[:4], edge, kinds, stk)
     return own + near + to_prev + to_next
 

time: 94.6 us -> 89.1 us (0.942)
  Pallas kernels: 29.5 us -> 24.5 us
  other arithmetic: 4.83 us -> 2.68 us
  starting transfers between devices: 20.4 us -> 22.2 us
  waiting for transfers between devices: 33.5 us -> 34.5 us
    pallas_call x3 -> x5, Pallas kernels: 13.5 us -> 11.1 us  [the longest x1 4.21 us: body(): pl.pallas_call(beside_kernel, out_shape=(grid,) * 5 + (shape_of(LANES, LA...]
    pallas_call x1, Pallas kernels: 5.61 us -> 3.85 us  [body(): pl.pallas_call(functools.partial(plane_kernel, slabs, planes), out_shape=...]
    all_to_all x2, starting transfers between devices: 5.35 us -> 7 us  [exchanged(): values = lax.all_to_all(values, axes, 0, 0, tiled=True)]
    another operation x2 -> x0, other arithmetic: 1.37 us -> none
    ppermute x9, waiting for transfers between devices: 15.2 us -> 16.5 us  [moved(): return lax.ppermute(values, both, pairs)]
    unnamed x28 -> x30, local copies, waits for them, and re-layouts: 3.68 us -> 3.4 us
  transfers between devices with their start and end apart: 11 -> 11, of which waited for: 6 -> 8; matrix products, arithmetic and copies ran while one was open for 0% -> 0% of each run, Pallas kernels for 11% -> 9%
where the time goes in v3:
time: 89.1 us; the launch traced here: 88.4 us
  waiting for transfers between devices  34.5 us (39%)
  Pallas kernels  24.5 us (27%)
  starting transfers between devices  22.2 us (25%)
  local copies, waits for them, and re-layouts  3.6 us (4%)
  other arithmetic  2.68 us (3%)
  between operations  0.94 us (1%)
    all_to_all x2, waiting for transfers between devices, exchanged(): values = lax.all_to_all(values, axes, 0, 0, tiled=True)  18 us
    ppermute x9, waiting for transfers between devices, moved(): return lax.ppermute(values, both, pairs)  16.5 us
    ppermute x9, starting transfers between devices, moved(): return lax.ppermute(values, both, pairs)  15.2 us
    all_to_all x2, starting transfers between devices, exchanged(): values = lax.all_to_all(values, axes, 0, 0, tiled=True)  7 us
    pallas_call x1, Pallas kernels, body(): pl.pallas_call(beside_kernel, out_shape=(grid,) * 5 + (shape_of(LANES, LA...  4.21 us
    pallas_call x1, Pallas kernels, body(): pl.pallas_call(beside_sample_kernel, out_shape=(sums, sums), in_specs=[SM...  4.1 us
    pallas_call x1, Pallas kernels, body(): pl.pallas_call(functools.partial(plane_kernel, slabs, planes), out_shape=...  3.85 us
    unnamed x30, local copies, waits for them, and re-layouts  3.4 us
  transfers between devices with their start and end apart: 11, of which 8 were waited for; matrix products, arithmetic and copies ran while one was open for 0% of the time, Pallas kernels for 9%

profile of v3, /device:TPU:0, one launch (start us, length us, event | category | flops | bytes accessed | tf_op | source)
XLA Modules:
  0.0 88.4 jit_solution(18029694156130665582)
XLA Ops:
  0.7 0.7 copy-done.7
  1.4 0.7 copy-done.8
  2.1 0.7 copy-done.11
  2.8 3.0 %collective-permute-start = (bf16[80,256]{1,0:T(8,128)(2,1)S(1)}, bf16[80,256]{1,0:T(8,128)(2,1)S(1)}, u32[]{:S(2)}, u32[]{:S(2)}) collective-permute-start(bf16[80,256]{1,0:T(8,128)(2,1)S(1)} %pack.1.packed_ref.a2), channel_id=1, source_target_pairs={{0,2},{1,3},{2,4},{3,5},{4,6},{5,7},{6,8},{7,9},{8,10},{9,11},{10,... | collective-permute-start | bytes 122888 | tf_op jit(solution)/shard_map/ppermute | solution.py:524
  5.8 4.1 %collective-permute-start.1 = (bf16[80,256]{1,0:T(8,128)(2,1)S(1)}, bf16[80,256]{1,0:T(8,128)(2,1)S(1)}, u32[]{:S(2)}, u32[]{:S(2)}) collective-permute-start(bf16[80,256]{1,0:T(8,128)(2,1)S(1)} %pack.1.packed_ref.a2), channel_id=1, source_target_pairs={{0,30},{1,31},{2,0},{3,1},{4,2},{5,3},{6,4},{7,5},{8,6},{9,7},{10,... | collective-permute-start | bytes 122888 | tf_op jit(solution)/shard_map/ppermute | solution.py:524
  9.8 1.2 %copy-done.1 = bf16[16,64,512]{2,1,0:T(8,128)(2,1)S(1)} copy-done((bf16[16,64,512]{2,1,0:T(8,128)(2,1)S(1)}, bf16[16,64,512]{2,1,0:T(8,128)(2,1)}, u32[]{:S(2)}) %copy-start.1) | copy-done | bytes 1048600
  11.1 3.3 %own_scatter.1 = (f32[520,128]{1,0:T(8,128)S(1)}, f32[520,128]{1,0:T(8,128)S(1)}, f32[520,128]{1,0:T(8,128)S(1)}, f32[520,128]{1,0:T(8,128)S(1)}, f32[520,128]{1,0:T(8,128)S(1)}, /*index=5*/bf16[1024,512]{1,0:T(8,128)(2,1)S(1)}) custom-call(s32[256]{0:T(256)S(1)} %copy-done.8, s32[1]{0:T(128)S(6)} %copy.25.live_ref, bf16[80,256]{1,0:T(8,128)(2,1)S(1)} %pack.1.packed_ref.a2, ...), custom_call_target="tpu_custom_call" | custom-call | tf_op jit(solution)/shard_map/own_scatter/pallas_call | solution.py:540
  14.4 0.0 collective-permute-done.prev_ref.a0
  14.4 0.0 copy-start
  14.4 4.2 %beside_scatter.1 = (f32[520,128]{1,0:T(8,128)S(1)}, f32[520,128]{1,0:T(8,128)S(1)}, f32[520,128]{1,0:T(8,128)S(1)}, f32[520,128]{1,0:T(8,128)S(1)}, f32[520,128...) custom-call(bf16[80,256]{1,0:T(8,128)(2,1)S(1)} %collective-permute-, ...), custom_call_target="tpu_custom_call", output_to_operand_aliasing={{0}: (3, {}), {1}: (4, {}), {2}: (5, {}), {3}: (6, {}), {4}... | custom-call | tf_op jit(solution)/shard_map/beside_scatter/pallas_call | solution.py:555
  18.6 0.1 collective-permute-start.2
  18.7 1.2 %collective-permute-done.2.edge_ref = f32[128,128]{1,0:T(8,128)S(1)} collective-permute-done((f32[128,128]{1,0:T(8,128)S(1)}, f32[128,128]{1,0:T(8,128)S(1)}, u32[]{:S(2)}, u32[]{:S(2)}) %collective-permute-start.2) | collective-permute-done | bytes 65568 | tf_op jit(solution)/shard_map/ppermute | solution.py:524
  20.0 2.2 %z_forward.1 = f32[2304,128]{1,0:T(8,128)S(1)} custom-call(f32[520,128]{1,0:T(8,128)S(1)} %get-tuple-element.38.g0, f32[520,128]{1,0:T(8,128)S(1)} %get-tuple-element.39.g1, f32[520,128]{1,0:T(8,128)S(1)} %get-tuple-element.40.g2, f32[520,128]{1,0:T(8,128)S(1)} %get-tuple-element.41.g3, f32[128,128]{1,0:T(8,128)S(1)} %collective-permute-done.2.edge_ref, ...), custom_call_target="tpu_custom_call" | custom-call | tf_op jit(solution)/shard_map/z_forward/pallas_call | solution.py:574
  22.1 0.0 copy-start.2
  22.2 0.0 copy-start.6
  22.2 0.9 %convert_element_type.12 = f16[2304,128]{1,0:T(8,128)(2,1)} convert(f32[2304,128]{1,0:T(8,128)S(1)} %z_forward.1) | non-fusion elementwise | flops 294912 | bytes 1769472 | tf_op jit(solution)/shard_map/convert_element_type | solution.py:584
  23.1 4.3 %all-to-all-start = ((f16[32,72,128]{2,1,0:T(8,128)(2,1)}), f16[32,72,128]{2,1,0:T(8,128)(2,1)S(1)}, u32[]{:S(2)}, u32[]{:S(2)}) async-start(f16[32,72,128]{2,1,0:T(8,128)(2,1)} %bitcast.20), calls=%async_computation | async-start | bytes 1179648 | tf_op jit(solution)/shard_map/all_to_all | solution.py:585
  27.3 0.3 collective-permute-start.3
  27.6 1.0 %collective-permute-done.3.a3 = bf16[80,256]{1,0:T(8,128)(2,1)S(1)} collective-permute-done((bf16[80,256]{1,0:T(8,128)(2,1)S(1)}, bf16[80,256]{1,0:T(8,128)(2,1)S(1)}, u32[]{:S(2)}, u32[]{:S(2)}) %collective-permute-start.3) | collective-permute-done | bytes 40992 | tf_op jit(solution)/shard_map/ppermute | solution.py:524
  28.6 1.8 %collective-permute-start.4 = (bf16[80,256]{1,0:T(8,128)(2,1)S(1)}, bf16[80,256]{1,0:T(8,128)(2,1)S(1)}, u32[]{:S(2)}, u32[]{:S(2)}) collective-permute-start(bf16[80,256]{1,0:T(8,128)(2,1)S(1)} %collective-permute-done.3.a3), channel_id=1, source_target_pairs={{0,2},{1,3},{2,4},{3,5},{4,6},{5,7},{6,8},{7,9},{8,10},{9,11},{10,... | collective-permute-start | bytes 122888 | tf_op jit(solution)/shard_map/ppermute | solution.py:524
  30.4 3.9 %collective-permute-start.5 = (bf16[80,256]{1,0:T(8,128)(2,1)S(1)}, bf16[80,256]{1,0:T(8,128)(2,1)S(1)}, u32[]{:S(2)}, u32[]{:S(2)}) collective-permute-start(bf16[80,256]{1,0:T(8,128)(2,1)S(1)} %collective-permute-done.3.a3), channel_id=1, source_target_pairs={{0,30},{1,31},{2,0},{3,1},{4,2},{5,3},{6,4},{7,5},{8,6},{9,7},{10,... | collective-permute-start | bytes 122888 | tf_op jit(solution)/shard_map/ppermute | solution.py:524
  34.2 0.3 hat_order.1.hat_ref
  34.5 0.0 copy-start.4
  34.5 0.0 copy-start.5
  34.5 9.7 %collective-permute-done.4.a1 = bf16[80,256]{1,0:T(8,128)(2,1)S(1)} collective-permute-done((bf16[80,256]{1,0:T(8,128)(2,1)S(1)}, bf16[80,256]{1,0:T(8,128)(2,1)S(1)}, u32[]{:S(2)}, u32[]{:S(2)}) %collective-permute-start.4) | collective-permute-done | bytes 40992 | tf_op jit(solution)/shard_map/ppermute | solution.py:524
  44.3 2.2 %all-to-all-done = f16[32,72,128]{2,1,0:T(8,128)(2,1)S(1)} async-done(((f16[32,72,128]{2,1,0:T(8,128)(2,1)}), f16[32,72,128]{2,1,0:T(8,128)(2,1)S(1)}, u32[]{:S(2)}, u32[]{:S(2)}) %all-to-all-start) | async-done | bytes 589856 | tf_op jit(solution)/shard_map/all_to_all | solution.py:585
  46.4 0.1 bitcast_convert_fusion.1.in_ref
  46.6 3.9 %plane_filter.1 = f32[2304,128]{1,0:T(8,128)S(1)} custom-call(f32[2304,128]{1,0:T(8,128)S(1)} %bitcast_convert_fusion.1.in_ref, f32[8,64,256]{2,1,0:T(8,128)S(1)} %hat_order.1.hat_ref, bf16[1024,256]{1,0:T(8,128)(2,1)S(1)} %copy-done.4, bf16[512,128]{1,0:T(8,128)(2,1)S(1)} %copy-done.5), custom_call_target="tpu_custom_call" | custom-call | tf_op jit(solution)/shard_map/plane_filter/pallas_call | solution.py:619
  50.4 0.0 copy-start.13
  50.5 0.9 %convert_element_type.13 = f16[2304,128]{1,0:T(8,128)(2,1)} convert(f32[2304,128]{1,0:T(8,128)S(1)} %plane_filter.1) | non-fusion elementwise | flops 294912 | bytes 1769472 | tf_op jit(solution)/shard_map/convert_element_type | solution.py:584
  51.3 2.7 %all-to-all-start.1 = ((f16[32,72,128]{2,1,0:T(8,128)(2,1)}), f16[32,72,128]{2,1,0:T(8,128)(2,1)S(1)}, u32[]{:S(2)}, u32[]{:S(2)}) async-start(f16[32,72,128]{2,1,0:T(8,128)(2,1)} %bitcast.6), calls=%async_computation.1 | async-start | bytes 1179648 | tf_op jit(solution)/shard_map/all_to_all | solution.py:585
  54.1 0.2 reshape.27.table_ref
  54.3 0.0 copy-start.3
  54.4 2.1 %near_field.1 = f32[64,256]{1,0:T(8,128)S(1)} custom-call(s32[1]{0:T(128)S(6)} %copy.25.live_ref, bf16[80,256]{1,0:T(8,128)(2,1)S(1)} %collective-permute-done.prev_ref.a0, bf16[80,256]{1,0:T(8,128)(2,1)S(1)} %collective-permute-done.4.a1, bf16[80,256]{1,0:T(8,128)(2,1)S(1)} %pack.1.packed_ref.a2, bf16[80,256]{1,0:T(8,128)(2,1)S(1)} %collective-permute-done.3.a3, ...), custom_call_target="tpu_custom_call" | custom-call | tf_op jit(solution)/shard_map/near_field/pallas_call | solution.py:610
  56.5 15.8 %all-to-all-done.1 = f16[32,72,128]{2,1,0:T(8,128)(2,1)S(1)} async-done(((f16[32,72,128]{2,1,0:T(8,128)(2,1)}), f16[32,72,128]{2,1,0:T(8,128)(2,1)S(1)}, u32[]{:S(2)}, u32[]{:S(2)}) %all-to-all-start.1) | async-done | bytes 589856 | tf_op jit(solution)/shard_map/all_to_all | solution.py:585
  72.3 0.1 bitcast_convert_fusion.in_ref
  72.5 1.9 %z_inverse.1 = (f32[520,128]{1,0:T(8,128)S(1)}, f32[520,128]{1,0:T(8,128)S(1)}, f32[520,128]{1,0:T(8,128)S(1)}, f32[520,128]{1,0:T(8,128)S(1)}, bf16[128,128]{1,0:T(8,128)(2,1)S(1)}) custom-call(f32[2304,128]{1,0:T(8,128)S(1)} %bitcast_convert_fusion.in_ref, bf16[1024,512]{1,0:T(8,128)(2,1)S(1)} %copy-done.3), custom_call_target="tpu_custom_call" | custom-call | tf_op jit(solution)/shard_map/z_inverse/pallas_call | solution.py:630
  74.4 0.0 copy-start.9
  74.4 0.0 copy-start.12
  74.4 0.1 collective-permute-start.6
  74.5 1.2 %collective-permute-done.6.edge_ref = bf16[128,128]{1,0:T(8,128)(2,1)S(1)} collective-permute-done((bf16[128,128]{1,0:T(8,128)(2,1)S(1)}, bf16[128,128]{1,0:T(8,128)(2,1)S(1)}, u32[]{:S(2)}, u32[]{:S(2)}) %collective-permute-start.6) | collective-permute-done | bytes 32800 | tf_op jit(solution)/shard_map/ppermute | solution.py:524
  75.7 4.1 %beside_sample.1 = (f32[64,256]{1,0:T(8,128)S(1)}, f32[64,256]{1,0:T(8,128)S(1)}) custom-call(s32[8,512]{1,0:T(8,128)S(1)} %get-tuple-element.56.facts_ref.kinds_ref, f32[520,128]{1,0:T(8,128)S(1)} %get-tuple-element.50.p0, f32[520,128]{1,0:T(8,128)S(1)} %get-tuple-element.51.p1, f32[520,128]{1,0:T(8,128)S(1)} %get-tuple-element.52.p2, ...), custom_call_target="tpu_custom_call" | custom-call | tf_op jit(solution)/shard_map/beside_sample/pallas_call | solution.py:644
  79.8 0.1 collective-permute-start.7
  79.8 2.0 %collective-permute-start.8 = (f32[64,256]{1,0:T(8,128)S(1)}, f32[64,256]{1,0:T(8,128)S(1)}, u32[]{:S(2)}, u32[]{:S(2)}) collective-permute-start(f32[64,256]{1,0:T(8,128)S(1)} %get-tuple-element.58), channel_id=1, source_target_pairs={{0,2},{1,3},{2,4},{3,5},{4,6},{5,7},{6,8},{7,9},{8,10},{9,11},{10,... | collective-permute-start | bytes 196616 | tf_op jit(solution)/shard_map/ppermute | solution.py:524
  81.9 2.5 %own_sample.1 = f32[64,256]{1,0:T(8,128)S(1)} custom-call(s32[256]{0:T(256)S(1)} %copy-done.9, s32[1]{0:T(128)S(6)} %copy.25.live_ref, f32[520,128]{1,0:T(8,128)S(1)} %get-tuple-element.50.p0, f32[520,128]{1,0:T(8,128)S(1)} %get-tuple-element.51.p1, f32[520,128]{1,0:T(8,128)S(1)} %get-tuple-element.52.p2, f32[520,128]{1,0:T(8,128)S(1)} %get-tuple-element.53.p3, ...), custom_call_target="tpu_custom_call" | custom-call | tf_op jit(solution)/shard_map/own_sample/pallas_call | solution.py:655
  84.4 0.3 collective-permute-done.7
  84.7 3.1 %collective-permute-done.8 = f32[64,256]{1,0:T(8,128)S(1)} collective-permute-done((f32[64,256]{1,0:T(8,128)S(1)}, f32[64,256]{1,0:T(8,128)S(1)}, u32[]{:S(2)}, u32[]{:S(2)}) %collective-permute-start.8) | collective-permute-done | bytes 65568 | tf_op jit(solution)/shard_map/ppermute | solution.py:524
  87.8 0.6 add_add_fusion
  (21 shorter events, 0.1 us)
Async XLA Ops:
  0.7 0.8 copy-start.7
  1.4 0.7 copy-start.8
  2.1 0.7 copy-start.11
  2.8 11.6 %collective-permute-start = (bf16[80,256]{1,0:T(8,128)(2,1)S(1)}, bf16[80,256]{1,0:T(8,128)(2,1)S(1)}, u32[]{:S(2)}, u32[]{:S(2)}) collective-permute-start(bf16[80,256]{1,0:T(8,128)(2,1)S(1)} %pack.1.packed_ref.a2), channel_id=1, source_target_pairs={{0,2},{1,3},{2,4},{3,5},{4,6},{5,7},{6,8},{7,9},{8,10},{9,11},{10,... | collective-permute-start | bytes 122888 | tf_op jit(solution)/shard_map/ppermute | solution.py:524
  5.8 8.6 %collective-permute-start.1 = (bf16[80,256]{1,0:T(8,128)(2,1)S(1)}, bf16[80,256]{1,0:T(8,128)(2,1)S(1)}, u32[]{:S(2)}, u32[]{:S(2)}) collective-permute-start(bf16[80,256]{1,0:T(8,128)(2,1)S(1)} %pack.1.packed_ref.a2), channel_id=1, source_target_pairs={{0,30},{1,31},{2,0},{3,1},{4,2},{5,3},{6,4},{7,5},{8,6},{9,7},{10,... | collective-permute-start | bytes 122888 | tf_op jit(solution)/shard_map/ppermute | solution.py:524
  9.8 1.2 %copy-start.1 = (bf16[16,64,512]{2,1,0:T(8,128)(2,1)S(1)}, bf16[16,64,512]{2,1,0:T(8,128)(2,1)}, u32[]{:S(2)}) copy-start(bf16[16,64,512]{2,1,0:T(8,128)(2,1)} %param.18) | copy-start | bytes 3145732
  14.4 5.6 %copy-start = (bf16[1024,512]{1,0:T(8,128)(2,1)S(1)}, bf16[1024,512]{1,0:T(8,128)(2,1)}, u32[]{:S(2)}) copy-start(bf16[1024,512]{1,0:T(8,128)(2,1)} %constant.65.clone.w_ref) | copy-start | bytes 3145732
  18.6 1.3 %collective-permute-start.2 = (f32[128,128]{1,0:T(8,128)S(1)}, f32[128,128]{1,0:T(8,128)S(1)}, u32[]{:S(2)}, u32[]{:S(2)}) collective-permute-start(f32[128,128]{1,0:T(8,128)S(1)} %get-tuple-element.42), channel_id=1, source_target_pairs={{0,1},{1,0},{2,3},{3,2},{4,5},{5,4},{6,7},{7,6},{8,9},{9,8},{10,11... | collective-permute-start | bytes 196616 | tf_op jit(solution)/shard_map/ppermute | solution.py:524
  22.1 12.1 %copy-start.2 = (f32[16,64,256]{2,1,0:T(8,128)S(1)}, f32[16,64,256]{2,1,0:T(8,128)}, u32[]{:S(2)}) copy-start(f32[16,64,256]{2,1,0:T(8,128)} %hat_ref) | copy-start | bytes 3145732
  22.2 12.1 %copy-start.6 = (bf16[128,128]{1,0:T(8,128)(2,1)S(1)}, bf16[128,128]{1,0:T(8,128)(2,1)}, u32[]{:S(2)}) copy-start(bf16[128,128]{1,0:T(8,128)(2,1)} %constant.66.clone.turn_ref) | copy-start | bytes 98308
  23.1 23.4 %all-to-all-start = ((f16[32,72,128]{2,1,0:T(8,128)(2,1)}), f16[32,72,128]{2,1,0:T(8,128)(2,1)S(1)}, u32[]{:S(2)}, u32[]{:S(2)}) async-start(f16[32,72,128]{2,1,0:T(8,128)(2,1)} %bitcast.20), calls=%async_computation | async-start | bytes 1179648 | tf_op jit(solution)/shard_map/all_to_all | solution.py:585
  27.3 1.3 %collective-permute-start.3 = (bf16[80,256]{1,0:T(8,128)(2,1)S(1)}, bf16[80,256]{1,0:T(8,128)(2,1)S(1)}, u32[]{:S(2)}, u32[]{:S(2)}) collective-permute-start(bf16[80,256]{1,0:T(8,128)(2,1)S(1)} %pack.1.packed_ref.a2), channel_id=1, source_target_pairs={{0,1},{1,0},{2,3},{3,2},{4,5},{5,4},{6,7},{7,6},{8,9},{9,8},{10,11... | collective-permute-start | bytes 122888 | tf_op jit(solution)/shard_map/ppermute | solution.py:524
  28.6 15.6 %collective-permute-start.4 = (bf16[80,256]{1,0:T(8,128)(2,1)S(1)}, bf16[80,256]{1,0:T(8,128)(2,1)S(1)}, u32[]{:S(2)}, u32[]{:S(2)}) collective-permute-start(bf16[80,256]{1,0:T(8,128)(2,1)S(1)} %collective-permute-done.3.a3), channel_id=1, source_target_pairs={{0,2},{1,3},{2,4},{3,5},{4,6},{5,7},{6,8},{7,9},{8,10},{9,11},{10,... | collective-permute-start | bytes 122888 | tf_op jit(solution)/shard_map/ppermute | solution.py:524
  30.4 13.9 %collective-permute-start.5 = (bf16[80,256]{1,0:T(8,128)(2,1)S(1)}, bf16[80,256]{1,0:T(8,128)(2,1)S(1)}, u32[]{:S(2)}, u32[]{:S(2)}) collective-permute-start(bf16[80,256]{1,0:T(8,128)(2,1)S(1)} %collective-permute-done.3.a3), channel_id=1, source_target_pairs={{0,30},{1,31},{2,0},{3,1},{4,2},{5,3},{6,4},{7,5},{8,6},{9,7},{10,... | collective-permute-start | bytes 122888 | tf_op jit(solution)/shard_map/ppermute | solution.py:524
  34.5 12.1 %copy-start.4 = (bf16[1024,256]{1,0:T(8,128)(2,1)S(1)}, bf16[1024,256]{1,0:T(8,128)(2,1)}, u32[]{:S(2)}) copy-start(bf16[1024,256]{1,0:T(8,128)(2,1)} %constant.67.clone.y_ref) | copy-start | bytes 1572868
  34.5 12.1 %copy-start.5 = (bf16[512,128]{1,0:T(8,128)(2,1)S(1)}, bf16[512,128]{1,0:T(8,128)(2,1)}, u32[]{:S(2)}) copy-start(bf16[512,128]{1,0:T(8,128)(2,1)} %constant.68.clone.x_ref) | copy-start | bytes 393220
  50.4 3.7 %copy-start.13 = (bf16[64,16,64]{2,1,0:T(8,128)(2,1)S(1)}, bf16[64,16,64]{2,1,0:T(8,128)(2,1)}, u32[]{:S(2)}) copy-start(bf16[64,16,64]{2,1,0:T(8,128)(2,1)} %param.21) | copy-start | bytes 393220
  51.3 3.0 %copy-start.14 = (s32[256,8]{0,1:T(8,128)S(1)}, s32[256,8]{0,1:T(8,128)}, u32[]{:S(2)}) copy-start(s32[256,8]{0,1:T(8,128)} %param.19) | copy-start | bytes 24580
  51.3 3.0 %copy-start.10 = (s32[256,8]{0,1:T(8,128)S(1)}, s32[256,8]{0,1:T(8,128)}, u32[]{:S(2)}) copy-start(s32[256,8]{0,1:T(8,128)} %param.20) | copy-start | bytes 24580
  51.3 21.0 %all-to-all-start.1 = ((f16[32,72,128]{2,1,0:T(8,128)(2,1)}), f16[32,72,128]{2,1,0:T(8,128)(2,1)S(1)}, u32[]{:S(2)}, u32[]{:S(2)}) async-start(f16[32,72,128]{2,1,0:T(8,128)(2,1)} %bitcast.6), calls=%async_computation.1 | async-start | bytes 1179648 | tf_op jit(solution)/shard_map/all_to_all | solution.py:585
  54.3 18.1 %copy-start.3 = (bf16[1024,512]{1,0:T(8,128)(2,1)S(1)}, bf16[1024,512]{1,0:T(8,128)(2,1)}, u32[]{:S(2)}) copy-start(bf16[1024,512]{1,0:T(8,128)(2,1)} %constant.69.clone.v_ref) | copy-start | bytes 3145732
  74.4 7.5 %copy-start.9 = (s32[256]{0:T(256)S(1)}, s32[256]{0:T(256)}, u32[]{:S(2)}) copy-start(s32[256]{0:T(256)} %brick_ref.3) | copy-start | bytes 3076
  74.4 7.5 %copy-start.12 = (s32[256]{0:T(256)S(1)}, s32[256]{0:T(256)}, u32[]{:S(2)}) copy-start(s32[256]{0:T(256)} %param.17) | copy-start | bytes 3076
  74.4 1.3 %collective-permute-start.6 = (bf16[128,128]{1,0:T(8,128)(2,1)S(1)}, bf16[128,128]{1,0:T(8,128)(2,1)S(1)}, u32[]{:S(2)}, u32[]{:S(2)}) collective-permute-start(bf16[128,128]{1,0:T(8,128)(2,1)S(1)} %get-tuple-element.54), channel_id=1, source_target_pairs={{0,1},{1,0},{2,3},{3,2},{4,5},{5,4},{6,7},{7,6},{8,9},{9,8},{10,11... | collective-permute-start | bytes 98312 | tf_op jit(solution)/shard_map/ppermute | solution.py:524
  79.8 4.9 %collective-permute-start.7 = (f32[64,256]{1,0:T(8,128)S(1)}, f32[64,256]{1,0:T(8,128)S(1)}, u32[]{:S(2)}, u32[]{:S(2)}) collective-permute-start(f32[64,256]{1,0:T(8,128)S(1)} %get-tuple-element.57), channel_id=1, source_target_pairs={{0,30},{1,31},{2,0},{3,1},{4,2},{5,3},{6,4},{7,5},{8,6},{9,7},{10,... | collective-permute-start | bytes 196616 | tf_op jit(solution)/shard_map/ppermute | solution.py:524
  79.8 7.9 %collective-permute-start.8 = (f32[64,256]{1,0:T(8,128)S(1)}, f32[64,256]{1,0:T(8,128)S(1)}, u32[]{:S(2)}, u32[]{:S(2)}) collective-permute-start(f32[64,256]{1,0:T(8,128)S(1)} %get-tuple-element.58), channel_id=1, source_target_pairs={{0,2},{1,3},{2,4},{3,5},{4,6},{5,7},{6,8},{7,9},{8,10},{9,11},{10,... | collective-permute-start | bytes 196616 | tf_op jit(solution)/shard_map/ppermute | solution.py:524

commit v4 on v3

--- a/solution.py
+++ b/solution.py
@@ -99,16 +99,17 @@
     )
 
 
-def footprints(charges, kinds, stk_ref, fp_ref, first):
-    count = charges.shape[1]
-    spread = by_kind(charges.astype(F32), kinds).astype(BF16)
+def footprints(packed, stk_ref, fp_ref, first):
+    count = packed.shape[1]
+    turned = jnp.transpose(packed.astype(F32))
+    kinds = turned[:, PANELS + 2 : PANELS + 3]
+    charges = jnp.concatenate([turned[:, :PANELS], turned[:, :PANELS]], axis=1)
+    offset = kinds - jnp.where(lane_of((count, LANES)) < PANELS, 0.0, 1.0)
+    spread = jnp.concatenate(
+        [jnp.where(offset == kind, charges, 0.0).astype(BF16) for kind in range(0, KS, 2)], axis=1
+    )
     for pair in range(4):
-        part = lax.dot_general(
-            spread,
-            stk_ref[:, pair * LANES : (pair + 1) * LANES],
-            (((0,), (0,)), ((), ())),
-            preferred_element_type=F32,
-        )
+        part = dot(spread, stk_ref[:, pair * LANES : (pair + 1) * LANES])
         fp_ref[pl.ds(first * 8 + 2 * pair, count, stride=8), :] = part
         fp_ref[pl.ds(first * 8 + 2 * pair + 1, count, stride=8), :] = pltpu.roll(part, 64, 1)
 
@@ -216,10 +217,6 @@
     out_ref[...] = jnp.concatenate([held, facts.astype(F32)], axis=0).astype(BF16)
 
 
-def facts_of(packed_ref):
-    return packed_ref[PANELS : PANELS + 8, :].astype(F32).astype(jnp.int32)
-
-
 def own_kernel(brick_ref, live_ref, packed_ref, stencil_ref,
                g0, g1, g2, g3, edge_ref, stk_ref, fp_ref, rows_ref, sem):
     copy = pltpu.make_async_copy(stencil_ref, rows_ref, sem)
@@ -230,19 +227,17 @@
     point = lax.broadcasted_iota(jnp.int32, shape, 0)
     target = (point & 7) * 64 + lax.shift_right_logical(point, 3)
     order = jnp.where(lane_of(shape) == target, 1.0, 0.0).astype(BF16)
-    kinds = facts_of(packed_ref)[2:3, :]
-    slots = packed_ref.shape[1]
     live = live_ref[0]
     copy.wait()
     stk_ref[...] = dot(rows_ref[...], order).astype(BF16)
 
     @pl.when(live > LANES)
     def _():
-        footprints(packed_ref[0:PANELS, :], kinds, stk_ref, fp_ref, 0)
+        footprints(packed_ref[...], stk_ref, fp_ref, 0)
 
     @pl.when(live <= LANES)
     def _():
-        footprints(packed_ref[0:PANELS, 0:LANES], kinds[:, 0:LANES], stk_ref, fp_ref, 0)
+        footprints(packed_ref[:, 0:LANES], stk_ref, fp_ref, 0)
 
     scatter_columns(fp_ref, 0, place_in_brick(brick_ref), live, (g0, g1, g2, g3), edge_ref, (0, 1, 2, 3), 2)
 
@@ -262,21 +257,43 @@
     )
 
 
-def beside_kernel(prev_ref, next_ref, stk_ref, i0, i1, i2, i3, iedge,
-                  g0, g1, g2, g3, edge_ref, out_edge, out_facts, fp_ref, facts_ref, sem):
-    slots = prev_ref.shape[1]
-    for side, source in enumerate((prev_ref, next_ref)):
-        out_facts[:, side * slots : (side + 1) * slots] = facts_of(source)
+def beside_kernel(odd_ref, own_ref, first_ref, second_ref, stk_ref, i0, i1, i2, i3, iedge,
+                  g0, g1, g2, g3, edge_ref, out_edge, out_facts, pool_ref, fp_ref, facts_ref, sem):
+    height, slots = own_ref.shape
+    before, after = pl.ds(0, height), pl.ds(2 * height, height)
+    pool_ref[height : 2 * height, :] = own_ref[...]
+
+    @pl.when(odd_ref[0] == 0)
+    def _():
+        pool_ref[after, :] = first_ref[...]
+        pool_ref[before, :] = second_ref[...]
+
+    @pl.when(odd_ref[0] != 0)
+    def _():
+        pool_ref[before, :] = first_ref[...]
+        pool_ref[after, :] = second_ref[...]
+
+    for side in range(2):
+        row = 2 * side * height + PANELS
+        facts = pool_ref[row : row + 16, :].astype(F32).astype(jnp.int32)
+        out_facts[:, side * slots : (side + 1) * slots] = facts[0:8, :]
     copy = pltpu.make_async_copy(out_facts, facts_ref, sem)
     copy.start()
+
+    def project(first):
+        here = slice(first, first + LANES)
+        packed = jnp.concatenate(
+            [pool_ref[0:height, here], pool_ref[2 * height : 3 * height, here]], axis=1
+        )
+        footprints(packed, stk_ref, fp_ref, 2 * first)
+
+    project(0)
     copy.wait()
     for first, counts in chunks_beside(facts_ref, slots):
-        @pl.when(counts[0] + counts[1] > 0)
-        def _(first=first):
-            here = slice(first, first + LANES)
-            charges = jnp.concatenate([prev_ref[0:PANELS, here], next_ref[0:PANELS, here]], axis=1)
-            kinds = both_sides(out_facts.at[2:3, :], slots, first)
-            footprints(charges, kinds, stk_ref, fp_ref, 2 * first)
+        if first:
+            @pl.when(counts[0] + counts[1] > 0)
+            def _(first=first):
+                project(first)
 
         for side, (planes, shift_i) in enumerate(BESIDE):
             scatter_columns(fp_ref, 2 * first + side * LANES, place_in_facts(facts_ref, side * slots + first),
@@ -452,7 +469,7 @@
         out_ref[:, LANES:slots] = jnp.zeros((PANELS, slots - LANES), F32)
 
 
-def beside_sample_kernel(facts_ref, p0, p1, p2, p3, edge_ref, kinds_ref, stk_ref, out0, out1, wide_ref, sp_ref):
+def beside_sample_kernel(odd_ref, facts_ref, p0, p1, p2, p3, edge_ref, kinds_ref, stk_ref, out0, out1, wide_ref, sp_ref):
     widen_edge(edge_ref, wide_ref)
     slots = kinds_ref.shape[1] // 2
     outs = (out0, out1)
@@ -466,8 +483,10 @@
         def _(first=first, counts=counts, here=here):
             kinds = both_sides(kinds_ref.at[2:3, :], slots, first)
             result = far_sums(sp_ref, kinds, stk_ref, 2 * first)
-            for side, out in enumerate(outs):
-                out[:, here] = masked(result[:, side * LANES : (side + 1) * LANES], counts[side])
+            sums = [masked(result[:, side * LANES : (side + 1) * LANES], counts[side]) for side in range(2)]
+            even = jnp.broadcast_to(odd_ref[0], sums[0].shape) == 0
+            out0[:, here] = jnp.where(even, sums[1], sums[0])
+            out1[:, here] = jnp.where(even, sums[0], sums[1])
 
         @pl.when(counts[0] + counts[1] <= 0)
         def _(here=here):
@@ -475,10 +494,14 @@
                 out[:, here] = jnp.zeros((PANELS, LANES), F32)
 
 
-def near_kernel(live_ref, a0, a1, a2, a3, a4, a5, source_ref, block_ref, table_ref, out_ref):
+def near_kernel(live_ref, here_ref, there_ref, source_ref, block_ref, table_ref, out_ref):
     live = live_ref[0]
     fanout, slots = source_ref.shape
-    pool = jnp.concatenate([ref[0:PANELS, :] for ref in (a0, a1, a2, a3, a4, a5)], axis=1)
+    height = here_ref.shape[0] // 3
+    pool = jnp.concatenate(
+        [ref[step * height : step * height + PANELS, :] for step in range(3) for ref in (here_ref, there_ref)],
+        axis=1,
+    )
     total = pool.shape[1]
     for first in range(0, slots, LANES):
         where = slice(first, first + LANES)
@@ -515,14 +538,24 @@
     axes = ("tile", "slab")
     both = ("slab", "tile")
 
-    def moved(values, step, swap):
+    def moved(values, step_of, swap=0):
         pairs = [
-            (a * tiles + b, (a + step) % slabs * tiles + (b + swap) % tiles)
+            (a * tiles + b, (a + step_of(a)) % slabs * tiles + (b + swap) % tiles)
             for a in range(slabs)
             for b in range(tiles)
         ]
         return lax.ppermute(values, both, pairs)
 
+    def to_first(values):
+        return moved(values, lambda a: 1 - 2 * (a % 2))
+
+    def to_second(values):
+        return moved(values, lambda a: 2 * (a % 2) - 1)
+
+    def to_other_tile(values):
+        return moved(values, lambda a: 0, 1)
+
+    odd = (lax.axis_index("slab") % 2)[None]
     kinds = slot_stencil[None, :]
     packed = pl.pallas_call(
         pack_kernel,
@@ -532,9 +565,8 @@
         compiler_params=PARAMS,
         name="pack",
     )(live_count, charges, slot_brick[None, :], kinds)
-    from_prev = moved(packed, 1, 0)
-    from_next = moved(packed, -1, 0)
-    swapped = moved(packed, 0, 1)
+    from_second = to_second(packed)
+    from_first = to_first(packed)
 
     grid = shape_of(ZROWS, LANES)
     g = pl.pallas_call(
@@ -554,20 +586,25 @@
 
     g = pl.pallas_call(
         beside_kernel,
-        out_shape=(grid,) * 5 + (shape_of(LANES, LANES), shape_of(8, 2 * slots, dtype=jnp.int32)),
-        in_specs=[VMEM] * 8,
-        out_specs=(VMEM,) * 7,
+        out_shape=(grid,) * 5
+        + (
+            shape_of(LANES, LANES),
+            shape_of(8, 2 * slots, dtype=jnp.int32),
+            shape_of(3 * (PANELS + 16), slots, dtype=BF16),
+        ),
+        in_specs=[SMEM] + [VMEM] * 9,
+        out_specs=(VMEM,) * 8,
         scratch_shapes=[
             pltpu.VMEM((2 * slots * 8, LANES), F32),
             pltpu.SMEM((8, 2 * slots), jnp.int32),
             pltpu.SemaphoreType.DMA,
         ],
-        input_output_aliases={3: 0, 4: 1, 5: 2, 6: 3, 7: 4},
+        input_output_aliases={5: 0, 6: 1, 7: 2, 8: 3, 9: 4},
         compiler_params=PARAMS,
         name="beside_scatter",
-    )(from_prev, from_next, stk, *grids)
+    )(odd, packed, from_first, from_second, stk, *grids)
     facts2 = g[6]
-    edge = moved(g[5], 0, 1)
+    edge = to_other_tile(g[5])
 
     forward, inverse = z_tables(slabs, tiles)
     rows = owners * (4 * parts + SCALE_ROWS)
@@ -601,16 +638,14 @@
         name="hat_order",
     )(offset, hat, jnp.asarray(reversal()))
 
-    swapped_prev = moved(swapped, 1, 0)
-    swapped_next = moved(swapped, -1, 0)
-    got, hat, swapped_prev, swapped_next = lax.optimization_barrier((got, hat, swapped_prev, swapped_next))
-    pool = [from_prev, swapped_prev, packed, swapped, from_next, swapped_next]
+    got, hat = lax.optimization_barrier((got, hat))
+    pool = (g[7], to_other_tile(g[7]))
     direction = near_source // slots
     pool_index = (direction // 3 * 2 + (direction % 3 != 1).astype(jnp.int32)) * slots + near_source % slots
     near = pl.pallas_call(
         near_kernel,
         out_shape=shape_of(PANELS, slots),
-        in_specs=[SMEM] + [VMEM] * 9,
+        in_specs=[SMEM] + [VMEM] * 5,
         out_specs=VMEM,
         compiler_params=PARAMS,
         name="near_field",
@@ -635,7 +670,7 @@
         compiler_params=PARAMS,
         name="z_inverse",
     )(widened(back), jnp.asarray(halves(inverse)))
-    edge = moved(pot[4], 0, 1)
+    edge = to_other_tile(pot[4])
 
     def sample_scratch(width):
         return [pltpu.VMEM((ZROWS, LANES), F32), pltpu.VMEM((width * 8, LANES), F32)]
@@ -644,14 +679,14 @@
     others = pl.pallas_call(
         beside_sample_kernel,
         out_shape=(sums, sums),
-        in_specs=[SMEM] + [VMEM] * 7,
+        in_specs=[SMEM] * 2 + [VMEM] * 7,
         out_specs=(VMEM, VMEM),
         scratch_shapes=sample_scratch(2 * slots),
         compiler_params=PARAMS,
         name="beside_sample",
-    )(facts2, *pot[:4], edge, facts2, stk)
-    to_prev = moved(others[0], -1, 0)
-    to_next = moved(others[1], 1, 0)
+    )(odd, facts2, *pot[:4], edge, facts2, stk)
+    second = to_second(others[1])
+    first = to_first(others[0])
     own = pl.pallas_call(
         own_sample_kernel,
         out_shape=sums,
@@ -661,7 +696,7 @@
         compiler_params=PARAMS,
         name="own_sample",
     )(slot_brick, live_count, *pot[:4], edge, kinds, stk)
-    return own + near + to_prev + to_next
+    return own + near + first + second
 
 
 def solution(mesh):

time: 89.1 us -> 87.8 us (0.985)
  waiting for transfers between devices: 34.5 us -> 41.8 us
  starting transfers between devices: 22.2 us -> 17.5 us
  Pallas kernels: 24.5 us -> 20.7 us
    all_to_all x2, waiting for transfers between devices: 18 us -> 32.4 us  [exchanged(): values = lax.all_to_all(values, axes, 0, 0, tiled=True)]
    ppermute x9 -> x7, waiting for transfers between devices: 16.5 us -> 9.41 us  [moved(): return lax.ppermute(values, both, pairs)]
    ppermute x9 -> x7, starting transfers between devices: 15.2 us -> 11 us  [moved(): return lax.ppermute(values, both, pairs)]
    pallas_call x1, Pallas kernels: 4.1 us -> 2.61 us  [body(): pl.pallas_call(beside_sample_kernel, out_shape=(sums, sums), in_specs=[SM...]
    pallas_call x1, Pallas kernels: 4.21 us -> 2.89 us  [body(): pl.pallas_call(beside_kernel, out_shape=(grid,) * 5 + (shape_of(LANES, LA...]
    unnamed x30 -> x32, local copies, waits for them, and re-layouts: 3.4 us -> 4.08 us
  transfers between devices with their start and end apart: 11 -> 9, of which waited for: 8 -> 7; matrix products, arithmetic and copies ran while one was open for 0% -> 0% of each run, Pallas kernels for 9% -> 8%
where the time goes in v4:
time: 87.8 us; the launch traced here: 87.9 us
  waiting for transfers between devices  41.8 us (48%)
  Pallas kernels  20.7 us (24%)
  starting transfers between devices  17.5 us (20%)
  local copies, waits for them, and re-layouts  4.28 us (5%)
  other arithmetic  2.71 us (3%)
  between operations  0.94 us (1%)
    all_to_all x2, waiting for transfers between devices, exchanged(): values = lax.all_to_all(values, axes, 0, 0, tiled=True)  32.4 us
    ppermute x7, starting transfers between devices, moved(): return lax.ppermute(values, both, pairs)  11 us
    ppermute x7, waiting for transfers between devices, moved(): return lax.ppermute(values, both, pairs)  9.41 us
    all_to_all x2, starting transfers between devices, exchanged(): values = lax.all_to_all(values, axes, 0, 0, tiled=True)  6.53 us
    unnamed x32, local copies, waits for them, and re-layouts  4.08 us
    pallas_call x1, Pallas kernels, body(): pl.pallas_call(functools.partial(plane_kernel, slabs, planes), out_shape=...  3.87 us
    pallas_call x1, Pallas kernels, body(): pl.pallas_call(beside_kernel, out_shape=(grid,) * 5 + (shape_of(LANES, LA...  2.89 us
    pallas_call x1, Pallas kernels, body(): pl.pallas_call(own_kernel, out_shape=(grid,) * 5 + (shape_of(KS * PANELS,...  2.87 us
  transfers between devices with their start and end apart: 9, of which 7 were waited for; matrix products, arithmetic and copies ran while one was open for 0% of the time, Pallas kernels for 8%

profile of v4, /device:TPU:0, one launch (start us, length us, event | category | flops | bytes accessed | tf_op | source)
XLA Modules:
  0.0 87.9 jit_solution(14607894240646293688)
XLA Ops:
  0.7 0.0 copy-start.7
  0.7 0.7 copy-done.7
  1.4 0.7 copy-done.8
  2.1 0.7 copy-done.12
  2.8 3.0 %collective-permute-start = (bf16[80,256]{1,0:T(8,128)(2,1)S(1)}, bf16[80,256]{1,0:T(8,128)(2,1)S(1)}, u32[]{:S(2)}, u32[]{:S(2)}) collective-permute-start(bf16[80,256]{1,0:T(8,128)(2,1)S(1)} %pack.1.packed_ref.own_ref), channel_id=1, source_target_pairs={{0,2},{1,3},{2,0},{3,1},{4,6},{5,7},{6,4},{7,5},{8,10},{9,11},{10,... | collective-permute-start | bytes 122888 | tf_op jit(solution)/shard_map/ppermute | solution.py:547
  5.8 4.5 %collective-permute-start.1 = (bf16[80,256]{1,0:T(8,128)(2,1)S(1)}, bf16[80,256]{1,0:T(8,128)(2,1)S(1)}, u32[]{:S(2)}, u32[]{:S(2)}) collective-permute-start(bf16[80,256]{1,0:T(8,128)(2,1)S(1)} %pack.1.packed_ref.own_ref), channel_id=1, source_target_pairs={{0,30},{1,31},{2,4},{3,5},{4,2},{5,3},{6,8},{7,9},{8,6},{9,7},{10,... | collective-permute-start | bytes 122888 | tf_op jit(solution)/shard_map/ppermute | solution.py:547
  10.3 1.2 %copy-done.1 = bf16[16,64,512]{2,1,0:T(8,128)(2,1)S(1)} copy-done((bf16[16,64,512]{2,1,0:T(8,128)(2,1)S(1)}, bf16[16,64,512]{2,1,0:T(8,128)(2,1)}, u32[]{:S(2)}) %copy-start.1) | copy-done | bytes 1048600
  11.5 0.7 copy-done.9
  12.2 2.9 %own_scatter.1 = (f32[520,128]{1,0:T(8,128)S(1)}, f32[520,128]{1,0:T(8,128)S(1)}, f32[520,128]{1,0:T(8,128)S(1)}, f32[520,128]{1,0:T(8,128)S(1)}, f32[520,128]{1,0:T(8,128)S(1)}, /*index=5*/bf16[1024,512]{1,0:T(8,128)(2,1)S(1)}) custom-call(s32[256]{0:T(256)S(1)} %copy-done.9, s32[1]{0:T(128)S(6)} %copy.25.live_ref, ...), custom_call_target="tpu_custom_call" | custom-call | tf_op jit(solution)/shard_map/own_scatter/pallas_call | solution.py:572
  15.1 0.0 collective-permute-done.first_ref
  15.1 0.0 collective-permute-done.1.second_ref
  15.1 0.0 copy-start
  15.1 2.9 %beside_scatter.1 = (f32[520,128]{1,0:T(8,128)S(1)}, f32[520,128]{1,0:T(8,128)S(1)}, f32[520,128]{1,0:T(8,128)S(1)}, f32[520,128]{1,0:T(8,128)S(1)}, f32[520,128...) custom-call(s32[1]{0:T(128)} %bitcast.odd_ref, ...), custom_call_target="tpu_custom_call", output_to_operand_aliasing={{0}: (5, {}), {1}: (6, {}), {2}: (7, {}), {3}: (8, {}), {4}... | custom-call | tf_op jit(solution)/shard_map/beside_scatter/pallas_call | solution.py:587
  18.0 0.2 collective-permute-start.2
  18.2 1.1 %collective-permute-done.2.edge_ref = f32[128,128]{1,0:T(8,128)S(1)} collective-permute-done((f32[128,128]{1,0:T(8,128)S(1)}, f32[128,128]{1,0:T(8,128)S(1)}, u32[]{:S(2)}, u32[]{:S(2)}) %collective-permute-start.2) | collective-permute-done | bytes 65568 | tf_op jit(solution)/shard_map/ppermute | solution.py:547
  19.4 2.2 %z_forward.1 = f32[2304,128]{1,0:T(8,128)S(1)} custom-call(f32[520,128]{1,0:T(8,128)S(1)} %get-tuple-element.37.g0, f32[520,128]{1,0:T(8,128)S(1)} %get-tuple-element.38.g1, f32[520,128]{1,0:T(8,128)S(1)} %get-tuple-element.39.g2, f32[520,128]{1,0:T(8,128)S(1)} %get-tuple-element.40.g3, f32[128,128]{1,0:T(8,128)S(1)} %collective-permute-done.2.edge_ref, ...), custom_call_target="tpu_custom_call" | custom-call | tf_op jit(solution)/shard_map/z_forward/pallas_call | solution.py:611
  21.5 0.0 copy-start.2
  21.6 0.0 copy-start.6
  21.6 0.9 %convert_element_type.12 = f16[2304,128]{1,0:T(8,128)(2,1)} convert(f32[2304,128]{1,0:T(8,128)S(1)} %z_forward.1) | non-fusion elementwise | flops 294912 | bytes 1769472 | tf_op jit(solution)/shard_map/convert_element_type | solution.py:621
  22.5 3.8 %all-to-all-start = ((f16[32,72,128]{2,1,0:T(8,128)(2,1)}), f16[32,72,128]{2,1,0:T(8,128)(2,1)S(1)}, u32[]{:S(2)}, u32[]{:S(2)}) async-start(f16[32,72,128]{2,1,0:T(8,128)(2,1)} %bitcast.4), calls=%async_computation | async-start | bytes 1179648 | tf_op jit(solution)/shard_map/all_to_all | solution.py:622
  26.3 0.3 hat_order.1.hat_ref
  26.6 0.0 copy-start.4
  26.6 0.0 copy-start.5
  26.6 17.9 %all-to-all-done = f16[32,72,128]{2,1,0:T(8,128)(2,1)S(1)} async-done(((f16[32,72,128]{2,1,0:T(8,128)(2,1)}), f16[32,72,128]{2,1,0:T(8,128)(2,1)S(1)}, u32[]{:S(2)}, u32[]{:S(2)}) %all-to-all-start) | async-done | bytes 589856 | tf_op jit(solution)/shard_map/all_to_all | solution.py:622
  44.5 0.1 bitcast_convert_fusion.1.in_ref
  44.6 3.9 %plane_filter.1 = f32[2304,128]{1,0:T(8,128)S(1)} custom-call(f32[2304,128]{1,0:T(8,128)S(1)} %bitcast_convert_fusion.1.in_ref, f32[8,64,256]{2,1,0:T(8,128)S(1)} %hat_order.1.hat_ref, bf16[1024,256]{1,0:T(8,128)(2,1)S(1)} %copy-done.4, bf16[512,128]{1,0:T(8,128)(2,1)S(1)} %copy-done.5), custom_call_target="tpu_custom_call" | custom-call | tf_op jit(solution)/shard_map/plane_filter/pallas_call | solution.py:654
  48.5 0.0 copy-start.14
  48.5 0.9 %convert_element_type.13 = f16[2304,128]{1,0:T(8,128)(2,1)} convert(f32[2304,128]{1,0:T(8,128)S(1)} %plane_filter.1) | non-fusion elementwise | flops 294912 | bytes 1769472 | tf_op jit(solution)/shard_map/convert_element_type | solution.py:621
  49.4 2.7 %all-to-all-start.1 = ((f16[32,72,128]{2,1,0:T(8,128)(2,1)}), f16[32,72,128]{2,1,0:T(8,128)(2,1)S(1)}, u32[]{:S(2)}, u32[]{:S(2)}) async-start(f16[32,72,128]{2,1,0:T(8,128)(2,1)} %bitcast.7), calls=%async_computation.1 | async-start | bytes 1179648 | tf_op jit(solution)/shard_map/all_to_all | solution.py:622
  52.2 0.2 reshape.27.table_ref
  52.4 0.0 copy-start.3
  52.4 0.2 collective-permute-start.3
  52.6 1.2 %collective-permute-done.3.there_ref = bf16[240,256]{1,0:T(8,128)(2,1)S(1)} collective-permute-done((bf16[240,256]{1,0:T(8,128)(2,1)S(1)}, bf16[240,256]{1,0:T(8,128)(2,1)S(1)}, u32[]{:S(2)}, u32[]{:S(2)}) %collective-permute-start.3) | collective-permute-done | bytes 122912 | tf_op jit(solution)/shard_map/ppermute | solution.py:547
  53.8 2.1 %near_field.1 = f32[64,256]{1,0:T(8,128)S(1)} custom-call(s32[1]{0:T(128)S(6)} %copy.25.live_ref, bf16[240,256]{1,0:T(8,128)(2,1)S(1)} %get-tuple-element.46.here_ref, bf16[240,256]{1,0:T(8,128)(2,1)S(1)} %collective-permute-done.3.there_ref, s32[8,256]{1,0:T(8,128)S(1)} %fusion.4.source_ref, s32[8,256]{1,0:T(8,128)S(1)} %bitcast.18, ...), custom_call_target="tpu_custom_call" | custom-call | tf_op jit(solution)/shard_map/near_field/pallas_call | solution.py:645
  56.0 14.5 %all-to-all-done.1 = f16[32,72,128]{2,1,0:T(8,128)(2,1)S(1)} async-done(((f16[32,72,128]{2,1,0:T(8,128)(2,1)}), f16[32,72,128]{2,1,0:T(8,128)(2,1)S(1)}, u32[]{:S(2)}, u32[]{:S(2)}) %all-to-all-start.1) | async-done | bytes 589856 | tf_op jit(solution)/shard_map/all_to_all | solution.py:622
  70.4 0.1 bitcast_convert_fusion.in_ref
  70.5 1.9 %z_inverse.1 = (f32[520,128]{1,0:T(8,128)S(1)}, f32[520,128]{1,0:T(8,128)S(1)}, f32[520,128]{1,0:T(8,128)S(1)}, f32[520,128]{1,0:T(8,128)S(1)}, bf16[128,128]{1,0:T(8,128)(2,1)S(1)}) custom-call(f32[2304,128]{1,0:T(8,128)S(1)} %bitcast_convert_fusion.in_ref, bf16[1024,512]{1,0:T(8,128)(2,1)S(1)} %copy-done.3), custom_call_target="tpu_custom_call" | custom-call | tf_op jit(solution)/shard_map/z_inverse/pallas_call | solution.py:665
  72.5 0.0 copy-start.10
  72.5 0.0 copy-start.13
  72.5 0.1 collective-permute-start.4
  72.6 1.2 %collective-permute-done.4.edge_ref = bf16[128,128]{1,0:T(8,128)(2,1)S(1)} collective-permute-done((bf16[128,128]{1,0:T(8,128)(2,1)S(1)}, bf16[128,128]{1,0:T(8,128)(2,1)S(1)}, u32[]{:S(2)}, u32[]{:S(2)}) %collective-permute-start.4) | collective-permute-done | bytes 32800 | tf_op jit(solution)/shard_map/ppermute | solution.py:547
  73.8 2.6 %beside_sample.1 = (f32[64,256]{1,0:T(8,128)S(1)}, f32[64,256]{1,0:T(8,128)S(1)}) custom-call(s32[1]{0:T(128)} %bitcast.odd_ref, s32[8,512]{1,0:T(8,128)S(1)} %get-tuple-element.54.facts_ref.kinds_ref, f32[520,128]{1,0:T(8,128)S(1)} %get-tuple-element.48.p0, f32[520,128]{1,0:T(8,128)S(1)} %get-tuple-element.49.p1, f32[520,128]{1,0:T(8,128)S(1)} %get-tuple-element.50.p2, ...), custom_call_target="tpu_custom_call" | custom-call | tf_op jit(solution)/shard_map/beside_sample/pallas_call | solution.py:679
  76.4 3.0 %collective-permute-start.5 = (f32[64,256]{1,0:T(8,128)S(1)}, f32[64,256]{1,0:T(8,128)S(1)}, u32[]{:S(2)}, u32[]{:S(2)}) collective-permute-start(f32[64,256]{1,0:T(8,128)S(1)} %get-tuple-element.55), channel_id=1, source_target_pairs={{0,2},{1,3},{2,0},{3,1},{4,6},{5,7},{6,4},{7,5},{8,10},{9,11},{10,... | collective-permute-start | bytes 196616 | tf_op jit(solution)/shard_map/ppermute | solution.py:547
  79.4 0.0 collective-permute-start.6
  79.4 1.9 %own_sample.1 = f32[64,256]{1,0:T(8,128)S(1)} custom-call(s32[256]{0:T(256)S(1)} %copy-done.10, s32[1]{0:T(128)S(6)} %copy.25.live_ref, f32[520,128]{1,0:T(8,128)S(1)} %get-tuple-element.48.p0, f32[520,128]{1,0:T(8,128)S(1)} %get-tuple-element.49.p1, f32[520,128]{1,0:T(8,128)S(1)} %get-tuple-element.50.p2, f32[520,128]{1,0:T(8,128)S(1)} %get-tuple-element.51.p3, ...), custom_call_target="tpu_custom_call" | custom-call | tf_op jit(solution)/shard_map/own_sample/pallas_call | solution.py:690
  81.4 0.7 collective-permute-done.5
  82.0 5.2 %collective-permute-done.6 = f32[64,256]{1,0:T(8,128)S(1)} collective-permute-done((f32[64,256]{1,0:T(8,128)S(1)}, f32[64,256]{1,0:T(8,128)S(1)}, u32[]{:S(2)}, u32[]{:S(2)}) %collective-permute-start.6) | collective-permute-done | bytes 65568 | tf_op jit(solution)/shard_map/ppermute | solution.py:547
  87.3 0.6 add_add_fusion
  (19 shorter events, 0.1 us)
Async XLA Ops:
  0.7 0.8 copy-start.7
  1.4 0.7 copy-start.8
  2.1 0.7 copy-start.12
  2.8 12.3 %collective-permute-start = (bf16[80,256]{1,0:T(8,128)(2,1)S(1)}, bf16[80,256]{1,0:T(8,128)(2,1)S(1)}, u32[]{:S(2)}, u32[]{:S(2)}) collective-permute-start(bf16[80,256]{1,0:T(8,128)(2,1)S(1)} %pack.1.packed_ref.own_ref), channel_id=1, source_target_pairs={{0,2},{1,3},{2,0},{3,1},{4,6},{5,7},{6,4},{7,5},{8,10},{9,11},{10,... | collective-permute-start | bytes 122888 | tf_op jit(solution)/shard_map/ppermute | solution.py:547
  5.8 9.3 %collective-permute-start.1 = (bf16[80,256]{1,0:T(8,128)(2,1)S(1)}, bf16[80,256]{1,0:T(8,128)(2,1)S(1)}, u32[]{:S(2)}, u32[]{:S(2)}) collective-permute-start(bf16[80,256]{1,0:T(8,128)(2,1)S(1)} %pack.1.packed_ref.own_ref), channel_id=1, source_target_pairs={{0,30},{1,31},{2,4},{3,5},{4,2},{5,3},{6,8},{7,9},{8,6},{9,7},{10,... | collective-permute-start | bytes 122888 | tf_op jit(solution)/shard_map/ppermute | solution.py:547
  10.3 1.2 %copy-start.1 = (bf16[16,64,512]{2,1,0:T(8,128)(2,1)S(1)}, bf16[16,64,512]{2,1,0:T(8,128)(2,1)}, u32[]{:S(2)}) copy-start(bf16[16,64,512]{2,1,0:T(8,128)(2,1)} %param.18) | copy-start | bytes 3145732
  11.5 0.7 copy-start.9
  15.1 4.2 %copy-start = (bf16[1024,512]{1,0:T(8,128)(2,1)S(1)}, bf16[1024,512]{1,0:T(8,128)(2,1)}, u32[]{:S(2)}) copy-start(bf16[1024,512]{1,0:T(8,128)(2,1)} %constant.74.clone.w_ref) | copy-start | bytes 3145732
  18.0 1.3 %collective-permute-start.2 = (f32[128,128]{1,0:T(8,128)S(1)}, f32[128,128]{1,0:T(8,128)S(1)}, u32[]{:S(2)}, u32[]{:S(2)}) collective-permute-start(f32[128,128]{1,0:T(8,128)S(1)} %get-tuple-element.41), channel_id=1, source_target_pairs={{0,1},{1,0},{2,3},{3,2},{4,5},{5,4},{6,7},{7,6},{8,9},{9,8},{10,11... | collective-permute-start | bytes 196616 | tf_op jit(solution)/shard_map/ppermute | solution.py:547
  21.5 4.7 %copy-start.2 = (f32[16,64,256]{2,1,0:T(8,128)S(1)}, f32[16,64,256]{2,1,0:T(8,128)}, u32[]{:S(2)}) copy-start(f32[16,64,256]{2,1,0:T(8,128)} %hat_ref) | copy-start | bytes 3145732
  21.6 4.7 %copy-start.6 = (bf16[128,128]{1,0:T(8,128)(2,1)S(1)}, bf16[128,128]{1,0:T(8,128)(2,1)}, u32[]{:S(2)}) copy-start(bf16[128,128]{1,0:T(8,128)(2,1)} %constant.75.clone.turn_ref) | copy-start | bytes 98308
  22.5 22.0 %all-to-all-start = ((f16[32,72,128]{2,1,0:T(8,128)(2,1)}), f16[32,72,128]{2,1,0:T(8,128)(2,1)S(1)}, u32[]{:S(2)}, u32[]{:S(2)}) async-start(f16[32,72,128]{2,1,0:T(8,128)(2,1)} %bitcast.4), calls=%async_computation | async-start | bytes 1179648 | tf_op jit(solution)/shard_map/all_to_all | solution.py:622
  26.6 18.1 %copy-start.4 = (bf16[1024,256]{1,0:T(8,128)(2,1)S(1)}, bf16[1024,256]{1,0:T(8,128)(2,1)}, u32[]{:S(2)}) copy-start(bf16[1024,256]{1,0:T(8,128)(2,1)} %constant.76.clone.y_ref) | copy-start | bytes 1572868
  26.6 18.1 %copy-start.5 = (bf16[512,128]{1,0:T(8,128)(2,1)S(1)}, bf16[512,128]{1,0:T(8,128)(2,1)}, u32[]{:S(2)}) copy-start(bf16[512,128]{1,0:T(8,128)(2,1)} %constant.77.clone.x_ref) | copy-start | bytes 393220
  48.5 3.7 %copy-start.14 = (bf16[64,16,64]{2,1,0:T(8,128)(2,1)S(1)}, bf16[64,16,64]{2,1,0:T(8,128)(2,1)}, u32[]{:S(2)}) copy-start(bf16[64,16,64]{2,1,0:T(8,128)(2,1)} %param.21) | copy-start | bytes 393220
  49.4 3.2 %copy-start.15 = (s32[256,8]{0,1:T(8,128)S(1)}, s32[256,8]{0,1:T(8,128)}, u32[]{:S(2)}) copy-start(s32[256,8]{0,1:T(8,128)} %param.19) | copy-start | bytes 24580
  49.4 4.4 %copy-start.11 = (s32[256,8]{0,1:T(8,128)S(1)}, s32[256,8]{0,1:T(8,128)}, u32[]{:S(2)}) copy-start(s32[256,8]{0,1:T(8,128)} %param.20) | copy-start | bytes 24580
  49.4 21.0 %all-to-all-start.1 = ((f16[32,72,128]{2,1,0:T(8,128)(2,1)}), f16[32,72,128]{2,1,0:T(8,128)(2,1)S(1)}, u32[]{:S(2)}, u32[]{:S(2)}) async-start(f16[32,72,128]{2,1,0:T(8,128)(2,1)} %bitcast.7), calls=%async_computation.1 | async-start | bytes 1179648 | tf_op jit(solution)/shard_map/all_to_all | solution.py:622
  52.4 18.1 %copy-start.3 = (bf16[1024,512]{1,0:T(8,128)(2,1)S(1)}, bf16[1024,512]{1,0:T(8,128)(2,1)}, u32[]{:S(2)}) copy-start(bf16[1024,512]{1,0:T(8,128)(2,1)} %constant.78.clone.v_ref) | copy-start | bytes 3145732
  52.4 1.4 %collective-permute-start.3 = (bf16[240,256]{1,0:T(8,128)(2,1)S(1)}, bf16[240,256]{1,0:T(8,128)(2,1)S(1)}, u32[]{:S(2)}, u32[]{:S(2)}) collective-permute-start(bf16[240,256]{1,0:T(8,128)(2,1)S(1)} %get-tuple-element.46.here_ref), channel_id=1, source_target_pairs={{0,1},{1,0},{2,3},{3,2},{4,5},{5,4},{6,7},{7,6},{8,9},{9,8},{10,11... | collective-permute-start | bytes 368648 | tf_op jit(solution)/shard_map/ppermute | solution.py:547
  72.5 7.0 %copy-start.10 = (s32[256]{0:T(256)S(1)}, s32[256]{0:T(256)}, u32[]{:S(2)}) copy-start(s32[256]{0:T(256)} %brick_ref.3) | copy-start | bytes 3076
  72.5 6.9 %copy-start.13 = (s32[256]{0:T(256)S(1)}, s32[256]{0:T(256)}, u32[]{:S(2)}) copy-start(s32[256]{0:T(256)} %param.17) | copy-start | bytes 3076
  72.5 1.3 %collective-permute-start.4 = (bf16[128,128]{1,0:T(8,128)(2,1)S(1)}, bf16[128,128]{1,0:T(8,128)(2,1)S(1)}, u32[]{:S(2)}, u32[]{:S(2)}) collective-permute-start(bf16[128,128]{1,0:T(8,128)(2,1)S(1)} %get-tuple-element.52), channel_id=1, source_target_pairs={{0,1},{1,0},{2,3},{3,2},{4,5},{5,4},{6,7},{7,6},{8,9},{9,8},{10,11... | collective-permute-start | bytes 98312 | tf_op jit(solution)/shard_map/ppermute | solution.py:547
  76.4 5.7 %collective-permute-start.5 = (f32[64,256]{1,0:T(8,128)S(1)}, f32[64,256]{1,0:T(8,128)S(1)}, u32[]{:S(2)}, u32[]{:S(2)}) collective-permute-start(f32[64,256]{1,0:T(8,128)S(1)} %get-tuple-element.55), channel_id=1, source_target_pairs={{0,2},{1,3},{2,0},{3,1},{4,6},{5,7},{6,4},{7,5},{8,10},{9,11},{10,... | collective-permute-start | bytes 196616 | tf_op jit(solution)/shard_map/ppermute | solution.py:547
  79.4 7.9 %collective-permute-start.6 = (f32[64,256]{1,0:T(8,128)S(1)}, f32[64,256]{1,0:T(8,128)S(1)}, u32[]{:S(2)}, u32[]{:S(2)}) collective-permute-start(f32[64,256]{1,0:T(8,128)S(1)} %get-tuple-element.56), channel_id=1, source_target_pairs={{0,30},{1,31},{2,4},{3,5},{4,2},{5,3},{6,8},{7,9},{8,6},{9,7},{10,... | collective-permute-start | bytes 196616 | tf_op jit(solution)/shard_map/ppermute | solution.py:547

commit v5 on v4

--- a/solution.py
+++ b/solution.py
@@ -194,42 +194,32 @@
     return result
 
 
-def place_in_brick(brick_ref):
-    def place_of(column):
-        brick = brick_ref[column]
-        return lax.shift_right_logical(brick, 7), brick & (NZ // 4 - 1)
-
-    return place_of
-
-
-def place_in_facts(facts_ref, start):
-    return lambda column: (facts_ref[0, start + column], facts_ref[1, start + column])
-
-
-def pack_kernel(live_ref, charges_ref, brick_ref, stencil_ref, out_ref):
-    slots = charges_ref.shape[1]
-    charges = charges_ref[...].astype(F32)
-    held = jnp.where(lane_of(charges.shape) < live_ref[0], charges, 0.0)
-    row = lax.broadcasted_iota(jnp.int32, (16, slots), 0)
-    brick = jnp.broadcast_to(brick_ref[...], (16, slots))
-    facts = jnp.where(row == 0, lax.shift_right_logical(brick, 7), brick & (NZ // 4 - 1))
-    facts = jnp.where(row == 2, stencil_ref[...], jnp.where(row == 3, live_ref[0], facts))
-    out_ref[...] = jnp.concatenate([held, facts.astype(F32)], axis=0).astype(BF16)
-
-
-def own_kernel(brick_ref, live_ref, packed_ref, stencil_ref,
-               g0, g1, g2, g3, edge_ref, stk_ref, fp_ref, rows_ref, sem):
-    copy = pltpu.make_async_copy(stencil_ref, rows_ref, sem)
+def place_in(facts_ref):
+    return lambda column: (facts_ref[0, column], facts_ref[1, column])
+
+
+def facts_copy(packed_ref, out_facts, facts_ref, sem):
+    out_facts[...] = packed_ref[PANELS : PANELS + 16, :].astype(F32).astype(jnp.int32)[0:8, :]
+    copy = pltpu.make_async_copy(out_facts, facts_ref, sem)
     copy.start()
+    return copy
+
+
+def own_kernel(packed_ref, stencil_ref,
+               g0, g1, g2, g3, edge_ref, stk_ref, out_facts, fp_ref, rows_ref, facts_ref, sems):
+    copy = pltpu.make_async_copy(stencil_ref, rows_ref, sems.at[0])
+    copy.start()
+    other_copy = facts_copy(packed_ref, out_facts, facts_ref, sems.at[1])
     for ref in (g0, g1, g2, g3, edge_ref):
         ref[...] = jnp.zeros_like(ref)
     shape = (POINTS, POINTS)
     point = lax.broadcasted_iota(jnp.int32, shape, 0)
     target = (point & 7) * 64 + lax.shift_right_logical(point, 3)
     order = jnp.where(lane_of(shape) == target, 1.0, 0.0).astype(BF16)
-    live = live_ref[0]
+    other_copy.wait()
     copy.wait()
     stk_ref[...] = dot(rows_ref[...], order).astype(BF16)
+    live = facts_ref[3, 0]
 
     @pl.when(live > LANES)
     def _():
@@ -239,70 +229,38 @@
     def _():
         footprints(packed_ref[:, 0:LANES], stk_ref, fp_ref, 0)
 
-    scatter_columns(fp_ref, 0, place_in_brick(brick_ref), live, (g0, g1, g2, g3), edge_ref, (0, 1, 2, 3), 2)
-
-
-BESIDE = (((0, 1), 6), ((2, 3), -2))
-
-
-def chunks_beside(facts_ref, slots):
-    for first in range(0, slots, LANES):
-        counts = [jnp.clip(facts_ref[3, side * slots] - first, 0, LANES) for side in range(2)]
-        yield first, counts
-
-
-def both_sides(ref, slots, first):
-    return jnp.concatenate(
-        [ref[:, side * slots + first : side * slots + first + LANES] for side in range(2)], axis=1
-    )
-
-
-def beside_kernel(odd_ref, own_ref, first_ref, second_ref, stk_ref, i0, i1, i2, i3, iedge,
-                  g0, g1, g2, g3, edge_ref, out_edge, out_facts, pool_ref, fp_ref, facts_ref, sem):
-    height, slots = own_ref.shape
-    before, after = pl.ds(0, height), pl.ds(2 * height, height)
-    pool_ref[height : 2 * height, :] = own_ref[...]
-
-    @pl.when(odd_ref[0] == 0)
+    scatter_columns(fp_ref, 0, place_in(facts_ref), live, (g0, g1, g2, g3), edge_ref, (0, 1, 2, 3), 2)
+
+
+BEFORE = ((0, 1), 6)
+AFTER = ((2, 3), -2)
+
+
+def partner_kernel(is_second, odd_ref, packed_ref, stk_ref, i0, i1, i2, i3, iedge,
+                   g0, g1, g2, g3, edge_ref, out_facts, *rest):
+    fp_ref, facts_ref, sem = rest[-3:]
+    slots = packed_ref.shape[1]
+    copy = facts_copy(packed_ref, out_facts, facts_ref, sem)
+    footprints(packed_ref[:, 0:LANES], stk_ref, fp_ref, 0)
+    copy.wait()
+    live = facts_ref[3, 0]
+
+    @pl.when(live > LANES)
     def _():
-        pool_ref[after, :] = first_ref[...]
-        pool_ref[before, :] = second_ref[...]
-
-    @pl.when(odd_ref[0] != 0)
-    def _():
-        pool_ref[before, :] = first_ref[...]
-        pool_ref[after, :] = second_ref[...]
-
-    for side in range(2):
-        row = 2 * side * height + PANELS
-        facts = pool_ref[row : row + 16, :].astype(F32).astype(jnp.int32)
-        out_facts[:, side * slots : (side + 1) * slots] = facts[0:8, :]
-    copy = pltpu.make_async_copy(out_facts, facts_ref, sem)
-    copy.start()
-
-    def project(first):
-        here = slice(first, first + LANES)
-        packed = jnp.concatenate(
-            [pool_ref[0:height, here], pool_ref[2 * height : 3 * height, here]], axis=1
-        )
-        footprints(packed, stk_ref, fp_ref, 2 * first)
-
-    project(0)
-    copy.wait()
-    for first, counts in chunks_beside(facts_ref, slots):
-        if first:
-            @pl.when(counts[0] + counts[1] > 0)
-            def _(first=first):
-                project(first)
-
-        for side, (planes, shift_i) in enumerate(BESIDE):
-            scatter_columns(fp_ref, 2 * first + side * LANES, place_in_facts(facts_ref, side * slots + first),
-                            counts[side], (g0, g1, g2, g3), edge_ref, planes, shift_i)
-    edge_ref[0:8, :] += edge_ref[NZ:ZROWS, :]
-    total = edge_ref[0:LANES, :]
-    for block in range(1, 4):
-        total += pltpu.roll(edge_ref[block * LANES : (block + 1) * LANES, :], 32 * block, 1)
-    out_edge[...] = total
+        footprints(packed_ref[:, LANES:slots], stk_ref, fp_ref, LANES)
+
+    for flag, (planes, shift_i) in enumerate((BEFORE, AFTER) if is_second else (AFTER, BEFORE)):
+        @pl.when(odd_ref[0] == flag)
+        def _(planes=planes, shift_i=shift_i):
+            scatter_columns(fp_ref, 0, place_in(facts_ref), live, (g0, g1, g2, g3), edge_ref, planes, shift_i)
+
+    if is_second:
+        out_edge = rest[0]
+        edge_ref[0:8, :] += edge_ref[NZ:ZROWS, :]
+        total = edge_ref[0:LANES, :]
+        for block in range(1, 4):
+            total += pltpu.roll(edge_ref[block * LANES : (block + 1) * LANES, :], 32 * block, 1)
+        out_edge[...] = total
 
 
 def exponent_of(values):
@@ -453,55 +411,42 @@
     return jnp.where(lane_of(values.shape) < live, values, 0.0)
 
 
-def own_sample_kernel(brick_ref, live_ref, p0, p1, p2, p3, edge_ref, kinds_ref, stk_ref, out_ref, wide_ref, sp_ref):
-    widen_edge(edge_ref, wide_ref)
-    live = live_ref[0]
+def write_sums(live, sp_ref, kinds_ref, stk_ref, out_ref):
     slots = kinds_ref.shape[1]
-    sample_columns((p0, p1, p2, p3), wide_ref, place_in_brick(brick_ref), live, sp_ref, 0, (0, 1, 2, 3), 2)
 
     @pl.when(live > LANES)
     def _():
-        out_ref[...] = masked(far_sums(sp_ref, kinds_ref[...], stk_ref, 0), live)
+        out_ref[...] = masked(far_sums(sp_ref, kinds_ref[2:3, :], stk_ref, 0), live)
 
     @pl.when(live <= LANES)
     def _():
-        out_ref[:, 0:LANES] = masked(far_sums(sp_ref, kinds_ref[:, 0:LANES], stk_ref, 0), live)
+        out_ref[:, 0:LANES] = masked(far_sums(sp_ref, kinds_ref[2:3, 0:LANES], stk_ref, 0), live)
         out_ref[:, LANES:slots] = jnp.zeros((PANELS, slots - LANES), F32)
 
 
-def beside_sample_kernel(odd_ref, facts_ref, p0, p1, p2, p3, edge_ref, kinds_ref, stk_ref, out0, out1, wide_ref, sp_ref):
-    widen_edge(edge_ref, wide_ref)
-    slots = kinds_ref.shape[1] // 2
-    outs = (out0, out1)
-    for first, counts in chunks_beside(facts_ref, slots):
-        here = slice(first, first + LANES)
-        for side, (planes, shift_i) in enumerate(BESIDE):
-            sample_columns((p0, p1, p2, p3), wide_ref, place_in_facts(facts_ref, side * slots + first),
-                           counts[side], sp_ref, 2 * first + side * LANES, planes, shift_i)
-
-        @pl.when(counts[0] + counts[1] > 0)
-        def _(first=first, counts=counts, here=here):
-            kinds = both_sides(kinds_ref.at[2:3, :], slots, first)
-            result = far_sums(sp_ref, kinds, stk_ref, 2 * first)
-            sums = [masked(result[:, side * LANES : (side + 1) * LANES], counts[side]) for side in range(2)]
-            even = jnp.broadcast_to(odd_ref[0], sums[0].shape) == 0
-            out0[:, here] = jnp.where(even, sums[1], sums[0])
-            out1[:, here] = jnp.where(even, sums[0], sums[1])
-
-        @pl.when(counts[0] + counts[1] <= 0)
-        def _(here=here):
-            for out in outs:
-                out[:, here] = jnp.zeros((PANELS, LANES), F32)
-
-
-def near_kernel(live_ref, here_ref, there_ref, source_ref, block_ref, table_ref, out_ref):
+def own_sample_kernel(facts_ref, p0, p1, p2, p3, wide_ref, kinds_ref, stk_ref, out_ref, sp_ref):
+    live = facts_ref[3, 0]
+    sample_columns((p0, p1, p2, p3), wide_ref, place_in(facts_ref), live, sp_ref, 0, (0, 1, 2, 3), 2)
+    write_sums(live, sp_ref, kinds_ref, stk_ref, out_ref)
+
+
+def partner_sample_kernel(is_second, odd_ref, facts_ref, p0, p1, p2, p3, edge_ref, kinds_ref, stk_ref, out_ref, *rest):
+    live = facts_ref[3, 0]
+    wide_ref, sp_ref = rest if is_second else (edge_ref, rest[0])
+    if is_second:
+        widen_edge(edge_ref, wide_ref)
+    for flag, (planes, shift_i) in enumerate((BEFORE, AFTER) if is_second else (AFTER, BEFORE)):
+        @pl.when(odd_ref[0] == flag)
+        def _(planes=planes, shift_i=shift_i):
+            sample_columns((p0, p1, p2, p3), wide_ref, place_in(facts_ref), live, sp_ref, 0, planes, shift_i)
+
+    write_sums(live, sp_ref, kinds_ref, stk_ref, out_ref)
+
+
+def near_kernel(live_ref, a0, a1, a2, a3, a4, a5, source_ref, block_ref, table_ref, out_ref):
     live = live_ref[0]
     fanout, slots = source_ref.shape
-    height = here_ref.shape[0] // 3
-    pool = jnp.concatenate(
-        [ref[step * height : step * height + PANELS, :] for step in range(3) for ref in (here_ref, there_ref)],
-        axis=1,
-    )
+    pool = jnp.concatenate([ref[0:PANELS, :] for ref in (a0, a1, a2, a3, a4, a5)], axis=1)
     total = pool.shape[1]
     for first in range(0, slots, LANES):
         where = slice(first, first + LANES)
@@ -556,55 +501,48 @@
         return moved(values, lambda a: 0, 1)
 
     odd = (lax.axis_index("slab") % 2)[None]
-    kinds = slot_stencil[None, :]
-    packed = pl.pallas_call(
-        pack_kernel,
-        out_shape=shape_of(PANELS + 16, slots, dtype=BF16),
-        in_specs=[SMEM] + [VMEM] * 3,
-        out_specs=VMEM,
-        compiler_params=PARAMS,
-        name="pack",
-    )(live_count, charges, slot_brick[None, :], kinds)
-    from_second = to_second(packed)
+    row = lax.broadcasted_iota(jnp.int32, (PANELS + 16, slots), 0)
+    column = lax.broadcasted_iota(jnp.int32, (PANELS + 16, slots), 1)
+    live = jnp.broadcast_to(live_count[0], row.shape)
+    brick = jnp.broadcast_to(slot_brick[None, :], row.shape)
+    facts = jnp.where(row == PANELS, lax.shift_right_logical(brick, 7), brick & (NZ // 4 - 1))
+    facts = jnp.where(row == PANELS + 2, slot_stencil[None, :], jnp.where(row == PANELS + 3, live, facts))
+    held = jnp.where(column < live, jnp.pad(charges, ((0, 16), (0, 0))), jnp.zeros((), BF16))
+    packed = jnp.where(row < PANELS, held, facts.astype(BF16))
     from_first = to_first(packed)
 
     grid = shape_of(ZROWS, LANES)
-    g = pl.pallas_call(
+    facts_shape = shape_of(8, slots, dtype=jnp.int32)
+    scratch = [pltpu.VMEM((slots * 8, LANES), F32), pltpu.SMEM((8, slots), jnp.int32)]
+    *grids, stk, facts = pl.pallas_call(
         own_kernel,
-        out_shape=(grid,) * 5 + (shape_of(KS * PANELS, POINTS, dtype=BF16),),
-        in_specs=[SMEM] * 2 + [VMEM, pl.BlockSpec(memory_space=pl.ANY)],
-        out_specs=(VMEM,) * 6,
+        out_shape=(grid,) * 5 + (shape_of(KS * PANELS, POINTS, dtype=BF16), facts_shape),
+        in_specs=[VMEM, pl.BlockSpec(memory_space=pltpu.HBM)],
+        out_specs=(VMEM,) * 7,
         scratch_shapes=[
-            pltpu.VMEM((slots * 8, LANES), F32),
-            pltpu.VMEM((KS * PANELS, POINTS), BF16),
-            pltpu.SemaphoreType.DMA,
+            scratch[0], pltpu.VMEM((KS * PANELS, POINTS), BF16), scratch[1], pltpu.SemaphoreType.DMA((2,))
         ],
         compiler_params=PARAMS,
         name="own_scatter",
-    )(slot_brick, live_count, packed, stencils.reshape(KS * PANELS, POINTS))
-    grids, stk = g[:5], g[5]
-
-    g = pl.pallas_call(
-        beside_kernel,
-        out_shape=(grid,) * 5
-        + (
-            shape_of(LANES, LANES),
-            shape_of(8, 2 * slots, dtype=jnp.int32),
-            shape_of(3 * (PANELS + 16), slots, dtype=BF16),
-        ),
-        in_specs=[SMEM] + [VMEM] * 9,
-        out_specs=(VMEM,) * 8,
-        scratch_shapes=[
-            pltpu.VMEM((2 * slots * 8, LANES), F32),
-            pltpu.SMEM((8, 2 * slots), jnp.int32),
-            pltpu.SemaphoreType.DMA,
-        ],
-        input_output_aliases={5: 0, 6: 1, 7: 2, 8: 3, 9: 4},
-        compiler_params=PARAMS,
-        name="beside_scatter",
-    )(odd, packed, from_first, from_second, stk, *grids)
-    facts2 = g[6]
-    edge = to_other_tile(g[5])
+    )(packed, stencils.reshape(KS * PANELS, POINTS))
+
+    def with_partner(is_second, values, grids):
+        return pl.pallas_call(
+            functools.partial(partner_kernel, is_second),
+            out_shape=(grid,) * 5 + (facts_shape,) + (shape_of(LANES, LANES),) * is_second,
+            in_specs=[SMEM] + [VMEM] * 7,
+            out_specs=(VMEM,) * (6 + is_second),
+            scratch_shapes=scratch + [pltpu.SemaphoreType.DMA],
+            input_output_aliases={3: 0, 4: 1, 5: 2, 6: 3, 7: 4},
+            compiler_params=PARAMS,
+            name="second_scatter" if is_second else "first_scatter",
+        )(odd, values, stk, *grids)
+
+    packed, grids[4] = lax.optimization_barrier((packed, grids[4]))
+    from_second = to_second(packed)
+    *grids, first_facts = with_partner(0, from_first, grids)
+    *grids, second_facts, edge = with_partner(1, from_second, grids)
+    edge = to_other_tile(edge)
 
     forward, inverse = z_tables(slabs, tiles)
     rows = owners * (4 * parts + SCALE_ROWS)
@@ -615,7 +553,7 @@
         out_specs=VMEM,
         compiler_params=PARAMS,
         name="z_forward",
-    )(*g[:4], edge, jnp.asarray(halves(forward)))
+    )(*grids[:4], edge, jnp.asarray(halves(forward)))
 
     def exchanged(values):
         values = values.astype(jnp.float16).reshape(owners, 4 * parts + SCALE_ROWS, LANES)
@@ -639,13 +577,17 @@
     )(offset, hat, jnp.asarray(reversal()))
 
     got, hat = lax.optimization_barrier((got, hat))
-    pool = (g[7], to_other_tile(g[7]))
+    pool = []
+    for values in (from_first, packed, from_second):
+        pool += [values, to_other_tile(values)]
     direction = near_source // slots
-    pool_index = (direction // 3 * 2 + (direction % 3 != 1).astype(jnp.int32)) * slots + near_source % slots
+    step = direction // 3 - 1
+    partner = jnp.where(step == 0, 1, jnp.where((step > 0) == (odd[0] == 0), 0, 2))
+    pool_index = (partner * 2 + (direction % 3 != 1).astype(jnp.int32)) * slots + near_source % slots
     near = pl.pallas_call(
         near_kernel,
         out_shape=shape_of(PANELS, slots),
-        in_specs=[SMEM] + [VMEM] * 5,
+        in_specs=[SMEM] + [VMEM] * 9,
         out_specs=VMEM,
         compiler_params=PARAMS,
         name="near_field",
@@ -672,30 +614,28 @@
     )(widened(back), jnp.asarray(halves(inverse)))
     edge = to_other_tile(pot[4])
 
-    def sample_scratch(width):
-        return [pltpu.VMEM((ZROWS, LANES), F32), pltpu.VMEM((width * 8, LANES), F32)]
-
     sums = shape_of(PANELS, slots)
-    others = pl.pallas_call(
-        beside_sample_kernel,
-        out_shape=(sums, sums),
-        in_specs=[SMEM] * 2 + [VMEM] * 7,
-        out_specs=(VMEM, VMEM),
-        scratch_shapes=sample_scratch(2 * slots),
-        compiler_params=PARAMS,
-        name="beside_sample",
-    )(odd, facts2, *pot[:4], edge, facts2, stk)
-    second = to_second(others[1])
-    first = to_first(others[0])
-    own = pl.pallas_call(
-        own_sample_kernel,
-        out_shape=sums,
-        in_specs=[SMEM] * 2 + [VMEM] * 7,
-        out_specs=VMEM,
-        scratch_shapes=sample_scratch(slots),
-        compiler_params=PARAMS,
-        name="own_sample",
-    )(slot_brick, live_count, *pot[:4], edge, kinds, stk)
+    wide = shape_of(ZROWS, LANES)
+
+    def sampled(kernel, name, facts, *edges, scalars=(), outs=(sums,)):
+        return pl.pallas_call(
+            kernel,
+            out_shape=outs,
+            in_specs=[SMEM] * (1 + len(scalars)) + [VMEM] * 7,
+            out_specs=(VMEM,) * len(outs),
+            scratch_shapes=[pltpu.VMEM((slots * 8, LANES), F32)],
+            compiler_params=PARAMS,
+            name=name,
+        )(*scalars, facts, *pot[:4], *edges, facts, stk)
+
+    second, edge = sampled(
+        functools.partial(partner_sample_kernel, 1), "second_sample", second_facts, edge,
+        scalars=(odd,), outs=(sums, wide),
+    )
+    second = to_second(second)
+    first, = sampled(functools.partial(partner_sample_kernel, 0), "first_sample", first_facts, edge, scalars=(odd,))
+    first = to_first(first)
+    own, = sampled(own_sample_kernel, "own_sample", facts, edge)
     return own + near + first + second
 
 

time: 87.8 us -> 90.8 us (1.034)
  Pallas kernels: 20.7 us -> 26 us
  local copies, waits for them, and re-layouts: 4.28 us -> 1.48 us
  other arithmetic: 2.71 us -> 4.3 us
  waiting for transfers between devices: 41.8 us -> 40.6 us
    pallas_call x4 -> x5, Pallas kernels: 7.45 us -> 12.2 us  [the longest x3 7.46 us: sampled(): pl.pallas_call(kernel, out_shape=outs, in_specs=[SMEM] * (1 + len(scalars...]
    unnamed x32 -> x20, local copies, waits for them, and re-layouts: 4.08 us -> 1.28 us
    ppermute x7 -> x9, starting transfers between devices: 11 us -> 9.22 us  [moved(): return lax.ppermute(values, both, pairs)]
    all_to_all x2, starting transfers between devices: 6.53 us -> 7.57 us  [exchanged(): values = lax.all_to_all(values, axes, 0, 0, tiled=True)]
    ppermute x7 -> x9, waiting for transfers between devices: 9.41 us -> 8.39 us  [moved(): return lax.ppermute(values, both, pairs)]
  transfers between devices with their start and end apart: 9 -> 11, of which waited for: 7 -> 10; matrix products, arithmetic and copies ran while one was open for 0% -> 0% of each run, Pallas kernels for 8% -> 12%
where the time goes in v5:
time: 90.8 us; the launch traced here: 90.1 us
  waiting for transfers between devices  40.6 us (45%)
  Pallas kernels  26 us (29%)
  starting transfers between devices  16.8 us (19%)
  other arithmetic  4.3 us (5%)
  local copies, waits for them, and re-layouts  1.48 us (2%)
  between operations  0.93 us (1%)
    all_to_all x2, waiting for transfers between devices, exchanged(): values = lax.all_to_all(values, axes, 0, 0, tiled=True)  32.2 us
    ppermute x9, starting transfers between devices, moved(): return lax.ppermute(values, both, pairs)  9.22 us
    ppermute x9, waiting for transfers between devices, moved(): return lax.ppermute(values, both, pairs)  8.39 us
    all_to_all x2, starting transfers between devices, exchanged(): values = lax.all_to_all(values, axes, 0, 0, tiled=True)  7.57 us
    pallas_call x3, Pallas kernels, sampled(): pl.pallas_call(kernel, out_shape=outs, in_specs=[SMEM] * (1 + len(scalars...  7.46 us
    pallas_call x2, Pallas kernels, with_partner(): pl.pallas_call(functools.partial(partner_kernel, is_second), out_shape=(g...  4.7 us
    pallas_call x1, Pallas kernels, body(): pl.pallas_call(functools.partial(plane_kernel, slabs, planes), out_shape=...  3.85 us
    pallas_call x1, Pallas kernels, body(): pl.pallas_call(own_kernel, out_shape=(grid,) * 5 + (shape_of(KS * PANELS,...  3.56 us
  transfers between devices with their start and end apart: 11, of which 10 were waited for; matrix products, arithmetic and copies ran while one was open for 0% of the time, Pallas kernels for 12%

profile of v5, /device:TPU:0, one launch (start us, length us, event | category | flops | bytes accessed | tf_op | source)
XLA Modules:
  0.0 90.1 jit_solution(13280295342659872585)
XLA Ops:
  0.7 0.7 broadcast_shift-right-logical_fusion
  1.4 0.9 fusion.packed_ref.a2
  2.3 3.0 %collective-permute-start.1 = (bf16[80,256]{1,0:T(8,128)(2,1)S(1)}, bf16[80,256]{1,0:T(8,128)(2,1)S(1)}, u32[]{:S(2)}, u32[]{:S(2)}) collective-permute-start(bf16[80,256]{1,0:T(8,128)(2,1)S(1)} %fusion.packed_ref.a2), channel_id=1, source_target_pairs={{0,2},{1,3},{2,0},{3,1},{4,6},{5,7},{6,4},{7,5},{8,10},{9,11},{10,... | collective-permute-start | bytes 122888 | tf_op jit(solution)/shard_map/ppermute | solution.py:492
  5.3 1.2 %copy-done.1 = bf16[16,64,512]{2,1,0:T(8,128)(2,1)S(1)} copy-done((bf16[16,64,512]{2,1,0:T(8,128)(2,1)S(1)}, bf16[16,64,512]{2,1,0:T(8,128)(2,1)}, u32[]{:S(2)}) %copy-start.1) | copy-done | bytes 1048600
  6.5 3.6 %own_scatter.1 = (f32[520,128]{1,0:T(8,128)S(1)}, f32[520,128]{1,0:T(8,128)S(1)}, f32[520,128]{1,0:T(8,128)S(1)}, f32[520,128]{1,0:T(8,128)S(1)}, f32[520,128]{1...) custom-call(bf16[80,256]{1,0:T(8,128)(2,1)S(1)} %fusion.packed_ref.a2, bf16[1024,512]{1,0:T(8,128)(2,1)S(1)} %bitcast.17), custom_call_target="tpu_custom_call" | custom-call | tf_op jit(solution)/shard_map/own_scatter/pallas_call | solution.py:517
  10.1 4.2 %collective-permute-start = (bf16[80,256]{1,0:T(8,128)(2,1)S(1)}, bf16[80,256]{1,0:T(8,128)(2,1)S(1)}, u32[]{:S(2)}, u32[]{:S(2)}) collective-permute-start(bf16[80,256]{1,0:T(8,128)(2,1)S(1)} %fusion.packed_ref.a2), channel_id=1, source_target_pairs={{0,30},{1,31},{2,4},{3,5},{4,2},{5,3},{6,8},{7,9},{8,6},{9,7},{10,... | collective-permute-start | bytes 122888 | tf_op jit(solution)/shard_map/ppermute | solution.py:492
  14.2 2.5 %first_scatter.1 = (f32[520,128]{1,0:T(8,128)S(1)}, f32[520,128]{1,0:T(8,128)S(1)}, f32[520,128]{1,0:T(8,128)S(1)}, f32[520,128]{1,0:T(8,128)S(1)}, f32[520,128]{1,0:T(8,128)S(1)}, /*index=5*/s32[8,256]{1,0:T(8,128)S(1)}) custom-call(s32[1]{0:T(128)} %bitcast.2.odd_ref, ...), custom_call_target="tpu_custom_call", output_to_operand_aliasing={{0}: (3, {}), {1}: (4, {}), {2}: (5, {}), {3}: (6, {}), {4}... | custom-call | tf_op jit(solution)/shard_map/first_scatter/pallas_call | solution.py:530
  16.7 1.0 %collective-permute-done.packed_ref.a4 = bf16[80,256]{1,0:T(8,128)(2,1)S(1)} collective-permute-done((bf16[80,256]{1,0:T(8,128)(2,1)S(1)}, bf16[80,256]{1,0:T(8,128)(2,1)S(1)}, u32[]{:S(2)}, u32[]{:S(2)}) %collective-permute-start) | collective-permute-done | bytes 40992 | tf_op jit(solution)/shard_map/ppermute | solution.py:492
  17.7 2.2 %second_scatter.1 = (f32[520,128]{1,0:T(8,128)S(1)}, f32[520,128]{1,0:T(8,128)S(1)}, f32[520,128]{1,0:T(8,128)S(1)}, f32[520,128]{1,0:T(8,128)S(1)}, f32[520,128...) custom-call(s32[1]{0:T(128)} %bitcast.2.odd_ref, ...), custom_call_target="tpu_custom_call", output_to_operand_aliasing={{0}: (3, {}), {1}: (4, {}), {2}: (5, {}), {3}: (6, {}), {4}... | custom-call | tf_op jit(solution)/shard_map/second_scatter/pallas_call | solution.py:530
  20.0 0.1 collective-permute-start.2
  20.0 1.2 %collective-permute-done.2.edge_ref = f32[128,128]{1,0:T(8,128)S(1)} collective-permute-done((f32[128,128]{1,0:T(8,128)S(1)}, f32[128,128]{1,0:T(8,128)S(1)}, u32[]{:S(2)}, u32[]{:S(2)}) %collective-permute-start.2) | collective-permute-done | bytes 65568 | tf_op jit(solution)/shard_map/ppermute | solution.py:492
  21.3 2.2 %z_forward.1 = f32[2304,128]{1,0:T(8,128)S(1)} custom-call(f32[520,128]{1,0:T(8,128)S(1)} %get-tuple-element.53.g0, f32[520,128]{1,0:T(8,128)S(1)} %get-tuple-element.54.g1, f32[520,128]{1,0:T(8,128)S(1)} %get-tuple-element.55.g2, f32[520,128]{1,0:T(8,128)S(1)} %get-tuple-element.56.g3, f32[128,128]{1,0:T(8,128)S(1)} %collective-permute-done.2.edge_ref, ...), custom_call_target="tpu_custom_call" | custom-call | tf_op jit(solution)/shard_map/z_forward/pallas_call | solution.py:549
  23.5 0.0 copy-start.2
  23.5 0.0 copy-start.6
  23.5 0.9 %convert_element_type.18 = f16[2304,128]{1,0:T(8,128)(2,1)} convert(f32[2304,128]{1,0:T(8,128)S(1)} %z_forward.1) | non-fusion elementwise | flops 294912 | bytes 1769472 | tf_op jit(solution)/shard_map/convert_element_type | solution.py:559
  24.4 4.8 %all-to-all-start = ((f16[32,72,128]{2,1,0:T(8,128)(2,1)}), f16[32,72,128]{2,1,0:T(8,128)(2,1)S(1)}, u32[]{:S(2)}, u32[]{:S(2)}) async-start(f16[32,72,128]{2,1,0:T(8,128)(2,1)} %bitcast.3), calls=%async_computation | async-start | bytes 1179648 | tf_op jit(solution)/shard_map/all_to_all | solution.py:560
  29.3 0.3 hat_order.1.hat_ref
  29.5 0.0 copy-start.4
  29.6 0.0 copy-start.5
  29.6 17.9 %all-to-all-done = f16[32,72,128]{2,1,0:T(8,128)(2,1)S(1)} async-done(((f16[32,72,128]{2,1,0:T(8,128)(2,1)}), f16[32,72,128]{2,1,0:T(8,128)(2,1)S(1)}, u32[]{:S(2)}, u32[]{:S(2)}) %all-to-all-start) | async-done | bytes 589856 | tf_op jit(solution)/shard_map/all_to_all | solution.py:560
  47.5 0.1 bitcast_convert_fusion.1.in_ref
  47.6 3.8 %plane_filter.1 = f32[2304,128]{1,0:T(8,128)S(1)} custom-call(f32[2304,128]{1,0:T(8,128)S(1)} %bitcast_convert_fusion.1.in_ref, f32[8,64,256]{2,1,0:T(8,128)S(1)} %hat_order.1.hat_ref, bf16[1024,256]{1,0:T(8,128)(2,1)S(1)} %copy-done.4, bf16[512,128]{1,0:T(8,128)(2,1)S(1)} %copy-done.5), custom_call_target="tpu_custom_call" | custom-call | tf_op jit(solution)/shard_map/plane_filter/pallas_call | solution.py:596
  51.5 0.0 copy-start.9
  51.5 0.0 copy-start.8
  51.5 0.9 %convert_element_type.19 = f16[2304,128]{1,0:T(8,128)(2,1)} convert(f32[2304,128]{1,0:T(8,128)S(1)} %plane_filter.1) | non-fusion elementwise | flops 294912 | bytes 1769472 | tf_op jit(solution)/shard_map/convert_element_type | solution.py:559
  52.4 2.7 %all-to-all-start.1 = ((f16[32,72,128]{2,1,0:T(8,128)(2,1)}), f16[32,72,128]{2,1,0:T(8,128)(2,1)S(1)}, u32[]{:S(2)}, u32[]{:S(2)}) async-start(f16[32,72,128]{2,1,0:T(8,128)(2,1)} %bitcast.6), calls=%async_computation.1 | async-start | bytes 1179648 | tf_op jit(solution)/shard_map/all_to_all | solution.py:560
  55.2 0.2 collective-permute-start.4
  55.3 0.4 collective-permute-start.3
  55.7 0.1 collective-permute-start.5
  55.9 0.2 reshape.29.table_ref
  56.1 0.0 copy-start.3
  56.1 0.3 collective-permute-done.4.a3
  56.4 0.2 collective-permute-done.3.a1
  56.6 0.3 collective-permute-done.5.a5
  57.0 2.1 %near_field.1 = f32[64,256]{1,0:T(8,128)S(1)} custom-call(s32[1]{0:T(128)} %copy.35.live_ref, bf16[80,256]{1,0:T(8,128)(2,1)S(1)} %collective-permute-done.1.packed_ref.a0, bf16[80,256]{1,0:T(8,128)(2,1)S(1)} %collective-permute-done.3.a1, bf16[80,256]{1,0:T(8,128)(2,1)S(1)} %fusion.packed_ref.a2, bf16[80,256]{1,0:T(8,128)(2,1)S(1)} %collective-permute-done.4.a3, ...), custom_call_target="tpu_custom_call" | custom-call | tf_op jit(solution)/shard_map/near_field/pallas_call | solution.py:587
  59.1 14.3 %all-to-all-done.1 = f16[32,72,128]{2,1,0:T(8,128)(2,1)S(1)} async-done(((f16[32,72,128]{2,1,0:T(8,128)(2,1)}), f16[32,72,128]{2,1,0:T(8,128)(2,1)S(1)}, u32[]{:S(2)}, u32[]{:S(2)}) %all-to-all-start.1) | async-done | bytes 589856 | tf_op jit(solution)/shard_map/all_to_all | solution.py:560
  73.4 0.1 bitcast_convert_fusion.in_ref
  73.5 1.9 %z_inverse.1 = (f32[520,128]{1,0:T(8,128)S(1)}, f32[520,128]{1,0:T(8,128)S(1)}, f32[520,128]{1,0:T(8,128)S(1)}, f32[520,128]{1,0:T(8,128)S(1)}, bf16[128,128]{1,0:T(8,128)(2,1)S(1)}) custom-call(f32[2304,128]{1,0:T(8,128)S(1)} %bitcast_convert_fusion.in_ref, bf16[1024,512]{1,0:T(8,128)(2,1)S(1)} %copy-done.3), custom_call_target="tpu_custom_call" | custom-call | tf_op jit(solution)/shard_map/z_inverse/pallas_call | solution.py:607
  75.4 0.1 collective-permute-start.6
  75.5 1.2 %collective-permute-done.6.edge_ref = bf16[128,128]{1,0:T(8,128)(2,1)S(1)} collective-permute-done((bf16[128,128]{1,0:T(8,128)(2,1)S(1)}, bf16[128,128]{1,0:T(8,128)(2,1)S(1)}, u32[]{:S(2)}, u32[]{:S(2)}) %collective-permute-start.6) | collective-permute-done | bytes 32800 | tf_op jit(solution)/shard_map/ppermute | solution.py:492
  76.7 2.2 %second_sample.1 = (f32[64,256]{1,0:T(8,128)S(1)}, f32[520,128]{1,0:T(8,128)S(1)}) custom-call(s32[1]{0:T(128)} %bitcast.2.odd_ref, s32[8,256]{1,0:T(8,128)S(1)} %get-tuple-element.67.facts_ref.kinds_ref, f32[520,128]{1,0:T(8,128)S(1)} %get-tuple-element.63.p0, f32[520,128]{1,0:T(8,128)S(1)} %get-tuple-element.64.p1, f32[520,128]{1,0:T(8,128)S(1)} %get-tuple-element.65.p2, ...), custom_call_target="tpu_custom_call" | custom-call | tf_op jit(solution)/shard_map/second_sample/pallas_call | solution.py:621
  78.9 2.5 %first_sample.1 = f32[64,256]{1,0:T(8,128)S(1)} custom-call(s32[1]{0:T(128)} %bitcast.2.odd_ref, s32[8,256]{1,0:T(8,128)S(1)} %get-tuple-element.71.facts_ref.kinds_ref, f32[520,128]{1,0:T(8,128)S(1)} %get-tuple-element.63.p0, f32[520,128]{1,0:T(8,128)S(1)} %get-tuple-element.64.p1, f32[520,128]{1,0:T(8,128)S(1)} %get-tuple-element.65.p2, ...), custom_call_target="tpu_custom_call" | custom-call | tf_op jit(solution)/shard_map/first_sample/pallas_call | solution.py:621
  81.5 0.1 collective-permute-start.7
  81.6 1.1 %collective-permute-start.8 = (f32[64,256]{1,0:T(8,128)S(1)}, f32[64,256]{1,0:T(8,128)S(1)}, u32[]{:S(2)}, u32[]{:S(2)}) collective-permute-start(f32[64,256]{1,0:T(8,128)S(1)} %get-tuple-element.72), channel_id=1, source_target_pairs={{0,30},{1,31},{2,4},{3,5},{4,2},{5,3},{6,8},{7,9},{8,6},{9,7},{10,... | collective-permute-start | bytes 196616 | tf_op jit(solution)/shard_map/ppermute | solution.py:492
  82.7 2.7 %own_sample.1 = f32[64,256]{1,0:T(8,128)S(1)} custom-call(s32[8,256]{1,0:T(8,128)S(1)} %get-tuple-element.39.facts_ref.kinds_ref, f32[520,128]{1,0:T(8,128)S(1)} %get-tuple-element.63.p0, f32[520,128]{1,0:T(8,128)S(1)} %get-tuple-element.64.p1, f32[520,128]{1,0:T(8,128)S(1)} %get-tuple-element.65.p2, f32[520,128]{1,0:T(8,128)S(1)} %get-tuple-element.66.p3, ...), custom_call_target="tpu_custom_call" | custom-call | tf_op jit(solution)/shard_map/own_sample/pallas_call | solution.py:621
  85.4 0.6 collective-permute-done.7
  86.0 3.5 %collective-permute-done.8 = f32[64,256]{1,0:T(8,128)S(1)} collective-permute-done((f32[64,256]{1,0:T(8,128)S(1)}, f32[64,256]{1,0:T(8,128)S(1)}, u32[]{:S(2)}, u32[]{:S(2)}) %collective-permute-start.8) | collective-permute-done | bytes 65568 | tf_op jit(solution)/shard_map/ppermute | solution.py:492
  89.5 0.6 add_add_fusion
  (17 shorter events, 0.1 us)
Async XLA Ops:
  2.3 12.0 %collective-permute-start.1 = (bf16[80,256]{1,0:T(8,128)(2,1)S(1)}, bf16[80,256]{1,0:T(8,128)(2,1)S(1)}, u32[]{:S(2)}, u32[]{:S(2)}) collective-permute-start(bf16[80,256]{1,0:T(8,128)(2,1)S(1)} %fusion.packed_ref.a2), channel_id=1, source_target_pairs={{0,2},{1,3},{2,0},{3,1},{4,6},{5,7},{6,4},{7,5},{8,10},{9,11},{10,... | collective-permute-start | bytes 122888 | tf_op jit(solution)/shard_map/ppermute | solution.py:492
  5.3 1.2 %copy-start.1 = (bf16[16,64,512]{2,1,0:T(8,128)(2,1)S(1)}, bf16[16,64,512]{2,1,0:T(8,128)(2,1)}, u32[]{:S(2)}) copy-start(bf16[16,64,512]{2,1,0:T(8,128)(2,1)} %param.18) | copy-start | bytes 3145732
  10.1 7.7 %collective-permute-start = (bf16[80,256]{1,0:T(8,128)(2,1)S(1)}, bf16[80,256]{1,0:T(8,128)(2,1)S(1)}, u32[]{:S(2)}, u32[]{:S(2)}) collective-permute-start(bf16[80,256]{1,0:T(8,128)(2,1)S(1)} %fusion.packed_ref.a2), channel_id=1, source_target_pairs={{0,30},{1,31},{2,4},{3,5},{4,2},{5,3},{6,8},{7,9},{8,6},{9,7},{10,... | collective-permute-start | bytes 122888 | tf_op jit(solution)/shard_map/ppermute | solution.py:492
  17.7 3.6 %copy-start = (bf16[1024,512]{1,0:T(8,128)(2,1)S(1)}, bf16[1024,512]{1,0:T(8,128)(2,1)}, u32[]{:S(2)}) copy-start(bf16[1024,512]{1,0:T(8,128)(2,1)} %constant.91.clone.w_ref) | copy-start | bytes 3145732
  20.0 1.3 %collective-permute-start.2 = (f32[128,128]{1,0:T(8,128)S(1)}, f32[128,128]{1,0:T(8,128)S(1)}, u32[]{:S(2)}, u32[]{:S(2)}) collective-permute-start(f32[128,128]{1,0:T(8,128)S(1)} %get-tuple-element.57), channel_id=1, source_target_pairs={{0,1},{1,0},{2,3},{3,2},{4,5},{5,4},{6,7},{7,6},{8,9},{9,8},{10,11... | collective-permute-start | bytes 196616 | tf_op jit(solution)/shard_map/ppermute | solution.py:492
  23.5 5.8 %copy-start.2 = (f32[16,64,256]{2,1,0:T(8,128)S(1)}, f32[16,64,256]{2,1,0:T(8,128)}, u32[]{:S(2)}) copy-start(f32[16,64,256]{2,1,0:T(8,128)} %hat_ref) | copy-start | bytes 3145732
  23.5 5.8 %copy-start.6 = (bf16[128,128]{1,0:T(8,128)(2,1)S(1)}, bf16[128,128]{1,0:T(8,128)(2,1)}, u32[]{:S(2)}) copy-start(bf16[128,128]{1,0:T(8,128)(2,1)} %constant.92.clone.turn_ref) | copy-start | bytes 98308
  24.4 23.1 %all-to-all-start = ((f16[32,72,128]{2,1,0:T(8,128)(2,1)}), f16[32,72,128]{2,1,0:T(8,128)(2,1)S(1)}, u32[]{:S(2)}, u32[]{:S(2)}) async-start(f16[32,72,128]{2,1,0:T(8,128)(2,1)} %bitcast.3), calls=%async_computation | async-start | bytes 1179648 | tf_op jit(solution)/shard_map/all_to_all | solution.py:560
  29.5 18.1 %copy-start.4 = (bf16[1024,256]{1,0:T(8,128)(2,1)S(1)}, bf16[1024,256]{1,0:T(8,128)(2,1)}, u32[]{:S(2)}) copy-start(bf16[1024,256]{1,0:T(8,128)(2,1)} %constant.93.clone.y_ref) | copy-start | bytes 1572868
  29.6 18.1 %copy-start.5 = (bf16[512,128]{1,0:T(8,128)(2,1)S(1)}, bf16[512,128]{1,0:T(8,128)(2,1)}, u32[]{:S(2)}) copy-start(bf16[512,128]{1,0:T(8,128)(2,1)} %constant.94.clone.x_ref) | copy-start | bytes 393220
  51.5 4.4 %copy-start.9 = (s32[256,8]{0,1:T(8,128)S(1)}, s32[256,8]{0,1:T(8,128)}, u32[]{:S(2)}) copy-start(s32[256,8]{0,1:T(8,128)} %param.19) | copy-start | bytes 24580
  51.5 4.4 %copy-start.8 = (bf16[64,16,64]{2,1,0:T(8,128)(2,1)S(1)}, bf16[64,16,64]{2,1,0:T(8,128)(2,1)}, u32[]{:S(2)}) copy-start(bf16[64,16,64]{2,1,0:T(8,128)(2,1)} %param.21) | copy-start | bytes 393220
  52.4 4.5 %copy-start.7 = (s32[256,8]{0,1:T(8,128)S(1)}, s32[256,8]{0,1:T(8,128)}, u32[]{:S(2)}) copy-start(s32[256,8]{0,1:T(8,128)} %param.20) | copy-start | bytes 24580
  52.4 21.0 %all-to-all-start.1 = ((f16[32,72,128]{2,1,0:T(8,128)(2,1)}), f16[32,72,128]{2,1,0:T(8,128)(2,1)S(1)}, u32[]{:S(2)}, u32[]{:S(2)}) async-start(f16[32,72,128]{2,1,0:T(8,128)(2,1)} %bitcast.6), calls=%async_computation.1 | async-start | bytes 1179648 | tf_op jit(solution)/shard_map/all_to_all | solution.py:560
  55.2 1.3 %collective-permute-start.4 = (bf16[80,256]{1,0:T(8,128)(2,1)S(1)}, bf16[80,256]{1,0:T(8,128)(2,1)S(1)}, u32[]{:S(2)}, u32[]{:S(2)}) collective-permute-start(bf16[80,256]{1,0:T(8,128)(2,1)S(1)} %fusion.packed_ref.a2), channel_id=1, source_target_pairs={{0,1},{1,0},{2,3},{3,2},{4,5},{5,4},{6,7},{7,6},{8,9},{9,8},{10,11... | collective-permute-start | bytes 122888 | tf_op jit(solution)/shard_map/ppermute | solution.py:492
  55.3 1.3 %collective-permute-start.3 = (bf16[80,256]{1,0:T(8,128)(2,1)S(1)}, bf16[80,256]{1,0:T(8,128)(2,1)S(1)}, u32[]{:S(2)}, u32[]{:S(2)}) collective-permute-start(bf16[80,256]{1,0:T(8,128)(2,1)S(1)} %collective-permute-done.1.packed_ref.a0), channel_id=1, source_target_pairs={{0,1},{1,0},{2,3},{3,2},{4,5},{5,4},{6,7},{7,6},{8,9},{9,8},{10,11... | collective-permute-start | bytes 122888 | tf_op jit(solution)/shard_map/ppermute | solution.py:492
  55.7 1.2 %collective-permute-start.5 = (bf16[80,256]{1,0:T(8,128)(2,1)S(1)}, bf16[80,256]{1,0:T(8,128)(2,1)S(1)}, u32[]{:S(2)}, u32[]{:S(2)}) collective-permute-start(bf16[80,256]{1,0:T(8,128)(2,1)S(1)} %collective-permute-done.packed_ref.a4), channel_id=1, source_target_pairs={{0,1},{1,0},{2,3},{3,2},{4,5},{5,4},{6,7},{7,6},{8,9},{9,8},{10,11... | collective-permute-start | bytes 122888 | tf_op jit(solution)/shard_map/ppermute | solution.py:492
  56.1 17.4 %copy-start.3 = (bf16[1024,512]{1,0:T(8,128)(2,1)S(1)}, bf16[1024,512]{1,0:T(8,128)(2,1)}, u32[]{:S(2)}) copy-start(bf16[1024,512]{1,0:T(8,128)(2,1)} %constant.95.clone.v_ref) | copy-start | bytes 3145732
  75.4 1.3 %collective-permute-start.6 = (bf16[128,128]{1,0:T(8,128)(2,1)S(1)}, bf16[128,128]{1,0:T(8,128)(2,1)S(1)}, u32[]{:S(2)}, u32[]{:S(2)}) collective-permute-start(bf16[128,128]{1,0:T(8,128)(2,1)S(1)} %get-tuple-element.68), channel_id=1, source_target_pairs={{0,1},{1,0},{2,3},{3,2},{4,5},{5,4},{6,7},{7,6},{8,9},{9,8},{10,11... | collective-permute-start | bytes 98312 | tf_op jit(solution)/shard_map/ppermute | solution.py:492
  81.5 4.5 %collective-permute-start.7 = (f32[64,256]{1,0:T(8,128)S(1)}, f32[64,256]{1,0:T(8,128)S(1)}, u32[]{:S(2)}, u32[]{:S(2)}) collective-permute-start(f32[64,256]{1,0:T(8,128)S(1)} %first_sample.1), channel_id=1, source_target_pairs={{0,2},{1,3},{2,0},{3,1},{4,6},{5,7},{6,4},{7,5},{8,10},{9,11},{10,... | collective-permute-start | bytes 196616 | tf_op jit(solution)/shard_map/ppermute | solution.py:492
  81.6 7.9 %collective-permute-start.8 = (f32[64,256]{1,0:T(8,128)S(1)}, f32[64,256]{1,0:T(8,128)S(1)}, u32[]{:S(2)}, u32[]{:S(2)}) collective-permute-start(f32[64,256]{1,0:T(8,128)S(1)} %get-tuple-element.72), channel_id=1, source_target_pairs={{0,30},{1,31},{2,4},{3,5},{4,2},{5,3},{6,8},{7,9},{8,6},{9,7},{10,... | collective-permute-start | bytes 196616 | tf_op jit(solution)/shard_map/ppermute | solution.py:492

commit v6 on v4

--- a/solution.py
+++ b/solution.py
@@ -1,4 +1,5 @@
 import functools
+import math
 
 import jax
 import jax.numpy as jnp
@@ -20,6 +21,8 @@
 UNROLL = 16
 HALF = NY // 2
 SCALE_ROWS = 8
+BOUND = 12.0
+HEADROOM = 15.0
 F32 = jnp.float32
 BF16 = jnp.bfloat16
 SMEM = pl.BlockSpec(memory_space=pltpu.SMEM)
@@ -194,42 +197,31 @@
     return result
 
 
-def place_in_brick(brick_ref):
-    def place_of(column):
-        brick = brick_ref[column]
-        return lax.shift_right_logical(brick, 7), brick & (NZ // 4 - 1)
-
-    return place_of
-
-
-def place_in_facts(facts_ref, start):
+def place_in_facts(facts_ref, start=0):
     return lambda column: (facts_ref[0, start + column], facts_ref[1, start + column])
 
 
-def pack_kernel(live_ref, charges_ref, brick_ref, stencil_ref, out_ref):
-    slots = charges_ref.shape[1]
-    charges = charges_ref[...].astype(F32)
-    held = jnp.where(lane_of(charges.shape) < live_ref[0], charges, 0.0)
-    row = lax.broadcasted_iota(jnp.int32, (16, slots), 0)
-    brick = jnp.broadcast_to(brick_ref[...], (16, slots))
-    facts = jnp.where(row == 0, lax.shift_right_logical(brick, 7), brick & (NZ // 4 - 1))
-    facts = jnp.where(row == 2, stencil_ref[...], jnp.where(row == 3, live_ref[0], facts))
-    out_ref[...] = jnp.concatenate([held, facts.astype(F32)], axis=0).astype(BF16)
-
-
-def own_kernel(brick_ref, live_ref, packed_ref, stencil_ref,
-               g0, g1, g2, g3, edge_ref, stk_ref, fp_ref, rows_ref, sem):
-    copy = pltpu.make_async_copy(stencil_ref, rows_ref, sem)
+def facts_of(packed_ref, row):
+    return packed_ref[row : row + 16, :].astype(F32).astype(jnp.int32)[0:8, :]
+
+
+def own_kernel(packed_ref, stencil_ref,
+               g0, g1, g2, g3, edge_ref, stk_ref, out_facts, fp_ref, rows_ref, facts_ref, sems):
+    copy = pltpu.make_async_copy(stencil_ref, rows_ref, sems.at[0])
     copy.start()
+    out_facts[...] = facts_of(packed_ref, PANELS)
+    facts_copy = pltpu.make_async_copy(out_facts, facts_ref, sems.at[1])
+    facts_copy.start()
     for ref in (g0, g1, g2, g3, edge_ref):
         ref[...] = jnp.zeros_like(ref)
     shape = (POINTS, POINTS)
     point = lax.broadcasted_iota(jnp.int32, shape, 0)
     target = (point & 7) * 64 + lax.shift_right_logical(point, 3)
     order = jnp.where(lane_of(shape) == target, 1.0, 0.0).astype(BF16)
-    live = live_ref[0]
+    facts_copy.wait()
     copy.wait()
     stk_ref[...] = dot(rows_ref[...], order).astype(BF16)
+    live = facts_ref[3, 0]
 
     @pl.when(live > LANES)
     def _():
@@ -239,7 +231,7 @@
     def _():
         footprints(packed_ref[:, 0:LANES], stk_ref, fp_ref, 0)
 
-    scatter_columns(fp_ref, 0, place_in_brick(brick_ref), live, (g0, g1, g2, g3), edge_ref, (0, 1, 2, 3), 2)
+    scatter_columns(fp_ref, 0, place_in_facts(facts_ref), live, (g0, g1, g2, g3), edge_ref, (0, 1, 2, 3), 2)
 
 
 BESIDE = (((0, 1), 6), ((2, 3), -2))
@@ -274,9 +266,7 @@
         pool_ref[after, :] = second_ref[...]
 
     for side in range(2):
-        row = 2 * side * height + PANELS
-        facts = pool_ref[row : row + 16, :].astype(F32).astype(jnp.int32)
-        out_facts[:, side * slots : (side + 1) * slots] = facts[0:8, :]
+        out_facts[:, side * slots : (side + 1) * slots] = facts_of(pool_ref, 2 * side * height + PANELS)
     copy = pltpu.make_async_copy(out_facts, facts_ref, sem)
     copy.start()
 
@@ -308,7 +298,7 @@
 def exponent_of(values):
     top = functools.reduce(jnp.maximum, [jnp.max(jnp.abs(v), axis=0, keepdims=True) for v in values])
     top = jnp.maximum(jnp.max(top, axis=1, keepdims=True), 2.0**-100)
-    return jnp.ceil(jnp.log2(top)) - 12.0
+    return jnp.ceil(jnp.log2(top)) - BOUND
 
 
 def z_kernel(owners, g0, g1, g2, g3, edge_ref, w_ref, out_ref):
@@ -355,7 +345,7 @@
         out_ref[plane] = jnp.concatenate([values[here, :HALF], upper[here, :]], axis=1)
 
 
-def plane_kernel(slabs, planes, in_ref, hat_ref, y_ref, x_ref, out_ref, ah_ref, al_ref):
+def plane_kernel(slabs, planes, in_ref, hat_ref, y_ref, x_ref, out_ref, exponent_ref, ah_ref, al_ref):
     length = 4 * slabs
     rows = planes * length
     parts = 2 * planes
@@ -366,16 +356,16 @@
             for part in range(2):
                 for xi in range(4):
                     for plane in range(planes):
-                        start = tile * slabs * stride + xi * parts + part * planes + plane
-                        row = (part * planes + plane) * length + xi * slabs
-                        yield tile, part, pl.ds(start, slabs, stride=stride), row
+                        yield tile, part, plane, xi
 
     scales = [
         jnp.exp2(in_ref[pl.ds(tile * slabs * stride + 4 * parts, slabs, stride=stride), :])
         for tile in range(2)
     ]
-    for tile, part, where, row in pieces():
-        high, low = split(in_ref[where, :] * scales[tile])
+    for tile, part, plane, xi in pieces():
+        start = tile * slabs * stride + xi * parts + part * planes + plane
+        row = (part * planes + plane) * length + xi * slabs
+        high, low = split(in_ref[pl.ds(start, slabs, stride=stride), :] * scales[tile])
         ah_ref[row : row + slabs, tile * LANES : (tile + 1) * LANES] = high
         al_ref[row : row + slabs, tile * LANES : (tile + 1) * LANES] = low
     first_lane = lane_of((rows, HALF)) == 0
@@ -407,31 +397,33 @@
         ah_ref[here, :], al_ref[here, :] = split(jnp.concatenate([even_r, odd_r], axis=1))
         ah_ref[there, :], al_ref[there, :] = split(jnp.concatenate([even_i, odd_i], axis=1))
     turned = dot3((ah_ref[...], al_ref[...]), (y_ref[2 * NY : 3 * NY, :], y_ref[3 * NY : 4 * NY, :]))
-    results = (turned[:rows], turned[rows:])
-    exponent = exponent_of(results)
-    scale = jnp.exp2(-exponent)
-    results = [result * scale for result in results]
-    for tile, part, where, row in pieces():
-        row -= part * rows
-        out_ref[where, :] = results[part][row : row + slabs, tile * LANES : (tile + 1) * LANES]
-    for row in range(SCALE_ROWS):
-        out_ref[pl.ds(4 * parts + row, 2 * slabs, stride=stride), :] = jnp.broadcast_to(
-            exponent, (2 * slabs, LANES)
+    tops = [
+        jnp.max(in_ref[pl.ds(tile * slabs * stride + 4 * parts, slabs, stride=stride), :], axis=0, keepdims=True)
+        for tile in range(2)
+    ]
+    exponent = jnp.broadcast_to(jnp.maximum(*tops) + BOUND - HEADROOM + math.ceil(math.log2(length * NY) / 2), (8, LANES))
+    exponent_ref[...] = exponent
+    scale = jnp.exp2(-exponent[0:1, 0:1])
+    for tile, part, plane, xi in pieces():
+        here = slice((part * planes + plane) * length + xi * slabs, (part * planes + plane) * length + (xi + 1) * slabs)
+        start = tile * slabs * 4 * parts + xi * parts + part * planes + plane
+        out_ref[pl.ds(start, slabs, stride=4 * parts), :] = (
+            turned[here, tile * LANES : (tile + 1) * LANES] * scale
         )
 
 
-def potential_kernel(owners, in_ref, v_ref, p0, p1, p2, p3, edge_ref):
+def potential_kernel(owners, in_ref, exponent_ref, v_ref, p0, p1, p2, p3, edge_ref):
     parts = NZ // owners
-    stride = 4 * parts + SCALE_ROWS
     lane = lane_of((LANES, LANES))
     edge = jnp.zeros((LANES, LANES), F32)
-    scale = jnp.exp2(in_ref[pl.ds(4 * parts, owners, stride=stride), :])
+    scale = jnp.exp2(exponent_ref[0:1, 0:1])
     for plane, pot in enumerate((p0, p1, p2, p3)):
         values = split(jnp.concatenate(
-            [in_ref[pl.ds(plane * parts + part, owners, stride=stride), :] * scale for part in range(parts)],
+            [in_ref[pl.ds(plane * parts + part, owners, stride=4 * parts), :] for part in range(parts)],
             axis=0,
         ))
-        result = dot3((v_ref[0:NZ, :], v_ref[NZ : 2 * NZ, :]), values).astype(BF16).astype(F32)
+        result = dot3((v_ref[0:NZ, :], v_ref[NZ : 2 * NZ, :]), values) * scale
+        result = result.astype(BF16).astype(F32)
         pot[0:NZ, :] = result
         pot[NZ:ZROWS, :] = result[0:8, :]
         for block in range(4):
@@ -453,19 +445,19 @@
     return jnp.where(lane_of(values.shape) < live, values, 0.0)
 
 
-def own_sample_kernel(brick_ref, live_ref, p0, p1, p2, p3, edge_ref, kinds_ref, stk_ref, out_ref, wide_ref, sp_ref):
+def own_sample_kernel(facts_ref, p0, p1, p2, p3, edge_ref, kinds_ref, stk_ref, out_ref, wide_ref, sp_ref):
     widen_edge(edge_ref, wide_ref)
-    live = live_ref[0]
+    live = facts_ref[3, 0]
     slots = kinds_ref.shape[1]
-    sample_columns((p0, p1, p2, p3), wide_ref, place_in_brick(brick_ref), live, sp_ref, 0, (0, 1, 2, 3), 2)
+    sample_columns((p0, p1, p2, p3), wide_ref, place_in_facts(facts_ref), live, sp_ref, 0, (0, 1, 2, 3), 2)
 
     @pl.when(live > LANES)
     def _():
-        out_ref[...] = masked(far_sums(sp_ref, kinds_ref[...], stk_ref, 0), live)
+        out_ref[...] = masked(far_sums(sp_ref, kinds_ref[2:3, :], stk_ref, 0), live)
 
     @pl.when(live <= LANES)
     def _():
-        out_ref[:, 0:LANES] = masked(far_sums(sp_ref, kinds_ref[:, 0:LANES], stk_ref, 0), live)
+        out_ref[:, 0:LANES] = masked(far_sums(sp_ref, kinds_ref[2:3, 0:LANES], stk_ref, 0), live)
         out_ref[:, LANES:slots] = jnp.zeros((PANELS, slots - LANES), F32)
 
 
@@ -556,33 +548,32 @@
         return moved(values, lambda a: 0, 1)
 
     odd = (lax.axis_index("slab") % 2)[None]
-    kinds = slot_stencil[None, :]
-    packed = pl.pallas_call(
-        pack_kernel,
-        out_shape=shape_of(PANELS + 16, slots, dtype=BF16),
-        in_specs=[SMEM] + [VMEM] * 3,
-        out_specs=VMEM,
-        compiler_params=PARAMS,
-        name="pack",
-    )(live_count, charges, slot_brick[None, :], kinds)
+    row = lax.broadcasted_iota(jnp.int32, (PANELS + 16, slots), 0)
+    column = lax.broadcasted_iota(jnp.int32, (PANELS + 16, slots), 1)
+    live = jnp.broadcast_to(live_count[0], row.shape)
+    brick = jnp.broadcast_to(slot_brick[None, :], row.shape)
+    facts = jnp.where(row == PANELS, lax.shift_right_logical(brick, 7), brick & (NZ // 4 - 1))
+    facts = jnp.where(row == PANELS + 2, slot_stencil[None, :], jnp.where(row == PANELS + 3, live, facts))
+    held = jnp.where(column < live, jnp.pad(charges, ((0, 16), (0, 0))), jnp.zeros((), BF16))
+    packed = jnp.where(row < PANELS, held, facts.astype(BF16))
     from_second = to_second(packed)
     from_first = to_first(packed)
 
     grid = shape_of(ZROWS, LANES)
-    g = pl.pallas_call(
+    *grids, stk, facts = pl.pallas_call(
         own_kernel,
-        out_shape=(grid,) * 5 + (shape_of(KS * PANELS, POINTS, dtype=BF16),),
-        in_specs=[SMEM] * 2 + [VMEM, pl.BlockSpec(memory_space=pl.ANY)],
-        out_specs=(VMEM,) * 6,
+        out_shape=(grid,) * 5 + (shape_of(KS * PANELS, POINTS, dtype=BF16), shape_of(8, slots, dtype=jnp.int32)),
+        in_specs=[VMEM, pl.BlockSpec(memory_space=pl.ANY)],
+        out_specs=(VMEM,) * 7,
         scratch_shapes=[
             pltpu.VMEM((slots * 8, LANES), F32),
             pltpu.VMEM((KS * PANELS, POINTS), BF16),
-            pltpu.SemaphoreType.DMA,
+            pltpu.SMEM((8, slots), jnp.int32),
+            pltpu.SemaphoreType.DMA((2,)),
         ],
         compiler_params=PARAMS,
         name="own_scatter",
-    )(slot_brick, live_count, packed, stencils.reshape(KS * PANELS, POINTS))
-    grids, stk = g[:5], g[5]
+    )(packed, stencils.reshape(KS * PANELS, POINTS))
 
     g = pl.pallas_call(
         beside_kernel,
@@ -618,12 +609,12 @@
     )(*g[:4], edge, jnp.asarray(halves(forward)))
 
     def exchanged(values):
-        values = values.astype(jnp.float16).reshape(owners, 4 * parts + SCALE_ROWS, LANES)
+        values = values.astype(jnp.float16).reshape(owners, -1, LANES)
         values = lax.all_to_all(values, axes, 0, 0, tiled=True)
         return values
 
     def widened(values):
-        return values.astype(F32).reshape(rows, LANES)
+        return values.astype(F32).reshape(-1, LANES)
 
     hat, sent = lax.optimization_barrier((kernel_hat, sent))
     got = exchanged(sent)
@@ -651,11 +642,11 @@
         name="near_field",
     )(live_count, *pool, pool_index.T, near_block.T, near_blocks.reshape(PANELS, KN * PANELS))
 
-    back = pl.pallas_call(
+    back, exponent = pl.pallas_call(
         functools.partial(plane_kernel, slabs, planes),
-        out_shape=shape_of(rows, LANES),
+        out_shape=(shape_of(owners * 4 * parts, LANES), shape_of(8, LANES)),
         in_specs=[VMEM] * 4,
-        out_specs=VMEM,
+        out_specs=(VMEM, VMEM),
         scratch_shapes=[pltpu.VMEM((2 * planes * length, NY), BF16)] * 2,
         compiler_params=PARAMS,
         name="plane_filter",
@@ -665,11 +656,11 @@
     pot = pl.pallas_call(
         functools.partial(potential_kernel, owners),
         out_shape=(grid,) * 4 + (shape_of(LANES, LANES, dtype=BF16),),
-        in_specs=[VMEM] * 2,
+        in_specs=[VMEM] * 3,
         out_specs=(VMEM,) * 5,
         compiler_params=PARAMS,
         name="z_inverse",
-    )(widened(back), jnp.asarray(halves(inverse)))
+    )(widened(back), exponent, jnp.asarray(halves(inverse)))
     edge = to_other_tile(pot[4])
 
     def sample_scratch(width):
@@ -690,12 +681,12 @@
     own = pl.pallas_call(
         own_sample_kernel,
         out_shape=sums,
-        in_specs=[SMEM] * 2 + [VMEM] * 7,
+        in_specs=[SMEM] + [VMEM] * 7,
         out_specs=VMEM,
         scratch_shapes=sample_scratch(slots),
         compiler_params=PARAMS,
         name="own_sample",
-    )(slot_brick, live_count, *pot[:4], edge, kinds, stk)
+    )(facts, *pot[:4], edge, facts, stk)
     return own + near + first + second
 
 

time: 87.8 us -> 85.7 us (0.976)
  waiting for transfers between devices: 41.8 us -> 38.6 us
  local copies, waits for them, and re-layouts: 4.28 us -> 1.48 us
  Pallas kernels: 20.7 us -> 22.7 us
  other arithmetic: 2.71 us -> 4.28 us
    unnamed x32 -> x20, local copies, waits for them, and re-layouts: 4.08 us -> 1.28 us
    ppermute x7, waiting for transfers between devices: 9.41 us -> 7.63 us  [moved(): return lax.ppermute(values, both, pairs)]
    all_to_all x2, waiting for transfers between devices: 32.4 us -> 31 us  [exchanged(): values = lax.all_to_all(values, axes, 0, 0, tiled=True)]
    select_n x0 -> x1, other arithmetic: none -> 0.88 us  [body(): packed = jnp.where(row < PANELS, held, facts.astype(BF16))]
    pallas_call x2 -> x1, Pallas kernels: 1.96 us -> 2.56 us  [body(): pl.pallas_call(own_sample_kernel, out_shape=sums, in_specs=[SMEM] + [VMEM...]
  transfers between devices with their start and end apart: 9 -> 9, of which waited for: 7 -> 6; matrix products, arithmetic and copies ran while one was open for 0% -> 0% of each run, Pallas kernels for 8% -> 10%
where the time goes in v6:
time: 85.7 us; the launch traced here: 85.4 us
  waiting for transfers between devices  38.6 us (45%)
  Pallas kernels  22.7 us (26%)
  starting transfers between devices  17.4 us (20%)
  other arithmetic  4.28 us (5%)
  local copies, waits for them, and re-layouts  1.48 us (2%)
  between operations  0.94 us (1%)
    all_to_all x2, waiting for transfers between devices, exchanged(): values = lax.all_to_all(values, axes, 0, 0, tiled=True)  31 us
    ppermute x7, starting transfers between devices, moved(): return lax.ppermute(values, both, pairs)  10.7 us
    ppermute x7, waiting for transfers between devices, moved(): return lax.ppermute(values, both, pairs)  7.63 us
    all_to_all x2, starting transfers between devices, exchanged(): values = lax.all_to_all(values, axes, 0, 0, tiled=True)  6.77 us
    pallas_call x1, Pallas kernels, body(): pl.pallas_call(functools.partial(plane_kernel, slabs, planes), out_shape=...  4.24 us
    pallas_call x1, Pallas kernels, body(): pl.pallas_call(own_kernel, out_shape=(grid,) * 5 + (shape_of(KS * PANELS,...  3.36 us
    pallas_call x1, Pallas kernels, body(): pl.pallas_call(beside_kernel, out_shape=(grid,) * 5 + (shape_of(LANES, LA...  3.06 us
    pallas_call x1, Pallas kernels, body(): pl.pallas_call(beside_sample_kernel, out_shape=(sums, sums), in_specs=[SM...  2.8 us
  transfers between devices with their start and end apart: 9, of which 6 were waited for; matrix products, arithmetic and copies ran while one was open for 0% of the time, Pallas kernels for 10%

profile of v6, /device:TPU:0, one launch (start us, length us, event | category | flops | bytes accessed | tf_op | source)
XLA Modules:
  0.0 85.4 jit_solution(1053500981212577069)
XLA Ops:
  0.7 0.7 broadcast_shift-right-logical_fusion
  1.4 0.9 %fusion.packed_ref.own_ref = bf16[80,256]{1,0:T(8,128)(2,1)S(1)} fusion(s32[256]{0:T(256)S(1)} %get-tuple-element.64, s32[256]{0:T(256)S(1)} %get-tuple-element.63, s32[]{:T(128)} %bitcast.16, s32[256]{0:T(256)} %param.17, bf16[64,256]{1,0:T(8,128)(2,1)} %param.14, pred[80]{0:T(512)(128)(4,1)S(1)} %get-tuple-element.65, ...), kind=kLoop, calls=%fused_computation.4 | loop fusion | flops 122880 | bytes 77380 | tf_op jit(solution)/shard_map/jit(_where)/select_n | solution.py:558
  2.3 3.0 %collective-permute-start = (bf16[80,256]{1,0:T(8,128)(2,1)S(1)}, bf16[80,256]{1,0:T(8,128)(2,1)S(1)}, u32[]{:S(2)}, u32[]{:S(2)}) collective-permute-start(bf16[80,256]{1,0:T(8,128)(2,1)S(1)} %fusion.packed_ref.own_ref), channel_id=1, source_target_pairs={{0,2},{1,3},{2,0},{3,1},{4,6},{5,7},{6,4},{7,5},{8,10},{9,11},{10,... | collective-permute-start | bytes 122888 | tf_op jit(solution)/shard_map/ppermute | solution.py:539
  5.3 4.5 %collective-permute-start.1 = (bf16[80,256]{1,0:T(8,128)(2,1)S(1)}, bf16[80,256]{1,0:T(8,128)(2,1)S(1)}, u32[]{:S(2)}, u32[]{:S(2)}) collective-permute-start(bf16[80,256]{1,0:T(8,128)(2,1)S(1)} %fusion.packed_ref.own_ref), channel_id=1, source_target_pairs={{0,30},{1,31},{2,4},{3,5},{4,2},{5,3},{6,8},{7,9},{8,6},{9,7},{10,... | collective-permute-start | bytes 122888 | tf_op jit(solution)/shard_map/ppermute | solution.py:539
  9.8 1.2 %copy-done.1 = bf16[16,64,512]{2,1,0:T(8,128)(2,1)S(1)} copy-done((bf16[16,64,512]{2,1,0:T(8,128)(2,1)S(1)}, bf16[16,64,512]{2,1,0:T(8,128)(2,1)}, u32[]{:S(2)}) %copy-start.1) | copy-done | bytes 1048600
  11.0 3.4 %own_scatter.1 = (f32[520,128]{1,0:T(8,128)S(1)}, f32[520,128]{1,0:T(8,128)S(1)}, f32[520,128]{1,0:T(8,128)S(1)}, f32[520,128]{1,0:T(8,128)S(1)}, f32[520,128]{1...) custom-call(bf16[80,256]{1,0:T(8,128)(2,1)S(1)} %fusion.packed_ref.own_ref, ...), custom_call_target="tpu_custom_call" | custom-call | tf_op jit(solution)/shard_map/own_scatter/pallas_call | solution.py:563
  14.4 0.0 collective-permute-done.first_ref
  14.4 0.0 collective-permute-done.1.second_ref
  14.4 0.0 copy-start
  14.4 3.1 %beside_scatter.1 = (f32[520,128]{1,0:T(8,128)S(1)}, f32[520,128]{1,0:T(8,128)S(1)}, f32[520,128]{1,0:T(8,128)S(1)}, f32[520,128]{1,0:T(8,128)S(1)}, f32[520,128...) custom-call(s32[1]{0:T(128)} %bitcast.2.odd_ref, ...), custom_call_target="tpu_custom_call", output_to_operand_aliasing={{0}: (5, {}), {1}: (6, {}), {2}: (7, {}), {3}: (8, {}), {4}... | custom-call | tf_op jit(solution)/shard_map/beside_scatter/pallas_call | solution.py:578
  17.5 0.8 collective-permute-start.2
  18.3 0.9 %collective-permute-done.2.edge_ref = f32[128,128]{1,0:T(8,128)S(1)} collective-permute-done((f32[128,128]{1,0:T(8,128)S(1)}, f32[128,128]{1,0:T(8,128)S(1)}, u32[]{:S(2)}, u32[]{:S(2)}) %collective-permute-start.2) | collective-permute-done | bytes 65568 | tf_op jit(solution)/shard_map/ppermute | solution.py:539
  19.2 0.0 copy-done
  19.2 2.2 %z_forward.1 = f32[2304,128]{1,0:T(8,128)S(1)} custom-call(f32[520,128]{1,0:T(8,128)S(1)} %get-tuple-element.41.g0, f32[520,128]{1,0:T(8,128)S(1)} %get-tuple-element.42.g1, f32[520,128]{1,0:T(8,128)S(1)} %get-tuple-element.43.g2, f32[520,128]{1,0:T(8,128)S(1)} %get-tuple-element.44.g3, f32[128,128]{1,0:T(8,128)S(1)} %collective-permute-done.2.edge_ref, ...), custom_call_target="tpu_custom_call" | custom-call | tf_op jit(solution)/shard_map/z_forward/pallas_call | solution.py:602
  21.4 0.0 copy-start.2
  21.4 0.0 copy-start.6
  21.4 0.9 %convert_element_type.18 = f16[2304,128]{1,0:T(8,128)(2,1)} convert(f32[2304,128]{1,0:T(8,128)S(1)} %z_forward.1) | non-fusion elementwise | flops 294912 | bytes 1769472 | tf_op jit(solution)/shard_map/convert_element_type | solution.py:612
  22.3 4.2 %all-to-all-start = ((f16[32,72,128]{2,1,0:T(8,128)(2,1)}), f16[32,72,128]{2,1,0:T(8,128)(2,1)S(1)}, u32[]{:S(2)}, u32[]{:S(2)}) async-start(f16[32,72,128]{2,1,0:T(8,128)(2,1)} %bitcast.19), calls=%async_computation | async-start | bytes 1179648 | tf_op jit(solution)/shard_map/all_to_all | solution.py:613
  26.5 0.3 hat_order.1.hat_ref
  26.8 0.0 copy-start.4
  26.8 0.0 copy-start.5
  26.8 17.9 %all-to-all-done = f16[32,72,128]{2,1,0:T(8,128)(2,1)S(1)} async-done(((f16[32,72,128]{2,1,0:T(8,128)(2,1)}), f16[32,72,128]{2,1,0:T(8,128)(2,1)S(1)}, u32[]{:S(2)}, u32[]{:S(2)}) %all-to-all-start) | async-done | bytes 589856 | tf_op jit(solution)/shard_map/all_to_all | solution.py:613
  44.7 0.1 bitcast_convert_fusion.in_ref
  44.8 4.2 %plane_filter.1 = (f32[2048,128]{1,0:T(8,128)S(1)}, f32[8,128]{1,0:T(8,128)S(1)}) custom-call(f32[2304,128]{1,0:T(8,128)S(1)} %bitcast_convert_fusion.in_ref, f32[8,64,256]{2,1,0:T(8,128)S(1)} %hat_order.1.hat_ref, bf16[1024,256]{1,0:T(8,128)(2,1)S(1)} %copy-done.4, bf16[512,128]{1,0:T(8,128)(2,1)S(1)} %copy-done.5), custom_call_target="tpu_custom_call" | custom-call | tf_op jit(solution)/shard_map/plane_filter/pallas_call | solution.py:645
  49.1 0.0 copy-start.8
  49.1 0.0 copy-start.9
  49.1 0.0 copy-start.7
  49.1 0.9 %convert_element_type.19 = f16[2048,128]{1,0:T(8,128)(2,1)} convert(f32[2048,128]{1,0:T(8,128)S(1)} %get-tuple-element.50) | non-fusion elementwise | flops 262144 | bytes 1572864 | tf_op jit(solution)/shard_map/convert_element_type | solution.py:612
  50.0 2.6 %all-to-all-start.1 = ((f16[32,64,128]{2,1,0:T(8,128)(2,1)}), f16[32,64,128]{2,1,0:T(8,128)(2,1)S(1)}, u32[]{:S(2)}, u32[]{:S(2)}) async-start(f16[32,64,128]{2,1,0:T(8,128)(2,1)} %bitcast.6), calls=%async_computation.1 | async-start | bytes 1048576 | tf_op jit(solution)/shard_map/all_to_all | solution.py:613
  52.6 0.0 copy-start.3
  52.6 0.2 reshape.29.table_ref
  52.8 0.2 collective-permute-start.3
  53.1 1.2 %collective-permute-done.3.there_ref = bf16[240,256]{1,0:T(8,128)(2,1)S(1)} collective-permute-done((bf16[240,256]{1,0:T(8,128)(2,1)S(1)}, bf16[240,256]{1,0:T(8,128)(2,1)S(1)}, u32[]{:S(2)}, u32[]{:S(2)}) %collective-permute-start.3) | collective-permute-done | bytes 122912 | tf_op jit(solution)/shard_map/ppermute | solution.py:539
  54.2 0.0 copy-done.7
  54.3 2.1 %near_field.1 = f32[64,256]{1,0:T(8,128)S(1)} custom-call(s32[1]{0:T(128)} %copy.25.live_ref, bf16[240,256]{1,0:T(8,128)(2,1)S(1)} %get-tuple-element.51.here_ref, bf16[240,256]{1,0:T(8,128)(2,1)S(1)} %collective-permute-done.3.there_ref, s32[8,256]{1,0:T(8,128)S(1)} %fusion.5.source_ref, s32[8,256]{1,0:T(8,128)S(1)} %bitcast.18, ...), custom_call_target="tpu_custom_call" | custom-call | tf_op jit(solution)/shard_map/near_field/pallas_call | solution.py:636
  56.4 13.1 %all-to-all-done.1 = f16[32,64,128]{2,1,0:T(8,128)(2,1)S(1)} async-done(((f16[32,64,128]{2,1,0:T(8,128)(2,1)}), f16[32,64,128]{2,1,0:T(8,128)(2,1)S(1)}, u32[]{:S(2)}, u32[]{:S(2)}) %all-to-all-start.1) | async-done | bytes 524320 | tf_op jit(solution)/shard_map/all_to_all | solution.py:613
  69.5 0.1 bitcast_convert_fusion.1.in_ref
  69.6 0.0 copy-done.3
  69.6 2.1 %z_inverse.1 = (f32[520,128]{1,0:T(8,128)S(1)}, f32[520,128]{1,0:T(8,128)S(1)}, f32[520,128]{1,0:T(8,128)S(1)}, f32[520,128]{1,0:T(8,128)S(1)}, bf16[128,128]{1,0:T(8,128)(2,1)S(1)}) custom-call(f32[2048,128]{1,0:T(8,128)S(1)} %bitcast_convert_fusion.1.in_ref, f32[8,128]{1,0:T(8,128)S(1)} %get-tuple-element.53.exponent_ref, bf16[1024,512]{1,0:T(8,128)(2,1)S(1)} %copy-done.3), custom_call_target="tpu_custom_call" | custom-call | tf_op jit(solution)/shard_map/z_inverse/pallas_call | solution.py:656
  71.7 0.1 collective-permute-start.4
  71.8 1.2 %collective-permute-done.4.edge_ref = bf16[128,128]{1,0:T(8,128)(2,1)S(1)} collective-permute-done((bf16[128,128]{1,0:T(8,128)(2,1)S(1)}, bf16[128,128]{1,0:T(8,128)(2,1)S(1)}, u32[]{:S(2)}, u32[]{:S(2)}) %collective-permute-start.4) | collective-permute-done | bytes 32800 | tf_op jit(solution)/shard_map/ppermute | solution.py:539
  73.0 2.8 %beside_sample.1 = (f32[64,256]{1,0:T(8,128)S(1)}, f32[64,256]{1,0:T(8,128)S(1)}) custom-call(s32[1]{0:T(128)} %bitcast.2.odd_ref, s32[8,512]{1,0:T(8,128)S(1)} %get-tuple-element.60.facts_ref.kinds_ref, f32[520,128]{1,0:T(8,128)S(1)} %get-tuple-element.54.p0, f32[520,128]{1,0:T(8,128)S(1)} %get-tuple-element.55.p1, f32[520,128]{1,0:T(8,128)S(1)} %get-tuple-element.56.p2, ...), custom_call_target="tpu_custom_call" | custom-call | tf_op jit(solution)/shard_map/beside_sample/pallas_call | solution.py:670
  75.8 1.1 %collective-permute-start.5 = (f32[64,256]{1,0:T(8,128)S(1)}, f32[64,256]{1,0:T(8,128)S(1)}, u32[]{:S(2)}, u32[]{:S(2)}) collective-permute-start(f32[64,256]{1,0:T(8,128)S(1)} %get-tuple-element.61), channel_id=1, source_target_pairs={{0,2},{1,3},{2,0},{3,1},{4,6},{5,7},{6,4},{7,5},{8,10},{9,11},{10,... | collective-permute-start | bytes 196616 | tf_op jit(solution)/shard_map/ppermute | solution.py:539
  76.9 1.0 %collective-permute-start.6 = (f32[64,256]{1,0:T(8,128)S(1)}, f32[64,256]{1,0:T(8,128)S(1)}, u32[]{:S(2)}, u32[]{:S(2)}) collective-permute-start(f32[64,256]{1,0:T(8,128)S(1)} %get-tuple-element.62), channel_id=1, source_target_pairs={{0,30},{1,31},{2,4},{3,5},{4,2},{5,3},{6,8},{7,9},{8,6},{9,7},{10,... | collective-permute-start | bytes 196616 | tf_op jit(solution)/shard_map/ppermute | solution.py:539
  77.9 2.6 %own_sample.1 = f32[64,256]{1,0:T(8,128)S(1)} custom-call(s32[8,256]{1,0:T(8,128)S(1)} %get-tuple-element.34.facts_ref.kinds_ref, f32[520,128]{1,0:T(8,128)S(1)} %get-tuple-element.54.p0, f32[520,128]{1,0:T(8,128)S(1)} %get-tuple-element.55.p1, f32[520,128]{1,0:T(8,128)S(1)} %get-tuple-element.56.p2, f32[520,128]{1,0:T(8,128)S(1)} %get-tuple-element.57.p3, ...), custom_call_target="tpu_custom_call" | custom-call | tf_op jit(solution)/shard_map/own_sample/pallas_call | solution.py:681
  80.5 0.0 collective-permute-done.5
  80.5 4.3 %collective-permute-done.6 = f32[64,256]{1,0:T(8,128)S(1)} collective-permute-done((f32[64,256]{1,0:T(8,128)S(1)}, f32[64,256]{1,0:T(8,128)S(1)}, u32[]{:S(2)}, u32[]{:S(2)}) %collective-permute-start.6) | collective-permute-done | bytes 65568 | tf_op jit(solution)/shard_map/ppermute | solution.py:539
  84.8 0.6 add_add_fusion
  (11 shorter events, 0.1 us)
Async XLA Ops:
  2.3 12.1 %collective-permute-start = (bf16[80,256]{1,0:T(8,128)(2,1)S(1)}, bf16[80,256]{1,0:T(8,128)(2,1)S(1)}, u32[]{:S(2)}, u32[]{:S(2)}) collective-permute-start(bf16[80,256]{1,0:T(8,128)(2,1)S(1)} %fusion.packed_ref.own_ref), channel_id=1, source_target_pairs={{0,2},{1,3},{2,0},{3,1},{4,6},{5,7},{6,4},{7,5},{8,10},{9,11},{10,... | collective-permute-start | bytes 122888 | tf_op jit(solution)/shard_map/ppermute | solution.py:539
  5.3 9.1 %collective-permute-start.1 = (bf16[80,256]{1,0:T(8,128)(2,1)S(1)}, bf16[80,256]{1,0:T(8,128)(2,1)S(1)}, u32[]{:S(2)}, u32[]{:S(2)}) collective-permute-start(bf16[80,256]{1,0:T(8,128)(2,1)S(1)} %fusion.packed_ref.own_ref), channel_id=1, source_target_pairs={{0,30},{1,31},{2,4},{3,5},{4,2},{5,3},{6,8},{7,9},{8,6},{9,7},{10,... | collective-permute-start | bytes 122888 | tf_op jit(solution)/shard_map/ppermute | solution.py:539
  9.8 1.2 %copy-start.1 = (bf16[16,64,512]{2,1,0:T(8,128)(2,1)S(1)}, bf16[16,64,512]{2,1,0:T(8,128)(2,1)}, u32[]{:S(2)}) copy-start(bf16[16,64,512]{2,1,0:T(8,128)(2,1)} %param.18) | copy-start | bytes 3145732
  14.4 4.8 %copy-start = (bf16[1024,512]{1,0:T(8,128)(2,1)S(1)}, bf16[1024,512]{1,0:T(8,128)(2,1)}, u32[]{:S(2)}) copy-start(bf16[1024,512]{1,0:T(8,128)(2,1)} %constant.88.clone.w_ref) | copy-start | bytes 3145732
  17.5 1.7 %collective-permute-start.2 = (f32[128,128]{1,0:T(8,128)S(1)}, f32[128,128]{1,0:T(8,128)S(1)}, u32[]{:S(2)}, u32[]{:S(2)}) collective-permute-start(f32[128,128]{1,0:T(8,128)S(1)} %get-tuple-element.45), channel_id=1, source_target_pairs={{0,1},{1,0},{2,3},{3,2},{4,5},{5,4},{6,7},{7,6},{8,9},{9,8},{10,11... | collective-permute-start | bytes 196616 | tf_op jit(solution)/shard_map/ppermute | solution.py:539
  21.4 5.1 %copy-start.2 = (f32[16,64,256]{2,1,0:T(8,128)S(1)}, f32[16,64,256]{2,1,0:T(8,128)}, u32[]{:S(2)}) copy-start(f32[16,64,256]{2,1,0:T(8,128)} %hat_ref) | copy-start | bytes 3145732
  21.4 5.1 %copy-start.6 = (bf16[128,128]{1,0:T(8,128)(2,1)S(1)}, bf16[128,128]{1,0:T(8,128)(2,1)}, u32[]{:S(2)}) copy-start(bf16[128,128]{1,0:T(8,128)(2,1)} %constant.89.clone.turn_ref) | copy-start | bytes 98308
  22.3 22.4 %all-to-all-start = ((f16[32,72,128]{2,1,0:T(8,128)(2,1)}), f16[32,72,128]{2,1,0:T(8,128)(2,1)S(1)}, u32[]{:S(2)}, u32[]{:S(2)}) async-start(f16[32,72,128]{2,1,0:T(8,128)(2,1)} %bitcast.19), calls=%async_computation | async-start | bytes 1179648 | tf_op jit(solution)/shard_map/all_to_all | solution.py:613
  26.8 18.1 %copy-start.4 = (bf16[1024,256]{1,0:T(8,128)(2,1)S(1)}, bf16[1024,256]{1,0:T(8,128)(2,1)}, u32[]{:S(2)}) copy-start(bf16[1024,256]{1,0:T(8,128)(2,1)} %constant.90.clone.y_ref) | copy-start | bytes 1572868
  26.8 18.1 %copy-start.5 = (bf16[512,128]{1,0:T(8,128)(2,1)S(1)}, bf16[512,128]{1,0:T(8,128)(2,1)}, u32[]{:S(2)}) copy-start(bf16[512,128]{1,0:T(8,128)(2,1)} %constant.91.clone.x_ref) | copy-start | bytes 393220
  49.1 3.5 %copy-start.8 = (bf16[64,16,64]{2,1,0:T(8,128)(2,1)S(1)}, bf16[64,16,64]{2,1,0:T(8,128)(2,1)}, u32[]{:S(2)}) copy-start(bf16[64,16,64]{2,1,0:T(8,128)(2,1)} %param.21) | copy-start | bytes 393220
  49.1 3.9 %copy-start.9 = (s32[256,8]{0,1:T(8,128)S(1)}, s32[256,8]{0,1:T(8,128)}, u32[]{:S(2)}) copy-start(s32[256,8]{0,1:T(8,128)} %param.19) | copy-start | bytes 24580
  49.1 5.1 %copy-start.7 = (s32[256,8]{0,1:T(8,128)S(1)}, s32[256,8]{0,1:T(8,128)}, u32[]{:S(2)}) copy-start(s32[256,8]{0,1:T(8,128)} %param.20) | copy-start | bytes 24580
  50.0 19.4 %all-to-all-start.1 = ((f16[32,64,128]{2,1,0:T(8,128)(2,1)}), f16[32,64,128]{2,1,0:T(8,128)(2,1)S(1)}, u32[]{:S(2)}, u32[]{:S(2)}) async-start(f16[32,64,128]{2,1,0:T(8,128)(2,1)} %bitcast.6), calls=%async_computation.1 | async-start | bytes 1048576 | tf_op jit(solution)/shard_map/all_to_all | solution.py:613
  52.6 16.9 %copy-start.3 = (bf16[1024,512]{1,0:T(8,128)(2,1)S(1)}, bf16[1024,512]{1,0:T(8,128)(2,1)}, u32[]{:S(2)}) copy-start(bf16[1024,512]{1,0:T(8,128)(2,1)} %constant.92.clone.v_ref) | copy-start | bytes 3145732
  52.8 1.4 %collective-permute-start.3 = (bf16[240,256]{1,0:T(8,128)(2,1)S(1)}, bf16[240,256]{1,0:T(8,128)(2,1)S(1)}, u32[]{:S(2)}, u32[]{:S(2)}) collective-permute-start(bf16[240,256]{1,0:T(8,128)(2,1)S(1)} %get-tuple-element.51.here_ref), channel_id=1, source_target_pairs={{0,1},{1,0},{2,3},{3,2},{4,5},{5,4},{6,7},{7,6},{8,9},{9,8},{10,11... | collective-permute-start | bytes 368648 | tf_op jit(solution)/shard_map/ppermute | solution.py:539
  71.7 1.3 %collective-permute-start.4 = (bf16[128,128]{1,0:T(8,128)(2,1)S(1)}, bf16[128,128]{1,0:T(8,128)(2,1)S(1)}, u32[]{:S(2)}, u32[]{:S(2)}) collective-permute-start(bf16[128,128]{1,0:T(8,128)(2,1)S(1)} %get-tuple-element.58), channel_id=1, source_target_pairs={{0,1},{1,0},{2,3},{3,2},{4,5},{5,4},{6,7},{7,6},{8,9},{9,8},{10,11... | collective-permute-start | bytes 98312 | tf_op jit(solution)/shard_map/ppermute | solution.py:539
  75.8 4.7 %collective-permute-start.5 = (f32[64,256]{1,0:T(8,128)S(1)}, f32[64,256]{1,0:T(8,128)S(1)}, u32[]{:S(2)}, u32[]{:S(2)}) collective-permute-start(f32[64,256]{1,0:T(8,128)S(1)} %get-tuple-element.61), channel_id=1, source_target_pairs={{0,2},{1,3},{2,0},{3,1},{4,6},{5,7},{6,4},{7,5},{8,10},{9,11},{10,... | collective-permute-start | bytes 196616 | tf_op jit(solution)/shard_map/ppermute | solution.py:539
  76.9 7.9 %collective-permute-start.6 = (f32[64,256]{1,0:T(8,128)S(1)}, f32[64,256]{1,0:T(8,128)S(1)}, u32[]{:S(2)}, u32[]{:S(2)}) collective-permute-start(f32[64,256]{1,0:T(8,128)S(1)} %get-tuple-element.62), channel_id=1, source_target_pairs={{0,30},{1,31},{2,4},{3,5},{4,2},{5,3},{6,8},{7,9},{8,6},{9,7},{10,... | collective-permute-start | bytes 196616 | tf_op jit(solution)/shard_map/ppermute | solution.py:539

commit v7 on v6

--- a/solution.py
+++ b/solution.py
@@ -117,10 +117,26 @@
         fp_ref[pl.ds(first * 8 + 2 * pair + 1, count, stride=8), :] = pltpu.roll(part, 64, 1)
 
 
+def lane_in(plane, shape):
+    return (lane_of(shape) - 8 * plane) & (LANES - 1)
+
+
+def edge_codes(planes, shape):
+    code = jnp.full(shape, 3, jnp.int32)
+    for plane in planes:
+        lane = lane_in(plane, shape)
+        code = jnp.where(lane >= LANES - 2, 0, jnp.where(lane < 2, 1, code))
+    return code
+
+
+def edge_of(by):
+    return jnp.where(by == 0, 0, jnp.where(by == NY // 8 - 1, 1, 2))
+
+
 def scatter_columns(fp_ref, first, place_of, count, grids, edge_ref, planes, shift_i):
-    lane = lane_of((8, LANES))
-    in_planes = (lane >= 8 * planes[0]) & (lane < 8 * (planes[-1] + 1))
-    point_j = lane & 7
+    shape = (8, LANES)
+    lanes = [lane_in(plane, shape) for plane in planes]
+    codes = edge_codes(planes, shape)
 
     def step(index, carry):
         updates = []
@@ -129,16 +145,9 @@
             by, bz = place_of(column)
             value = fp_ref[pl.ds(pl.multiple_of((first + column) * 8, 8), 8), :]
             begin = 4 * by - 2
-            mask = ((lane - begin) & -8) == 0
-            terms = []
-            for plane in planes:
-                turned = pltpu.roll(value, (begin - 8 * (plane + shift_i)) & (LANES - 1), 1)
-                terms.append(jnp.where(mask, turned, 0.0))
-            is_last = (by == NY // 8 - 1).astype(jnp.int32)
-            low = jnp.where(by == 0, 0, jnp.where(by == NY // 8 - 1, 2, 8))
-            turned = pltpu.roll(value, (-8 * shift_i - 4 * is_last) & (LANES - 1), 1)
-            mask = in_planes & (((point_j - low) & -2) == 0)
-            terms.append(jnp.where(mask, turned, 0.0))
+            turned = pltpu.roll(value, (begin - 8 * shift_i) & (LANES - 1), 1)
+            terms = [jnp.where(((lane - begin) & -8) == 0, turned, 0.0) for lane in lanes]
+            terms.append(jnp.where(codes == edge_of(by), turned, 0.0))
             updates.append((pl.ds(4 * bz, 8), terms))
         refs = [grids[plane] for plane in planes] + [edge_ref]
         for where, terms in updates:
@@ -151,9 +160,9 @@
 
 
 def sample_columns(pot_refs, edge_ref, place_of, count, sp_ref, first, planes, shift_i):
-    lane = lane_of((8, LANES))
-    point_j = lane & 7
-    inside = (lane >= 8 * (planes[0] + shift_i)) & (lane < 8 * (planes[-1] + shift_i + 1))
+    shape = (8, LANES)
+    lanes = [lane_in(plane, shape) for plane in planes]
+    codes = edge_codes(planes, shape)
 
     def step(index, carry):
         results = []
@@ -162,16 +171,11 @@
             by, bz = place_of(column)
             where = pl.ds(4 * bz, 8)
             begin = 4 * by - 2
-            result = jnp.zeros((8, LANES), F32)
-            for plane in planes:
-                low = 8 * (plane + shift_i)
-                turned = pltpu.roll(pot_refs[plane][where, :], (low - begin) & (LANES - 1), 1)
-                result = jnp.where(((lane - low) & -8) == 0, turned, result)
-            is_last = (by == NY // 8 - 1).astype(jnp.int32)
-            low = jnp.where(by == 0, 0, jnp.where(by == NY // 8 - 1, 6, 8))
-            turned = pltpu.roll(edge_ref[where, :], (8 * shift_i + 4 * is_last) & (LANES - 1), 1)
-            mask = inside & (((point_j - low) & -2) == 0)
-            results.append((pl.ds(pl.multiple_of((first + column) * 8, 8), 8), jnp.where(mask, turned, result)))
+            result = jnp.where(codes == edge_of(by), edge_ref[where, :], 0.0)
+            for plane, lane in zip(planes, lanes):
+                result = jnp.where(((lane - begin) & -8) == 0, pot_refs[plane][where, :], result)
+            turned = pltpu.roll(result, (8 * shift_i - begin) & (LANES - 1), 1)
+            results.append((pl.ds(pl.multiple_of((first + column) * 8, 8), 8), turned))
         for where, result in results:
             sp_ref[where, :] = result
         return carry
@@ -289,9 +293,9 @@
             scatter_columns(fp_ref, 2 * first + side * LANES, place_in_facts(facts_ref, side * slots + first),
                             counts[side], (g0, g1, g2, g3), edge_ref, planes, shift_i)
     edge_ref[0:8, :] += edge_ref[NZ:ZROWS, :]
-    total = edge_ref[0:LANES, :]
+    total = pltpu.roll(edge_ref[0:LANES, :], 2, 1)
     for block in range(1, 4):
-        total += pltpu.roll(edge_ref[block * LANES : (block + 1) * LANES, :], 32 * block, 1)
+        total += pltpu.roll(edge_ref[block * LANES : (block + 1) * LANES, :], 32 * block + 2, 1)
     out_edge[...] = total
 
 
@@ -302,21 +306,22 @@
 
 
 def z_kernel(owners, g0, g1, g2, g3, edge_ref, w_ref, out_ref):
-    lane = lane_of((LANES, LANES))
-    at_edge = (lane < 2) | (lane >= LANES - 2)
+    shape = (LANES, LANES)
     parts = NZ // owners
     stride = 4 * parts + SCALE_ROWS
+    edges = [pltpu.roll(edge_ref[...], (LANES - 2 - 32 * block) % LANES, 1) for block in range(4)]
     results = []
     for plane, grid in enumerate((g0, g1, g2, g3)):
-        blocks = []
-        for block in range(4):
-            turned = pltpu.roll(edge_ref[...], (LANES - 2 - 32 * block - 8 * plane) % LANES, 1)
-            blocks.append(
-                grid[block * LANES : (block + 1) * LANES, :] + jnp.where(at_edge, turned, 0.0)
-            )
+        at_edge = edge_codes((plane,), shape) < 2
+        blocks = [
+            grid[block * LANES : (block + 1) * LANES, :] + jnp.where(at_edge, edges[block], 0.0)
+            for block in range(4)
+        ]
         blocks[0] = jnp.concatenate([blocks[0][0:8] + grid[NZ:ZROWS, :], blocks[0][8:]], axis=0)
-        values = split(jnp.concatenate(blocks, axis=0))
-        results.append(dot3((w_ref[0:NZ, :], w_ref[NZ : 2 * NZ, :]), values))
+        values = jnp.concatenate(blocks, axis=0)
+        if plane:
+            values = pltpu.roll(values, LANES - 8 * plane, 1)
+        results.append(dot3((w_ref[0:NZ, :], w_ref[NZ : 2 * NZ, :]), split(values)))
     exponent = exponent_of(results)
     scale = jnp.exp2(-exponent)
     for plane, result in enumerate(results):
@@ -414,8 +419,8 @@
 
 def potential_kernel(owners, in_ref, exponent_ref, v_ref, p0, p1, p2, p3, edge_ref):
     parts = NZ // owners
-    lane = lane_of((LANES, LANES))
-    edge = jnp.zeros((LANES, LANES), F32)
+    shape = (LANES, LANES)
+    edges = [jnp.zeros(shape, F32)] * 4
     scale = jnp.exp2(exponent_ref[0:1, 0:1])
     for plane, pot in enumerate((p0, p1, p2, p3)):
         values = split(jnp.concatenate(
@@ -424,19 +429,25 @@
         ))
         result = dot3((v_ref[0:NZ, :], v_ref[NZ : 2 * NZ, :]), values) * scale
         result = result.astype(BF16).astype(F32)
+        if plane:
+            result = pltpu.roll(result, 8 * plane, 1)
         pot[0:NZ, :] = result
         pot[NZ:ZROWS, :] = result[0:8, :]
-        for block in range(4):
-            low = 32 * block + 8 * plane
-            turned = pltpu.roll(result[block * LANES : (block + 1) * LANES, :], low + 2, 1)
-            edge = jnp.where((lane >= low) & (lane < low + 4), turned, edge)
+        at_edge = edge_codes((plane,), shape) < 2
+        edges = [
+            jnp.where(at_edge, result[block * LANES : (block + 1) * LANES, :], edge)
+            for block, edge in enumerate(edges)
+        ]
+    edge = pltpu.roll(edges[0], 2, 1)
+    for block in range(1, 4):
+        edge += pltpu.roll(edges[block], 32 * block + 2, 1)
     edge_ref[...] = edge.astype(BF16)
 
 
 def widen_edge(edge_ref, wide_ref):
     for block in range(4):
         wide_ref[block * LANES : (block + 1) * LANES, :] = pltpu.roll(
-            edge_ref[...].astype(F32), (LANES - 32 * block) % LANES, 1
+            edge_ref[...].astype(F32), (LANES - 2 - 32 * block) % LANES, 1
         )
     wide_ref[NZ:ZROWS, :] = wide_ref[0:8, :]
 

time: 85.7 us -> 85.3 us (level)
  starting transfers between devices: 17.4 us -> 15.6 us
  waiting for transfers between devices: 38.6 us -> 39.7 us
    all_to_all x2, starting transfers between devices: 6.77 us -> 5.21 us  [exchanged(): values = lax.all_to_all(values, axes, 0, 0, tiled=True)]
    ppermute x7, waiting for transfers between devices: 7.63 us -> 8.72 us  [moved(): return lax.ppermute(values, both, pairs)]
    pallas_call x1, Pallas kernels: 2.56 us -> 1.6 us  [body(): pl.pallas_call(own_sample_kernel, out_shape=sums, in_specs=[SMEM] + [VMEM...]
    pallas_call x1, Pallas kernels: 3.36 us -> 2.48 us  [body(): pl.pallas_call(own_kernel, out_shape=(grid,) * 5 + (shape_of(KS * PANELS,...]
  transfers between devices with their start and end apart: 9 -> 9, of which waited for: 6 -> 7; matrix products, arithmetic and copies ran while one was open for 0% -> 0% of each run, Pallas kernels for 10% -> 8%
where the time goes in v7:
time: 85.3 us; the launch traced here: 84.4 us
  waiting for transfers between devices  39.7 us (47%)
  Pallas kernels  22.5 us (26%)
  starting transfers between devices  15.6 us (18%)
  other arithmetic  4.28 us (5%)
  local copies, waits for them, and re-layouts  1.48 us (2%)
  between operations  0.94 us (1%)
    all_to_all x2, waiting for transfers between devices, exchanged(): values = lax.all_to_all(values, axes, 0, 0, tiled=True)  31 us
    ppermute x7, starting transfers between devices, moved(): return lax.ppermute(values, both, pairs)  10.4 us
    ppermute x7, waiting for transfers between devices, moved(): return lax.ppermute(values, both, pairs)  8.72 us
    all_to_all x2, starting transfers between devices, exchanged(): values = lax.all_to_all(values, axes, 0, 0, tiled=True)  5.21 us
    pallas_call x1, Pallas kernels, body(): pl.pallas_call(functools.partial(plane_kernel, slabs, planes), out_shape=...  4.23 us
    pallas_call x1, Pallas kernels, body(): pl.pallas_call(beside_kernel, out_shape=(grid,) * 5 + (shape_of(LANES, LA...  3.82 us
    pallas_call x1, Pallas kernels, body(): pl.pallas_call(beside_sample_kernel, out_shape=(sums, sums), in_specs=[SM...  3.5 us
    pallas_call x1, Pallas kernels, body(): pl.pallas_call(own_kernel, out_shape=(grid,) * 5 + (shape_of(KS * PANELS,...  2.48 us
  transfers between devices with their start and end apart: 9, of which 7 were waited for; matrix products, arithmetic and copies ran while one was open for 0% of the time, Pallas kernels for 8%

profile of v7, /device:TPU:0, one launch (start us, length us, event | category | flops | bytes accessed | tf_op | source)
XLA Modules:
  0.0 84.4 jit_solution(8621060458514855115)
XLA Ops:
  0.7 0.7 broadcast_shift-right-logical_fusion
  1.4 0.9 %fusion.packed_ref.own_ref = bf16[80,256]{1,0:T(8,128)(2,1)S(1)} fusion(s32[256]{0:T(256)S(1)} %get-tuple-element.64, s32[256]{0:T(256)S(1)} %get-tuple-element.63, s32[]{:T(128)} %bitcast.16, s32[256]{0:T(256)} %param.17, bf16[64,256]{1,0:T(8,128)(2,1)} %param.14, pred[80]{0:T(512)(128)(4,1)S(1)} %get-tuple-element.65, ...), kind=kLoop, calls=%fused_computation.4 | loop fusion | flops 122880 | bytes 77380 | tf_op jit(solution)/shard_map/jit(_where)/select_n | solution.py:569
  2.3 3.0 %collective-permute-start = (bf16[80,256]{1,0:T(8,128)(2,1)S(1)}, bf16[80,256]{1,0:T(8,128)(2,1)S(1)}, u32[]{:S(2)}, u32[]{:S(2)}) collective-permute-start(bf16[80,256]{1,0:T(8,128)(2,1)S(1)} %fusion.packed_ref.own_ref), channel_id=1, source_target_pairs={{0,2},{1,3},{2,0},{3,1},{4,6},{5,7},{6,4},{7,5},{8,10},{9,11},{10,... | collective-permute-start | bytes 122888 | tf_op jit(solution)/shard_map/ppermute | solution.py:550
  5.3 4.5 %collective-permute-start.1 = (bf16[80,256]{1,0:T(8,128)(2,1)S(1)}, bf16[80,256]{1,0:T(8,128)(2,1)S(1)}, u32[]{:S(2)}, u32[]{:S(2)}) collective-permute-start(bf16[80,256]{1,0:T(8,128)(2,1)S(1)} %fusion.packed_ref.own_ref), channel_id=1, source_target_pairs={{0,30},{1,31},{2,4},{3,5},{4,2},{5,3},{6,8},{7,9},{8,6},{9,7},{10,... | collective-permute-start | bytes 122888 | tf_op jit(solution)/shard_map/ppermute | solution.py:550
  9.8 1.2 %copy-done.1 = bf16[16,64,512]{2,1,0:T(8,128)(2,1)S(1)} copy-done((bf16[16,64,512]{2,1,0:T(8,128)(2,1)S(1)}, bf16[16,64,512]{2,1,0:T(8,128)(2,1)}, u32[]{:S(2)}) %copy-start.1) | copy-done | bytes 1048600
  11.0 2.5 %own_scatter.1 = (f32[520,128]{1,0:T(8,128)S(1)}, f32[520,128]{1,0:T(8,128)S(1)}, f32[520,128]{1,0:T(8,128)S(1)}, f32[520,128]{1,0:T(8,128)S(1)}, f32[520,128]{1...) custom-call(bf16[80,256]{1,0:T(8,128)(2,1)S(1)} %fusion.packed_ref.own_ref, ...), custom_call_target="tpu_custom_call" | custom-call | tf_op jit(solution)/shard_map/own_scatter/pallas_call | solution.py:574
  13.5 0.0 collective-permute-done.first_ref
  13.5 0.0 collective-permute-done.1.second_ref
  13.5 0.0 copy-start
  13.5 3.8 %beside_scatter.1 = (f32[520,128]{1,0:T(8,128)S(1)}, f32[520,128]{1,0:T(8,128)S(1)}, f32[520,128]{1,0:T(8,128)S(1)}, f32[520,128]{1,0:T(8,128)S(1)}, f32[520,128...) custom-call(s32[1]{0:T(128)} %bitcast.2.odd_ref, ...), custom_call_target="tpu_custom_call", output_to_operand_aliasing={{0}: (5, {}), {1}: (6, {}), {2}: (7, {}), {3}: (8, {}), {4}... | custom-call | tf_op jit(solution)/shard_map/beside_scatter/pallas_call | solution.py:589
  17.4 1.6 %collective-permute-start.2 = (f32[128,128]{1,0:T(8,128)S(1)}, f32[128,128]{1,0:T(8,128)S(1)}, u32[]{:S(2)}, u32[]{:S(2)}) collective-permute-start(f32[128,128]{1,0:T(8,128)S(1)} %get-tuple-element.45), channel_id=1, source_target_pairs={{0,1},{1,0},{2,3},{3,2},{4,5},{5,4},{6,7},{7,6},{8,9},{9,8},{10,11... | collective-permute-start | bytes 196616 | tf_op jit(solution)/shard_map/ppermute | solution.py:550
  19.0 0.9 %collective-permute-done.2.edge_ref = f32[128,128]{1,0:T(8,128)S(1)} collective-permute-done((f32[128,128]{1,0:T(8,128)S(1)}, f32[128,128]{1,0:T(8,128)S(1)}, u32[]{:S(2)}, u32[]{:S(2)}) %collective-permute-start.2) | collective-permute-done | bytes 65568 | tf_op jit(solution)/shard_map/ppermute | solution.py:550
  19.9 0.0 copy-done
  19.9 2.2 %z_forward.1 = f32[2304,128]{1,0:T(8,128)S(1)} custom-call(f32[520,128]{1,0:T(8,128)S(1)} %get-tuple-element.41.g0, f32[520,128]{1,0:T(8,128)S(1)} %get-tuple-element.42.g1, f32[520,128]{1,0:T(8,128)S(1)} %get-tuple-element.43.g2, f32[520,128]{1,0:T(8,128)S(1)} %get-tuple-element.44.g3, f32[128,128]{1,0:T(8,128)S(1)} %collective-permute-done.2.edge_ref, ...), custom_call_target="tpu_custom_call" | custom-call | tf_op jit(solution)/shard_map/z_forward/pallas_call | solution.py:613
  22.1 0.0 copy-start.2
  22.1 0.0 copy-start.6
  22.1 0.9 %convert_element_type.18 = f16[2304,128]{1,0:T(8,128)(2,1)} convert(f32[2304,128]{1,0:T(8,128)S(1)} %z_forward.1) | non-fusion elementwise | flops 294912 | bytes 1769472 | tf_op jit(solution)/shard_map/convert_element_type | solution.py:623
  23.1 2.6 %all-to-all-start = ((f16[32,72,128]{2,1,0:T(8,128)(2,1)}), f16[32,72,128]{2,1,0:T(8,128)(2,1)S(1)}, u32[]{:S(2)}, u32[]{:S(2)}) async-start(f16[32,72,128]{2,1,0:T(8,128)(2,1)} %bitcast.19), calls=%async_computation | async-start | bytes 1179648 | tf_op jit(solution)/shard_map/all_to_all | solution.py:624
  25.7 0.0 copy-done.2
  25.7 0.0 copy-done.6
  25.7 0.3 hat_order.1.hat_ref
  26.0 0.0 copy-start.4
  26.0 0.0 copy-start.5
  26.0 17.9 %all-to-all-done = f16[32,72,128]{2,1,0:T(8,128)(2,1)S(1)} async-done(((f16[32,72,128]{2,1,0:T(8,128)(2,1)}), f16[32,72,128]{2,1,0:T(8,128)(2,1)S(1)}, u32[]{:S(2)}, u32[]{:S(2)}) %all-to-all-start) | async-done | bytes 589856 | tf_op jit(solution)/shard_map/all_to_all | solution.py:624
  43.9 0.1 bitcast_convert_fusion.in_ref
  44.1 4.2 %plane_filter.1 = (f32[2048,128]{1,0:T(8,128)S(1)}, f32[8,128]{1,0:T(8,128)S(1)}) custom-call(f32[2304,128]{1,0:T(8,128)S(1)} %bitcast_convert_fusion.in_ref, f32[8,64,256]{2,1,0:T(8,128)S(1)} %hat_order.1.hat_ref, bf16[1024,256]{1,0:T(8,128)(2,1)S(1)} %copy-done.4, bf16[512,128]{1,0:T(8,128)(2,1)S(1)} %copy-done.5), custom_call_target="tpu_custom_call" | custom-call | tf_op jit(solution)/shard_map/plane_filter/pallas_call | solution.py:656
  48.3 0.0 copy-start.8
  48.3 0.0 copy-start.9
  48.3 0.0 copy-start.7
  48.3 0.9 %convert_element_type.19 = f16[2048,128]{1,0:T(8,128)(2,1)} convert(f32[2048,128]{1,0:T(8,128)S(1)} %get-tuple-element.50) | non-fusion elementwise | flops 262144 | bytes 1572864 | tf_op jit(solution)/shard_map/convert_element_type | solution.py:623
  49.2 2.6 %all-to-all-start.1 = ((f16[32,64,128]{2,1,0:T(8,128)(2,1)}), f16[32,64,128]{2,1,0:T(8,128)(2,1)S(1)}, u32[]{:S(2)}, u32[]{:S(2)}) async-start(f16[32,64,128]{2,1,0:T(8,128)(2,1)} %bitcast.6), calls=%async_computation.1 | async-start | bytes 1048576 | tf_op jit(solution)/shard_map/all_to_all | solution.py:624
  51.8 0.0 copy-start.3
  51.9 0.2 reshape.29.table_ref
  52.1 0.2 collective-permute-start.3
  52.3 1.2 %collective-permute-done.3.there_ref = bf16[240,256]{1,0:T(8,128)(2,1)S(1)} collective-permute-done((bf16[240,256]{1,0:T(8,128)(2,1)S(1)}, bf16[240,256]{1,0:T(8,128)(2,1)S(1)}, u32[]{:S(2)}, u32[]{:S(2)}) %collective-permute-start.3) | collective-permute-done | bytes 122912 | tf_op jit(solution)/shard_map/ppermute | solution.py:550
  53.5 2.1 %near_field.1 = f32[64,256]{1,0:T(8,128)S(1)} custom-call(s32[1]{0:T(128)} %copy.25.live_ref, bf16[240,256]{1,0:T(8,128)(2,1)S(1)} %get-tuple-element.51.here_ref, bf16[240,256]{1,0:T(8,128)(2,1)S(1)} %collective-permute-done.3.there_ref, s32[8,256]{1,0:T(8,128)S(1)} %fusion.5.source_ref, s32[8,256]{1,0:T(8,128)S(1)} %bitcast.18, ...), custom_call_target="tpu_custom_call" | custom-call | tf_op jit(solution)/shard_map/near_field/pallas_call | solution.py:647
  55.6 13.1 %all-to-all-done.1 = f16[32,64,128]{2,1,0:T(8,128)(2,1)S(1)} async-done(((f16[32,64,128]{2,1,0:T(8,128)(2,1)}), f16[32,64,128]{2,1,0:T(8,128)(2,1)S(1)}, u32[]{:S(2)}, u32[]{:S(2)}) %all-to-all-start.1) | async-done | bytes 524320 | tf_op jit(solution)/shard_map/all_to_all | solution.py:624
  68.7 0.1 bitcast_convert_fusion.1.in_ref
  68.8 2.2 %z_inverse.1 = (f32[520,128]{1,0:T(8,128)S(1)}, f32[520,128]{1,0:T(8,128)S(1)}, f32[520,128]{1,0:T(8,128)S(1)}, f32[520,128]{1,0:T(8,128)S(1)}, bf16[128,128]{1,0:T(8,128)(2,1)S(1)}) custom-call(f32[2048,128]{1,0:T(8,128)S(1)} %bitcast_convert_fusion.1.in_ref, f32[8,128]{1,0:T(8,128)S(1)} %get-tuple-element.53.exponent_ref, bf16[1024,512]{1,0:T(8,128)(2,1)S(1)} %copy-done.3), custom_call_target="tpu_custom_call" | custom-call | tf_op jit(solution)/shard_map/z_inverse/pallas_call | solution.py:667
  71.0 0.1 collective-permute-start.4
  71.1 1.2 %collective-permute-done.4.edge_ref = bf16[128,128]{1,0:T(8,128)(2,1)S(1)} collective-permute-done((bf16[128,128]{1,0:T(8,128)(2,1)S(1)}, bf16[128,128]{1,0:T(8,128)(2,1)S(1)}, u32[]{:S(2)}, u32[]{:S(2)}) %collective-permute-start.4) | collective-permute-done | bytes 32800 | tf_op jit(solution)/shard_map/ppermute | solution.py:550
  72.3 3.5 %beside_sample.1 = (f32[64,256]{1,0:T(8,128)S(1)}, f32[64,256]{1,0:T(8,128)S(1)}) custom-call(s32[1]{0:T(128)} %bitcast.2.odd_ref, s32[8,512]{1,0:T(8,128)S(1)} %get-tuple-element.60.facts_ref.kinds_ref, f32[520,128]{1,0:T(8,128)S(1)} %get-tuple-element.54.p0, f32[520,128]{1,0:T(8,128)S(1)} %get-tuple-element.55.p1, f32[520,128]{1,0:T(8,128)S(1)} %get-tuple-element.56.p2, ...), custom_call_target="tpu_custom_call" | custom-call | tf_op jit(solution)/shard_map/beside_sample/pallas_call | solution.py:681
  75.8 0.1 collective-permute-start.5
  75.9 0.9 %collective-permute-start.6 = (f32[64,256]{1,0:T(8,128)S(1)}, f32[64,256]{1,0:T(8,128)S(1)}, u32[]{:S(2)}, u32[]{:S(2)}) collective-permute-start(f32[64,256]{1,0:T(8,128)S(1)} %get-tuple-element.62), channel_id=1, source_target_pairs={{0,30},{1,31},{2,4},{3,5},{4,2},{5,3},{6,8},{7,9},{8,6},{9,7},{10,... | collective-permute-start | bytes 196616 | tf_op jit(solution)/shard_map/ppermute | solution.py:550
  76.7 1.6 %own_sample.1 = f32[64,256]{1,0:T(8,128)S(1)} custom-call(s32[8,256]{1,0:T(8,128)S(1)} %get-tuple-element.34.facts_ref.kinds_ref, f32[520,128]{1,0:T(8,128)S(1)} %get-tuple-element.54.p0, f32[520,128]{1,0:T(8,128)S(1)} %get-tuple-element.55.p1, f32[520,128]{1,0:T(8,128)S(1)} %get-tuple-element.56.p2, f32[520,128]{1,0:T(8,128)S(1)} %get-tuple-element.57.p3, ...), custom_call_target="tpu_custom_call" | custom-call | tf_op jit(solution)/shard_map/own_sample/pallas_call | solution.py:692
  78.4 1.7 %collective-permute-done.5 = f32[64,256]{1,0:T(8,128)S(1)} collective-permute-done((f32[64,256]{1,0:T(8,128)S(1)}, f32[64,256]{1,0:T(8,128)S(1)}, u32[]{:S(2)}, u32[]{:S(2)}) %collective-permute-start.5) | collective-permute-done | bytes 65568 | tf_op jit(solution)/shard_map/ppermute | solution.py:550
  80.1 3.7 %collective-permute-done.6 = f32[64,256]{1,0:T(8,128)S(1)} collective-permute-done((f32[64,256]{1,0:T(8,128)S(1)}, f32[64,256]{1,0:T(8,128)S(1)}, u32[]{:S(2)}, u32[]{:S(2)}) %collective-permute-start.6) | collective-permute-done | bytes 65568 | tf_op jit(solution)/shard_map/ppermute | solution.py:550
  83.8 0.6 add_add_fusion
  (11 shorter events, 0.1 us)
Async XLA Ops:
  2.3 11.3 %collective-permute-start = (bf16[80,256]{1,0:T(8,128)(2,1)S(1)}, bf16[80,256]{1,0:T(8,128)(2,1)S(1)}, u32[]{:S(2)}, u32[]{:S(2)}) collective-permute-start(bf16[80,256]{1,0:T(8,128)(2,1)S(1)} %fusion.packed_ref.own_ref), channel_id=1, source_target_pairs={{0,2},{1,3},{2,0},{3,1},{4,6},{5,7},{6,4},{7,5},{8,10},{9,11},{10,... | collective-permute-start | bytes 122888 | tf_op jit(solution)/shard_map/ppermute | solution.py:550
  5.3 8.3 %collective-permute-start.1 = (bf16[80,256]{1,0:T(8,128)(2,1)S(1)}, bf16[80,256]{1,0:T(8,128)(2,1)S(1)}, u32[]{:S(2)}, u32[]{:S(2)}) collective-permute-start(bf16[80,256]{1,0:T(8,128)(2,1)S(1)} %fusion.packed_ref.own_ref), channel_id=1, source_target_pairs={{0,30},{1,31},{2,4},{3,5},{4,2},{5,3},{6,8},{7,9},{8,6},{9,7},{10,... | collective-permute-start | bytes 122888 | tf_op jit(solution)/shard_map/ppermute | solution.py:550
  9.8 1.2 %copy-start.1 = (bf16[16,64,512]{2,1,0:T(8,128)(2,1)S(1)}, bf16[16,64,512]{2,1,0:T(8,128)(2,1)}, u32[]{:S(2)}) copy-start(bf16[16,64,512]{2,1,0:T(8,128)(2,1)} %param.18) | copy-start | bytes 3145732
  13.5 6.4 %copy-start = (bf16[1024,512]{1,0:T(8,128)(2,1)S(1)}, bf16[1024,512]{1,0:T(8,128)(2,1)}, u32[]{:S(2)}) copy-start(bf16[1024,512]{1,0:T(8,128)(2,1)} %constant.88.clone.w_ref) | copy-start | bytes 3145732
  17.4 2.5 %collective-permute-start.2 = (f32[128,128]{1,0:T(8,128)S(1)}, f32[128,128]{1,0:T(8,128)S(1)}, u32[]{:S(2)}, u32[]{:S(2)}) collective-permute-start(f32[128,128]{1,0:T(8,128)S(1)} %get-tuple-element.45), channel_id=1, source_target_pairs={{0,1},{1,0},{2,3},{3,2},{4,5},{5,4},{6,7},{7,6},{8,9},{9,8},{10,11... | collective-permute-start | bytes 196616 | tf_op jit(solution)/shard_map/ppermute | solution.py:550
  22.1 3.6 %copy-start.2 = (f32[16,64,256]{2,1,0:T(8,128)S(1)}, f32[16,64,256]{2,1,0:T(8,128)}, u32[]{:S(2)}) copy-start(f32[16,64,256]{2,1,0:T(8,128)} %hat_ref) | copy-start | bytes 3145732
  22.1 3.6 %copy-start.6 = (bf16[128,128]{1,0:T(8,128)(2,1)S(1)}, bf16[128,128]{1,0:T(8,128)(2,1)}, u32[]{:S(2)}) copy-start(bf16[128,128]{1,0:T(8,128)(2,1)} %constant.89.clone.turn_ref) | copy-start | bytes 98308
  23.1 20.9 %all-to-all-start = ((f16[32,72,128]{2,1,0:T(8,128)(2,1)}), f16[32,72,128]{2,1,0:T(8,128)(2,1)S(1)}, u32[]{:S(2)}, u32[]{:S(2)}) async-start(f16[32,72,128]{2,1,0:T(8,128)(2,1)} %bitcast.19), calls=%async_computation | async-start | bytes 1179648 | tf_op jit(solution)/shard_map/all_to_all | solution.py:624
  26.0 18.1 %copy-start.4 = (bf16[1024,256]{1,0:T(8,128)(2,1)S(1)}, bf16[1024,256]{1,0:T(8,128)(2,1)}, u32[]{:S(2)}) copy-start(bf16[1024,256]{1,0:T(8,128)(2,1)} %constant.90.clone.y_ref) | copy-start | bytes 1572868
  26.0 18.1 %copy-start.5 = (bf16[512,128]{1,0:T(8,128)(2,1)S(1)}, bf16[512,128]{1,0:T(8,128)(2,1)}, u32[]{:S(2)}) copy-start(bf16[512,128]{1,0:T(8,128)(2,1)} %constant.91.clone.x_ref) | copy-start | bytes 393220
  48.3 3.5 %copy-start.8 = (bf16[64,16,64]{2,1,0:T(8,128)(2,1)S(1)}, bf16[64,16,64]{2,1,0:T(8,128)(2,1)}, u32[]{:S(2)}) copy-start(bf16[64,16,64]{2,1,0:T(8,128)(2,1)} %param.21) | copy-start | bytes 393220
  48.3 3.9 %copy-start.9 = (s32[256,8]{0,1:T(8,128)S(1)}, s32[256,8]{0,1:T(8,128)}, u32[]{:S(2)}) copy-start(s32[256,8]{0,1:T(8,128)} %param.19) | copy-start | bytes 24580
  48.3 5.1 %copy-start.7 = (s32[256,8]{0,1:T(8,128)S(1)}, s32[256,8]{0,1:T(8,128)}, u32[]{:S(2)}) copy-start(s32[256,8]{0,1:T(8,128)} %param.20) | copy-start | bytes 24580
  49.2 19.4 %all-to-all-start.1 = ((f16[32,64,128]{2,1,0:T(8,128)(2,1)}), f16[32,64,128]{2,1,0:T(8,128)(2,1)S(1)}, u32[]{:S(2)}, u32[]{:S(2)}) async-start(f16[32,64,128]{2,1,0:T(8,128)(2,1)} %bitcast.6), calls=%async_computation.1 | async-start | bytes 1048576 | tf_op jit(solution)/shard_map/all_to_all | solution.py:624
  51.8 16.9 %copy-start.3 = (bf16[1024,512]{1,0:T(8,128)(2,1)S(1)}, bf16[1024,512]{1,0:T(8,128)(2,1)}, u32[]{:S(2)}) copy-start(bf16[1024,512]{1,0:T(8,128)(2,1)} %constant.92.clone.v_ref) | copy-start | bytes 3145732
  52.1 1.4 %collective-permute-start.3 = (bf16[240,256]{1,0:T(8,128)(2,1)S(1)}, bf16[240,256]{1,0:T(8,128)(2,1)S(1)}, u32[]{:S(2)}, u32[]{:S(2)}) collective-permute-start(bf16[240,256]{1,0:T(8,128)(2,1)S(1)} %get-tuple-element.51.here_ref), channel_id=1, source_target_pairs={{0,1},{1,0},{2,3},{3,2},{4,5},{5,4},{6,7},{7,6},{8,9},{9,8},{10,11... | collective-permute-start | bytes 368648 | tf_op jit(solution)/shard_map/ppermute | solution.py:550
  71.0 1.3 %collective-permute-start.4 = (bf16[128,128]{1,0:T(8,128)(2,1)S(1)}, bf16[128,128]{1,0:T(8,128)(2,1)S(1)}, u32[]{:S(2)}, u32[]{:S(2)}) collective-permute-start(bf16[128,128]{1,0:T(8,128)(2,1)S(1)} %get-tuple-element.58), channel_id=1, source_target_pairs={{0,1},{1,0},{2,3},{3,2},{4,5},{5,4},{6,7},{7,6},{8,9},{9,8},{10,11... | collective-permute-start | bytes 98312 | tf_op jit(solution)/shard_map/ppermute | solution.py:550
  75.8 4.3 %collective-permute-start.5 = (f32[64,256]{1,0:T(8,128)S(1)}, f32[64,256]{1,0:T(8,128)S(1)}, u32[]{:S(2)}, u32[]{:S(2)}) collective-permute-start(f32[64,256]{1,0:T(8,128)S(1)} %get-tuple-element.61), channel_id=1, source_target_pairs={{0,2},{1,3},{2,0},{3,1},{4,6},{5,7},{6,4},{7,5},{8,10},{9,11},{10,... | collective-permute-start | bytes 196616 | tf_op jit(solution)/shard_map/ppermute | solution.py:550
  75.9 7.9 %collective-permute-start.6 = (f32[64,256]{1,0:T(8,128)S(1)}, f32[64,256]{1,0:T(8,128)S(1)}, u32[]{:S(2)}, u32[]{:S(2)}) collective-permute-start(f32[64,256]{1,0:T(8,128)S(1)} %get-tuple-element.62), channel_id=1, source_target_pairs={{0,30},{1,31},{2,4},{3,5},{4,2},{5,3},{6,8},{7,9},{8,6},{9,7},{10,... | collective-permute-start | bytes 196616 | tf_op jit(solution)/shard_map/ppermute | solution.py:550

commit v8 on v7

--- a/solution.py
+++ b/solution.py
@@ -38,21 +38,25 @@
     return np.concatenate(parts, axis=0)
 
 
-def owner_frequencies(slabs, tiles):
-    devices = slabs * tiles
-    planes = NZ // devices
-    owner = np.array([a * tiles + b for b in range(tiles) for a in range(slabs)])
-    plane = np.arange(planes // 2)
-    return (owner[None, :] * planes + plane[:, None] + (owner[None, :] >= devices // 2)).reshape(-1)
-
-
 def z_tables(slabs, tiles):
-    freq = owner_frequencies(slabs, tiles)
-    cell = np.arange(NZ) - 2
-    angle = (freq[:, None] * cell[None, :] % NZ) * (2 * np.pi / NZ)
-    forward = np.concatenate([np.cos(angle), -np.sin(angle)], axis=0)
-    weight = np.where(freq % NZ == 0, 1.0, 2.0)[:, None] / NZ
-    inverse = np.concatenate([weight * np.cos(angle), -weight * np.sin(angle)], axis=0).T
+    half = slabs // 2
+    planes = NZ // (slabs * tiles) // 2
+    plane = np.arange(planes + 1)[:, None, None]
+    tile = np.arange(tiles)[None, :, None]
+    slab = np.arange(half)[None, None, :]
+    owner = slab * tiles + tile
+    freq = (owner * 2 * planes + plane).reshape(-1)
+    forward, inverse = [], []
+    for parity in range(2):
+        cell = np.arange(parity, NZ, 2) - 2
+        angle = (freq[:, None] * cell[None, :] % NZ) * (2 * np.pi / NZ)
+        forward.append(np.concatenate([np.cos(angle), -np.sin(angle)], axis=0))
+        upper = (plane[:-1] + parity) % 2
+        back = ((upper * half * tiles + owner) * 2 * planes + plane[:-1] + upper).reshape(-1)
+        cell = np.arange(NZ // 2) - 2
+        angle = (back[:, None] * cell[None, :] % NZ) * (2 * np.pi / NZ)
+        weight = np.where(back == 0, 1.0, 2.0)[:, None] / NZ
+        inverse.append(np.concatenate([weight * np.cos(angle), -weight * np.sin(angle)], axis=0).T)
     return forward, inverse
 
 
@@ -292,7 +296,8 @@
         for side, (planes, shift_i) in enumerate(BESIDE):
             scatter_columns(fp_ref, 2 * first + side * LANES, place_in_facts(facts_ref, side * slots + first),
                             counts[side], (g0, g1, g2, g3), edge_ref, planes, shift_i)
-    edge_ref[0:8, :] += edge_ref[NZ:ZROWS, :]
+    for ref in (g0, g1, g2, g3, edge_ref):
+        ref[0:8, :] += ref[NZ:ZROWS, :]
     total = pltpu.roll(edge_ref[0:LANES, :], 2, 1)
     for block in range(1, 4):
         total += pltpu.roll(edge_ref[block * LANES : (block + 1) * LANES, :], 32 * block + 2, 1)
@@ -305,34 +310,43 @@
     return jnp.ceil(jnp.log2(top)) - BOUND
 
 
-def z_kernel(owners, g0, g1, g2, g3, edge_ref, w_ref, out_ref):
-    shape = (LANES, LANES)
-    parts = NZ // owners
+def quarter(table_ref, index):
+    rows = table_ref.shape[0] // 4
+    return tuple(table_ref[part * rows : (part + 1) * rows, :] for part in (2 * index, 2 * index + 1))
+
+
+def z_kernel(slabs, g0, g1, g2, g3, edge_ref, w_ref, out_ref, wide_ref):
+    widen_edge(edge_ref, wide_ref)
+    half = slabs // 2
+    parts = NZ // (2 * slabs)
+    planes = parts // 2
     stride = 4 * parts + SCALE_ROWS
-    edges = [pltpu.roll(edge_ref[...], (LANES - 2 - 32 * block) % LANES, 1) for block in range(4)]
-    results = []
-    for plane, grid in enumerate((g0, g1, g2, g3)):
-        at_edge = edge_codes((plane,), shape) < 2
-        blocks = [
-            grid[block * LANES : (block + 1) * LANES, :] + jnp.where(at_edge, edges[block], 0.0)
-            for block in range(4)
-        ]
-        blocks[0] = jnp.concatenate([blocks[0][0:8] + grid[NZ:ZROWS, :], blocks[0][8:]], axis=0)
-        values = jnp.concatenate(blocks, axis=0)
-        if plane:
-            values = pltpu.roll(values, LANES - 8 * plane, 1)
-        results.append(dot3((w_ref[0:NZ, :], w_ref[NZ : 2 * NZ, :]), split(values)))
+    sums = []
+    for parity in range(2):
+        where = pl.ds(parity, NZ // 2, stride=2)
+        columns = []
+        for plane, grid in enumerate((g0, g1, g2, g3)):
+            at_edge = edge_codes((plane,), (NZ // 2, LANES)) < 2
+            values = grid[where, :] + jnp.where(at_edge, wide_ref[where, :], 0.0)
+            columns.append(pltpu.roll(values, LANES - 8 * plane, 1) if plane else values)
+        sums.append(dot3(quarter(w_ref, parity), split(jnp.concatenate(columns, axis=1))))
+    results = (sums[0] + sums[1], sums[0] - sums[1])
     exponent = exponent_of(results)
     scale = jnp.exp2(-exponent)
-    for plane, result in enumerate(results):
-        result = result * scale
+    results = [result * scale for result in results]
+    for upper, result in enumerate(results):
         for part in range(parts):
-            out_ref[pl.ds(plane * parts + part, owners, stride=stride), :] = result[
-                part * owners : (part + 1) * owners, :
-            ]
+            index = part // planes * (planes + 1) + part % planes + upper
+            for tile in range(2):
+                rows = result[(index * 2 + tile) * half : (index * 2 + tile + 1) * half, :]
+                start = (tile * slabs + upper * half) * stride + part
+                for plane in range(4):
+                    out_ref[pl.ds(start + plane * parts, half, stride=stride), :] = rows[
+                        :, plane * LANES : (plane + 1) * LANES
+                    ]
     for row in range(SCALE_ROWS):
-        out_ref[pl.ds(4 * parts + row, owners, stride=stride), :] = jnp.broadcast_to(
-            exponent, (owners, LANES)
+        out_ref[pl.ds(4 * parts + row, 2 * slabs, stride=stride), :] = jnp.broadcast_to(
+            exponent, (2 * slabs, LANES)
         )
 
 
@@ -385,14 +399,20 @@
         [even[1] - zero_odd[0], jnp.where(first_lane, odd[1], even[1] + zero_odd[0])], axis=1
     )
     size = 2 * length
-    forward = (x_ref[0:size, :], x_ref[size : 2 * size, :])
-    inverse = (x_ref[2 * size : 3 * size, :], x_ref[3 * size : 4 * size, :])
+
+    def along_x(values, first):
+        high, low = split(values)
+        table = x_ref[first * size : (first + 1) * size, :]
+        rest = x_ref[(first + 1) * size : (first + 2) * size, :]
+        both = dot(jnp.concatenate([table, table], axis=1), jnp.concatenate([high, low], axis=0))
+        return both + dot(rest, high)
+
     for plane in range(planes):
         here = slice(plane * length, (plane + 1) * length)
         there = slice(rows + plane * length, rows + (plane + 1) * length)
-        values = dot3(forward, split(jnp.concatenate([real[here], imag[here]], axis=0)))
+        values = along_x(jnp.concatenate([real[here], imag[here]], axis=0), 0)
         values = values * jnp.concatenate([hat_ref[plane], hat_ref[plane]], axis=0)
-        values = dot3(inverse, split(values))
+        values = along_x(values, 2)
         low, high = values[:, :HALF], values[:, HALF:]
         lane = first_lane[:length]
         even_r = jnp.where(lane, low[:length], low[:length] + high[:length])
@@ -411,33 +431,45 @@
     scale = jnp.exp2(-exponent[0:1, 0:1])
     for tile, part, plane, xi in pieces():
         here = slice((part * planes + plane) * length + xi * slabs, (part * planes + plane) * length + (xi + 1) * slabs)
-        start = tile * slabs * 4 * parts + xi * parts + part * planes + plane
-        out_ref[pl.ds(start, slabs, stride=4 * parts), :] = (
+        start = tile * slabs * stride + xi * parts + part * planes + plane
+        out_ref[pl.ds(start, slabs, stride=stride), :] = (
             turned[here, tile * LANES : (tile + 1) * LANES] * scale
         )
 
 
-def potential_kernel(owners, in_ref, exponent_ref, v_ref, p0, p1, p2, p3, edge_ref):
-    parts = NZ // owners
+def potential_kernel(slabs, in_ref, exponent_ref, v_ref, p0, p1, p2, p3, edge_ref):
+    half = slabs // 2
+    parts = NZ // (2 * slabs)
+    planes = parts // 2
+    stride = 4 * parts
+    sums = []
+    for parity in range(2):
+        columns = []
+        for plane in range(4):
+            rows = []
+            for part in range(parts):
+                upper = (part % planes + parity) % 2
+                for tile in range(2):
+                    start = (tile * slabs + upper * half) * stride + plane * parts + part
+                    rows.append(in_ref[pl.ds(start, half, stride=stride), :])
+            columns.append(jnp.concatenate(rows, axis=0))
+        sums.append(dot3(quarter(v_ref, parity), split(jnp.concatenate(columns, axis=1))))
+    scale = jnp.exp2(exponent_ref[0:1, 0:1])
     shape = (LANES, LANES)
     edges = [jnp.zeros(shape, F32)] * 4
-    scale = jnp.exp2(exponent_ref[0:1, 0:1])
+    halves_of_z = [((sums[0] + sums[1]) * scale), ((sums[0] - sums[1]) * scale)]
     for plane, pot in enumerate((p0, p1, p2, p3)):
-        values = split(jnp.concatenate(
-            [in_ref[pl.ds(plane * parts + part, owners, stride=4 * parts), :] for part in range(parts)],
-            axis=0,
-        ))
-        result = dot3((v_ref[0:NZ, :], v_ref[NZ : 2 * NZ, :]), values) * scale
-        result = result.astype(BF16).astype(F32)
-        if plane:
-            result = pltpu.roll(result, 8 * plane, 1)
-        pot[0:NZ, :] = result
-        pot[NZ:ZROWS, :] = result[0:8, :]
         at_edge = edge_codes((plane,), shape) < 2
-        edges = [
-            jnp.where(at_edge, result[block * LANES : (block + 1) * LANES, :], edge)
-            for block, edge in enumerate(edges)
-        ]
+        for upper in range(2):
+            result = halves_of_z[upper][:, plane * LANES : (plane + 1) * LANES].astype(BF16).astype(F32)
+            if plane:
+                result = pltpu.roll(result, 8 * plane, 1)
+            pot[upper * (NZ // 2) : (upper + 1) * (NZ // 2), :] = result
+            for block in range(2):
+                edges[2 * upper + block] = jnp.where(
+                    at_edge, result[block * LANES : (block + 1) * LANES, :], edges[2 * upper + block]
+                )
+        pot[NZ:ZROWS, :] = pot[0:8, :]
     edge = pltpu.roll(edges[0], 2, 1)
     for block in range(1, 4):
         edge += pltpu.roll(edges[block], 32 * block + 2, 1)
@@ -563,7 +595,7 @@
     column = lax.broadcasted_iota(jnp.int32, (PANELS + 16, slots), 1)
     live = jnp.broadcast_to(live_count[0], row.shape)
     brick = jnp.broadcast_to(slot_brick[None, :], row.shape)
-    facts = jnp.where(row == PANELS, lax.shift_right_logical(brick, 7), brick & (NZ // 4 - 1))
+    facts = lax.shift_right_logical(brick, jnp.where(row == PANELS, 7, 0)) & (NZ // 4 - 1)
     facts = jnp.where(row == PANELS + 2, slot_stencil[None, :], jnp.where(row == PANELS + 3, live, facts))
     held = jnp.where(column < live, jnp.pad(charges, ((0, 16), (0, 0))), jnp.zeros((), BF16))
     packed = jnp.where(row < PANELS, held, facts.astype(BF16))
@@ -611,16 +643,17 @@
     forward, inverse = z_tables(slabs, tiles)
     rows = owners * (4 * parts + SCALE_ROWS)
     sent = pl.pallas_call(
-        functools.partial(z_kernel, owners),
+        functools.partial(z_kernel, slabs),
         out_shape=shape_of(rows, LANES),
         in_specs=[VMEM] * 6,
         out_specs=VMEM,
+        scratch_shapes=[pltpu.VMEM((ZROWS, LANES), F32)],
         compiler_params=PARAMS,
         name="z_forward",
-    )(*g[:4], edge, jnp.asarray(halves(forward)))
-
-    def exchanged(values):
-        values = values.astype(jnp.float16).reshape(owners, -1, LANES)
+    )(*g[:4], edge, jnp.asarray(halves(*forward)))
+
+    def exchanged(values, kept):
+        values = values.reshape(owners, -1, LANES)[:, :kept].astype(jnp.float16)
         values = lax.all_to_all(values, axes, 0, 0, tiled=True)
         return values
 
@@ -628,7 +661,7 @@
         return values.astype(F32).reshape(-1, LANES)
 
     hat, sent = lax.optimization_barrier((kernel_hat, sent))
-    got = exchanged(sent)
+    got = exchanged(sent, 4 * parts + SCALE_ROWS)
     me = lax.axis_index("slab") * tiles + lax.axis_index("tile")
     offset = (me >= owners // 2).astype(jnp.int32)[None]
     hat = pl.pallas_call(
@@ -655,23 +688,23 @@
 
     back, exponent = pl.pallas_call(
         functools.partial(plane_kernel, slabs, planes),
-        out_shape=(shape_of(owners * 4 * parts, LANES), shape_of(8, LANES)),
+        out_shape=(shape_of(rows, LANES), shape_of(8, LANES)),
         in_specs=[VMEM] * 4,
         out_specs=(VMEM, VMEM),
         scratch_shapes=[pltpu.VMEM((2 * planes * length, NY), BF16)] * 2,
         compiler_params=PARAMS,
         name="plane_filter",
     )(widened(got), hat, jnp.asarray(halves(y_table(), y_table().T)), jnp.asarray(halves(*x_tables(slabs))))
-    back, near = lax.optimization_barrier((exchanged(back), near))
+    back, near = lax.optimization_barrier((exchanged(back, 4 * parts), near))
 
     pot = pl.pallas_call(
-        functools.partial(potential_kernel, owners),
+        functools.partial(potential_kernel, slabs),
         out_shape=(grid,) * 4 + (shape_of(LANES, LANES, dtype=BF16),),
         in_specs=[VMEM] * 3,
         out_specs=(VMEM,) * 5,
         compiler_params=PARAMS,
         name="z_inverse",
-    )(widened(back), exponent, jnp.asarray(halves(inverse)))
+    )(widened(back), exponent, jnp.asarray(halves(*inverse)))
     edge = to_other_tile(pot[4])
 
     def sample_scratch(width):

time: 85.3 us -> 84.9 us (level)
  Pallas kernels: 22.5 us -> 24.5 us
  starting transfers between devices: 15.6 us -> 13.9 us
  other arithmetic: 4.28 us -> 2.83 us
  local copies, waits for them, and re-layouts: 1.48 us -> 2.42 us
    pallas_call x1, Pallas kernels: 3.82 us -> 6.1 us  [body(): pl.pallas_call(beside_kernel, out_shape=(grid,) * 5 + (shape_of(LANES, LA...]
    pallas_call x1, Pallas kernels: 3.5 us -> 5.43 us  [body(): pl.pallas_call(beside_sample_kernel, out_shape=(sums, sums), in_specs=[SM...]
    pallas_call x2, Pallas kernels: 4.42 us -> 2.68 us  [the longest x1 1.38 us: body(): pl.pallas_call(functools.partial(potential_kernel, slabs), out_shape=(gri...]
    ppermute x7, starting transfers between devices: 10.4 us -> 8.68 us  [moved(): return lax.ppermute(values, both, pairs)]
    slice x0 -> x1, local copies, waits for them, and re-layouts: none -> 0.94 us  [exchanged(): values = values.reshape(owners, -1, LANES)[:, :kept].astype(jnp.float16)]
    convert_element_type x2 -> x1, other arithmetic: 1.81 us -> 0.93 us  [exchanged(): values = values.reshape(owners, -1, LANES)[:, :kept].astype(jnp.float16)]
where the time goes in v8:
time: 84.9 us; the launch traced here: 84.6 us
  waiting for transfers between devices  40 us (47%)
  Pallas kernels  24.5 us (29%)
  starting transfers between devices  13.9 us (16%)
  other arithmetic  2.83 us (3%)
  local copies, waits for them, and re-layouts  2.42 us (3%)
  between operations  0.96 us (1%)
    all_to_all x2, waiting for transfers between devices, exchanged(): values = lax.all_to_all(values, axes, 0, 0, tiled=True)  31 us
    ppermute x7, waiting for transfers between devices, moved(): return lax.ppermute(values, both, pairs)  9.02 us
    ppermute x7, starting transfers between devices, moved(): return lax.ppermute(values, both, pairs)  8.68 us
    pallas_call x1, Pallas kernels, body(): pl.pallas_call(beside_kernel, out_shape=(grid,) * 5 + (shape_of(LANES, LA...  6.1 us
    pallas_call x1, Pallas kernels, body(): pl.pallas_call(beside_sample_kernel, out_shape=(sums, sums), in_specs=[SM...  5.43 us
    all_to_all x2, starting transfers between devices, exchanged(): values = lax.all_to_all(values, axes, 0, 0, tiled=True)  5.21 us
    pallas_call x1, Pallas kernels, body(): pl.pallas_call(functools.partial(plane_kernel, slabs, planes), out_shape=...  3.46 us
    pallas_call x1, Pallas kernels, body(): pl.pallas_call(own_kernel, out_shape=(grid,) * 5 + (shape_of(KS * PANELS,...  2.64 us
  transfers between devices with their start and end apart: 9, of which 7 were waited for; matrix products, arithmetic and copies ran while one was open for 0% of the time, Pallas kernels for 8%

profile of v8, /device:TPU:0, one launch (start us, length us, event | category | flops | bytes accessed | tf_op | source)
XLA Modules:
  0.0 84.6 jit_solution(5062987723082235533)
XLA Ops:
  0.7 0.9 %fusion.packed_ref.own_ref = bf16[80,256]{1,0:T(8,128)(2,1)S(1)} fusion(s32[80]{0:T(128)S(1)} %compare_select_fusion, s32[256]{0:T(256)} %param.16, s32[]{:T(128)} %bitcast.16, s32[256]{0:T(256)} %param.17, bf16[64,256]{1,0:T(8,128)(2,1)} %param.14, pred[80]{0:T(512)(128)(4,1)S(1)} %get-tuple-element.63, pred[80]{0:T(512)(128)(4,1)S(1)} %get-tuple-element.64, ...), kind=kLoop, calls=%fused_computation.4 | loop fusion | flops 143360 | bytes 76596 | tf_op jit(solution)/shard_map/jit(_where)/select_n | solution.py:601
  1.6 3.0 %collective-permute-start = (bf16[80,256]{1,0:T(8,128)(2,1)S(1)}, bf16[80,256]{1,0:T(8,128)(2,1)S(1)}, u32[]{:S(2)}, u32[]{:S(2)}) collective-permute-start(bf16[80,256]{1,0:T(8,128)(2,1)S(1)} %fusion.packed_ref.own_ref), channel_id=1, source_target_pairs={{0,2},{1,3},{2,0},{3,1},{4,6},{5,7},{6,4},{7,5},{8,10},{9,11},{10,... | collective-permute-start | bytes 122888 | tf_op jit(solution)/shard_map/ppermute | solution.py:582
  4.6 4.5 %collective-permute-start.1 = (bf16[80,256]{1,0:T(8,128)(2,1)S(1)}, bf16[80,256]{1,0:T(8,128)(2,1)S(1)}, u32[]{:S(2)}, u32[]{:S(2)}) collective-permute-start(bf16[80,256]{1,0:T(8,128)(2,1)S(1)} %fusion.packed_ref.own_ref), channel_id=1, source_target_pairs={{0,30},{1,31},{2,4},{3,5},{4,2},{5,3},{6,8},{7,9},{8,6},{9,7},{10,... | collective-permute-start | bytes 122888 | tf_op jit(solution)/shard_map/ppermute | solution.py:582
  9.1 1.2 %copy-done = bf16[16,64,512]{2,1,0:T(8,128)(2,1)S(1)} copy-done((bf16[16,64,512]{2,1,0:T(8,128)(2,1)S(1)}, bf16[16,64,512]{2,1,0:T(8,128)(2,1)}, u32[]{:S(2)}) %copy-start) | copy-done | bytes 1048600
  10.3 2.6 %own_scatter.1 = (f32[520,128]{1,0:T(8,128)S(1)}, f32[520,128]{1,0:T(8,128)S(1)}, f32[520,128]{1,0:T(8,128)S(1)}, f32[520,128]{1,0:T(8,128)S(1)}, f32[520,128]{1...) custom-call(bf16[80,256]{1,0:T(8,128)(2,1)S(1)} %fusion.packed_ref.own_ref, ...), custom_call_target="tpu_custom_call" | custom-call | tf_op jit(solution)/shard_map/own_scatter/pallas_call | solution.py:606
  13.0 0.0 collective-permute-done.first_ref
  13.0 0.0 collective-permute-done.1.second_ref
  13.0 0.0 copy-start.2
  13.0 6.1 %beside_scatter.1 = (f32[520,128]{1,0:T(8,128)S(1)}, f32[520,128]{1,0:T(8,128)S(1)}, f32[520,128]{1,0:T(8,128)S(1)}, f32[520,128]{1,0:T(8,128)S(1)}, f32[520,128...) custom-call(s32[1]{0:T(128)} %bitcast.2.odd_ref, ...), custom_call_target="tpu_custom_call", output_to_operand_aliasing={{0}: (5, {}), {1}: (6, {}), {2}: (7, {}), {3}: (8, {}), {4}... | custom-call | tf_op jit(solution)/shard_map/beside_scatter/pallas_call | solution.py:621
  19.1 0.1 collective-permute-start.2
  19.2 1.2 %collective-permute-done.2.edge_ref = f32[128,128]{1,0:T(8,128)S(1)} collective-permute-done((f32[128,128]{1,0:T(8,128)S(1)}, f32[128,128]{1,0:T(8,128)S(1)}, u32[]{:S(2)}, u32[]{:S(2)}) %collective-permute-start.2) | collective-permute-done | bytes 65568 | tf_op jit(solution)/shard_map/ppermute | solution.py:582
  20.5 0.0 copy-done.2
  20.5 1.3 %z_forward.1 = f32[2304,128]{1,0:T(8,128)S(1)} custom-call(f32[520,128]{1,0:T(8,128)S(1)} %get-tuple-element.41.g0, f32[520,128]{1,0:T(8,128)S(1)} %get-tuple-element.42.g1, f32[520,128]{1,0:T(8,128)S(1)} %get-tuple-element.43.g2, f32[520,128]{1,0:T(8,128)S(1)} %get-tuple-element.44.g3, f32[128,128]{1,0:T(8,128)S(1)} %collective-permute-done.2.edge_ref, ...), custom_call_target="tpu_custom_call" | custom-call | tf_op jit(solution)/shard_map/z_forward/pallas_call | solution.py:645
  21.8 0.0 copy-start.1
  21.8 0.0 copy-start.6
  21.8 0.9 %convert_element_type.19 = f16[2304,128]{1,0:T(8,128)(2,1)} convert(f32[2304,128]{1,0:T(8,128)S(1)} %z_forward.1) | non-fusion elementwise | flops 294912 | bytes 1769472 | tf_op jit(solution)/shard_map/convert_element_type | solution.py:656
  22.7 2.6 %all-to-all-start = ((f16[32,72,128]{2,1,0:T(8,128)(2,1)}), f16[32,72,128]{2,1,0:T(8,128)(2,1)S(1)}, u32[]{:S(2)}, u32[]{:S(2)}) async-start(f16[32,72,128]{2,1,0:T(8,128)(2,1)} %bitcast.19), calls=%async_computation | async-start | bytes 1179648 | tf_op jit(solution)/shard_map/all_to_all | solution.py:657
  25.4 0.0 copy-done.1
  25.4 0.3 hat_order.1.hat_ref
  25.6 0.0 copy-start.4
  25.7 0.0 copy-start.5
  25.7 17.9 %all-to-all-done = f16[32,72,128]{2,1,0:T(8,128)(2,1)S(1)} async-done(((f16[32,72,128]{2,1,0:T(8,128)(2,1)}), f16[32,72,128]{2,1,0:T(8,128)(2,1)S(1)}, u32[]{:S(2)}, u32[]{:S(2)}) %all-to-all-start) | async-done | bytes 589856 | tf_op jit(solution)/shard_map/all_to_all | solution.py:657
  43.6 0.1 bitcast_convert_fusion.in_ref
  43.7 3.5 %plane_filter.1 = (f32[2304,128]{1,0:T(8,128)S(1)}, f32[8,128]{1,0:T(8,128)S(1)}) custom-call(f32[2304,128]{1,0:T(8,128)S(1)} %bitcast_convert_fusion.in_ref, f32[8,64,256]{2,1,0:T(8,128)S(1)} %hat_order.1.hat_ref, bf16[1024,256]{1,0:T(8,128)(2,1)S(1)} %copy-done.4, bf16[512,128]{1,0:T(8,128)(2,1)S(1)} %copy-done.5), custom_call_target="tpu_custom_call" | custom-call | tf_op jit(solution)/shard_map/plane_filter/pallas_call | solution.py:689
  47.2 0.1 convert.7
  47.3 0.0 copy-start.8
  47.3 0.0 copy-start.9
  47.3 0.0 copy-start.7
  47.3 0.9 %slice.5 = f16[32,64,128]{2,1,0:T(8,128)(2,1)} slice(f16[32,72,128]{2,1,0:T(8,128)(2,1)S(1)} %bitcast.20), slice={[0:32], [0:64], [0:128]} | slice | bytes 1048576 | tf_op jit(solution)/shard_map/slice | solution.py:656
  48.3 2.6 %all-to-all-start.1 = ((f16[32,64,128]{2,1,0:T(8,128)(2,1)}), f16[32,64,128]{2,1,0:T(8,128)(2,1)S(1)}, u32[]{:S(2)}, u32[]{:S(2)}) async-start(f16[32,64,128]{2,1,0:T(8,128)(2,1)} %slice.5), calls=%async_computation.1 | async-start | bytes 1048576 | tf_op jit(solution)/shard_map/all_to_all | solution.py:657
  50.9 0.0 copy-start.3
  50.9 0.2 reshape.28.table_ref
  51.1 0.2 collective-permute-start.3
  51.3 0.0 copy-done.9
  51.3 1.2 %collective-permute-done.3.there_ref = bf16[240,256]{1,0:T(8,128)(2,1)S(1)} collective-permute-done((bf16[240,256]{1,0:T(8,128)(2,1)S(1)}, bf16[240,256]{1,0:T(8,128)(2,1)S(1)}, u32[]{:S(2)}, u32[]{:S(2)}) %collective-permute-start.3) | collective-permute-done | bytes 122912 | tf_op jit(solution)/shard_map/ppermute | solution.py:582
  52.5 2.1 %near_field.1 = f32[64,256]{1,0:T(8,128)S(1)} custom-call(s32[1]{0:T(128)} %copy.25.live_ref, bf16[240,256]{1,0:T(8,128)(2,1)S(1)} %get-tuple-element.51.here_ref, bf16[240,256]{1,0:T(8,128)(2,1)S(1)} %collective-permute-done.3.there_ref, s32[8,256]{1,0:T(8,128)S(1)} %fusion.5.source_ref, s32[8,256]{1,0:T(8,128)S(1)} %bitcast.18, ...), custom_call_target="tpu_custom_call" | custom-call | tf_op jit(solution)/shard_map/near_field/pallas_call | solution.py:680
  54.6 13.1 %all-to-all-done.1 = f16[32,64,128]{2,1,0:T(8,128)(2,1)S(1)} async-done(((f16[32,64,128]{2,1,0:T(8,128)(2,1)}), f16[32,64,128]{2,1,0:T(8,128)(2,1)S(1)}, u32[]{:S(2)}, u32[]{:S(2)}) %all-to-all-start.1) | async-done | bytes 524320 | tf_op jit(solution)/shard_map/all_to_all | solution.py:657
  67.7 0.1 bitcast_convert_fusion.1.in_ref
  67.8 1.4 %z_inverse.1 = (f32[520,128]{1,0:T(8,128)S(1)}, f32[520,128]{1,0:T(8,128)S(1)}, f32[520,128]{1,0:T(8,128)S(1)}, f32[520,128]{1,0:T(8,128)S(1)}, bf16[128,128]{1,0:T(8,128)(2,1)S(1)}) custom-call(f32[2048,128]{1,0:T(8,128)S(1)} %bitcast_convert_fusion.1.in_ref, f32[8,128]{1,0:T(8,128)S(1)} %get-tuple-element.53.exponent_ref, bf16[1024,256]{1,0:T(8,128)(2,1)S(1)} %copy-done.3), custom_call_target="tpu_custom_call" | custom-call | tf_op jit(solution)/shard_map/z_inverse/pallas_call | solution.py:700
  69.2 0.1 collective-permute-start.4
  69.3 1.2 %collective-permute-done.4.edge_ref = bf16[128,128]{1,0:T(8,128)(2,1)S(1)} collective-permute-done((bf16[128,128]{1,0:T(8,128)(2,1)S(1)}, bf16[128,128]{1,0:T(8,128)(2,1)S(1)}, u32[]{:S(2)}, u32[]{:S(2)}) %collective-permute-start.4) | collective-permute-done | bytes 32800 | tf_op jit(solution)/shard_map/ppermute | solution.py:582
  70.5 5.4 %beside_sample.1 = (f32[64,256]{1,0:T(8,128)S(1)}, f32[64,256]{1,0:T(8,128)S(1)}) custom-call(s32[1]{0:T(128)} %bitcast.2.odd_ref, s32[8,512]{1,0:T(8,128)S(1)} %get-tuple-element.60.facts_ref.kinds_ref, f32[520,128]{1,0:T(8,128)S(1)} %get-tuple-element.54.p0, f32[520,128]{1,0:T(8,128)S(1)} %get-tuple-element.55.p1, f32[520,128]{1,0:T(8,128)S(1)} %get-tuple-element.56.p2, ...), custom_call_target="tpu_custom_call" | custom-call | tf_op jit(solution)/shard_map/beside_sample/pallas_call | solution.py:714
  75.9 0.1 collective-permute-start.5
  76.0 0.8 collective-permute-start.6
  76.7 1.8 %own_sample.1 = f32[64,256]{1,0:T(8,128)S(1)} custom-call(s32[8,256]{1,0:T(8,128)S(1)} %get-tuple-element.34.facts_ref.kinds_ref, f32[520,128]{1,0:T(8,128)S(1)} %get-tuple-element.54.p0, f32[520,128]{1,0:T(8,128)S(1)} %get-tuple-element.55.p1, f32[520,128]{1,0:T(8,128)S(1)} %get-tuple-element.56.p2, f32[520,128]{1,0:T(8,128)S(1)} %get-tuple-element.57.p3, ...), custom_call_target="tpu_custom_call" | custom-call | tf_op jit(solution)/shard_map/own_sample/pallas_call | solution.py:725
  78.5 1.7 %collective-permute-done.5 = f32[64,256]{1,0:T(8,128)S(1)} collective-permute-done((f32[64,256]{1,0:T(8,128)S(1)}, f32[64,256]{1,0:T(8,128)S(1)}, u32[]{:S(2)}, u32[]{:S(2)}) %collective-permute-start.5) | collective-permute-done | bytes 65568 | tf_op jit(solution)/shard_map/ppermute | solution.py:582
  80.2 3.7 %collective-permute-done.6 = f32[64,256]{1,0:T(8,128)S(1)} collective-permute-done((f32[64,256]{1,0:T(8,128)S(1)}, f32[64,256]{1,0:T(8,128)S(1)}, u32[]{:S(2)}, u32[]{:S(2)}) %collective-permute-start.6) | collective-permute-done | bytes 65568 | tf_op jit(solution)/shard_map/ppermute | solution.py:582
  83.9 0.6 add_add_fusion
  (12 shorter events, 0.1 us)
Async XLA Ops:
  1.6 11.4 %collective-permute-start = (bf16[80,256]{1,0:T(8,128)(2,1)S(1)}, bf16[80,256]{1,0:T(8,128)(2,1)S(1)}, u32[]{:S(2)}, u32[]{:S(2)}) collective-permute-start(bf16[80,256]{1,0:T(8,128)(2,1)S(1)} %fusion.packed_ref.own_ref), channel_id=1, source_target_pairs={{0,2},{1,3},{2,0},{3,1},{4,6},{5,7},{6,4},{7,5},{8,10},{9,11},{10,... | collective-permute-start | bytes 122888 | tf_op jit(solution)/shard_map/ppermute | solution.py:582
  4.6 8.4 %collective-permute-start.1 = (bf16[80,256]{1,0:T(8,128)(2,1)S(1)}, bf16[80,256]{1,0:T(8,128)(2,1)S(1)}, u32[]{:S(2)}, u32[]{:S(2)}) collective-permute-start(bf16[80,256]{1,0:T(8,128)(2,1)S(1)} %fusion.packed_ref.own_ref), channel_id=1, source_target_pairs={{0,30},{1,31},{2,4},{3,5},{4,2},{5,3},{6,8},{7,9},{8,6},{9,7},{10,... | collective-permute-start | bytes 122888 | tf_op jit(solution)/shard_map/ppermute | solution.py:582
  9.1 1.2 %copy-start = (bf16[16,64,512]{2,1,0:T(8,128)(2,1)S(1)}, bf16[16,64,512]{2,1,0:T(8,128)(2,1)}, u32[]{:S(2)}) copy-start(bf16[16,64,512]{2,1,0:T(8,128)(2,1)} %param.18) | copy-start | bytes 3145732
  13.0 7.4 %copy-start.2 = (bf16[1152,256]{1,0:T(8,128)(2,1)S(1)}, bf16[1152,256]{1,0:T(8,128)(2,1)}, u32[]{:S(2)}) copy-start(bf16[1152,256]{1,0:T(8,128)(2,1)} %constant.88.clone.w_ref) | copy-start | bytes 1769476
  19.1 1.3 %collective-permute-start.2 = (f32[128,128]{1,0:T(8,128)S(1)}, f32[128,128]{1,0:T(8,128)S(1)}, u32[]{:S(2)}, u32[]{:S(2)}) collective-permute-start(f32[128,128]{1,0:T(8,128)S(1)} %get-tuple-element.45), channel_id=1, source_target_pairs={{0,1},{1,0},{2,3},{3,2},{4,5},{5,4},{6,7},{7,6},{8,9},{9,8},{10,11... | collective-permute-start | bytes 196616 | tf_op jit(solution)/shard_map/ppermute | solution.py:582
  21.8 3.6 %copy-start.1 = (f32[16,64,256]{2,1,0:T(8,128)S(1)}, f32[16,64,256]{2,1,0:T(8,128)}, u32[]{:S(2)}) copy-start(f32[16,64,256]{2,1,0:T(8,128)} %hat_ref) | copy-start | bytes 3145732
  21.8 3.6 %copy-start.6 = (bf16[128,128]{1,0:T(8,128)(2,1)S(1)}, bf16[128,128]{1,0:T(8,128)(2,1)}, u32[]{:S(2)}) copy-start(bf16[128,128]{1,0:T(8,128)(2,1)} %constant.89.clone.turn_ref) | copy-start | bytes 98308
  22.7 20.9 %all-to-all-start = ((f16[32,72,128]{2,1,0:T(8,128)(2,1)}), f16[32,72,128]{2,1,0:T(8,128)(2,1)S(1)}, u32[]{:S(2)}, u32[]{:S(2)}) async-start(f16[32,72,128]{2,1,0:T(8,128)(2,1)} %bitcast.19), calls=%async_computation | async-start | bytes 1179648 | tf_op jit(solution)/shard_map/all_to_all | solution.py:657
  25.6 18.1 %copy-start.4 = (bf16[1024,256]{1,0:T(8,128)(2,1)S(1)}, bf16[1024,256]{1,0:T(8,128)(2,1)}, u32[]{:S(2)}) copy-start(bf16[1024,256]{1,0:T(8,128)(2,1)} %constant.90.clone.y_ref) | copy-start | bytes 1572868
  25.7 18.1 %copy-start.5 = (bf16[512,128]{1,0:T(8,128)(2,1)S(1)}, bf16[512,128]{1,0:T(8,128)(2,1)}, u32[]{:S(2)}) copy-start(bf16[512,128]{1,0:T(8,128)(2,1)} %constant.91.clone.x_ref) | copy-start | bytes 393220
  47.3 3.6 %copy-start.8 = (bf16[64,16,64]{2,1,0:T(8,128)(2,1)S(1)}, bf16[64,16,64]{2,1,0:T(8,128)(2,1)}, u32[]{:S(2)}) copy-start(bf16[64,16,64]{2,1,0:T(8,128)(2,1)} %param.21) | copy-start | bytes 393220
  47.3 4.0 %copy-start.9 = (s32[256,8]{0,1:T(8,128)S(1)}, s32[256,8]{0,1:T(8,128)}, u32[]{:S(2)}) copy-start(s32[256,8]{0,1:T(8,128)} %param.19) | copy-start | bytes 24580
  47.3 5.2 %copy-start.7 = (s32[256,8]{0,1:T(8,128)S(1)}, s32[256,8]{0,1:T(8,128)}, u32[]{:S(2)}) copy-start(s32[256,8]{0,1:T(8,128)} %param.20) | copy-start | bytes 24580
  48.3 19.4 %all-to-all-start.1 = ((f16[32,64,128]{2,1,0:T(8,128)(2,1)}), f16[32,64,128]{2,1,0:T(8,128)(2,1)S(1)}, u32[]{:S(2)}, u32[]{:S(2)}) async-start(f16[32,64,128]{2,1,0:T(8,128)(2,1)} %slice.5), calls=%async_computation.1 | async-start | bytes 1048576 | tf_op jit(solution)/shard_map/all_to_all | solution.py:657
  50.9 16.9 %copy-start.3 = (bf16[1024,256]{1,0:T(8,128)(2,1)S(1)}, bf16[1024,256]{1,0:T(8,128)(2,1)}, u32[]{:S(2)}) copy-start(bf16[1024,256]{1,0:T(8,128)(2,1)} %constant.92.clone.v_ref) | copy-start | bytes 1572868
  51.1 1.4 %collective-permute-start.3 = (bf16[240,256]{1,0:T(8,128)(2,1)S(1)}, bf16[240,256]{1,0:T(8,128)(2,1)S(1)}, u32[]{:S(2)}, u32[]{:S(2)}) collective-permute-start(bf16[240,256]{1,0:T(8,128)(2,1)S(1)} %get-tuple-element.51.here_ref), channel_id=1, source_target_pairs={{0,1},{1,0},{2,3},{3,2},{4,5},{5,4},{6,7},{7,6},{8,9},{9,8},{10,11... | collective-permute-start | bytes 368648 | tf_op jit(solution)/shard_map/ppermute | solution.py:582
  69.2 1.3 %collective-permute-start.4 = (bf16[128,128]{1,0:T(8,128)(2,1)S(1)}, bf16[128,128]{1,0:T(8,128)(2,1)S(1)}, u32[]{:S(2)}, u32[]{:S(2)}) collective-permute-start(bf16[128,128]{1,0:T(8,128)(2,1)S(1)} %get-tuple-element.58), channel_id=1, source_target_pairs={{0,1},{1,0},{2,3},{3,2},{4,5},{5,4},{6,7},{7,6},{8,9},{9,8},{10,11... | collective-permute-start | bytes 98312 | tf_op jit(solution)/shard_map/ppermute | solution.py:582
  75.9 4.3 %collective-permute-start.5 = (f32[64,256]{1,0:T(8,128)S(1)}, f32[64,256]{1,0:T(8,128)S(1)}, u32[]{:S(2)}, u32[]{:S(2)}) collective-permute-start(f32[64,256]{1,0:T(8,128)S(1)} %get-tuple-element.61), channel_id=1, source_target_pairs={{0,2},{1,3},{2,0},{3,1},{4,6},{5,7},{6,4},{7,5},{8,10},{9,11},{10,... | collective-permute-start | bytes 196616 | tf_op jit(solution)/shard_map/ppermute | solution.py:582
  76.0 7.9 %collective-permute-start.6 = (f32[64,256]{1,0:T(8,128)S(1)}, f32[64,256]{1,0:T(8,128)S(1)}, u32[]{:S(2)}, u32[]{:S(2)}) collective-permute-start(f32[64,256]{1,0:T(8,128)S(1)} %get-tuple-element.62), channel_id=1, source_target_pairs={{0,30},{1,31},{2,4},{3,5},{4,2},{5,3},{6,8},{7,9},{8,6},{9,7},{10,... | collective-permute-start | bytes 196616 | tf_op jit(solution)/shard_map/ppermute | solution.py:582

commit v9 on v8

--- a/solution.py
+++ b/solution.py
@@ -133,11 +133,7 @@
     return code
 
 
-def edge_of(by):
-    return jnp.where(by == 0, 0, jnp.where(by == NY // 8 - 1, 1, 2))
-
-
-def scatter_columns(fp_ref, first, place_of, count, grids, edge_ref, planes, shift_i):
+def scatter_columns(fp_ref, first, place_of, count, grids, edge_ref, planes):
     shape = (8, LANES)
     lanes = [lane_in(plane, shape) for plane in planes]
     codes = edge_codes(planes, shape)
@@ -146,13 +142,12 @@
         updates = []
         for inner in range(UNROLL):
             column = index * UNROLL + inner
-            by, bz = place_of(column)
+            row, begin, edge, turn, _ = place_of(column)
             value = fp_ref[pl.ds(pl.multiple_of((first + column) * 8, 8), 8), :]
-            begin = 4 * by - 2
-            turned = pltpu.roll(value, (begin - 8 * shift_i) & (LANES - 1), 1)
+            turned = pltpu.roll(value, turn, 1)
             terms = [jnp.where(((lane - begin) & -8) == 0, turned, 0.0) for lane in lanes]
-            terms.append(jnp.where(codes == edge_of(by), turned, 0.0))
-            updates.append((pl.ds(4 * bz, 8), terms))
+            terms.append(jnp.where(codes == edge, turned, 0.0))
+            updates.append((pl.ds(row, 8), terms))
         refs = [grids[plane] for plane in planes] + [edge_ref]
         for where, terms in updates:
             sums = [ref[where, :] + term for ref, term in zip(refs, terms)]
@@ -163,7 +158,7 @@
     lax.fori_loop(0, lax.shift_right_logical(count + UNROLL - 1, 4), step, 0)
 
 
-def sample_columns(pot_refs, edge_ref, place_of, count, sp_ref, first, planes, shift_i):
+def sample_columns(pot_refs, edge_ref, place_of, count, sp_ref, first, planes):
     shape = (8, LANES)
     lanes = [lane_in(plane, shape) for plane in planes]
     codes = edge_codes(planes, shape)
@@ -172,13 +167,12 @@
         results = []
         for inner in range(UNROLL):
             column = index * UNROLL + inner
-            by, bz = place_of(column)
-            where = pl.ds(4 * bz, 8)
-            begin = 4 * by - 2
-            result = jnp.where(codes == edge_of(by), edge_ref[where, :], 0.0)
+            row, begin, edge, _, turn = place_of(column)
+            where = pl.ds(row, 8)
+            result = jnp.where(codes == edge, edge_ref[where, :], 0.0)
             for plane, lane in zip(planes, lanes):
                 result = jnp.where(((lane - begin) & -8) == 0, pot_refs[plane][where, :], result)
-            turned = pltpu.roll(result, (8 * shift_i - begin) & (LANES - 1), 1)
+            turned = pltpu.roll(result, turn, 1)
             results.append((pl.ds(pl.multiple_of((first + column) * 8, 8), 8), turned))
         for where, result in results:
             sp_ref[where, :] = result
@@ -205,19 +199,29 @@
     return result
 
 
+OWN = ((0, 1, 2, 3), 2)
+BESIDE = (((0, 1), 6), ((2, 3), -2))
+
+
 def place_in_facts(facts_ref, start=0):
-    return lambda column: (facts_ref[0, start + column], facts_ref[1, start + column])
-
-
-def facts_of(packed_ref, row):
-    return packed_ref[row : row + 16, :].astype(F32).astype(jnp.int32)[0:8, :]
+    return lambda column: [facts_ref[row, start + column] for row in (0, 1, 4, 5, 6)]
+
+
+def facts_of(packed_ref, row, shift_i):
+    facts = packed_ref[row : row + 16, :].astype(F32).astype(jnp.int32)
+    by, bz, kinds, live = (facts[index : index + 1, :] for index in range(4))
+    begin = 4 * by - 2
+    edge = jnp.where(by == 0, 0, jnp.where(by == NY // 8 - 1, 1, 2))
+    turn = begin - 8 * shift_i
+    rows = [4 * bz, begin, kinds, live, edge, turn & (LANES - 1), -turn & (LANES - 1), by]
+    return jnp.concatenate(rows, axis=0)
 
 
 def own_kernel(packed_ref, stencil_ref,
                g0, g1, g2, g3, edge_ref, stk_ref, out_facts, fp_ref, rows_ref, facts_ref, sems):
     copy = pltpu.make_async_copy(stencil_ref, rows_ref, sems.at[0])
     copy.start()
-    out_facts[...] = facts_of(packed_ref, PANELS)
+    out_facts[...] = facts_of(packed_ref, PANELS, OWN[1])
     facts_copy = pltpu.make_async_copy(out_facts, facts_ref, sems.at[1])
     facts_copy.start()
     for ref in (g0, g1, g2, g3, edge_ref):
@@ -239,10 +243,7 @@
     def _():
         footprints(packed_ref[:, 0:LANES], stk_ref, fp_ref, 0)
 
-    scatter_columns(fp_ref, 0, place_in_facts(facts_ref), live, (g0, g1, g2, g3), edge_ref, (0, 1, 2, 3), 2)
-
-
-BESIDE = (((0, 1), 6), ((2, 3), -2))
+    scatter_columns(fp_ref, 0, place_in_facts(facts_ref), live, (g0, g1, g2, g3), edge_ref, OWN[0])
 
 
 def chunks_beside(facts_ref, slots):
@@ -273,8 +274,8 @@
         pool_ref[before, :] = first_ref[...]
         pool_ref[after, :] = second_ref[...]
 
-    for side in range(2):
-        out_facts[:, side * slots : (side + 1) * slots] = facts_of(pool_ref, 2 * side * height + PANELS)
+    for side, (_, shift_i) in enumerate(BESIDE):
+        out_facts[:, side * slots : (side + 1) * slots] = facts_of(pool_ref, 2 * side * height + PANELS, shift_i)
     copy = pltpu.make_async_copy(out_facts, facts_ref, sem)
     copy.start()
 
@@ -293,9 +294,9 @@
             def _(first=first):
                 project(first)
 
-        for side, (planes, shift_i) in enumerate(BESIDE):
+        for side, (planes, _) in enumerate(BESIDE):
             scatter_columns(fp_ref, 2 * first + side * LANES, place_in_facts(facts_ref, side * slots + first),
-                            counts[side], (g0, g1, g2, g3), edge_ref, planes, shift_i)
+                            counts[side], (g0, g1, g2, g3), edge_ref, planes)
     for ref in (g0, g1, g2, g3, edge_ref):
         ref[0:8, :] += ref[NZ:ZROWS, :]
     total = pltpu.roll(edge_ref[0:LANES, :], 2, 1)
@@ -492,7 +493,7 @@
     widen_edge(edge_ref, wide_ref)
     live = facts_ref[3, 0]
     slots = kinds_ref.shape[1]
-    sample_columns((p0, p1, p2, p3), wide_ref, place_in_facts(facts_ref), live, sp_ref, 0, (0, 1, 2, 3), 2)
+    sample_columns((p0, p1, p2, p3), wide_ref, place_in_facts(facts_ref), live, sp_ref, 0, OWN[0])
 
     @pl.when(live > LANES)
     def _():
@@ -510,9 +511,9 @@
     outs = (out0, out1)
     for first, counts in chunks_beside(facts_ref, slots):
         here = slice(first, first + LANES)
-        for side, (planes, shift_i) in enumerate(BESIDE):
+        for side, (planes, _) in enumerate(BESIDE):
             sample_columns((p0, p1, p2, p3), wide_ref, place_in_facts(facts_ref, side * slots + first),
-                           counts[side], sp_ref, 2 * first + side * LANES, planes, shift_i)
+                           counts[side], sp_ref, 2 * first + side * LANES, planes)
 
         @pl.when(counts[0] + counts[1] > 0)
         def _(first=first, counts=counts, here=here):

time: 84.9 us -> 81.6 us (0.961)
  Pallas kernels: 24.5 us -> 20.1 us
  starting transfers between devices: 13.9 us -> 15.3 us
    pallas_call x1, Pallas kernels: 6.1 us -> 3.65 us  [body(): pl.pallas_call(beside_kernel, out_shape=(grid,) * 5 + (shape_of(LANES, LA...]
    pallas_call x1, Pallas kernels: 5.43 us -> 3.24 us  [body(): pl.pallas_call(beside_sample_kernel, out_shape=(sums, sums), in_specs=[SM...]
    all_to_all x2, starting transfers between devices: 5.21 us -> 6.14 us  [exchanged(): values = lax.all_to_all(values, axes, 0, 0, tiled=True)]
  transfers between devices with their start and end apart: 9 -> 9, of which waited for: 7 -> 7; matrix products, arithmetic and copies ran while one was open for 0% -> 0% of each run, Pallas kernels for 8% -> 9%
where the time goes in v9:
time: 81.6 us; the launch traced here: 81 us
  waiting for transfers between devices  39.4 us (48%)
  Pallas kernels  20.1 us (25%)
  starting transfers between devices  15.3 us (19%)
  other arithmetic  2.83 us (3%)
  local copies, waits for them, and re-layouts  2.42 us (3%)
  between operations  0.96 us (1%)
    all_to_all x2, waiting for transfers between devices, exchanged(): values = lax.all_to_all(values, axes, 0, 0, tiled=True)  31 us
    ppermute x7, starting transfers between devices, moved(): return lax.ppermute(values, both, pairs)  9.13 us
    ppermute x7, waiting for transfers between devices, moved(): return lax.ppermute(values, both, pairs)  8.45 us
    all_to_all x2, starting transfers between devices, exchanged(): values = lax.all_to_all(values, axes, 0, 0, tiled=True)  6.14 us
    pallas_call x1, Pallas kernels, body(): pl.pallas_call(beside_kernel, out_shape=(grid,) * 5 + (shape_of(LANES, LA...  3.65 us
    pallas_call x1, Pallas kernels, body(): pl.pallas_call(functools.partial(plane_kernel, slabs, planes), out_shape=...  3.46 us
    pallas_call x1, Pallas kernels, body(): pl.pallas_call(beside_sample_kernel, out_shape=(sums, sums), in_specs=[SM...  3.24 us
    pallas_call x1, Pallas kernels, body(): pl.pallas_call(own_kernel, out_shape=(grid,) * 5 + (shape_of(KS * PANELS,...  2.79 us
  transfers between devices with their start and end apart: 9, of which 7 were waited for; matrix products, arithmetic and copies ran while one was open for 0% of the time, Pallas kernels for 9%

profile of v9, /device:TPU:0, one launch (start us, length us, event | category | flops | bytes accessed | tf_op | source)
XLA Modules:
  0.0 81.0 jit_solution(5321813822295184944)
XLA Ops:
  0.7 0.9 %fusion.packed_ref.own_ref = bf16[80,256]{1,0:T(8,128)(2,1)S(1)} fusion(s32[80]{0:T(128)S(1)} %compare_select_fusion, s32[256]{0:T(256)} %param.16, s32[]{:T(128)} %bitcast.16, s32[256]{0:T(256)} %param.17, bf16[64,256]{1,0:T(8,128)(2,1)} %param.14, pred[80]{0:T(512)(128)(4,1)S(1)} %get-tuple-element.63, pred[80]{0:T(512)(128)(4,1)S(1)} %get-tuple-element.64, ...), kind=kLoop, calls=%fused_computation.4 | loop fusion | flops 143360 | bytes 76596 | tf_op jit(solution)/shard_map/jit(_where)/select_n | solution.py:602
  1.6 3.0 %collective-permute-start = (bf16[80,256]{1,0:T(8,128)(2,1)S(1)}, bf16[80,256]{1,0:T(8,128)(2,1)S(1)}, u32[]{:S(2)}, u32[]{:S(2)}) collective-permute-start(bf16[80,256]{1,0:T(8,128)(2,1)S(1)} %fusion.packed_ref.own_ref), channel_id=1, source_target_pairs={{0,2},{1,3},{2,0},{3,1},{4,6},{5,7},{6,4},{7,5},{8,10},{9,11},{10,... | collective-permute-start | bytes 122888 | tf_op jit(solution)/shard_map/ppermute | solution.py:583
  4.6 4.5 %collective-permute-start.1 = (bf16[80,256]{1,0:T(8,128)(2,1)S(1)}, bf16[80,256]{1,0:T(8,128)(2,1)S(1)}, u32[]{:S(2)}, u32[]{:S(2)}) collective-permute-start(bf16[80,256]{1,0:T(8,128)(2,1)S(1)} %fusion.packed_ref.own_ref), channel_id=1, source_target_pairs={{0,30},{1,31},{2,4},{3,5},{4,2},{5,3},{6,8},{7,9},{8,6},{9,7},{10,... | collective-permute-start | bytes 122888 | tf_op jit(solution)/shard_map/ppermute | solution.py:583
  9.1 1.2 %copy-done = bf16[16,64,512]{2,1,0:T(8,128)(2,1)S(1)} copy-done((bf16[16,64,512]{2,1,0:T(8,128)(2,1)S(1)}, bf16[16,64,512]{2,1,0:T(8,128)(2,1)}, u32[]{:S(2)}) %copy-start) | copy-done | bytes 1048600
  10.3 2.8 %own_scatter.1 = (f32[520,128]{1,0:T(8,128)S(1)}, f32[520,128]{1,0:T(8,128)S(1)}, f32[520,128]{1,0:T(8,128)S(1)}, f32[520,128]{1,0:T(8,128)S(1)}, f32[520,128]{1...) custom-call(bf16[80,256]{1,0:T(8,128)(2,1)S(1)} %fusion.packed_ref.own_ref, ...), custom_call_target="tpu_custom_call" | custom-call | tf_op jit(solution)/shard_map/own_scatter/pallas_call | solution.py:607
  13.2 0.0 collective-permute-done.first_ref
  13.2 0.0 collective-permute-done.1.second_ref
  13.2 0.0 copy-start.2
  13.2 3.7 %beside_scatter.1 = (f32[520,128]{1,0:T(8,128)S(1)}, f32[520,128]{1,0:T(8,128)S(1)}, f32[520,128]{1,0:T(8,128)S(1)}, f32[520,128]{1,0:T(8,128)S(1)}, f32[520,128...) custom-call(s32[1]{0:T(128)} %bitcast.2.odd_ref, ...), custom_call_target="tpu_custom_call", output_to_operand_aliasing={{0}: (5, {}), {1}: (6, {}), {2}: (7, {}), {3}: (8, {}), {4}... | custom-call | tf_op jit(solution)/shard_map/beside_scatter/pallas_call | solution.py:622
  16.8 0.1 collective-permute-start.2
  16.9 1.2 %collective-permute-done.2.edge_ref = f32[128,128]{1,0:T(8,128)S(1)} collective-permute-done((f32[128,128]{1,0:T(8,128)S(1)}, f32[128,128]{1,0:T(8,128)S(1)}, u32[]{:S(2)}, u32[]{:S(2)}) %collective-permute-start.2) | collective-permute-done | bytes 65568 | tf_op jit(solution)/shard_map/ppermute | solution.py:583
  18.2 1.3 %z_forward.1 = f32[2304,128]{1,0:T(8,128)S(1)} custom-call(f32[520,128]{1,0:T(8,128)S(1)} %get-tuple-element.41.g0, f32[520,128]{1,0:T(8,128)S(1)} %get-tuple-element.42.g1, f32[520,128]{1,0:T(8,128)S(1)} %get-tuple-element.43.g2, f32[520,128]{1,0:T(8,128)S(1)} %get-tuple-element.44.g3, f32[128,128]{1,0:T(8,128)S(1)} %collective-permute-done.2.edge_ref, ...), custom_call_target="tpu_custom_call" | custom-call | tf_op jit(solution)/shard_map/z_forward/pallas_call | solution.py:646
  19.5 0.0 copy-start.1
  19.5 0.0 copy-start.6
  19.5 0.9 %convert_element_type.19 = f16[2304,128]{1,0:T(8,128)(2,1)} convert(f32[2304,128]{1,0:T(8,128)S(1)} %z_forward.1) | non-fusion elementwise | flops 294912 | bytes 1769472 | tf_op jit(solution)/shard_map/convert_element_type | solution.py:657
  20.4 3.5 %all-to-all-start = ((f16[32,72,128]{2,1,0:T(8,128)(2,1)}), f16[32,72,128]{2,1,0:T(8,128)(2,1)S(1)}, u32[]{:S(2)}, u32[]{:S(2)}) async-start(f16[32,72,128]{2,1,0:T(8,128)(2,1)} %bitcast.19), calls=%async_computation | async-start | bytes 1179648 | tf_op jit(solution)/shard_map/all_to_all | solution.py:658
  24.0 0.3 hat_order.1.hat_ref
  24.3 0.0 copy-start.4
  24.3 0.0 copy-start.5
  24.3 17.9 %all-to-all-done = f16[32,72,128]{2,1,0:T(8,128)(2,1)S(1)} async-done(((f16[32,72,128]{2,1,0:T(8,128)(2,1)}), f16[32,72,128]{2,1,0:T(8,128)(2,1)S(1)}, u32[]{:S(2)}, u32[]{:S(2)}) %all-to-all-start) | async-done | bytes 589856 | tf_op jit(solution)/shard_map/all_to_all | solution.py:658
  42.2 0.1 bitcast_convert_fusion.in_ref
  42.3 0.0 copy-done.4
  42.3 0.0 copy-done.5
  42.3 3.5 %plane_filter.1 = (f32[2304,128]{1,0:T(8,128)S(1)}, f32[8,128]{1,0:T(8,128)S(1)}) custom-call(f32[2304,128]{1,0:T(8,128)S(1)} %bitcast_convert_fusion.in_ref, f32[8,64,256]{2,1,0:T(8,128)S(1)} %hat_order.1.hat_ref, bf16[1024,256]{1,0:T(8,128)(2,1)S(1)} %copy-done.4, bf16[512,128]{1,0:T(8,128)(2,1)S(1)} %copy-done.5), custom_call_target="tpu_custom_call" | custom-call | tf_op jit(solution)/shard_map/plane_filter/pallas_call | solution.py:690
  45.8 0.1 convert.7
  45.9 0.0 copy-start.8
  45.9 0.0 copy-start.9
  45.9 0.0 copy-start.7
  45.9 0.9 %slice.5 = f16[32,64,128]{2,1,0:T(8,128)(2,1)} slice(f16[32,72,128]{2,1,0:T(8,128)(2,1)S(1)} %bitcast.20), slice={[0:32], [0:64], [0:128]} | slice | bytes 1048576 | tf_op jit(solution)/shard_map/slice | solution.py:657
  46.9 2.6 %all-to-all-start.1 = ((f16[32,64,128]{2,1,0:T(8,128)(2,1)}), f16[32,64,128]{2,1,0:T(8,128)(2,1)S(1)}, u32[]{:S(2)}, u32[]{:S(2)}) async-start(f16[32,64,128]{2,1,0:T(8,128)(2,1)} %slice.5), calls=%async_computation.1 | async-start | bytes 1048576 | tf_op jit(solution)/shard_map/all_to_all | solution.py:658
  49.5 0.0 copy-start.3
  49.5 0.2 reshape.28.table_ref
  49.7 0.2 collective-permute-start.3
  49.9 1.2 %collective-permute-done.3.there_ref = bf16[240,256]{1,0:T(8,128)(2,1)S(1)} collective-permute-done((bf16[240,256]{1,0:T(8,128)(2,1)S(1)}, bf16[240,256]{1,0:T(8,128)(2,1)S(1)}, u32[]{:S(2)}, u32[]{:S(2)}) %collective-permute-start.3) | collective-permute-done | bytes 122912 | tf_op jit(solution)/shard_map/ppermute | solution.py:583
  51.1 0.0 copy-done.7
  51.1 2.1 %near_field.1 = f32[64,256]{1,0:T(8,128)S(1)} custom-call(s32[1]{0:T(128)} %copy.25.live_ref, bf16[240,256]{1,0:T(8,128)(2,1)S(1)} %get-tuple-element.51.here_ref, bf16[240,256]{1,0:T(8,128)(2,1)S(1)} %collective-permute-done.3.there_ref, s32[8,256]{1,0:T(8,128)S(1)} %fusion.5.source_ref, s32[8,256]{1,0:T(8,128)S(1)} %bitcast.18, ...), custom_call_target="tpu_custom_call" | custom-call | tf_op jit(solution)/shard_map/near_field/pallas_call | solution.py:681
  53.3 13.1 %all-to-all-done.1 = f16[32,64,128]{2,1,0:T(8,128)(2,1)S(1)} async-done(((f16[32,64,128]{2,1,0:T(8,128)(2,1)}), f16[32,64,128]{2,1,0:T(8,128)(2,1)S(1)}, u32[]{:S(2)}, u32[]{:S(2)}) %all-to-all-start.1) | async-done | bytes 524320 | tf_op jit(solution)/shard_map/all_to_all | solution.py:658
  66.3 0.1 bitcast_convert_fusion.1.in_ref
  66.4 1.4 %z_inverse.1 = (f32[520,128]{1,0:T(8,128)S(1)}, f32[520,128]{1,0:T(8,128)S(1)}, f32[520,128]{1,0:T(8,128)S(1)}, f32[520,128]{1,0:T(8,128)S(1)}, bf16[128,128]{1,0:T(8,128)(2,1)S(1)}) custom-call(f32[2048,128]{1,0:T(8,128)S(1)} %bitcast_convert_fusion.1.in_ref, f32[8,128]{1,0:T(8,128)S(1)} %get-tuple-element.53.exponent_ref, bf16[1024,256]{1,0:T(8,128)(2,1)S(1)} %copy-done.3), custom_call_target="tpu_custom_call" | custom-call | tf_op jit(solution)/shard_map/z_inverse/pallas_call | solution.py:701
  67.8 0.1 collective-permute-start.4
  67.9 1.2 %collective-permute-done.4.edge_ref = bf16[128,128]{1,0:T(8,128)(2,1)S(1)} collective-permute-done((bf16[128,128]{1,0:T(8,128)(2,1)S(1)}, bf16[128,128]{1,0:T(8,128)(2,1)S(1)}, u32[]{:S(2)}, u32[]{:S(2)}) %collective-permute-start.4) | collective-permute-done | bytes 32800 | tf_op jit(solution)/shard_map/ppermute | solution.py:583
  69.1 3.2 %beside_sample.1 = (f32[64,256]{1,0:T(8,128)S(1)}, f32[64,256]{1,0:T(8,128)S(1)}) custom-call(s32[1]{0:T(128)} %bitcast.2.odd_ref, s32[8,512]{1,0:T(8,128)S(1)} %get-tuple-element.60.facts_ref.kinds_ref, f32[520,128]{1,0:T(8,128)S(1)} %get-tuple-element.54.p0, f32[520,128]{1,0:T(8,128)S(1)} %get-tuple-element.55.p1, f32[520,128]{1,0:T(8,128)S(1)} %get-tuple-element.56.p2, ...), custom_call_target="tpu_custom_call" | custom-call | tf_op jit(solution)/shard_map/beside_sample/pallas_call | solution.py:715
  72.4 0.1 collective-permute-start.5
  72.4 1.2 %collective-permute-start.6 = (f32[64,256]{1,0:T(8,128)S(1)}, f32[64,256]{1,0:T(8,128)S(1)}, u32[]{:S(2)}, u32[]{:S(2)}) collective-permute-start(f32[64,256]{1,0:T(8,128)S(1)} %get-tuple-element.62), channel_id=1, source_target_pairs={{0,30},{1,31},{2,4},{3,5},{4,2},{5,3},{6,8},{7,9},{8,6},{9,7},{10,... | collective-permute-start | bytes 196616 | tf_op jit(solution)/shard_map/ppermute | solution.py:583
  73.6 1.9 %own_sample.1 = f32[64,256]{1,0:T(8,128)S(1)} custom-call(s32[8,256]{1,0:T(8,128)S(1)} %get-tuple-element.34.facts_ref.kinds_ref, f32[520,128]{1,0:T(8,128)S(1)} %get-tuple-element.54.p0, f32[520,128]{1,0:T(8,128)S(1)} %get-tuple-element.55.p1, f32[520,128]{1,0:T(8,128)S(1)} %get-tuple-element.56.p2, f32[520,128]{1,0:T(8,128)S(1)} %get-tuple-element.57.p3, ...), custom_call_target="tpu_custom_call" | custom-call | tf_op jit(solution)/shard_map/own_sample/pallas_call | solution.py:726
  75.5 1.4 %collective-permute-done.5 = f32[64,256]{1,0:T(8,128)S(1)} collective-permute-done((f32[64,256]{1,0:T(8,128)S(1)}, f32[64,256]{1,0:T(8,128)S(1)}, u32[]{:S(2)}, u32[]{:S(2)}) %collective-permute-start.5) | collective-permute-done | bytes 65568 | tf_op jit(solution)/shard_map/ppermute | solution.py:583
  77.0 3.4 %collective-permute-done.6 = f32[64,256]{1,0:T(8,128)S(1)} collective-permute-done((f32[64,256]{1,0:T(8,128)S(1)}, f32[64,256]{1,0:T(8,128)S(1)}, u32[]{:S(2)}, u32[]{:S(2)}) %collective-permute-start.6) | collective-permute-done | bytes 65568 | tf_op jit(solution)/shard_map/ppermute | solution.py:583
  80.4 0.6 add_add_fusion
  (12 shorter events, 0.1 us)
Async XLA Ops:
  1.6 11.6 %collective-permute-start = (bf16[80,256]{1,0:T(8,128)(2,1)S(1)}, bf16[80,256]{1,0:T(8,128)(2,1)S(1)}, u32[]{:S(2)}, u32[]{:S(2)}) collective-permute-start(bf16[80,256]{1,0:T(8,128)(2,1)S(1)} %fusion.packed_ref.own_ref), channel_id=1, source_target_pairs={{0,2},{1,3},{2,0},{3,1},{4,6},{5,7},{6,4},{7,5},{8,10},{9,11},{10,... | collective-permute-start | bytes 122888 | tf_op jit(solution)/shard_map/ppermute | solution.py:583
  4.6 8.6 %collective-permute-start.1 = (bf16[80,256]{1,0:T(8,128)(2,1)S(1)}, bf16[80,256]{1,0:T(8,128)(2,1)S(1)}, u32[]{:S(2)}, u32[]{:S(2)}) collective-permute-start(bf16[80,256]{1,0:T(8,128)(2,1)S(1)} %fusion.packed_ref.own_ref), channel_id=1, source_target_pairs={{0,30},{1,31},{2,4},{3,5},{4,2},{5,3},{6,8},{7,9},{8,6},{9,7},{10,... | collective-permute-start | bytes 122888 | tf_op jit(solution)/shard_map/ppermute | solution.py:583
  9.1 1.2 %copy-start = (bf16[16,64,512]{2,1,0:T(8,128)(2,1)S(1)}, bf16[16,64,512]{2,1,0:T(8,128)(2,1)}, u32[]{:S(2)}) copy-start(bf16[16,64,512]{2,1,0:T(8,128)(2,1)} %param.18) | copy-start | bytes 3145732
  13.2 5.0 %copy-start.2 = (bf16[1152,256]{1,0:T(8,128)(2,1)S(1)}, bf16[1152,256]{1,0:T(8,128)(2,1)}, u32[]{:S(2)}) copy-start(bf16[1152,256]{1,0:T(8,128)(2,1)} %constant.88.clone.w_ref) | copy-start | bytes 1769476
  16.8 1.3 %collective-permute-start.2 = (f32[128,128]{1,0:T(8,128)S(1)}, f32[128,128]{1,0:T(8,128)S(1)}, u32[]{:S(2)}, u32[]{:S(2)}) collective-permute-start(f32[128,128]{1,0:T(8,128)S(1)} %get-tuple-element.45), channel_id=1, source_target_pairs={{0,1},{1,0},{2,3},{3,2},{4,5},{5,4},{6,7},{7,6},{8,9},{9,8},{10,11... | collective-permute-start | bytes 196616 | tf_op jit(solution)/shard_map/ppermute | solution.py:583
  19.5 4.5 %copy-start.1 = (f32[16,64,256]{2,1,0:T(8,128)S(1)}, f32[16,64,256]{2,1,0:T(8,128)}, u32[]{:S(2)}) copy-start(f32[16,64,256]{2,1,0:T(8,128)} %hat_ref) | copy-start | bytes 3145732
  19.5 4.5 %copy-start.6 = (bf16[128,128]{1,0:T(8,128)(2,1)S(1)}, bf16[128,128]{1,0:T(8,128)(2,1)}, u32[]{:S(2)}) copy-start(bf16[128,128]{1,0:T(8,128)(2,1)} %constant.89.clone.turn_ref) | copy-start | bytes 98308
  20.4 21.8 %all-to-all-start = ((f16[32,72,128]{2,1,0:T(8,128)(2,1)}), f16[32,72,128]{2,1,0:T(8,128)(2,1)S(1)}, u32[]{:S(2)}, u32[]{:S(2)}) async-start(f16[32,72,128]{2,1,0:T(8,128)(2,1)} %bitcast.19), calls=%async_computation | async-start | bytes 1179648 | tf_op jit(solution)/shard_map/all_to_all | solution.py:658
  24.3 18.1 %copy-start.4 = (bf16[1024,256]{1,0:T(8,128)(2,1)S(1)}, bf16[1024,256]{1,0:T(8,128)(2,1)}, u32[]{:S(2)}) copy-start(bf16[1024,256]{1,0:T(8,128)(2,1)} %constant.90.clone.y_ref) | copy-start | bytes 1572868
  24.3 18.1 %copy-start.5 = (bf16[512,128]{1,0:T(8,128)(2,1)S(1)}, bf16[512,128]{1,0:T(8,128)(2,1)}, u32[]{:S(2)}) copy-start(bf16[512,128]{1,0:T(8,128)(2,1)} %constant.91.clone.x_ref) | copy-start | bytes 393220
  45.9 3.6 %copy-start.8 = (bf16[64,16,64]{2,1,0:T(8,128)(2,1)S(1)}, bf16[64,16,64]{2,1,0:T(8,128)(2,1)}, u32[]{:S(2)}) copy-start(bf16[64,16,64]{2,1,0:T(8,128)(2,1)} %param.21) | copy-start | bytes 393220
  45.9 4.0 %copy-start.9 = (s32[256,8]{0,1:T(8,128)S(1)}, s32[256,8]{0,1:T(8,128)}, u32[]{:S(2)}) copy-start(s32[256,8]{0,1:T(8,128)} %param.19) | copy-start | bytes 24580
  45.9 5.2 %copy-start.7 = (s32[256,8]{0,1:T(8,128)S(1)}, s32[256,8]{0,1:T(8,128)}, u32[]{:S(2)}) copy-start(s32[256,8]{0,1:T(8,128)} %param.20) | copy-start | bytes 24580
  46.9 19.4 %all-to-all-start.1 = ((f16[32,64,128]{2,1,0:T(8,128)(2,1)}), f16[32,64,128]{2,1,0:T(8,128)(2,1)S(1)}, u32[]{:S(2)}, u32[]{:S(2)}) async-start(f16[32,64,128]{2,1,0:T(8,128)(2,1)} %slice.5), calls=%async_computation.1 | async-start | bytes 1048576 | tf_op jit(solution)/shard_map/all_to_all | solution.py:658
  49.5 16.9 %copy-start.3 = (bf16[1024,256]{1,0:T(8,128)(2,1)S(1)}, bf16[1024,256]{1,0:T(8,128)(2,1)}, u32[]{:S(2)}) copy-start(bf16[1024,256]{1,0:T(8,128)(2,1)} %constant.92.clone.v_ref) | copy-start | bytes 1572868
  49.7 1.4 %collective-permute-start.3 = (bf16[240,256]{1,0:T(8,128)(2,1)S(1)}, bf16[240,256]{1,0:T(8,128)(2,1)S(1)}, u32[]{:S(2)}, u32[]{:S(2)}) collective-permute-start(bf16[240,256]{1,0:T(8,128)(2,1)S(1)} %get-tuple-element.51.here_ref), channel_id=1, source_target_pairs={{0,1},{1,0},{2,3},{3,2},{4,5},{5,4},{6,7},{7,6},{8,9},{9,8},{10,11... | collective-permute-start | bytes 368648 | tf_op jit(solution)/shard_map/ppermute | solution.py:583
  67.8 1.3 %collective-permute-start.4 = (bf16[128,128]{1,0:T(8,128)(2,1)S(1)}, bf16[128,128]{1,0:T(8,128)(2,1)S(1)}, u32[]{:S(2)}, u32[]{:S(2)}) collective-permute-start(bf16[128,128]{1,0:T(8,128)(2,1)S(1)} %get-tuple-element.58), channel_id=1, source_target_pairs={{0,1},{1,0},{2,3},{3,2},{4,5},{5,4},{6,7},{7,6},{8,9},{9,8},{10,11... | collective-permute-start | bytes 98312 | tf_op jit(solution)/shard_map/ppermute | solution.py:583
  72.4 4.6 %collective-permute-start.5 = (f32[64,256]{1,0:T(8,128)S(1)}, f32[64,256]{1,0:T(8,128)S(1)}, u32[]{:S(2)}, u32[]{:S(2)}) collective-permute-start(f32[64,256]{1,0:T(8,128)S(1)} %get-tuple-element.61), channel_id=1, source_target_pairs={{0,2},{1,3},{2,0},{3,1},{4,6},{5,7},{6,4},{7,5},{8,10},{9,11},{10,... | collective-permute-start | bytes 196616 | tf_op jit(solution)/shard_map/ppermute | solution.py:583
  72.4 7.9 %collective-permute-start.6 = (f32[64,256]{1,0:T(8,128)S(1)}, f32[64,256]{1,0:T(8,128)S(1)}, u32[]{:S(2)}, u32[]{:S(2)}) collective-permute-start(f32[64,256]{1,0:T(8,128)S(1)} %get-tuple-element.62), channel_id=1, source_target_pairs={{0,30},{1,31},{2,4},{3,5},{4,2},{5,3},{6,8},{7,9},{8,6},{9,7},{10,... | collective-permute-start | bytes 196616 | tf_op jit(solution)/shard_map/ppermute | solution.py:583

commit v10 on v9

--- a/solution.py
+++ b/solution.py
@@ -115,8 +115,9 @@
     spread = jnp.concatenate(
         [jnp.where(offset == kind, charges, 0.0).astype(BF16) for kind in range(0, KS, 2)], axis=1
     )
+    result = dot(spread, stk_ref[...])
     for pair in range(4):
-        part = dot(spread, stk_ref[:, pair * LANES : (pair + 1) * LANES])
+        part = result[:, pair * LANES : (pair + 1) * LANES]
         fp_ref[pl.ds(first * 8 + 2 * pair, count, stride=8), :] = part
         fp_ref[pl.ds(first * 8 + 2 * pair + 1, count, stride=8), :] = pltpu.roll(part, 64, 1)
 
@@ -133,7 +134,7 @@
     return code
 
 
-def scatter_columns(fp_ref, first, place_of, count, grids, edge_ref, planes):
+def scatter_columns(fp_ref, first, place_of, count, sets, planes):
     shape = (8, LANES)
     lanes = [lane_in(plane, shape) for plane in planes]
     codes = edge_codes(planes, shape)
@@ -148,8 +149,9 @@
             terms = [jnp.where(((lane - begin) & -8) == 0, turned, 0.0) for lane in lanes]
             terms.append(jnp.where(codes == edge, turned, 0.0))
             updates.append((pl.ds(row, 8), terms))
-        refs = [grids[plane] for plane in planes] + [edge_ref]
-        for where, terms in updates:
+        for inner, (where, terms) in enumerate(updates):
+            grids = sets[inner % 2]
+            refs = [grids[plane] for plane in planes] + [grids[4]]
             sums = [ref[where, :] + term for ref, term in zip(refs, terms)]
             for ref, total in zip(refs, sums):
                 ref[where, :] = total
@@ -217,14 +219,14 @@
     return jnp.concatenate(rows, axis=0)
 
 
-def own_kernel(packed_ref, stencil_ref,
-               g0, g1, g2, g3, edge_ref, stk_ref, out_facts, fp_ref, rows_ref, facts_ref, sems):
+def own_kernel(packed_ref, stencil_ref, *refs):
+    grids, (stk_ref, out_facts, fp_ref, rows_ref, facts_ref, sems) = refs[:10], refs[10:]
     copy = pltpu.make_async_copy(stencil_ref, rows_ref, sems.at[0])
     copy.start()
     out_facts[...] = facts_of(packed_ref, PANELS, OWN[1])
     facts_copy = pltpu.make_async_copy(out_facts, facts_ref, sems.at[1])
     facts_copy.start()
-    for ref in (g0, g1, g2, g3, edge_ref):
+    for ref in grids:
         ref[...] = jnp.zeros_like(ref)
     shape = (POINTS, POINTS)
     point = lax.broadcasted_iota(jnp.int32, shape, 0)
@@ -243,7 +245,7 @@
     def _():
         footprints(packed_ref[:, 0:LANES], stk_ref, fp_ref, 0)
 
-    scatter_columns(fp_ref, 0, place_in_facts(facts_ref), live, (g0, g1, g2, g3), edge_ref, OWN[0])
+    scatter_columns(fp_ref, 0, place_in_facts(facts_ref), live, (grids[:5], grids[5:]), OWN[0])
 
 
 def chunks_beside(facts_ref, slots):
@@ -258,8 +260,8 @@
     )
 
 
-def beside_kernel(odd_ref, own_ref, first_ref, second_ref, stk_ref, i0, i1, i2, i3, iedge,
-                  g0, g1, g2, g3, edge_ref, out_edge, out_facts, pool_ref, fp_ref, facts_ref, sem):
+def beside_kernel(odd_ref, own_ref, first_ref, second_ref, stk_ref, *refs):
+    grids, (out_edge, out_facts, pool_ref, fp_ref, facts_ref, sem) = refs[10:20], refs[20:]
     height, slots = own_ref.shape
     before, after = pl.ds(0, height), pl.ds(2 * height, height)
     pool_ref[height : 2 * height, :] = own_ref[...]
@@ -296,9 +298,11 @@
 
         for side, (planes, _) in enumerate(BESIDE):
             scatter_columns(fp_ref, 2 * first + side * LANES, place_in_facts(facts_ref, side * slots + first),
-                            counts[side], (g0, g1, g2, g3), edge_ref, planes)
-    for ref in (g0, g1, g2, g3, edge_ref):
+                            counts[side], (grids[:5], grids[5:]), planes)
+    for ref, other in zip(grids[:5], grids[5:]):
+        ref[...] += other[...]
         ref[0:8, :] += ref[NZ:ZROWS, :]
+    edge_ref = grids[4]
     total = pltpu.roll(edge_ref[0:LANES, :], 2, 1)
     for block in range(1, 4):
         total += pltpu.roll(edge_ref[block * LANES : (block + 1) * LANES, :], 32 * block + 2, 1)
@@ -606,9 +610,9 @@
     grid = shape_of(ZROWS, LANES)
     *grids, stk, facts = pl.pallas_call(
         own_kernel,
-        out_shape=(grid,) * 5 + (shape_of(KS * PANELS, POINTS, dtype=BF16), shape_of(8, slots, dtype=jnp.int32)),
+        out_shape=(grid,) * 10 + (shape_of(KS * PANELS, POINTS, dtype=BF16), shape_of(8, slots, dtype=jnp.int32)),
         in_specs=[VMEM, pl.BlockSpec(memory_space=pl.ANY)],
-        out_specs=(VMEM,) * 7,
+        out_specs=(VMEM,) * 12,
         scratch_shapes=[
             pltpu.VMEM((slots * 8, LANES), F32),
             pltpu.VMEM((KS * PANELS, POINTS), BF16),
@@ -621,25 +625,25 @@
 
     g = pl.pallas_call(
         beside_kernel,
-        out_shape=(grid,) * 5
+        out_shape=(grid,) * 10
         + (
             shape_of(LANES, LANES),
             shape_of(8, 2 * slots, dtype=jnp.int32),
             shape_of(3 * (PANELS + 16), slots, dtype=BF16),
         ),
-        in_specs=[SMEM] + [VMEM] * 9,
-        out_specs=(VMEM,) * 8,
+        in_specs=[SMEM] + [VMEM] * 14,
+        out_specs=(VMEM,) * 13,
         scratch_shapes=[
             pltpu.VMEM((2 * slots * 8, LANES), F32),
             pltpu.SMEM((8, 2 * slots), jnp.int32),
             pltpu.SemaphoreType.DMA,
         ],
-        input_output_aliases={5: 0, 6: 1, 7: 2, 8: 3, 9: 4},
+        input_output_aliases={5 + index: index for index in range(10)},
         compiler_params=PARAMS,
         name="beside_scatter",
     )(odd, packed, from_first, from_second, stk, *grids)
-    facts2 = g[6]
-    edge = to_other_tile(g[5])
+    facts2 = g[11]
+    edge = to_other_tile(g[10])
 
     forward, inverse = z_tables(slabs, tiles)
     rows = owners * (4 * parts + SCALE_ROWS)
@@ -675,7 +679,7 @@
     )(offset, hat, jnp.asarray(reversal()))
 
     got, hat = lax.optimization_barrier((got, hat))
-    pool = (g[7], to_other_tile(g[7]))
+    pool = (g[12], to_other_tile(g[12]))
     direction = near_source // slots
     pool_index = (direction // 3 * 2 + (direction % 3 != 1).astype(jnp.int32)) * slots + near_source % slots
     near = pl.pallas_call(

time: 81.6 us -> 83.3 us (1.021)
  local copies, waits for them, and re-layouts: 2.42 us -> 4.1 us
  Pallas kernels: 20.1 us -> 21.1 us
    unnamed x20 -> x28, local copies, waits for them, and re-layouts: 1.28 us -> 2.94 us
where the time goes in v10:
time: 83.3 us; the launch traced here: 83.2 us
  waiting for transfers between devices  39.4 us (47%)
  Pallas kernels  21.1 us (25%)
  starting transfers between devices  14.9 us (18%)
  local copies, waits for them, and re-layouts  4.1 us (5%)
  other arithmetic  2.8 us (3%)
  between operations  0.97 us (1%)
    all_to_all x2, waiting for transfers between devices, exchanged(): values = lax.all_to_all(values, axes, 0, 0, tiled=True)  31 us
    ppermute x7, starting transfers between devices, moved(): return lax.ppermute(values, both, pairs)  8.96 us
    ppermute x7, waiting for transfers between devices, moved(): return lax.ppermute(values, both, pairs)  8.49 us
    all_to_all x2, starting transfers between devices, exchanged(): values = lax.all_to_all(values, axes, 0, 0, tiled=True)  5.9 us
    pallas_call x1, Pallas kernels, body(): pl.pallas_call(beside_kernel, out_shape=(grid,) * 10 + (shape_of(LANES, L...  4.02 us
    pallas_call x1, Pallas kernels, body(): pl.pallas_call(functools.partial(plane_kernel, slabs, planes), out_shape=...  3.46 us
    pallas_call x1, Pallas kernels, body(): pl.pallas_call(beside_sample_kernel, out_shape=(sums, sums), in_specs=[SM...  3.25 us
    pallas_call x1, Pallas kernels, body(): pl.pallas_call(own_kernel, out_shape=(grid,) * 10 + (shape_of(KS * PANELS...  3.05 us
  transfers between devices with their start and end apart: 9, of which 7 were waited for; matrix products, arithmetic and copies ran while one was open for 0% of the time, Pallas kernels for 9%

profile of v10, /device:TPU:0, one launch (start us, length us, event | category | flops | bytes accessed | tf_op | source)
XLA Modules:
  0.0 83.2 jit_solution(18102665395160200764)
XLA Ops:
  0.7 0.9 %fusion.packed_ref.own_ref = bf16[80,256]{1,0:T(8,128)(2,1)S(1)} fusion(s32[80]{0:T(128)S(1)} %compare_select_fusion, s32[256]{0:T(256)} %param.16, s32[]{:T(128)} %bitcast.16, s32[256]{0:T(256)} %param.17, bf16[64,256]{1,0:T(8,128)(2,1)} %param.14, pred[80]{0:T(512)(128)(4,1)S(1)} %get-tuple-element.73, pred[80]{0:T(512)(128)(4,1)S(1)} %get-tuple-element.74, ...), kind=kLoop, calls=%fused_computation.4 | loop fusion | flops 143360 | bytes 76596 | tf_op jit(solution)/shard_map/jit(_where)/select_n | solution.py:606
  1.6 3.0 %collective-permute-start = (bf16[80,256]{1,0:T(8,128)(2,1)S(1)}, bf16[80,256]{1,0:T(8,128)(2,1)S(1)}, u32[]{:S(2)}, u32[]{:S(2)}) collective-permute-start(bf16[80,256]{1,0:T(8,128)(2,1)S(1)} %fusion.packed_ref.own_ref), channel_id=1, source_target_pairs={{0,2},{1,3},{2,0},{3,1},{4,6},{5,7},{6,4},{7,5},{8,10},{9,11},{10,... | collective-permute-start | bytes 122888 | tf_op jit(solution)/shard_map/ppermute | solution.py:587
  4.6 4.5 %collective-permute-start.1 = (bf16[80,256]{1,0:T(8,128)(2,1)S(1)}, bf16[80,256]{1,0:T(8,128)(2,1)}, u32[]{:S(2)}, u32[]{:S(2)}) collective-permute-start(bf16[80,256]{1,0:T(8,128)(2,1)S(1)} %fusion.packed_ref.own_ref), channel_id=1, source_target_pairs={{0,30},{1,31},{2,4},{3,5},{4,2},{5,3},{6,8},{7,9},{8,6},{9,7},{10,... | collective-permute-start | bytes 122888 | tf_op jit(solution)/shard_map/ppermute | solution.py:587
  9.1 1.2 %copy-done = bf16[16,64,512]{2,1,0:T(8,128)(2,1)S(1)} copy-done((bf16[16,64,512]{2,1,0:T(8,128)(2,1)S(1)}, bf16[16,64,512]{2,1,0:T(8,128)(2,1)}, u32[]{:S(2)}) %copy-start) | copy-done | bytes 1048600
  10.3 3.0 %own_scatter.1 = (f32[520,128]{1,0:T(8,128)S(1)}, f32[520,128]{1,0:T(8,128)S(1)}, f32[520,128]{1,0:T(8,128)S(1)}, f32[520,128]{1,0:T(8,128)S(1)}, f32[520,128]{1...) custom-call(bf16[80,256]{1,0:T(8,128)(2,1)S(1)} %fusion.packed_ref.o, ...), custom_call_target="tpu_custom_call" | custom-call | tf_op jit(solution)/shard_map/own_scatter/pallas_call | solution.py:611
  13.4 0.7 copy-done.5
  14.1 0.0 collective-permute-done.first_ref
  14.1 0.0 collective-permute-done.1.second_ref
  14.1 0.9 %copy-done.6 = f32[520,128]{1,0:T(8,128)S(1)} copy-done((f32[520,128]{1,0:T(8,128)S(1)}, f32[520,128]{1,0:T(8,128)}, u32[]{:S(2)}) %copy-start.6) | copy-done | bytes 266264
  15.1 4.0 %beside_scatter.1 = (f32[520,128]{1,0:T(8,128)S(1)}, f32[520,128]{1,0:T(8,128)S(1)}, f32[520,128]{1,0:T(8,128)S(1)}, f32[520,128]{1,0:T(8,128)S(1)}, f32[520,128...) custom-call(s32[1]{0:T(128)} %bitcast.2.odd_ref, ...), custom_call_target="tpu_custom_call", output_to_operand_aliasing={{0}: (5, {}), {1}: (6, {}), {2}: (7, {}), {3}: (8, {}), {4}... | custom-call | tf_op jit(solution)/shard_map/beside_scatter/pallas_call | solution.py:626
  19.1 0.1 collective-permute-start.2
  19.2 1.2 %collective-permute-done.2.edge_ref = f32[128,128]{1,0:T(8,128)S(1)} collective-permute-done((f32[128,128]{1,0:T(8,128)S(1)}, f32[128,128]{1,0:T(8,128)S(1)}, u32[]{:S(2)}, u32[]{:S(2)}) %collective-permute-start.2) | collective-permute-done | bytes 65568 | tf_op jit(solution)/shard_map/ppermute | solution.py:587
  20.4 0.0 copy-done.2
  20.4 1.3 %z_forward.1 = f32[2304,128]{1,0:T(8,128)S(1)} custom-call(f32[520,128]{1,0:T(8,128)S(1)} %get-tuple-element.51.g0, f32[520,128]{1,0:T(8,128)S(1)} %get-tuple-element.52.g1, f32[520,128]{1,0:T(8,128)S(1)} %get-tuple-element.53.g2, f32[520,128]{1,0:T(8,128)S(1)} %get-tuple-element.54.g3, f32[128,128]{1,0:T(8,128)S(1)} %collective-permute-done.2.edge_ref, ...), custom_call_target="tpu_custom_call" | custom-call | tf_op jit(solution)/shard_map/z_forward/pallas_call | solution.py:650
  21.7 0.0 copy-start.1
  21.7 0.0 copy-start.10
  21.8 0.9 %convert_element_type.19 = f16[2304,128]{1,0:T(8,128)(2,1)} convert(f32[2304,128]{1,0:T(8,128)S(1)} %z_forward.1) | non-fusion elementwise | flops 294912 | bytes 1769472 | tf_op jit(solution)/shard_map/convert_element_type | solution.py:661
  22.7 3.3 %all-to-all-start = ((f16[32,72,128]{2,1,0:T(8,128)(2,1)}), f16[32,72,128]{2,1,0:T(8,128)(2,1)S(1)}, u32[]{:S(2)}, u32[]{:S(2)}) async-start(f16[32,72,128]{2,1,0:T(8,128)(2,1)} %bitcast.19), calls=%async_computation | async-start | bytes 1179648 | tf_op jit(solution)/shard_map/all_to_all | solution.py:662
  26.0 0.3 hat_order.1.hat_ref
  26.3 0.0 copy-start.4
  26.3 0.0 copy-start.7
  26.3 17.9 %all-to-all-done = f16[32,72,128]{2,1,0:T(8,128)(2,1)S(1)} async-done(((f16[32,72,128]{2,1,0:T(8,128)(2,1)}), f16[32,72,128]{2,1,0:T(8,128)(2,1)S(1)}, u32[]{:S(2)}, u32[]{:S(2)}) %all-to-all-start) | async-done | bytes 589856 | tf_op jit(solution)/shard_map/all_to_all | solution.py:662
  44.2 0.1 bitcast_convert_fusion.in_ref
  44.3 0.0 copy-done.4
  44.3 3.5 %plane_filter.1 = (f32[2304,128]{1,0:T(8,128)S(1)}, f32[8,128]{1,0:T(8,128)S(1)}) custom-call(f32[2304,128]{1,0:T(8,128)S(1)} %bitcast_convert_fusion.in_ref, f32[8,64,256]{2,1,0:T(8,128)S(1)} %hat_order.1.hat_ref, bf16[1024,256]{1,0:T(8,128)(2,1)S(1)} %copy-done.4, bf16[512,128]{1,0:T(8,128)(2,1)S(1)} %copy-done.7), custom_call_target="tpu_custom_call" | custom-call | tf_op jit(solution)/shard_map/plane_filter/pallas_call | solution.py:694
  47.8 0.1 convert.7
  47.9 0.0 copy-start.12
  47.9 0.0 copy-start.13
  47.9 0.0 copy-start.11
  47.9 1.0 %slice.5 = f16[32,64,128]{2,1,0:T(8,128)(2,1)} slice(f16[32,72,128]{2,1,0:T(8,128)(2,1)S(1)} %bitcast.20), slice={[0:32], [0:64], [0:128]} | slice | bytes 1048576 | tf_op jit(solution)/shard_map/slice | solution.py:661
  48.9 2.6 %all-to-all-start.1 = ((f16[32,64,128]{2,1,0:T(8,128)(2,1)}), f16[32,64,128]{2,1,0:T(8,128)(2,1)S(1)}, u32[]{:S(2)}, u32[]{:S(2)}) async-start(f16[32,64,128]{2,1,0:T(8,128)(2,1)} %slice.5), calls=%async_computation.1 | async-start | bytes 1048576 | tf_op jit(solution)/shard_map/all_to_all | solution.py:662
  51.5 0.0 copy-start.3
  51.5 0.2 reshape.28.table_ref
  51.8 0.2 collective-permute-start.3
  52.0 1.2 %collective-permute-done.3.there_ref = bf16[240,256]{1,0:T(8,128)(2,1)S(1)} collective-permute-done((bf16[240,256]{1,0:T(8,128)(2,1)S(1)}, bf16[240,256]{1,0:T(8,128)(2,1)S(1)}, u32[]{:S(2)}, u32[]{:S(2)}) %collective-permute-start.3) | collective-permute-done | bytes 122912 | tf_op jit(solution)/shard_map/ppermute | solution.py:587
  53.2 2.1 %near_field.1 = f32[64,256]{1,0:T(8,128)S(1)} custom-call(s32[1]{0:T(128)} %copy.35.live_ref, bf16[240,256]{1,0:T(8,128)(2,1)S(1)} %copy-done.9, bf16[240,256]{1,0:T(8,128)(2,1)S(1)} %collective-permute-done.3.there_ref, s32[8,256]{1,0:T(8,128)S(1)} %fusion.5.source_ref, s32[8,256]{1,0:T(8,128)S(1)} %bitcast.18, bf16[64,1024]{1,0:T(8,128)(2,1)S(1)} %reshape.28.table_ref), custom_call_target="tpu_custom_call" | custom-call | tf_op jit(solution)/shard_map/near_field/pallas_call | solution.py:685
  55.3 13.0 %all-to-all-done.1 = f16[32,64,128]{2,1,0:T(8,128)(2,1)S(1)} async-done(((f16[32,64,128]{2,1,0:T(8,128)(2,1)}), f16[32,64,128]{2,1,0:T(8,128)(2,1)S(1)}, u32[]{:S(2)}, u32[]{:S(2)}) %all-to-all-start.1) | async-done | bytes 524320 | tf_op jit(solution)/shard_map/all_to_all | solution.py:662
  68.4 0.1 bitcast_convert_fusion.1.in_ref
  68.5 1.4 %z_inverse.1 = (f32[520,128]{1,0:T(8,128)S(1)}, f32[520,128]{1,0:T(8,128)S(1)}, f32[520,128]{1,0:T(8,128)S(1)}, f32[520,128]{1,0:T(8,128)S(1)}, bf16[128,128]{1,0:T(8,128)(2,1)S(1)}) custom-call(f32[2048,128]{1,0:T(8,128)S(1)} %bitcast_convert_fusion.1.in_ref, f32[8,128]{1,0:T(8,128)S(1)} %get-tuple-element.63.exponent_ref, bf16[1024,256]{1,0:T(8,128)(2,1)S(1)} %copy-done.3), custom_call_target="tpu_custom_call" | custom-call | tf_op jit(solution)/shard_map/z_inverse/pallas_call | solution.py:705
  69.9 0.1 collective-permute-start.4
  69.9 1.2 %collective-permute-done.4.edge_ref = bf16[128,128]{1,0:T(8,128)(2,1)S(1)} collective-permute-done((bf16[128,128]{1,0:T(8,128)(2,1)S(1)}, bf16[128,128]{1,0:T(8,128)(2,1)S(1)}, u32[]{:S(2)}, u32[]{:S(2)}) %collective-permute-start.4) | collective-permute-done | bytes 32800 | tf_op jit(solution)/shard_map/ppermute | solution.py:587
  71.1 3.3 %beside_sample.1 = (f32[64,256]{1,0:T(8,128)S(1)}, f32[64,256]{1,0:T(8,128)S(1)}) custom-call(s32[1]{0:T(128)} %bitcast.2.odd_ref, s32[8,512]{1,0:T(8,128)S(1)} %get-tuple-element.70.facts_ref.kinds_ref, f32[520,128]{1,0:T(8,128)S(1)} %get-tuple-element.64.p0, f32[520,128]{1,0:T(8,128)S(1)} %get-tuple-element.65.p1, f32[520,128]{1,0:T(8,128)S(1)} %get-tuple-element.66.p2, ...), custom_call_target="tpu_custom_call" | custom-call | tf_op jit(solution)/shard_map/beside_sample/pallas_call | solution.py:719
  74.4 0.3 collective-permute-start.5
  74.7 0.8 collective-permute-start.6
  75.5 2.2 %own_sample.1 = f32[64,256]{1,0:T(8,128)S(1)} custom-call(s32[8,256]{1,0:T(8,128)S(1)} %get-tuple-element.39.facts_ref.kinds_ref, f32[520,128]{1,0:T(8,128)S(1)} %get-tuple-element.64.p0, f32[520,128]{1,0:T(8,128)S(1)} %get-tuple-element.65.p1, f32[520,128]{1,0:T(8,128)S(1)} %get-tuple-element.66.p2, f32[520,128]{1,0:T(8,128)S(1)} %get-tuple-element.67.p3, ...), custom_call_target="tpu_custom_call" | custom-call | tf_op jit(solution)/shard_map/own_sample/pallas_call | solution.py:730
  77.7 1.0 %collective-permute-done.5 = f32[64,256]{1,0:T(8,128)S(1)} collective-permute-done((f32[64,256]{1,0:T(8,128)S(1)}, f32[64,256]{1,0:T(8,128)S(1)}, u32[]{:S(2)}, u32[]{:S(2)}) %collective-permute-start.5) | collective-permute-done | bytes 65568 | tf_op jit(solution)/shard_map/ppermute | solution.py:587
  78.8 3.8 %collective-permute-done.6 = f32[64,256]{1,0:T(8,128)S(1)} collective-permute-done((f32[64,256]{1,0:T(8,128)S(1)}, f32[64,256]{1,0:T(8,128)S(1)}, u32[]{:S(2)}, u32[]{:S(2)}) %collective-permute-start.6) | collective-permute-done | bytes 65568 | tf_op jit(solution)/shard_map/ppermute | solution.py:587
  82.6 0.6 add_add_fusion
  (20 shorter events, 0.1 us)
Async XLA Ops:
  1.6 12.5 %collective-permute-start = (bf16[80,256]{1,0:T(8,128)(2,1)S(1)}, bf16[80,256]{1,0:T(8,128)(2,1)S(1)}, u32[]{:S(2)}, u32[]{:S(2)}) collective-permute-start(bf16[80,256]{1,0:T(8,128)(2,1)S(1)} %fusion.packed_ref.own_ref), channel_id=1, source_target_pairs={{0,2},{1,3},{2,0},{3,1},{4,6},{5,7},{6,4},{7,5},{8,10},{9,11},{10,... | collective-permute-start | bytes 122888 | tf_op jit(solution)/shard_map/ppermute | solution.py:587
  4.6 9.5 %collective-permute-start.1 = (bf16[80,256]{1,0:T(8,128)(2,1)S(1)}, bf16[80,256]{1,0:T(8,128)(2,1)}, u32[]{:S(2)}, u32[]{:S(2)}) collective-permute-start(bf16[80,256]{1,0:T(8,128)(2,1)S(1)} %fusion.packed_ref.own_ref), channel_id=1, source_target_pairs={{0,30},{1,31},{2,4},{3,5},{4,2},{5,3},{6,8},{7,9},{8,6},{9,7},{10,... | collective-permute-start | bytes 122888 | tf_op jit(solution)/shard_map/ppermute | solution.py:587
  9.1 1.2 %copy-start = (bf16[16,64,512]{2,1,0:T(8,128)(2,1)S(1)}, bf16[16,64,512]{2,1,0:T(8,128)(2,1)}, u32[]{:S(2)}) copy-start(bf16[16,64,512]{2,1,0:T(8,128)(2,1)} %param.18) | copy-start | bytes 3145732
  13.4 0.7 copy-start.5
  14.1 1.0 %copy-start.6 = (f32[520,128]{1,0:T(8,128)S(1)}, f32[520,128]{1,0:T(8,128)}, u32[]{:S(2)}) copy-start(f32[520,128]{1,0:T(8,128)} %copy-done.5) | copy-start | bytes 798724
  15.1 5.4 %copy-start.2 = (bf16[1152,256]{1,0:T(8,128)(2,1)S(1)}, bf16[1152,256]{1,0:T(8,128)(2,1)}, u32[]{:S(2)}) copy-start(bf16[1152,256]{1,0:T(8,128)(2,1)} %constant.88.clone.w_ref) | copy-start | bytes 1769476
  19.1 2.6 %copy-start.8 = (bf16[240,256]{1,0:T(8,128)(2,1)}, bf16[240,256]{1,0:T(8,128)(2,1)S(1)}, u32[]{:S(2)}) copy-start(bf16[240,256]{1,0:T(8,128)(2,1)S(1)} %get-tuple-element.61.here_ref) | copy-start | bytes 368644
  19.1 1.3 %collective-permute-start.2 = (f32[128,128]{1,0:T(8,128)S(1)}, f32[128,128]{1,0:T(8,128)S(1)}, u32[]{:S(2)}, u32[]{:S(2)}) collective-permute-start(f32[128,128]{1,0:T(8,128)S(1)} %get-tuple-element.55), channel_id=1, source_target_pairs={{0,1},{1,0},{2,3},{3,2},{4,5},{5,4},{6,7},{7,6},{8,9},{9,8},{10,11... | collective-permute-start | bytes 196616 | tf_op jit(solution)/shard_map/ppermute | solution.py:587
  21.7 4.2 %copy-start.1 = (f32[16,64,256]{2,1,0:T(8,128)S(1)}, f32[16,64,256]{2,1,0:T(8,128)}, u32[]{:S(2)}) copy-start(f32[16,64,256]{2,1,0:T(8,128)} %hat_ref) | copy-start | bytes 3145732
  21.7 4.2 %copy-start.10 = (bf16[128,128]{1,0:T(8,128)(2,1)S(1)}, bf16[128,128]{1,0:T(8,128)(2,1)}, u32[]{:S(2)}) copy-start(bf16[128,128]{1,0:T(8,128)(2,1)} %constant.89.clone.turn_ref) | copy-start | bytes 98308
  22.7 21.5 %all-to-all-start = ((f16[32,72,128]{2,1,0:T(8,128)(2,1)}), f16[32,72,128]{2,1,0:T(8,128)(2,1)S(1)}, u32[]{:S(2)}, u32[]{:S(2)}) async-start(f16[32,72,128]{2,1,0:T(8,128)(2,1)} %bitcast.19), calls=%async_computation | async-start | bytes 1179648 | tf_op jit(solution)/shard_map/all_to_all | solution.py:662
  26.3 18.1 %copy-start.4 = (bf16[1024,256]{1,0:T(8,128)(2,1)S(1)}, bf16[1024,256]{1,0:T(8,128)(2,1)}, u32[]{:S(2)}) copy-start(bf16[1024,256]{1,0:T(8,128)(2,1)} %constant.90.clone.y_ref) | copy-start | bytes 1572868
  26.3 18.1 %copy-start.7 = (bf16[512,128]{1,0:T(8,128)(2,1)S(1)}, bf16[512,128]{1,0:T(8,128)(2,1)}, u32[]{:S(2)}) copy-start(bf16[512,128]{1,0:T(8,128)(2,1)} %constant.91.clone.x_ref) | copy-start | bytes 393220
  47.9 3.6 %copy-start.12 = (bf16[64,16,64]{2,1,0:T(8,128)(2,1)S(1)}, bf16[64,16,64]{2,1,0:T(8,128)(2,1)}, u32[]{:S(2)}) copy-start(bf16[64,16,64]{2,1,0:T(8,128)(2,1)} %param.21) | copy-start | bytes 393220
  47.9 3.8 %copy-start.9 = (bf16[240,256]{1,0:T(8,128)(2,1)S(1)}, bf16[240,256]{1,0:T(8,128)(2,1)}, u32[]{:S(2)}) copy-start(bf16[240,256]{1,0:T(8,128)(2,1)} %copy-done.8) | copy-start | bytes 368644
  47.9 4.0 %copy-start.13 = (s32[256,8]{0,1:T(8,128)S(1)}, s32[256,8]{0,1:T(8,128)}, u32[]{:S(2)}) copy-start(s32[256,8]{0,1:T(8,128)} %param.19) | copy-start | bytes 24580
  47.9 5.2 %copy-start.11 = (s32[256,8]{0,1:T(8,128)S(1)}, s32[256,8]{0,1:T(8,128)}, u32[]{:S(2)}) copy-start(s32[256,8]{0,1:T(8,128)} %param.20) | copy-start | bytes 24580
  48.9 19.4 %all-to-all-start.1 = ((f16[32,64,128]{2,1,0:T(8,128)(2,1)}), f16[32,64,128]{2,1,0:T(8,128)(2,1)S(1)}, u32[]{:S(2)}, u32[]{:S(2)}) async-start(f16[32,64,128]{2,1,0:T(8,128)(2,1)} %slice.5), calls=%async_computation.1 | async-start | bytes 1048576 | tf_op jit(solution)/shard_map/all_to_all | solution.py:662
  51.5 16.9 %copy-start.3 = (bf16[1024,256]{1,0:T(8,128)(2,1)S(1)}, bf16[1024,256]{1,0:T(8,128)(2,1)}, u32[]{:S(2)}) copy-start(bf16[1024,256]{1,0:T(8,128)(2,1)} %constant.92.clone.v_ref) | copy-start | bytes 1572868
  51.8 1.4 %collective-permute-start.3 = (bf16[240,256]{1,0:T(8,128)(2,1)S(1)}, bf16[240,256]{1,0:T(8,128)(2,1)S(1)}, u32[]{:S(2)}, u32[]{:S(2)}) collective-permute-start(bf16[240,256]{1,0:T(8,128)(2,1)S(1)} %copy-done.9), channel_id=1, source_target_pairs={{0,1},{1,0},{2,3},{3,2},{4,5},{5,4},{6,7},{7,6},{8,9},{9,8},{10,11... | collective-permute-start | bytes 368648 | tf_op jit(solution)/shard_map/ppermute | solution.py:587
  69.9 1.3 %collective-permute-start.4 = (bf16[128,128]{1,0:T(8,128)(2,1)S(1)}, bf16[128,128]{1,0:T(8,128)(2,1)S(1)}, u32[]{:S(2)}, u32[]{:S(2)}) collective-permute-start(bf16[128,128]{1,0:T(8,128)(2,1)S(1)} %get-tuple-element.68), channel_id=1, source_target_pairs={{0,1},{1,0},{2,3},{3,2},{4,5},{5,4},{6,7},{7,6},{8,9},{9,8},{10,11... | collective-permute-start | bytes 98312 | tf_op jit(solution)/shard_map/ppermute | solution.py:587
  74.4 4.4 %collective-permute-start.5 = (f32[64,256]{1,0:T(8,128)S(1)}, f32[64,256]{1,0:T(8,128)S(1)}, u32[]{:S(2)}, u32[]{:S(2)}) collective-permute-start(f32[64,256]{1,0:T(8,128)S(1)} %get-tuple-element.71), channel_id=1, source_target_pairs={{0,2},{1,3},{2,0},{3,1},{4,6},{5,7},{6,4},{7,5},{8,10},{9,11},{10,... | collective-permute-start | bytes 196616 | tf_op jit(solution)/shard_map/ppermute | solution.py:587
  74.7 7.9 %collective-permute-start.6 = (f32[64,256]{1,0:T(8,128)S(1)}, f32[64,256]{1,0:T(8,128)S(1)}, u32[]{:S(2)}, u32[]{:S(2)}) collective-permute-start(f32[64,256]{1,0:T(8,128)S(1)} %get-tuple-element.72), channel_id=1, source_target_pairs={{0,30},{1,31},{2,4},{3,5},{4,2},{5,3},{6,8},{7,9},{8,6},{9,7},{10,... | collective-permute-start | bytes 196616 | tf_op jit(solution)/shard_map/ppermute | solution.py:587

commit v11 on v9

--- a/solution.py
+++ b/solution.py
@@ -18,7 +18,7 @@
 KN = 16
 LANES = 128
 ZROWS = NZ + 8
-UNROLL = 16
+UNROLL = 32
 HALF = NY // 2
 SCALE_ROWS = 8
 BOUND = 12.0
@@ -115,8 +115,9 @@
     spread = jnp.concatenate(
         [jnp.where(offset == kind, charges, 0.0).astype(BF16) for kind in range(0, KS, 2)], axis=1
     )
+    result = dot(spread, stk_ref[...])
     for pair in range(4):
-        part = dot(spread, stk_ref[:, pair * LANES : (pair + 1) * LANES])
+        part = result[:, pair * LANES : (pair + 1) * LANES]
         fp_ref[pl.ds(first * 8 + 2 * pair, count, stride=8), :] = part
         fp_ref[pl.ds(first * 8 + 2 * pair + 1, count, stride=8), :] = pltpu.roll(part, 64, 1)
 
@@ -155,7 +156,7 @@
                 ref[where, :] = total
         return carry
 
-    lax.fori_loop(0, lax.shift_right_logical(count + UNROLL - 1, 4), step, 0)
+    lax.fori_loop(0, lax.shift_right_logical(count + UNROLL - 1, 5), step, 0)
 
 
 def sample_columns(pot_refs, edge_ref, place_of, count, sp_ref, first, planes):
@@ -178,7 +179,7 @@
             sp_ref[where, :] = result
         return carry
 
-    lax.fori_loop(0, lax.shift_right_logical(count + UNROLL - 1, 4), step, 0)
+    lax.fori_loop(0, lax.shift_right_logical(count + UNROLL - 1, 5), step, 0)
 
 
 def far_sums(sp_ref, kinds, stk_ref, first):

time: 81.6 us -> 80.7 us (0.989)
  Pallas kernels: 20.1 us -> 18.4 us
  transfers between devices with their start and end apart: 9 -> 9, of which waited for: 7 -> 7; matrix products, arithmetic and copies ran while one was open for 0% -> 0% of each run, Pallas kernels for 9% -> 8%
where the time goes in v11:
time: 80.7 us; the launch traced here: 80.1 us
  waiting for transfers between devices  39.4 us (49%)
  Pallas kernels  18.4 us (23%)
  starting transfers between devices  16 us (20%)
  other arithmetic  2.83 us (4%)
  local copies, waits for them, and re-layouts  2.42 us (3%)
  between operations  0.96 us (1%)
    all_to_all x2, waiting for transfers between devices, exchanged(): values = lax.all_to_all(values, axes, 0, 0, tiled=True)  31 us
    ppermute x7, starting transfers between devices, moved(): return lax.ppermute(values, both, pairs)  9.36 us
    ppermute x7, waiting for transfers between devices, moved(): return lax.ppermute(values, both, pairs)  8.47 us
    all_to_all x2, starting transfers between devices, exchanged(): values = lax.all_to_all(values, axes, 0, 0, tiled=True)  6.62 us
    pallas_call x1, Pallas kernels, body(): pl.pallas_call(functools.partial(plane_kernel, slabs, planes), out_shape=...  3.46 us
    pallas_call x1, Pallas kernels, body(): pl.pallas_call(beside_kernel, out_shape=(grid,) * 5 + (shape_of(LANES, LA...  2.88 us
    pallas_call x1, Pallas kernels, body(): pl.pallas_call(own_kernel, out_shape=(grid,) * 5 + (shape_of(KS * PANELS,...  2.65 us
    pallas_call x1, Pallas kernels, body(): pl.pallas_call(beside_sample_kernel, out_shape=(sums, sums), in_specs=[SM...  2.61 us
  transfers between devices with their start and end apart: 9, of which 7 were waited for; matrix products, arithmetic and copies ran while one was open for 0% of the time, Pallas kernels for 8%

profile of v11, /device:TPU:0, one launch (start us, length us, event | category | flops | bytes accessed | tf_op | source)
XLA Modules:
  0.0 80.1 jit_solution(12425450132478922562)
XLA Ops:
  0.7 0.9 %fusion.packed_ref.own_ref = bf16[80,256]{1,0:T(8,128)(2,1)S(1)} fusion(s32[80]{0:T(128)S(1)} %compare_select_fusion, s32[256]{0:T(256)} %param.16, s32[]{:T(128)} %bitcast.16, s32[256]{0:T(256)} %param.17, bf16[64,256]{1,0:T(8,128)(2,1)} %param.14, pred[80]{0:T(512)(128)(4,1)S(1)} %get-tuple-element.63, pred[80]{0:T(512)(128)(4,1)S(1)} %get-tuple-element.64, ...), kind=kLoop, calls=%fused_computation.4 | loop fusion | flops 143360 | bytes 76596 | tf_op jit(solution)/shard_map/jit(_where)/select_n | solution.py:603
  1.6 3.0 %collective-permute-start = (bf16[80,256]{1,0:T(8,128)(2,1)S(1)}, bf16[80,256]{1,0:T(8,128)(2,1)S(1)}, u32[]{:S(2)}, u32[]{:S(2)}) collective-permute-start(bf16[80,256]{1,0:T(8,128)(2,1)S(1)} %fusion.packed_ref.own_ref), channel_id=1, source_target_pairs={{0,2},{1,3},{2,0},{3,1},{4,6},{5,7},{6,4},{7,5},{8,10},{9,11},{10,... | collective-permute-start | bytes 122888 | tf_op jit(solution)/shard_map/ppermute | solution.py:584
  4.6 4.5 %collective-permute-start.1 = (bf16[80,256]{1,0:T(8,128)(2,1)S(1)}, bf16[80,256]{1,0:T(8,128)(2,1)S(1)}, u32[]{:S(2)}, u32[]{:S(2)}) collective-permute-start(bf16[80,256]{1,0:T(8,128)(2,1)S(1)} %fusion.packed_ref.own_ref), channel_id=1, source_target_pairs={{0,30},{1,31},{2,4},{3,5},{4,2},{5,3},{6,8},{7,9},{8,6},{9,7},{10,... | collective-permute-start | bytes 122888 | tf_op jit(solution)/shard_map/ppermute | solution.py:584
  9.1 1.2 %copy-done = bf16[16,64,512]{2,1,0:T(8,128)(2,1)S(1)} copy-done((bf16[16,64,512]{2,1,0:T(8,128)(2,1)S(1)}, bf16[16,64,512]{2,1,0:T(8,128)(2,1)}, u32[]{:S(2)}) %copy-start) | copy-done | bytes 1048600
  10.3 2.7 %own_scatter.1 = (f32[520,128]{1,0:T(8,128)S(1)}, f32[520,128]{1,0:T(8,128)S(1)}, f32[520,128]{1,0:T(8,128)S(1)}, f32[520,128]{1,0:T(8,128)S(1)}, f32[520,128]{1...) custom-call(bf16[80,256]{1,0:T(8,128)(2,1)S(1)} %fusion.packed_ref.own_ref, ...), custom_call_target="tpu_custom_call" | custom-call | tf_op jit(solution)/shard_map/own_scatter/pallas_call | solution.py:608
  13.0 0.0 collective-permute-done.first_ref
  13.0 0.0 collective-permute-done.1.second_ref
  13.0 0.0 copy-start.2
  13.1 2.9 %beside_scatter.1 = (f32[520,128]{1,0:T(8,128)S(1)}, f32[520,128]{1,0:T(8,128)S(1)}, f32[520,128]{1,0:T(8,128)S(1)}, f32[520,128]{1,0:T(8,128)S(1)}, f32[520,128...) custom-call(s32[1]{0:T(128)} %bitcast.2.odd_ref, ...), custom_call_target="tpu_custom_call", output_to_operand_aliasing={{0}: (5, {}), {1}: (6, {}), {2}: (7, {}), {3}: (8, {}), {4}... | custom-call | tf_op jit(solution)/shard_map/beside_scatter/pallas_call | solution.py:623
  15.9 0.1 collective-permute-start.2
  16.0 1.2 %collective-permute-done.2.edge_ref = f32[128,128]{1,0:T(8,128)S(1)} collective-permute-done((f32[128,128]{1,0:T(8,128)S(1)}, f32[128,128]{1,0:T(8,128)S(1)}, u32[]{:S(2)}, u32[]{:S(2)}) %collective-permute-start.2) | collective-permute-done | bytes 65568 | tf_op jit(solution)/shard_map/ppermute | solution.py:584
  17.3 1.3 %z_forward.1 = f32[2304,128]{1,0:T(8,128)S(1)} custom-call(f32[520,128]{1,0:T(8,128)S(1)} %get-tuple-element.41.g0, f32[520,128]{1,0:T(8,128)S(1)} %get-tuple-element.42.g1, f32[520,128]{1,0:T(8,128)S(1)} %get-tuple-element.43.g2, f32[520,128]{1,0:T(8,128)S(1)} %get-tuple-element.44.g3, f32[128,128]{1,0:T(8,128)S(1)} %collective-permute-done.2.edge_ref, ...), custom_call_target="tpu_custom_call" | custom-call | tf_op jit(solution)/shard_map/z_forward/pallas_call | solution.py:647
  18.6 0.0 copy-start.1
  18.6 0.0 copy-start.6
  18.6 0.9 %convert_element_type.19 = f16[2304,128]{1,0:T(8,128)(2,1)} convert(f32[2304,128]{1,0:T(8,128)S(1)} %z_forward.1) | non-fusion elementwise | flops 294912 | bytes 1769472 | tf_op jit(solution)/shard_map/convert_element_type | solution.py:658
  19.5 4.0 %all-to-all-start = ((f16[32,72,128]{2,1,0:T(8,128)(2,1)}), f16[32,72,128]{2,1,0:T(8,128)(2,1)S(1)}, u32[]{:S(2)}, u32[]{:S(2)}) async-start(f16[32,72,128]{2,1,0:T(8,128)(2,1)} %bitcast.19), calls=%async_computation | async-start | bytes 1179648 | tf_op jit(solution)/shard_map/all_to_all | solution.py:659
  23.6 0.0 copy-done.1
  23.6 0.0 copy-done.6
  23.6 0.3 hat_order.1.hat_ref
  23.8 0.0 copy-start.4
  23.9 0.0 copy-start.5
  23.9 17.9 %all-to-all-done = f16[32,72,128]{2,1,0:T(8,128)(2,1)S(1)} async-done(((f16[32,72,128]{2,1,0:T(8,128)(2,1)}), f16[32,72,128]{2,1,0:T(8,128)(2,1)S(1)}, u32[]{:S(2)}, u32[]{:S(2)}) %all-to-all-start) | async-done | bytes 589856 | tf_op jit(solution)/shard_map/all_to_all | solution.py:659
  41.8 0.1 bitcast_convert_fusion.in_ref
  41.9 3.5 %plane_filter.1 = (f32[2304,128]{1,0:T(8,128)S(1)}, f32[8,128]{1,0:T(8,128)S(1)}) custom-call(f32[2304,128]{1,0:T(8,128)S(1)} %bitcast_convert_fusion.in_ref, f32[8,64,256]{2,1,0:T(8,128)S(1)} %hat_order.1.hat_ref, bf16[1024,256]{1,0:T(8,128)(2,1)S(1)} %copy-done.4, bf16[512,128]{1,0:T(8,128)(2,1)S(1)} %copy-done.5), custom_call_target="tpu_custom_call" | custom-call | tf_op jit(solution)/shard_map/plane_filter/pallas_call | solution.py:691
  45.4 0.1 convert.7
  45.5 0.0 copy-start.8
  45.5 0.0 copy-start.9
  45.5 0.0 copy-start.7
  45.5 0.9 %slice.5 = f16[32,64,128]{2,1,0:T(8,128)(2,1)} slice(f16[32,72,128]{2,1,0:T(8,128)(2,1)S(1)} %bitcast.20), slice={[0:32], [0:64], [0:128]} | slice | bytes 1048576 | tf_op jit(solution)/shard_map/slice | solution.py:658
  46.5 2.6 %all-to-all-start.1 = ((f16[32,64,128]{2,1,0:T(8,128)(2,1)}), f16[32,64,128]{2,1,0:T(8,128)(2,1)S(1)}, u32[]{:S(2)}, u32[]{:S(2)}) async-start(f16[32,64,128]{2,1,0:T(8,128)(2,1)} %slice.5), calls=%async_computation.1 | async-start | bytes 1048576 | tf_op jit(solution)/shard_map/all_to_all | solution.py:659
  49.1 0.0 copy-done.8
  49.1 0.0 copy-start.3
  49.1 0.2 reshape.28.table_ref
  49.3 0.2 collective-permute-start.3
  49.5 1.2 %collective-permute-done.3.there_ref = bf16[240,256]{1,0:T(8,128)(2,1)S(1)} collective-permute-done((bf16[240,256]{1,0:T(8,128)(2,1)S(1)}, bf16[240,256]{1,0:T(8,128)(2,1)S(1)}, u32[]{:S(2)}, u32[]{:S(2)}) %collective-permute-start.3) | collective-permute-done | bytes 122912 | tf_op jit(solution)/shard_map/ppermute | solution.py:584
  50.7 2.1 %near_field.1 = f32[64,256]{1,0:T(8,128)S(1)} custom-call(s32[1]{0:T(128)} %copy.25.live_ref, bf16[240,256]{1,0:T(8,128)(2,1)S(1)} %get-tuple-element.51.here_ref, bf16[240,256]{1,0:T(8,128)(2,1)S(1)} %collective-permute-done.3.there_ref, s32[8,256]{1,0:T(8,128)S(1)} %fusion.5.source_ref, s32[8,256]{1,0:T(8,128)S(1)} %bitcast.18, ...), custom_call_target="tpu_custom_call" | custom-call | tf_op jit(solution)/shard_map/near_field/pallas_call | solution.py:682
  52.8 13.1 %all-to-all-done.1 = f16[32,64,128]{2,1,0:T(8,128)(2,1)S(1)} async-done(((f16[32,64,128]{2,1,0:T(8,128)(2,1)}), f16[32,64,128]{2,1,0:T(8,128)(2,1)S(1)}, u32[]{:S(2)}, u32[]{:S(2)}) %all-to-all-start.1) | async-done | bytes 524320 | tf_op jit(solution)/shard_map/all_to_all | solution.py:659
  65.9 0.1 bitcast_convert_fusion.1.in_ref
  66.0 1.4 %z_inverse.1 = (f32[520,128]{1,0:T(8,128)S(1)}, f32[520,128]{1,0:T(8,128)S(1)}, f32[520,128]{1,0:T(8,128)S(1)}, f32[520,128]{1,0:T(8,128)S(1)}, bf16[128,128]{1,0:T(8,128)(2,1)S(1)}) custom-call(f32[2048,128]{1,0:T(8,128)S(1)} %bitcast_convert_fusion.1.in_ref, f32[8,128]{1,0:T(8,128)S(1)} %get-tuple-element.53.exponent_ref, bf16[1024,256]{1,0:T(8,128)(2,1)S(1)} %copy-done.3), custom_call_target="tpu_custom_call" | custom-call | tf_op jit(solution)/shard_map/z_inverse/pallas_call | solution.py:702
  67.4 0.1 collective-permute-start.4
  67.5 1.2 %collective-permute-done.4.edge_ref = bf16[128,128]{1,0:T(8,128)(2,1)S(1)} collective-permute-done((bf16[128,128]{1,0:T(8,128)(2,1)S(1)}, bf16[128,128]{1,0:T(8,128)(2,1)S(1)}, u32[]{:S(2)}, u32[]{:S(2)}) %collective-permute-start.4) | collective-permute-done | bytes 32800 | tf_op jit(solution)/shard_map/ppermute | solution.py:584
  68.7 2.6 %beside_sample.1 = (f32[64,256]{1,0:T(8,128)S(1)}, f32[64,256]{1,0:T(8,128)S(1)}) custom-call(s32[1]{0:T(128)} %bitcast.2.odd_ref, s32[8,512]{1,0:T(8,128)S(1)} %get-tuple-element.60.facts_ref.kinds_ref, f32[520,128]{1,0:T(8,128)S(1)} %get-tuple-element.54.p0, f32[520,128]{1,0:T(8,128)S(1)} %get-tuple-element.55.p1, f32[520,128]{1,0:T(8,128)S(1)} %get-tuple-element.56.p2, ...), custom_call_target="tpu_custom_call" | custom-call | tf_op jit(solution)/shard_map/beside_sample/pallas_call | solution.py:716
  71.3 0.1 collective-permute-start.5
  71.4 1.4 %collective-permute-start.6 = (f32[64,256]{1,0:T(8,128)S(1)}, f32[64,256]{1,0:T(8,128)S(1)}, u32[]{:S(2)}, u32[]{:S(2)}) collective-permute-start(f32[64,256]{1,0:T(8,128)S(1)} %get-tuple-element.62), channel_id=1, source_target_pairs={{0,30},{1,31},{2,4},{3,5},{4,2},{5,3},{6,8},{7,9},{8,6},{9,7},{10,... | collective-permute-start | bytes 196616 | tf_op jit(solution)/shard_map/ppermute | solution.py:584
  72.8 1.8 %own_sample.1 = f32[64,256]{1,0:T(8,128)S(1)} custom-call(s32[8,256]{1,0:T(8,128)S(1)} %get-tuple-element.34.facts_ref.kinds_ref, f32[520,128]{1,0:T(8,128)S(1)} %get-tuple-element.54.p0, f32[520,128]{1,0:T(8,128)S(1)} %get-tuple-element.55.p1, f32[520,128]{1,0:T(8,128)S(1)} %get-tuple-element.56.p2, f32[520,128]{1,0:T(8,128)S(1)} %get-tuple-element.57.p3, ...), custom_call_target="tpu_custom_call" | custom-call | tf_op jit(solution)/shard_map/own_sample/pallas_call | solution.py:727
  74.6 1.7 %collective-permute-done.5 = f32[64,256]{1,0:T(8,128)S(1)} collective-permute-done((f32[64,256]{1,0:T(8,128)S(1)}, f32[64,256]{1,0:T(8,128)S(1)}, u32[]{:S(2)}, u32[]{:S(2)}) %collective-permute-start.5) | collective-permute-done | bytes 65568 | tf_op jit(solution)/shard_map/ppermute | solution.py:584
  76.3 3.1 %collective-permute-done.6 = f32[64,256]{1,0:T(8,128)S(1)} collective-permute-done((f32[64,256]{1,0:T(8,128)S(1)}, f32[64,256]{1,0:T(8,128)S(1)}, u32[]{:S(2)}, u32[]{:S(2)}) %collective-permute-start.6) | collective-permute-done | bytes 65568 | tf_op jit(solution)/shard_map/ppermute | solution.py:584
  79.4 0.6 add_add_fusion
  (12 shorter events, 0.1 us)
Async XLA Ops:
  1.6 11.4 %collective-permute-start = (bf16[80,256]{1,0:T(8,128)(2,1)S(1)}, bf16[80,256]{1,0:T(8,128)(2,1)S(1)}, u32[]{:S(2)}, u32[]{:S(2)}) collective-permute-start(bf16[80,256]{1,0:T(8,128)(2,1)S(1)} %fusion.packed_ref.own_ref), channel_id=1, source_target_pairs={{0,2},{1,3},{2,0},{3,1},{4,6},{5,7},{6,4},{7,5},{8,10},{9,11},{10,... | collective-permute-start | bytes 122888 | tf_op jit(solution)/shard_map/ppermute | solution.py:584
  4.6 8.4 %collective-permute-start.1 = (bf16[80,256]{1,0:T(8,128)(2,1)S(1)}, bf16[80,256]{1,0:T(8,128)(2,1)S(1)}, u32[]{:S(2)}, u32[]{:S(2)}) collective-permute-start(bf16[80,256]{1,0:T(8,128)(2,1)S(1)} %fusion.packed_ref.own_ref), channel_id=1, source_target_pairs={{0,30},{1,31},{2,4},{3,5},{4,2},{5,3},{6,8},{7,9},{8,6},{9,7},{10,... | collective-permute-start | bytes 122888 | tf_op jit(solution)/shard_map/ppermute | solution.py:584
  9.1 1.2 %copy-start = (bf16[16,64,512]{2,1,0:T(8,128)(2,1)S(1)}, bf16[16,64,512]{2,1,0:T(8,128)(2,1)}, u32[]{:S(2)}) copy-start(bf16[16,64,512]{2,1,0:T(8,128)(2,1)} %param.18) | copy-start | bytes 3145732
  13.0 4.2 %copy-start.2 = (bf16[1152,256]{1,0:T(8,128)(2,1)S(1)}, bf16[1152,256]{1,0:T(8,128)(2,1)}, u32[]{:S(2)}) copy-start(bf16[1152,256]{1,0:T(8,128)(2,1)} %constant.88.clone.w_ref) | copy-start | bytes 1769476
  15.9 1.3 %collective-permute-start.2 = (f32[128,128]{1,0:T(8,128)S(1)}, f32[128,128]{1,0:T(8,128)S(1)}, u32[]{:S(2)}, u32[]{:S(2)}) collective-permute-start(f32[128,128]{1,0:T(8,128)S(1)} %get-tuple-element.45), channel_id=1, source_target_pairs={{0,1},{1,0},{2,3},{3,2},{4,5},{5,4},{6,7},{7,6},{8,9},{9,8},{10,11... | collective-permute-start | bytes 196616 | tf_op jit(solution)/shard_map/ppermute | solution.py:584
  18.6 5.0 %copy-start.1 = (f32[16,64,256]{2,1,0:T(8,128)S(1)}, f32[16,64,256]{2,1,0:T(8,128)}, u32[]{:S(2)}) copy-start(f32[16,64,256]{2,1,0:T(8,128)} %hat_ref) | copy-start | bytes 3145732
  18.6 5.0 %copy-start.6 = (bf16[128,128]{1,0:T(8,128)(2,1)S(1)}, bf16[128,128]{1,0:T(8,128)(2,1)}, u32[]{:S(2)}) copy-start(bf16[128,128]{1,0:T(8,128)(2,1)} %constant.89.clone.turn_ref) | copy-start | bytes 98308
  19.5 22.3 %all-to-all-start = ((f16[32,72,128]{2,1,0:T(8,128)(2,1)}), f16[32,72,128]{2,1,0:T(8,128)(2,1)S(1)}, u32[]{:S(2)}, u32[]{:S(2)}) async-start(f16[32,72,128]{2,1,0:T(8,128)(2,1)} %bitcast.19), calls=%async_computation | async-start | bytes 1179648 | tf_op jit(solution)/shard_map/all_to_all | solution.py:659
  23.8 18.1 %copy-start.4 = (bf16[1024,256]{1,0:T(8,128)(2,1)S(1)}, bf16[1024,256]{1,0:T(8,128)(2,1)}, u32[]{:S(2)}) copy-start(bf16[1024,256]{1,0:T(8,128)(2,1)} %constant.90.clone.y_ref) | copy-start | bytes 1572868
  23.9 18.1 %copy-start.5 = (bf16[512,128]{1,0:T(8,128)(2,1)S(1)}, bf16[512,128]{1,0:T(8,128)(2,1)}, u32[]{:S(2)}) copy-start(bf16[512,128]{1,0:T(8,128)(2,1)} %constant.91.clone.x_ref) | copy-start | bytes 393220
  45.5 3.6 %copy-start.8 = (bf16[64,16,64]{2,1,0:T(8,128)(2,1)S(1)}, bf16[64,16,64]{2,1,0:T(8,128)(2,1)}, u32[]{:S(2)}) copy-start(bf16[64,16,64]{2,1,0:T(8,128)(2,1)} %param.21) | copy-start | bytes 393220
  45.5 4.0 %copy-start.9 = (s32[256,8]{0,1:T(8,128)S(1)}, s32[256,8]{0,1:T(8,128)}, u32[]{:S(2)}) copy-start(s32[256,8]{0,1:T(8,128)} %param.19) | copy-start | bytes 24580
  45.5 5.2 %copy-start.7 = (s32[256,8]{0,1:T(8,128)S(1)}, s32[256,8]{0,1:T(8,128)}, u32[]{:S(2)}) copy-start(s32[256,8]{0,1:T(8,128)} %param.20) | copy-start | bytes 24580
  46.5 19.4 %all-to-all-start.1 = ((f16[32,64,128]{2,1,0:T(8,128)(2,1)}), f16[32,64,128]{2,1,0:T(8,128)(2,1)S(1)}, u32[]{:S(2)}, u32[]{:S(2)}) async-start(f16[32,64,128]{2,1,0:T(8,128)(2,1)} %slice.5), calls=%async_computation.1 | async-start | bytes 1048576 | tf_op jit(solution)/shard_map/all_to_all | solution.py:659
  49.1 16.9 %copy-start.3 = (bf16[1024,256]{1,0:T(8,128)(2,1)S(1)}, bf16[1024,256]{1,0:T(8,128)(2,1)}, u32[]{:S(2)}) copy-start(bf16[1024,256]{1,0:T(8,128)(2,1)} %constant.92.clone.v_ref) | copy-start | bytes 1572868
  49.3 1.4 %collective-permute-start.3 = (bf16[240,256]{1,0:T(8,128)(2,1)S(1)}, bf16[240,256]{1,0:T(8,128)(2,1)S(1)}, u32[]{:S(2)}, u32[]{:S(2)}) collective-permute-start(bf16[240,256]{1,0:T(8,128)(2,1)S(1)} %get-tuple-element.51.here_ref), channel_id=1, source_target_pairs={{0,1},{1,0},{2,3},{3,2},{4,5},{5,4},{6,7},{7,6},{8,9},{9,8},{10,11... | collective-permute-start | bytes 368648 | tf_op jit(solution)/shard_map/ppermute | solution.py:584
  67.4 1.3 %collective-permute-start.4 = (bf16[128,128]{1,0:T(8,128)(2,1)S(1)}, bf16[128,128]{1,0:T(8,128)(2,1)S(1)}, u32[]{:S(2)}, u32[]{:S(2)}) collective-permute-start(bf16[128,128]{1,0:T(8,128)(2,1)S(1)} %get-tuple-element.58), channel_id=1, source_target_pairs={{0,1},{1,0},{2,3},{3,2},{4,5},{5,4},{6,7},{7,6},{8,9},{9,8},{10,11... | collective-permute-start | bytes 98312 | tf_op jit(solution)/shard_map/ppermute | solution.py:584
  71.3 5.0 %collective-permute-start.5 = (f32[64,256]{1,0:T(8,128)S(1)}, f32[64,256]{1,0:T(8,128)S(1)}, u32[]{:S(2)}, u32[]{:S(2)}) collective-permute-start(f32[64,256]{1,0:T(8,128)S(1)} %get-tuple-element.61), channel_id=1, source_target_pairs={{0,2},{1,3},{2,0},{3,1},{4,6},{5,7},{6,4},{7,5},{8,10},{9,11},{10,... | collective-permute-start | bytes 196616 | tf_op jit(solution)/shard_map/ppermute | solution.py:584
  71.4 8.0 %collective-permute-start.6 = (f32[64,256]{1,0:T(8,128)S(1)}, f32[64,256]{1,0:T(8,128)S(1)}, u32[]{:S(2)}, u32[]{:S(2)}) collective-permute-start(f32[64,256]{1,0:T(8,128)S(1)} %get-tuple-element.62), channel_id=1, source_target_pairs={{0,30},{1,31},{2,4},{3,5},{4,2},{5,3},{6,8},{7,9},{8,6},{9,7},{10,... | collective-permute-start | bytes 196616 | tf_op jit(solution)/shard_map/ppermute | solution.py:584

commit v12 on v11

--- a/solution.py
+++ b/solution.py
@@ -722,8 +722,8 @@
         compiler_params=PARAMS,
         name="beside_sample",
     )(odd, facts2, *pot[:4], edge, facts2, stk)
+    first = to_first(others[0])
     second = to_second(others[1])
-    first = to_first(others[0])
     own = pl.pallas_call(
         own_sample_kernel,
         out_shape=sums,

time: 80.7 us -> 81.9 us (1.015)
  Pallas kernels: 18.4 us -> 20.8 us
  transfers between devices with their start and end apart: 9 -> 9, of which waited for: 7 -> 7; matrix products, arithmetic and copies ran while one was open for 0% -> 0% of each run, Pallas kernels for 8% -> 10%
where the time goes in v12:
time: 81.9 us; the launch traced here: 81.3 us
  waiting for transfers between devices  39.1 us (48%)
  Pallas kernels  20.8 us (25%)
  starting transfers between devices  15.2 us (19%)
  other arithmetic  2.83 us (3%)
  local copies, waits for them, and re-layouts  2.42 us (3%)
  between operations  0.96 us (1%)
    all_to_all x2, waiting for transfers between devices, exchanged(): values = lax.all_to_all(values, axes, 0, 0, tiled=True)  31 us
    ppermute x7, starting transfers between devices, moved(): return lax.ppermute(values, both, pairs)  9.12 us
    ppermute x7, waiting for transfers between devices, moved(): return lax.ppermute(values, both, pairs)  8.1 us
    all_to_all x2, starting transfers between devices, exchanged(): values = lax.all_to_all(values, axes, 0, 0, tiled=True)  6.08 us
    pallas_call x1, Pallas kernels, body(): pl.pallas_call(beside_kernel, out_shape=(grid,) * 5 + (shape_of(LANES, LA...  3.58 us
    pallas_call x1, Pallas kernels, body(): pl.pallas_call(functools.partial(plane_kernel, slabs, planes), out_shape=...  3.46 us
    pallas_call x1, Pallas kernels, body(): pl.pallas_call(beside_sample_kernel, out_shape=(sums, sums), in_specs=[SM...  3.27 us
    pallas_call x1, Pallas kernels, body(): pl.pallas_call(own_kernel, out_shape=(grid,) * 5 + (shape_of(KS * PANELS,...  3.21 us
  transfers between devices with their start and end apart: 9, of which 7 were waited for; matrix products, arithmetic and copies ran while one was open for 0% of the time, Pallas kernels for 10%

profile of v12, /device:TPU:0, one launch (start us, length us, event | category | flops | bytes accessed | tf_op | source)
XLA Modules:
  0.0 81.3 jit_solution(12425450132478922562)
XLA Ops:
  0.7 0.9 %fusion.packed_ref.own_ref = bf16[80,256]{1,0:T(8,128)(2,1)S(1)} fusion(s32[80]{0:T(128)S(1)} %compare_select_fusion, s32[256]{0:T(256)} %param.16, s32[]{:T(128)} %bitcast.16, s32[256]{0:T(256)} %param.17, bf16[64,256]{1,0:T(8,128)(2,1)} %param.14, pred[80]{0:T(512)(128)(4,1)S(1)} %get-tuple-element.63, pred[80]{0:T(512)(128)(4,1)S(1)} %get-tuple-element.64, ...), kind=kLoop, calls=%fused_computation.4 | loop fusion | flops 143360 | bytes 76596 | tf_op jit(solution)/shard_map/jit(_where)/select_n | solution.py:603
  1.6 3.0 %collective-permute-start = (bf16[80,256]{1,0:T(8,128)(2,1)S(1)}, bf16[80,256]{1,0:T(8,128)(2,1)S(1)}, u32[]{:S(2)}, u32[]{:S(2)}) collective-permute-start(bf16[80,256]{1,0:T(8,128)(2,1)S(1)} %fusion.packed_ref.own_ref), channel_id=1, source_target_pairs={{0,2},{1,3},{2,0},{3,1},{4,6},{5,7},{6,4},{7,5},{8,10},{9,11},{10,... | collective-permute-start | bytes 122888 | tf_op jit(solution)/shard_map/ppermute | solution.py:584
  4.6 4.5 %collective-permute-start.1 = (bf16[80,256]{1,0:T(8,128)(2,1)S(1)}, bf16[80,256]{1,0:T(8,128)(2,1)S(1)}, u32[]{:S(2)}, u32[]{:S(2)}) collective-permute-start(bf16[80,256]{1,0:T(8,128)(2,1)S(1)} %fusion.packed_ref.own_ref), channel_id=1, source_target_pairs={{0,30},{1,31},{2,4},{3,5},{4,2},{5,3},{6,8},{7,9},{8,6},{9,7},{10,... | collective-permute-start | bytes 122888 | tf_op jit(solution)/shard_map/ppermute | solution.py:584
  9.1 1.2 %copy-done = bf16[16,64,512]{2,1,0:T(8,128)(2,1)S(1)} copy-done((bf16[16,64,512]{2,1,0:T(8,128)(2,1)S(1)}, bf16[16,64,512]{2,1,0:T(8,128)(2,1)}, u32[]{:S(2)}) %copy-start) | copy-done | bytes 1048600
  10.3 3.2 %own_scatter.1 = (f32[520,128]{1,0:T(8,128)S(1)}, f32[520,128]{1,0:T(8,128)S(1)}, f32[520,128]{1,0:T(8,128)S(1)}, f32[520,128]{1,0:T(8,128)S(1)}, f32[520,128]{1...) custom-call(bf16[80,256]{1,0:T(8,128)(2,1)S(1)} %fusion.packed_ref.own_ref, ...), custom_call_target="tpu_custom_call" | custom-call | tf_op jit(solution)/shard_map/own_scatter/pallas_call | solution.py:608
  13.6 0.0 collective-permute-done.first_ref
  13.6 0.0 collective-permute-done.1.second_ref
  13.6 0.0 copy-start.2
  13.6 3.6 %beside_scatter.1 = (f32[520,128]{1,0:T(8,128)S(1)}, f32[520,128]{1,0:T(8,128)S(1)}, f32[520,128]{1,0:T(8,128)S(1)}, f32[520,128]{1,0:T(8,128)S(1)}, f32[520,128...) custom-call(s32[1]{0:T(128)} %bitcast.2.odd_ref, ...), custom_call_target="tpu_custom_call", output_to_operand_aliasing={{0}: (5, {}), {1}: (6, {}), {2}: (7, {}), {3}: (8, {}), {4}... | custom-call | tf_op jit(solution)/shard_map/beside_scatter/pallas_call | solution.py:623
  17.2 0.1 collective-permute-start.2
  17.3 1.2 %collective-permute-done.2.edge_ref = f32[128,128]{1,0:T(8,128)S(1)} collective-permute-done((f32[128,128]{1,0:T(8,128)S(1)}, f32[128,128]{1,0:T(8,128)S(1)}, u32[]{:S(2)}, u32[]{:S(2)}) %collective-permute-start.2) | collective-permute-done | bytes 65568 | tf_op jit(solution)/shard_map/ppermute | solution.py:584
  18.5 1.3 %z_forward.1 = f32[2304,128]{1,0:T(8,128)S(1)} custom-call(f32[520,128]{1,0:T(8,128)S(1)} %get-tuple-element.41.g0, f32[520,128]{1,0:T(8,128)S(1)} %get-tuple-element.42.g1, f32[520,128]{1,0:T(8,128)S(1)} %get-tuple-element.43.g2, f32[520,128]{1,0:T(8,128)S(1)} %get-tuple-element.44.g3, f32[128,128]{1,0:T(8,128)S(1)} %collective-permute-done.2.edge_ref, ...), custom_call_target="tpu_custom_call" | custom-call | tf_op jit(solution)/shard_map/z_forward/pallas_call | solution.py:647
  19.8 0.0 copy-start.1
  19.8 0.0 copy-start.6
  19.8 0.9 %convert_element_type.19 = f16[2304,128]{1,0:T(8,128)(2,1)} convert(f32[2304,128]{1,0:T(8,128)S(1)} %z_forward.1) | non-fusion elementwise | flops 294912 | bytes 1769472 | tf_op jit(solution)/shard_map/convert_element_type | solution.py:658
  20.8 3.5 %all-to-all-start = ((f16[32,72,128]{2,1,0:T(8,128)(2,1)}), f16[32,72,128]{2,1,0:T(8,128)(2,1)S(1)}, u32[]{:S(2)}, u32[]{:S(2)}) async-start(f16[32,72,128]{2,1,0:T(8,128)(2,1)} %bitcast.19), calls=%async_computation | async-start | bytes 1179648 | tf_op jit(solution)/shard_map/all_to_all | solution.py:659
  24.3 0.0 copy-done.1
  24.3 0.0 copy-done.6
  24.3 0.3 hat_order.1.hat_ref
  24.6 0.0 copy-start.4
  24.6 0.0 copy-start.5
  24.6 17.9 %all-to-all-done = f16[32,72,128]{2,1,0:T(8,128)(2,1)S(1)} async-done(((f16[32,72,128]{2,1,0:T(8,128)(2,1)}), f16[32,72,128]{2,1,0:T(8,128)(2,1)S(1)}, u32[]{:S(2)}, u32[]{:S(2)}) %all-to-all-start) | async-done | bytes 589856 | tf_op jit(solution)/shard_map/all_to_all | solution.py:659
  42.5 0.1 bitcast_convert_fusion.in_ref
  42.6 3.5 %plane_filter.1 = (f32[2304,128]{1,0:T(8,128)S(1)}, f32[8,128]{1,0:T(8,128)S(1)}) custom-call(f32[2304,128]{1,0:T(8,128)S(1)} %bitcast_convert_fusion.in_ref, f32[8,64,256]{2,1,0:T(8,128)S(1)} %hat_order.1.hat_ref, bf16[1024,256]{1,0:T(8,128)(2,1)S(1)} %copy-done.4, bf16[512,128]{1,0:T(8,128)(2,1)S(1)} %copy-done.5), custom_call_target="tpu_custom_call" | custom-call | tf_op jit(solution)/shard_map/plane_filter/pallas_call | solution.py:691
  46.1 0.1 convert.7
  46.2 0.0 copy-start.8
  46.2 0.0 copy-start.9
  46.2 0.0 copy-start.7
  46.2 0.9 %slice.5 = f16[32,64,128]{2,1,0:T(8,128)(2,1)} slice(f16[32,72,128]{2,1,0:T(8,128)(2,1)S(1)} %bitcast.20), slice={[0:32], [0:64], [0:128]} | slice | bytes 1048576 | tf_op jit(solution)/shard_map/slice | solution.py:658
  47.2 2.6 %all-to-all-start.1 = ((f16[32,64,128]{2,1,0:T(8,128)(2,1)}), f16[32,64,128]{2,1,0:T(8,128)(2,1)S(1)}, u32[]{:S(2)}, u32[]{:S(2)}) async-start(f16[32,64,128]{2,1,0:T(8,128)(2,1)} %slice.5), calls=%async_computation.1 | async-start | bytes 1048576 | tf_op jit(solution)/shard_map/all_to_all | solution.py:659
  49.8 0.0 copy-start.3
  49.8 0.2 reshape.28.table_ref
  50.0 0.2 collective-permute-start.3
  50.2 1.2 %collective-permute-done.3.there_ref = bf16[240,256]{1,0:T(8,128)(2,1)S(1)} collective-permute-done((bf16[240,256]{1,0:T(8,128)(2,1)S(1)}, bf16[240,256]{1,0:T(8,128)(2,1)S(1)}, u32[]{:S(2)}, u32[]{:S(2)}) %collective-permute-start.3) | collective-permute-done | bytes 122912 | tf_op jit(solution)/shard_map/ppermute | solution.py:584
  51.4 2.1 %near_field.1 = f32[64,256]{1,0:T(8,128)S(1)} custom-call(s32[1]{0:T(128)} %copy.25.live_ref, bf16[240,256]{1,0:T(8,128)(2,1)S(1)} %get-tuple-element.51.here_ref, bf16[240,256]{1,0:T(8,128)(2,1)S(1)} %collective-permute-done.3.there_ref, s32[8,256]{1,0:T(8,128)S(1)} %fusion.5.source_ref, s32[8,256]{1,0:T(8,128)S(1)} %bitcast.18, ...), custom_call_target="tpu_custom_call" | custom-call | tf_op jit(solution)/shard_map/near_field/pallas_call | solution.py:682
  53.6 13.1 %all-to-all-done.1 = f16[32,64,128]{2,1,0:T(8,128)(2,1)S(1)} async-done(((f16[32,64,128]{2,1,0:T(8,128)(2,1)}), f16[32,64,128]{2,1,0:T(8,128)(2,1)S(1)}, u32[]{:S(2)}, u32[]{:S(2)}) %all-to-all-start.1) | async-done | bytes 524320 | tf_op jit(solution)/shard_map/all_to_all | solution.py:659
  66.6 0.1 bitcast_convert_fusion.1.in_ref
  66.7 0.0 copy-done.3
  66.7 1.4 %z_inverse.1 = (f32[520,128]{1,0:T(8,128)S(1)}, f32[520,128]{1,0:T(8,128)S(1)}, f32[520,128]{1,0:T(8,128)S(1)}, f32[520,128]{1,0:T(8,128)S(1)}, bf16[128,128]{1,0:T(8,128)(2,1)S(1)}) custom-call(f32[2048,128]{1,0:T(8,128)S(1)} %bitcast_convert_fusion.1.in_ref, f32[8,128]{1,0:T(8,128)S(1)} %get-tuple-element.53.exponent_ref, bf16[1024,256]{1,0:T(8,128)(2,1)S(1)} %copy-done.3), custom_call_target="tpu_custom_call" | custom-call | tf_op jit(solution)/shard_map/z_inverse/pallas_call | solution.py:702
  68.1 0.1 collective-permute-start.4
  68.2 1.2 %collective-permute-done.4.edge_ref = bf16[128,128]{1,0:T(8,128)(2,1)S(1)} collective-permute-done((bf16[128,128]{1,0:T(8,128)(2,1)S(1)}, bf16[128,128]{1,0:T(8,128)(2,1)S(1)}, u32[]{:S(2)}, u32[]{:S(2)}) %collective-permute-start.4) | collective-permute-done | bytes 32800 | tf_op jit(solution)/shard_map/ppermute | solution.py:584
  69.4 3.3 %beside_sample.1 = (f32[64,256]{1,0:T(8,128)S(1)}, f32[64,256]{1,0:T(8,128)S(1)}) custom-call(s32[1]{0:T(128)} %bitcast.2.odd_ref, s32[8,512]{1,0:T(8,128)S(1)} %get-tuple-element.60.facts_ref.kinds_ref, f32[520,128]{1,0:T(8,128)S(1)} %get-tuple-element.54.p0, f32[520,128]{1,0:T(8,128)S(1)} %get-tuple-element.55.p1, f32[520,128]{1,0:T(8,128)S(1)} %get-tuple-element.56.p2, ...), custom_call_target="tpu_custom_call" | custom-call | tf_op jit(solution)/shard_map/beside_sample/pallas_call | solution.py:716
  72.7 0.1 collective-permute-start.5
  72.8 1.2 %collective-permute-start.6 = (f32[64,256]{1,0:T(8,128)S(1)}, f32[64,256]{1,0:T(8,128)S(1)}, u32[]{:S(2)}, u32[]{:S(2)}) collective-permute-start(f32[64,256]{1,0:T(8,128)S(1)} %get-tuple-element.62), channel_id=1, source_target_pairs={{0,30},{1,31},{2,4},{3,5},{4,2},{5,3},{6,8},{7,9},{8,6},{9,7},{10,... | collective-permute-start | bytes 196616 | tf_op jit(solution)/shard_map/ppermute | solution.py:584
  74.0 2.3 %own_sample.1 = f32[64,256]{1,0:T(8,128)S(1)} custom-call(s32[8,256]{1,0:T(8,128)S(1)} %get-tuple-element.34.facts_ref.kinds_ref, f32[520,128]{1,0:T(8,128)S(1)} %get-tuple-element.54.p0, f32[520,128]{1,0:T(8,128)S(1)} %get-tuple-element.55.p1, f32[520,128]{1,0:T(8,128)S(1)} %get-tuple-element.56.p2, f32[520,128]{1,0:T(8,128)S(1)} %get-tuple-element.57.p3, ...), custom_call_target="tpu_custom_call" | custom-call | tf_op jit(solution)/shard_map/own_sample/pallas_call | solution.py:727
  76.2 1.4 %collective-permute-done.5 = f32[64,256]{1,0:T(8,128)S(1)} collective-permute-done((f32[64,256]{1,0:T(8,128)S(1)}, f32[64,256]{1,0:T(8,128)S(1)}, u32[]{:S(2)}, u32[]{:S(2)}) %collective-permute-start.5) | collective-permute-done | bytes 65568 | tf_op jit(solution)/shard_map/ppermute | solution.py:584
  77.6 3.1 %collective-permute-done.6 = f32[64,256]{1,0:T(8,128)S(1)} collective-permute-done((f32[64,256]{1,0:T(8,128)S(1)}, f32[64,256]{1,0:T(8,128)S(1)}, u32[]{:S(2)}, u32[]{:S(2)}) %collective-permute-start.6) | collective-permute-done | bytes 65568 | tf_op jit(solution)/shard_map/ppermute | solution.py:584
  80.7 0.6 add_add_fusion
  (12 shorter events, 0.1 us)
Async XLA Ops:
  1.6 12.0 %collective-permute-start = (bf16[80,256]{1,0:T(8,128)(2,1)S(1)}, bf16[80,256]{1,0:T(8,128)(2,1)S(1)}, u32[]{:S(2)}, u32[]{:S(2)}) collective-permute-start(bf16[80,256]{1,0:T(8,128)(2,1)S(1)} %fusion.packed_ref.own_ref), channel_id=1, source_target_pairs={{0,2},{1,3},{2,0},{3,1},{4,6},{5,7},{6,4},{7,5},{8,10},{9,11},{10,... | collective-permute-start | bytes 122888 | tf_op jit(solution)/shard_map/ppermute | solution.py:584
  4.6 9.0 %collective-permute-start.1 = (bf16[80,256]{1,0:T(8,128)(2,1)S(1)}, bf16[80,256]{1,0:T(8,128)(2,1)S(1)}, u32[]{:S(2)}, u32[]{:S(2)}) collective-permute-start(bf16[80,256]{1,0:T(8,128)(2,1)S(1)} %fusion.packed_ref.own_ref), channel_id=1, source_target_pairs={{0,30},{1,31},{2,4},{3,5},{4,2},{5,3},{6,8},{7,9},{8,6},{9,7},{10,... | collective-permute-start | bytes 122888 | tf_op jit(solution)/shard_map/ppermute | solution.py:584
  9.1 1.2 %copy-start = (bf16[16,64,512]{2,1,0:T(8,128)(2,1)S(1)}, bf16[16,64,512]{2,1,0:T(8,128)(2,1)}, u32[]{:S(2)}) copy-start(bf16[16,64,512]{2,1,0:T(8,128)(2,1)} %param.18) | copy-start | bytes 3145732
  13.6 4.9 %copy-start.2 = (bf16[1152,256]{1,0:T(8,128)(2,1)S(1)}, bf16[1152,256]{1,0:T(8,128)(2,1)}, u32[]{:S(2)}) copy-start(bf16[1152,256]{1,0:T(8,128)(2,1)} %constant.88.clone.w_ref) | copy-start | bytes 1769476
  17.2 1.3 %collective-permute-start.2 = (f32[128,128]{1,0:T(8,128)S(1)}, f32[128,128]{1,0:T(8,128)S(1)}, u32[]{:S(2)}, u32[]{:S(2)}) collective-permute-start(f32[128,128]{1,0:T(8,128)S(1)} %get-tuple-element.45), channel_id=1, source_target_pairs={{0,1},{1,0},{2,3},{3,2},{4,5},{5,4},{6,7},{7,6},{8,9},{9,8},{10,11... | collective-permute-start | bytes 196616 | tf_op jit(solution)/shard_map/ppermute | solution.py:584
  19.8 4.5 %copy-start.1 = (f32[16,64,256]{2,1,0:T(8,128)S(1)}, f32[16,64,256]{2,1,0:T(8,128)}, u32[]{:S(2)}) copy-start(f32[16,64,256]{2,1,0:T(8,128)} %hat_ref) | copy-start | bytes 3145732
  19.8 4.5 %copy-start.6 = (bf16[128,128]{1,0:T(8,128)(2,1)S(1)}, bf16[128,128]{1,0:T(8,128)(2,1)}, u32[]{:S(2)}) copy-start(bf16[128,128]{1,0:T(8,128)(2,1)} %constant.89.clone.turn_ref) | copy-start | bytes 98308
  20.8 21.7 %all-to-all-start = ((f16[32,72,128]{2,1,0:T(8,128)(2,1)}), f16[32,72,128]{2,1,0:T(8,128)(2,1)S(1)}, u32[]{:S(2)}, u32[]{:S(2)}) async-start(f16[32,72,128]{2,1,0:T(8,128)(2,1)} %bitcast.19), calls=%async_computation | async-start | bytes 1179648 | tf_op jit(solution)/shard_map/all_to_all | solution.py:659
  24.6 18.1 %copy-start.4 = (bf16[1024,256]{1,0:T(8,128)(2,1)S(1)}, bf16[1024,256]{1,0:T(8,128)(2,1)}, u32[]{:S(2)}) copy-start(bf16[1024,256]{1,0:T(8,128)(2,1)} %constant.90.clone.y_ref) | copy-start | bytes 1572868
  24.6 18.1 %copy-start.5 = (bf16[512,128]{1,0:T(8,128)(2,1)S(1)}, bf16[512,128]{1,0:T(8,128)(2,1)}, u32[]{:S(2)}) copy-start(bf16[512,128]{1,0:T(8,128)(2,1)} %constant.91.clone.x_ref) | copy-start | bytes 393220
  46.2 3.6 %copy-start.8 = (bf16[64,16,64]{2,1,0:T(8,128)(2,1)S(1)}, bf16[64,16,64]{2,1,0:T(8,128)(2,1)}, u32[]{:S(2)}) copy-start(bf16[64,16,64]{2,1,0:T(8,128)(2,1)} %param.21) | copy-start | bytes 393220
  46.2 4.0 %copy-start.9 = (s32[256,8]{0,1:T(8,128)S(1)}, s32[256,8]{0,1:T(8,128)}, u32[]{:S(2)}) copy-start(s32[256,8]{0,1:T(8,128)} %param.19) | copy-start | bytes 24580
  46.2 5.2 %copy-start.7 = (s32[256,8]{0,1:T(8,128)S(1)}, s32[256,8]{0,1:T(8,128)}, u32[]{:S(2)}) copy-start(s32[256,8]{0,1:T(8,128)} %param.20) | copy-start | bytes 24580
  47.2 19.4 %all-to-all-start.1 = ((f16[32,64,128]{2,1,0:T(8,128)(2,1)}), f16[32,64,128]{2,1,0:T(8,128)(2,1)S(1)}, u32[]{:S(2)}, u32[]{:S(2)}) async-start(f16[32,64,128]{2,1,0:T(8,128)(2,1)} %slice.5), calls=%async_computation.1 | async-start | bytes 1048576 | tf_op jit(solution)/shard_map/all_to_all | solution.py:659
  49.8 16.9 %copy-start.3 = (bf16[1024,256]{1,0:T(8,128)(2,1)S(1)}, bf16[1024,256]{1,0:T(8,128)(2,1)}, u32[]{:S(2)}) copy-start(bf16[1024,256]{1,0:T(8,128)(2,1)} %constant.92.clone.v_ref) | copy-start | bytes 1572868
  50.0 1.4 %collective-permute-start.3 = (bf16[240,256]{1,0:T(8,128)(2,1)S(1)}, bf16[240,256]{1,0:T(8,128)(2,1)S(1)}, u32[]{:S(2)}, u32[]{:S(2)}) collective-permute-start(bf16[240,256]{1,0:T(8,128)(2,1)S(1)} %get-tuple-element.51.here_ref), channel_id=1, source_target_pairs={{0,1},{1,0},{2,3},{3,2},{4,5},{5,4},{6,7},{7,6},{8,9},{9,8},{10,11... | collective-permute-start | bytes 368648 | tf_op jit(solution)/shard_map/ppermute | solution.py:584
  68.1 1.3 %collective-permute-start.4 = (bf16[128,128]{1,0:T(8,128)(2,1)S(1)}, bf16[128,128]{1,0:T(8,128)(2,1)S(1)}, u32[]{:S(2)}, u32[]{:S(2)}) collective-permute-start(bf16[128,128]{1,0:T(8,128)(2,1)S(1)} %get-tuple-element.58), channel_id=1, source_target_pairs={{0,1},{1,0},{2,3},{3,2},{4,5},{5,4},{6,7},{7,6},{8,9},{9,8},{10,11... | collective-permute-start | bytes 98312 | tf_op jit(solution)/shard_map/ppermute | solution.py:584
  72.7 4.9 %collective-permute-start.5 = (f32[64,256]{1,0:T(8,128)S(1)}, f32[64,256]{1,0:T(8,128)S(1)}, u32[]{:S(2)}, u32[]{:S(2)}) collective-permute-start(f32[64,256]{1,0:T(8,128)S(1)} %get-tuple-element.61), channel_id=1, source_target_pairs={{0,2},{1,3},{2,0},{3,1},{4,6},{5,7},{6,4},{7,5},{8,10},{9,11},{10,... | collective-permute-start | bytes 196616 | tf_op jit(solution)/shard_map/ppermute | solution.py:584
  72.8 7.9 %collective-permute-start.6 = (f32[64,256]{1,0:T(8,128)S(1)}, f32[64,256]{1,0:T(8,128)S(1)}, u32[]{:S(2)}, u32[]{:S(2)}) collective-permute-start(f32[64,256]{1,0:T(8,128)S(1)} %get-tuple-element.62), channel_id=1, source_target_pairs={{0,30},{1,31},{2,4},{3,5},{4,2},{5,3},{6,8},{7,9},{8,6},{9,7},{10,... | collective-permute-start | bytes 196616 | tf_op jit(solution)/shard_map/ppermute | solution.py:584

commit v13 on v12

--- a/solution.py
+++ b/solution.py
@@ -601,8 +601,8 @@
     facts = jnp.where(row == PANELS + 2, slot_stencil[None, :], jnp.where(row == PANELS + 3, live, facts))
     held = jnp.where(column < live, jnp.pad(charges, ((0, 16), (0, 0))), jnp.zeros((), BF16))
     packed = jnp.where(row < PANELS, held, facts.astype(BF16))
+    from_first = to_first(packed)
     from_second = to_second(packed)
-    from_first = to_first(packed)
 
     grid = shape_of(ZROWS, LANES)
     *grids, stk, facts = pl.pallas_call(

time: 81.9 us -> 80.7 us (0.985)
  Pallas kernels: 20.8 us -> 18.4 us
  starting transfers between devices: 15.2 us -> 16.1 us
    ppermute x7, starting transfers between devices: 9.12 us -> 10.9 us  [moved(): return lax.ppermute(values, both, pairs)]
    all_to_all x2, starting transfers between devices: 6.08 us -> 5.21 us  [exchanged(): values = lax.all_to_all(values, axes, 0, 0, tiled=True)]
  transfers between devices with their start and end apart: 9 -> 9, of which waited for: 7 -> 7; matrix products, arithmetic and copies ran while one was open for 0% -> 0% of each run, Pallas kernels for 10% -> 9%
where the time goes in v13:
time: 80.7 us; the launch traced here: 80.1 us
  waiting for transfers between devices  39.4 us (49%)
  Pallas kernels  18.4 us (23%)
  starting transfers between devices  16.1 us (20%)
  other arithmetic  2.83 us (4%)
  local copies, waits for them, and re-layouts  2.42 us (3%)
  between operations  0.95 us (1%)
    all_to_all x2, waiting for transfers between devices, exchanged(): values = lax.all_to_all(values, axes, 0, 0, tiled=True)  31 us
    ppermute x7, starting transfers between devices, moved(): return lax.ppermute(values, both, pairs)  10.9 us
    ppermute x7, waiting for transfers between devices, moved(): return lax.ppermute(values, both, pairs)  8.46 us
    all_to_all x2, starting transfers between devices, exchanged(): values = lax.all_to_all(values, axes, 0, 0, tiled=True)  5.21 us
    pallas_call x1, Pallas kernels, body(): pl.pallas_call(functools.partial(plane_kernel, slabs, planes), out_shape=...  3.46 us
    pallas_call x1, Pallas kernels, body(): pl.pallas_call(beside_kernel, out_shape=(grid,) * 5 + (shape_of(LANES, LA...  2.88 us
    pallas_call x1, Pallas kernels, body(): pl.pallas_call(own_kernel, out_shape=(grid,) * 5 + (shape_of(KS * PANELS,...  2.65 us
    pallas_call x1, Pallas kernels, body(): pl.pallas_call(beside_sample_kernel, out_shape=(sums, sums), in_specs=[SM...  2.6 us
  transfers between devices with their start and end apart: 9, of which 7 were waited for; matrix products, arithmetic and copies ran while one was open for 0% of the time, Pallas kernels for 9%

profile of v13, /device:TPU:0, one launch (start us, length us, event | category | flops | bytes accessed | tf_op | source)
XLA Modules:
  0.0 80.1 jit_solution(12425450132478922562)
XLA Ops:
  0.7 0.9 %fusion.packed_ref.own_ref = bf16[80,256]{1,0:T(8,128)(2,1)S(1)} fusion(s32[80]{0:T(128)S(1)} %compare_select_fusion, s32[256]{0:T(256)} %param.16, s32[]{:T(128)} %bitcast.16, s32[256]{0:T(256)} %param.17, bf16[64,256]{1,0:T(8,128)(2,1)} %param.14, pred[80]{0:T(512)(128)(4,1)S(1)} %get-tuple-element.63, pred[80]{0:T(512)(128)(4,1)S(1)} %get-tuple-element.64, ...), kind=kLoop, calls=%fused_computation.4 | loop fusion | flops 143360 | bytes 76596 | tf_op jit(solution)/shard_map/jit(_where)/select_n | solution.py:603
  1.6 3.0 %collective-permute-start = (bf16[80,256]{1,0:T(8,128)(2,1)S(1)}, bf16[80,256]{1,0:T(8,128)(2,1)S(1)}, u32[]{:S(2)}, u32[]{:S(2)}) collective-permute-start(bf16[80,256]{1,0:T(8,128)(2,1)S(1)} %fusion.packed_ref.own_ref), channel_id=1, source_target_pairs={{0,2},{1,3},{2,0},{3,1},{4,6},{5,7},{6,4},{7,5},{8,10},{9,11},{10,... | collective-permute-start | bytes 122888 | tf_op jit(solution)/shard_map/ppermute | solution.py:584
  4.6 4.5 %collective-permute-start.1 = (bf16[80,256]{1,0:T(8,128)(2,1)S(1)}, bf16[80,256]{1,0:T(8,128)(2,1)S(1)}, u32[]{:S(2)}, u32[]{:S(2)}) collective-permute-start(bf16[80,256]{1,0:T(8,128)(2,1)S(1)} %fusion.packed_ref.own_ref), channel_id=1, source_target_pairs={{0,30},{1,31},{2,4},{3,5},{4,2},{5,3},{6,8},{7,9},{8,6},{9,7},{10,... | collective-permute-start | bytes 122888 | tf_op jit(solution)/shard_map/ppermute | solution.py:584
  9.1 1.2 %copy-done = bf16[16,64,512]{2,1,0:T(8,128)(2,1)S(1)} copy-done((bf16[16,64,512]{2,1,0:T(8,128)(2,1)S(1)}, bf16[16,64,512]{2,1,0:T(8,128)(2,1)}, u32[]{:S(2)}) %copy-start) | copy-done | bytes 1048600
  10.3 2.7 %own_scatter.1 = (f32[520,128]{1,0:T(8,128)S(1)}, f32[520,128]{1,0:T(8,128)S(1)}, f32[520,128]{1,0:T(8,128)S(1)}, f32[520,128]{1,0:T(8,128)S(1)}, f32[520,128]{1...) custom-call(bf16[80,256]{1,0:T(8,128)(2,1)S(1)} %fusion.packed_ref.own_ref, ...), custom_call_target="tpu_custom_call" | custom-call | tf_op jit(solution)/shard_map/own_scatter/pallas_call | solution.py:608
  13.0 0.0 collective-permute-done.first_ref
  13.0 0.0 collective-permute-done.1.second_ref
  13.0 0.0 copy-start.2
  13.1 2.9 %beside_scatter.1 = (f32[520,128]{1,0:T(8,128)S(1)}, f32[520,128]{1,0:T(8,128)S(1)}, f32[520,128]{1,0:T(8,128)S(1)}, f32[520,128]{1,0:T(8,128)S(1)}, f32[520,128...) custom-call(s32[1]{0:T(128)} %bitcast.2.odd_ref, ...), custom_call_target="tpu_custom_call", output_to_operand_aliasing={{0}: (5, {}), {1}: (6, {}), {2}: (7, {}), {3}: (8, {}), {4}... | custom-call | tf_op jit(solution)/shard_map/beside_scatter/pallas_call | solution.py:623
  15.9 2.0 %collective-permute-start.2 = (f32[128,128]{1,0:T(8,128)S(1)}, f32[128,128]{1,0:T(8,128)S(1)}, u32[]{:S(2)}, u32[]{:S(2)}) collective-permute-start(f32[128,128]{1,0:T(8,128)S(1)} %get-tuple-element.45), channel_id=1, source_target_pairs={{0,1},{1,0},{2,3},{3,2},{4,5},{5,4},{6,7},{7,6},{8,9},{9,8},{10,11... | collective-permute-start | bytes 196616 | tf_op jit(solution)/shard_map/ppermute | solution.py:584
  18.0 0.9 %collective-permute-done.2.edge_ref = f32[128,128]{1,0:T(8,128)S(1)} collective-permute-done((f32[128,128]{1,0:T(8,128)S(1)}, f32[128,128]{1,0:T(8,128)S(1)}, u32[]{:S(2)}, u32[]{:S(2)}) %collective-permute-start.2) | collective-permute-done | bytes 65568 | tf_op jit(solution)/shard_map/ppermute | solution.py:584
  18.9 0.0 copy-done.2
  18.9 1.3 %z_forward.1 = f32[2304,128]{1,0:T(8,128)S(1)} custom-call(f32[520,128]{1,0:T(8,128)S(1)} %get-tuple-element.41.g0, f32[520,128]{1,0:T(8,128)S(1)} %get-tuple-element.42.g1, f32[520,128]{1,0:T(8,128)S(1)} %get-tuple-element.43.g2, f32[520,128]{1,0:T(8,128)S(1)} %get-tuple-element.44.g3, f32[128,128]{1,0:T(8,128)S(1)} %collective-permute-done.2.edge_ref, ...), custom_call_target="tpu_custom_call" | custom-call | tf_op jit(solution)/shard_map/z_forward/pallas_call | solution.py:647
  20.2 0.0 copy-start.1
  20.2 0.0 copy-start.6
  20.2 0.9 %convert_element_type.19 = f16[2304,128]{1,0:T(8,128)(2,1)} convert(f32[2304,128]{1,0:T(8,128)S(1)} %z_forward.1) | non-fusion elementwise | flops 294912 | bytes 1769472 | tf_op jit(solution)/shard_map/convert_element_type | solution.py:658
  21.1 2.6 %all-to-all-start = ((f16[32,72,128]{2,1,0:T(8,128)(2,1)}), f16[32,72,128]{2,1,0:T(8,128)(2,1)S(1)}, u32[]{:S(2)}, u32[]{:S(2)}) async-start(f16[32,72,128]{2,1,0:T(8,128)(2,1)} %bitcast.19), calls=%async_computation | async-start | bytes 1179648 | tf_op jit(solution)/shard_map/all_to_all | solution.py:659
  23.8 0.3 hat_order.1.hat_ref
  24.0 0.0 copy-start.4
  24.1 0.0 copy-start.5
  24.1 17.9 %all-to-all-done = f16[32,72,128]{2,1,0:T(8,128)(2,1)S(1)} async-done(((f16[32,72,128]{2,1,0:T(8,128)(2,1)}), f16[32,72,128]{2,1,0:T(8,128)(2,1)S(1)}, u32[]{:S(2)}, u32[]{:S(2)}) %all-to-all-start) | async-done | bytes 589856 | tf_op jit(solution)/shard_map/all_to_all | solution.py:659
  42.0 0.1 bitcast_convert_fusion.in_ref
  42.1 0.0 copy-done.4
  42.1 0.0 copy-done.5
  42.1 3.5 %plane_filter.1 = (f32[2304,128]{1,0:T(8,128)S(1)}, f32[8,128]{1,0:T(8,128)S(1)}) custom-call(f32[2304,128]{1,0:T(8,128)S(1)} %bitcast_convert_fusion.in_ref, f32[8,64,256]{2,1,0:T(8,128)S(1)} %hat_order.1.hat_ref, bf16[1024,256]{1,0:T(8,128)(2,1)S(1)} %copy-done.4, bf16[512,128]{1,0:T(8,128)(2,1)S(1)} %copy-done.5), custom_call_target="tpu_custom_call" | custom-call | tf_op jit(solution)/shard_map/plane_filter/pallas_call | solution.py:691
  45.6 0.1 convert.7
  45.7 0.0 copy-start.8
  45.7 0.0 copy-start.9
  45.7 0.0 copy-start.7
  45.7 0.9 %slice.5 = f16[32,64,128]{2,1,0:T(8,128)(2,1)} slice(f16[32,72,128]{2,1,0:T(8,128)(2,1)S(1)} %bitcast.20), slice={[0:32], [0:64], [0:128]} | slice | bytes 1048576 | tf_op jit(solution)/shard_map/slice | solution.py:658
  46.7 2.6 %all-to-all-start.1 = ((f16[32,64,128]{2,1,0:T(8,128)(2,1)}), f16[32,64,128]{2,1,0:T(8,128)(2,1)S(1)}, u32[]{:S(2)}, u32[]{:S(2)}) async-start(f16[32,64,128]{2,1,0:T(8,128)(2,1)} %slice.5), calls=%async_computation.1 | async-start | bytes 1048576 | tf_op jit(solution)/shard_map/all_to_all | solution.py:659
  49.3 0.0 copy-start.3
  49.3 0.2 reshape.28.table_ref
  49.5 0.2 collective-permute-start.3
  49.7 1.2 %collective-permute-done.3.there_ref = bf16[240,256]{1,0:T(8,128)(2,1)S(1)} collective-permute-done((bf16[240,256]{1,0:T(8,128)(2,1)S(1)}, bf16[240,256]{1,0:T(8,128)(2,1)S(1)}, u32[]{:S(2)}, u32[]{:S(2)}) %collective-permute-start.3) | collective-permute-done | bytes 122912 | tf_op jit(solution)/shard_map/ppermute | solution.py:584
  50.9 2.1 %near_field.1 = f32[64,256]{1,0:T(8,128)S(1)} custom-call(s32[1]{0:T(128)} %copy.25.live_ref, bf16[240,256]{1,0:T(8,128)(2,1)S(1)} %get-tuple-element.51.here_ref, bf16[240,256]{1,0:T(8,128)(2,1)S(1)} %collective-permute-done.3.there_ref, s32[8,256]{1,0:T(8,128)S(1)} %fusion.5.source_ref, s32[8,256]{1,0:T(8,128)S(1)} %bitcast.18, ...), custom_call_target="tpu_custom_call" | custom-call | tf_op jit(solution)/shard_map/near_field/pallas_call | solution.py:682
  53.0 13.1 %all-to-all-done.1 = f16[32,64,128]{2,1,0:T(8,128)(2,1)S(1)} async-done(((f16[32,64,128]{2,1,0:T(8,128)(2,1)}), f16[32,64,128]{2,1,0:T(8,128)(2,1)S(1)}, u32[]{:S(2)}, u32[]{:S(2)}) %all-to-all-start.1) | async-done | bytes 524320 | tf_op jit(solution)/shard_map/all_to_all | solution.py:659
  66.1 0.1 bitcast_convert_fusion.1.in_ref
  66.2 1.4 %z_inverse.1 = (f32[520,128]{1,0:T(8,128)S(1)}, f32[520,128]{1,0:T(8,128)S(1)}, f32[520,128]{1,0:T(8,128)S(1)}, f32[520,128]{1,0:T(8,128)S(1)}, bf16[128,128]{1,0:T(8,128)(2,1)S(1)}) custom-call(f32[2048,128]{1,0:T(8,128)S(1)} %bitcast_convert_fusion.1.in_ref, f32[8,128]{1,0:T(8,128)S(1)} %get-tuple-element.53.exponent_ref, bf16[1024,256]{1,0:T(8,128)(2,1)S(1)} %copy-done.3), custom_call_target="tpu_custom_call" | custom-call | tf_op jit(solution)/shard_map/z_inverse/pallas_call | solution.py:702
  67.6 0.1 collective-permute-start.4
  67.7 1.2 %collective-permute-done.4.edge_ref = bf16[128,128]{1,0:T(8,128)(2,1)S(1)} collective-permute-done((bf16[128,128]{1,0:T(8,128)(2,1)S(1)}, bf16[128,128]{1,0:T(8,128)(2,1)S(1)}, u32[]{:S(2)}, u32[]{:S(2)}) %collective-permute-start.4) | collective-permute-done | bytes 32800 | tf_op jit(solution)/shard_map/ppermute | solution.py:584
  68.9 2.6 %beside_sample.1 = (f32[64,256]{1,0:T(8,128)S(1)}, f32[64,256]{1,0:T(8,128)S(1)}) custom-call(s32[1]{0:T(128)} %bitcast.2.odd_ref, s32[8,512]{1,0:T(8,128)S(1)} %get-tuple-element.60.facts_ref.kinds_ref, f32[520,128]{1,0:T(8,128)S(1)} %get-tuple-element.54.p0, f32[520,128]{1,0:T(8,128)S(1)} %get-tuple-element.55.p1, f32[520,128]{1,0:T(8,128)S(1)} %get-tuple-element.56.p2, ...), custom_call_target="tpu_custom_call" | custom-call | tf_op jit(solution)/shard_map/beside_sample/pallas_call | solution.py:716
  71.5 0.1 collective-permute-start.5
  71.6 1.0 %collective-permute-start.6 = (f32[64,256]{1,0:T(8,128)S(1)}, f32[64,256]{1,0:T(8,128)S(1)}, u32[]{:S(2)}, u32[]{:S(2)}) collective-permute-start(f32[64,256]{1,0:T(8,128)S(1)} %get-tuple-element.62), channel_id=1, source_target_pairs={{0,30},{1,31},{2,4},{3,5},{4,2},{5,3},{6,8},{7,9},{8,6},{9,7},{10,... | collective-permute-start | bytes 196616 | tf_op jit(solution)/shard_map/ppermute | solution.py:584
  72.5 1.8 %own_sample.1 = f32[64,256]{1,0:T(8,128)S(1)} custom-call(s32[8,256]{1,0:T(8,128)S(1)} %get-tuple-element.34.facts_ref.kinds_ref, f32[520,128]{1,0:T(8,128)S(1)} %get-tuple-element.54.p0, f32[520,128]{1,0:T(8,128)S(1)} %get-tuple-element.55.p1, f32[520,128]{1,0:T(8,128)S(1)} %get-tuple-element.56.p2, f32[520,128]{1,0:T(8,128)S(1)} %get-tuple-element.57.p3, ...), custom_call_target="tpu_custom_call" | custom-call | tf_op jit(solution)/shard_map/own_sample/pallas_call | solution.py:727
  74.3 1.5 %collective-permute-done.5 = f32[64,256]{1,0:T(8,128)S(1)} collective-permute-done((f32[64,256]{1,0:T(8,128)S(1)}, f32[64,256]{1,0:T(8,128)S(1)}, u32[]{:S(2)}, u32[]{:S(2)}) %collective-permute-start.5) | collective-permute-done | bytes 65568 | tf_op jit(solution)/shard_map/ppermute | solution.py:584
  75.8 3.7 %collective-permute-done.6 = f32[64,256]{1,0:T(8,128)S(1)} collective-permute-done((f32[64,256]{1,0:T(8,128)S(1)}, f32[64,256]{1,0:T(8,128)S(1)}, u32[]{:S(2)}, u32[]{:S(2)}) %collective-permute-start.6) | collective-permute-done | bytes 65568 | tf_op jit(solution)/shard_map/ppermute | solution.py:584
  79.5 0.6 add_add_fusion
  (12 shorter events, 0.1 us)
Async XLA Ops:
  1.6 11.4 %collective-permute-start = (bf16[80,256]{1,0:T(8,128)(2,1)S(1)}, bf16[80,256]{1,0:T(8,128)(2,1)S(1)}, u32[]{:S(2)}, u32[]{:S(2)}) collective-permute-start(bf16[80,256]{1,0:T(8,128)(2,1)S(1)} %fusion.packed_ref.own_ref), channel_id=1, source_target_pairs={{0,2},{1,3},{2,0},{3,1},{4,6},{5,7},{6,4},{7,5},{8,10},{9,11},{10,... | collective-permute-start | bytes 122888 | tf_op jit(solution)/shard_map/ppermute | solution.py:584
  4.6 8.4 %collective-permute-start.1 = (bf16[80,256]{1,0:T(8,128)(2,1)S(1)}, bf16[80,256]{1,0:T(8,128)(2,1)S(1)}, u32[]{:S(2)}, u32[]{:S(2)}) collective-permute-start(bf16[80,256]{1,0:T(8,128)(2,1)S(1)} %fusion.packed_ref.own_ref), channel_id=1, source_target_pairs={{0,30},{1,31},{2,4},{3,5},{4,2},{5,3},{6,8},{7,9},{8,6},{9,7},{10,... | collective-permute-start | bytes 122888 | tf_op jit(solution)/shard_map/ppermute | solution.py:584
  9.1 1.2 %copy-start = (bf16[16,64,512]{2,1,0:T(8,128)(2,1)S(1)}, bf16[16,64,512]{2,1,0:T(8,128)(2,1)}, u32[]{:S(2)}) copy-start(bf16[16,64,512]{2,1,0:T(8,128)(2,1)} %param.18) | copy-start | bytes 3145732
  13.0 5.8 %copy-start.2 = (bf16[1152,256]{1,0:T(8,128)(2,1)S(1)}, bf16[1152,256]{1,0:T(8,128)(2,1)}, u32[]{:S(2)}) copy-start(bf16[1152,256]{1,0:T(8,128)(2,1)} %constant.88.clone.w_ref) | copy-start | bytes 1769476
  15.9 2.9 %collective-permute-start.2 = (f32[128,128]{1,0:T(8,128)S(1)}, f32[128,128]{1,0:T(8,128)S(1)}, u32[]{:S(2)}, u32[]{:S(2)}) collective-permute-start(f32[128,128]{1,0:T(8,128)S(1)} %get-tuple-element.45), channel_id=1, source_target_pairs={{0,1},{1,0},{2,3},{3,2},{4,5},{5,4},{6,7},{7,6},{8,9},{9,8},{10,11... | collective-permute-start | bytes 196616 | tf_op jit(solution)/shard_map/ppermute | solution.py:584
  20.2 3.6 %copy-start.1 = (f32[16,64,256]{2,1,0:T(8,128)S(1)}, f32[16,64,256]{2,1,0:T(8,128)}, u32[]{:S(2)}) copy-start(f32[16,64,256]{2,1,0:T(8,128)} %hat_ref) | copy-start | bytes 3145732
  20.2 3.6 %copy-start.6 = (bf16[128,128]{1,0:T(8,128)(2,1)S(1)}, bf16[128,128]{1,0:T(8,128)(2,1)}, u32[]{:S(2)}) copy-start(bf16[128,128]{1,0:T(8,128)(2,1)} %constant.89.clone.turn_ref) | copy-start | bytes 98308
  21.1 20.9 %all-to-all-start = ((f16[32,72,128]{2,1,0:T(8,128)(2,1)}), f16[32,72,128]{2,1,0:T(8,128)(2,1)S(1)}, u32[]{:S(2)}, u32[]{:S(2)}) async-start(f16[32,72,128]{2,1,0:T(8,128)(2,1)} %bitcast.19), calls=%async_computation | async-start | bytes 1179648 | tf_op jit(solution)/shard_map/all_to_all | solution.py:659
  24.0 18.1 %copy-start.4 = (bf16[1024,256]{1,0:T(8,128)(2,1)S(1)}, bf16[1024,256]{1,0:T(8,128)(2,1)}, u32[]{:S(2)}) copy-start(bf16[1024,256]{1,0:T(8,128)(2,1)} %constant.90.clone.y_ref) | copy-start | bytes 1572868
  24.1 18.1 %copy-start.5 = (bf16[512,128]{1,0:T(8,128)(2,1)S(1)}, bf16[512,128]{1,0:T(8,128)(2,1)}, u32[]{:S(2)}) copy-start(bf16[512,128]{1,0:T(8,128)(2,1)} %constant.91.clone.x_ref) | copy-start | bytes 393220
  45.7 3.6 %copy-start.8 = (bf16[64,16,64]{2,1,0:T(8,128)(2,1)S(1)}, bf16[64,16,64]{2,1,0:T(8,128)(2,1)}, u32[]{:S(2)}) copy-start(bf16[64,16,64]{2,1,0:T(8,128)(2,1)} %param.21) | copy-start | bytes 393220
  45.7 4.0 %copy-start.9 = (s32[256,8]{0,1:T(8,128)S(1)}, s32[256,8]{0,1:T(8,128)}, u32[]{:S(2)}) copy-start(s32[256,8]{0,1:T(8,128)} %param.19) | copy-start | bytes 24580
  45.7 5.2 %copy-start.7 = (s32[256,8]{0,1:T(8,128)S(1)}, s32[256,8]{0,1:T(8,128)}, u32[]{:S(2)}) copy-start(s32[256,8]{0,1:T(8,128)} %param.20) | copy-start | bytes 24580
  46.7 19.4 %all-to-all-start.1 = ((f16[32,64,128]{2,1,0:T(8,128)(2,1)}), f16[32,64,128]{2,1,0:T(8,128)(2,1)S(1)}, u32[]{:S(2)}, u32[]{:S(2)}) async-start(f16[32,64,128]{2,1,0:T(8,128)(2,1)} %slice.5), calls=%async_computation.1 | async-start | bytes 1048576 | tf_op jit(solution)/shard_map/all_to_all | solution.py:659
  49.3 16.9 %copy-start.3 = (bf16[1024,256]{1,0:T(8,128)(2,1)S(1)}, bf16[1024,256]{1,0:T(8,128)(2,1)}, u32[]{:S(2)}) copy-start(bf16[1024,256]{1,0:T(8,128)(2,1)} %constant.92.clone.v_ref) | copy-start | bytes 1572868
  49.5 1.4 %collective-permute-start.3 = (bf16[240,256]{1,0:T(8,128)(2,1)S(1)}, bf16[240,256]{1,0:T(8,128)(2,1)S(1)}, u32[]{:S(2)}, u32[]{:S(2)}) collective-permute-start(bf16[240,256]{1,0:T(8,128)(2,1)S(1)} %get-tuple-element.51.here_ref), channel_id=1, source_target_pairs={{0,1},{1,0},{2,3},{3,2},{4,5},{5,4},{6,7},{7,6},{8,9},{9,8},{10,11... | collective-permute-start | bytes 368648 | tf_op jit(solution)/shard_map/ppermute | solution.py:584
  67.6 1.3 %collective-permute-start.4 = (bf16[128,128]{1,0:T(8,128)(2,1)S(1)}, bf16[128,128]{1,0:T(8,128)(2,1)S(1)}, u32[]{:S(2)}, u32[]{:S(2)}) collective-permute-start(bf16[128,128]{1,0:T(8,128)(2,1)S(1)} %get-tuple-element.58), channel_id=1, source_target_pairs={{0,1},{1,0},{2,3},{3,2},{4,5},{5,4},{6,7},{7,6},{8,9},{9,8},{10,11... | collective-permute-start | bytes 98312 | tf_op jit(solution)/shard_map/ppermute | solution.py:584
  71.5 4.3 %collective-permute-start.5 = (f32[64,256]{1,0:T(8,128)S(1)}, f32[64,256]{1,0:T(8,128)S(1)}, u32[]{:S(2)}, u32[]{:S(2)}) collective-permute-start(f32[64,256]{1,0:T(8,128)S(1)} %get-tuple-element.61), channel_id=1, source_target_pairs={{0,2},{1,3},{2,0},{3,1},{4,6},{5,7},{6,4},{7,5},{8,10},{9,11},{10,... | collective-permute-start | bytes 196616 | tf_op jit(solution)/shard_map/ppermute | solution.py:584
  71.6 7.9 %collective-permute-start.6 = (f32[64,256]{1,0:T(8,128)S(1)}, f32[64,256]{1,0:T(8,128)S(1)}, u32[]{:S(2)}, u32[]{:S(2)}) collective-permute-start(f32[64,256]{1,0:T(8,128)S(1)} %get-tuple-element.62), channel_id=1, source_target_pairs={{0,30},{1,31},{2,4},{3,5},{4,2},{5,3},{6,8},{7,9},{8,6},{9,7},{10,... | collective-permute-start | bytes 196616 | tf_op jit(solution)/shard_map/ppermute | solution.py:584

commit v14 on v12

--- a/solution.py
+++ b/solution.py
@@ -80,6 +80,14 @@
     forward = np.block([[cosine, sine], [-sine, cosine]])
     inverse = np.block([[cosine.T, -sine.T], [sine.T, cosine.T]])
     return forward, inverse
+
+
+def joined(tables):
+    result = []
+    for table in tables:
+        high, low = np.split(halves(table), 2)
+        result.append(np.block([[high, high], [low, np.zeros_like(low)]]))
+    return np.concatenate(result, axis=0)
 
 
 def split(values):
@@ -404,10 +412,9 @@
 
     def along_x(values, first):
         high, low = split(values)
-        table = x_ref[first * size : (first + 1) * size, :]
-        rest = x_ref[(first + 1) * size : (first + 2) * size, :]
-        both = dot(jnp.concatenate([table, table], axis=1), jnp.concatenate([high, low], axis=0))
-        return both + dot(rest, high)
+        table = x_ref[first * size : (first + 2) * size, :]
+        both = dot(table, jnp.concatenate([high, low], axis=0))
+        return both[:size] + both[size:]
 
     for plane in range(planes):
         here = slice(plane * length, (plane + 1) * length)
@@ -696,7 +703,7 @@
         scratch_shapes=[pltpu.VMEM((2 * planes * length, NY), BF16)] * 2,
         compiler_params=PARAMS,
         name="plane_filter",
-    )(widened(got), hat, jnp.asarray(halves(y_table(), y_table().T)), jnp.asarray(halves(*x_tables(slabs))))
+    )(widened(got), hat, jnp.asarray(halves(y_table(), y_table().T)), jnp.asarray(joined(x_tables(slabs))))
     back, near = lax.optimization_barrier((exchanged(back, 4 * parts), near))
 
     pot = pl.pallas_call(

time: 81.9 us -> 81.3 us (level)
  Pallas kernels: 20.8 us -> 19.6 us
    ppermute x7, starting transfers between devices: 9.12 us -> 10.3 us  [moved(): return lax.ppermute(values, both, pairs)]
  transfers between devices with their start and end apart: 9 -> 9, of which waited for: 7 -> 7; matrix products, arithmetic and copies ran while one was open for 0% -> 0% of each run, Pallas kernels for 10% -> 8%
where the time goes in v14:
time: 81.3 us; the launch traced here: 81.1 us
  waiting for transfers between devices  39.7 us (49%)
  Pallas kernels  19.6 us (24%)
  starting transfers between devices  15.6 us (19%)
  other arithmetic  2.83 us (3%)
  local copies, waits for them, and re-layouts  2.42 us (3%)
  between operations  0.95 us (1%)
    all_to_all x2, waiting for transfers between devices, exchanged(): values = lax.all_to_all(values, axes, 0, 0, tiled=True)  31 us
    ppermute x7, starting transfers between devices, moved(): return lax.ppermute(values, both, pairs)  10.3 us
    ppermute x7, waiting for transfers between devices, moved(): return lax.ppermute(values, both, pairs)  8.71 us
    all_to_all x2, starting transfers between devices, exchanged(): values = lax.all_to_all(values, axes, 0, 0, tiled=True)  5.32 us
    pallas_call x1, Pallas kernels, body(): pl.pallas_call(beside_kernel, out_shape=(grid,) * 5 + (shape_of(LANES, LA...  3.57 us
    pallas_call x1, Pallas kernels, body(): pl.pallas_call(functools.partial(plane_kernel, slabs, planes), out_shape=...  3.3 us
    pallas_call x1, Pallas kernels, body(): pl.pallas_call(beside_sample_kernel, out_shape=(sums, sums), in_specs=[SM...  3.27 us
    pallas_call x1, Pallas kernels, body(): pl.pallas_call(own_kernel, out_shape=(grid,) * 5 + (shape_of(KS * PANELS,...  2.66 us
  transfers between devices with their start and end apart: 9, of which 7 were waited for; matrix products, arithmetic and copies ran while one was open for 0% of the time, Pallas kernels for 8%

profile of v14, /device:TPU:0, one launch (start us, length us, event | category | flops | bytes accessed | tf_op | source)
XLA Modules:
  0.0 81.1 jit_solution(9227970967432957307)
XLA Ops:
  0.7 0.9 %fusion.packed_ref.own_ref = bf16[80,256]{1,0:T(8,128)(2,1)S(1)} fusion(s32[80]{0:T(128)S(1)} %compare_select_fusion, s32[256]{0:T(256)} %param.16, s32[]{:T(128)} %bitcast.16, s32[256]{0:T(256)} %param.17, bf16[64,256]{1,0:T(8,128)(2,1)} %param.14, pred[80]{0:T(512)(128)(4,1)S(1)} %get-tuple-element.63, pred[80]{0:T(512)(128)(4,1)S(1)} %get-tuple-element.64, ...), kind=kLoop, calls=%fused_computation.4 | loop fusion | flops 143360 | bytes 76596 | tf_op jit(solution)/shard_map/jit(_where)/select_n | solution.py:610
  1.6 3.0 %collective-permute-start = (bf16[80,256]{1,0:T(8,128)(2,1)S(1)}, bf16[80,256]{1,0:T(8,128)(2,1)S(1)}, u32[]{:S(2)}, u32[]{:S(2)}) collective-permute-start(bf16[80,256]{1,0:T(8,128)(2,1)S(1)} %fusion.packed_ref.own_ref), channel_id=1, source_target_pairs={{0,2},{1,3},{2,0},{3,1},{4,6},{5,7},{6,4},{7,5},{8,10},{9,11},{10,... | collective-permute-start | bytes 122888 | tf_op jit(solution)/shard_map/ppermute | solution.py:591
  4.6 4.5 %collective-permute-start.1 = (bf16[80,256]{1,0:T(8,128)(2,1)S(1)}, bf16[80,256]{1,0:T(8,128)(2,1)S(1)}, u32[]{:S(2)}, u32[]{:S(2)}) collective-permute-start(bf16[80,256]{1,0:T(8,128)(2,1)S(1)} %fusion.packed_ref.own_ref), channel_id=1, source_target_pairs={{0,30},{1,31},{2,4},{3,5},{4,2},{5,3},{6,8},{7,9},{8,6},{9,7},{10,... | collective-permute-start | bytes 122888 | tf_op jit(solution)/shard_map/ppermute | solution.py:591
  9.1 1.2 %copy-done = bf16[16,64,512]{2,1,0:T(8,128)(2,1)S(1)} copy-done((bf16[16,64,512]{2,1,0:T(8,128)(2,1)S(1)}, bf16[16,64,512]{2,1,0:T(8,128)(2,1)}, u32[]{:S(2)}) %copy-start) | copy-done | bytes 1048600
  10.3 2.7 %own_scatter.1 = (f32[520,128]{1,0:T(8,128)S(1)}, f32[520,128]{1,0:T(8,128)S(1)}, f32[520,128]{1,0:T(8,128)S(1)}, f32[520,128]{1,0:T(8,128)S(1)}, f32[520,128]{1...) custom-call(bf16[80,256]{1,0:T(8,128)(2,1)S(1)} %fusion.packed_ref.own_ref, ...), custom_call_target="tpu_custom_call" | custom-call | tf_op jit(solution)/shard_map/own_scatter/pallas_call | solution.py:615
  13.0 0.0 collective-permute-done.first_ref
  13.0 0.0 collective-permute-done.1.second_ref
  13.0 0.0 copy-start.2
  13.1 3.6 %beside_scatter.1 = (f32[520,128]{1,0:T(8,128)S(1)}, f32[520,128]{1,0:T(8,128)S(1)}, f32[520,128]{1,0:T(8,128)S(1)}, f32[520,128]{1,0:T(8,128)S(1)}, f32[520,128...) custom-call(s32[1]{0:T(128)} %bitcast.2.odd_ref, ...), custom_call_target="tpu_custom_call", output_to_operand_aliasing={{0}: (5, {}), {1}: (6, {}), {2}: (7, {}), {3}: (8, {}), {4}... | custom-call | tf_op jit(solution)/shard_map/beside_scatter/pallas_call | solution.py:630
  16.6 1.2 %collective-permute-start.2 = (f32[128,128]{1,0:T(8,128)S(1)}, f32[128,128]{1,0:T(8,128)S(1)}, u32[]{:S(2)}, u32[]{:S(2)}) collective-permute-start(f32[128,128]{1,0:T(8,128)S(1)} %get-tuple-element.45), channel_id=1, source_target_pairs={{0,1},{1,0},{2,3},{3,2},{4,5},{5,4},{6,7},{7,6},{8,9},{9,8},{10,11... | collective-permute-start | bytes 196616 | tf_op jit(solution)/shard_map/ppermute | solution.py:591
  17.8 0.9 %collective-permute-done.2.edge_ref = f32[128,128]{1,0:T(8,128)S(1)} collective-permute-done((f32[128,128]{1,0:T(8,128)S(1)}, f32[128,128]{1,0:T(8,128)S(1)}, u32[]{:S(2)}, u32[]{:S(2)}) %collective-permute-start.2) | collective-permute-done | bytes 65568 | tf_op jit(solution)/shard_map/ppermute | solution.py:591
  18.7 0.0 copy-done.2
  18.8 1.3 %z_forward.1 = f32[2304,128]{1,0:T(8,128)S(1)} custom-call(f32[520,128]{1,0:T(8,128)S(1)} %get-tuple-element.41.g0, f32[520,128]{1,0:T(8,128)S(1)} %get-tuple-element.42.g1, f32[520,128]{1,0:T(8,128)S(1)} %get-tuple-element.43.g2, f32[520,128]{1,0:T(8,128)S(1)} %get-tuple-element.44.g3, f32[128,128]{1,0:T(8,128)S(1)} %collective-permute-done.2.edge_ref, ...), custom_call_target="tpu_custom_call" | custom-call | tf_op jit(solution)/shard_map/z_forward/pallas_call | solution.py:654
  20.1 0.0 copy-start.1
  20.1 0.0 copy-start.6
  20.1 0.9 %convert_element_type.19 = f16[2304,128]{1,0:T(8,128)(2,1)} convert(f32[2304,128]{1,0:T(8,128)S(1)} %z_forward.1) | non-fusion elementwise | flops 294912 | bytes 1769472 | tf_op jit(solution)/shard_map/convert_element_type | solution.py:665
  21.0 2.7 %all-to-all-start = ((f16[32,72,128]{2,1,0:T(8,128)(2,1)}), f16[32,72,128]{2,1,0:T(8,128)(2,1)S(1)}, u32[]{:S(2)}, u32[]{:S(2)}) async-start(f16[32,72,128]{2,1,0:T(8,128)(2,1)} %bitcast.19), calls=%async_computation | async-start | bytes 1179648 | tf_op jit(solution)/shard_map/all_to_all | solution.py:666
  23.8 0.3 hat_order.1.hat_ref
  24.0 0.0 copy-start.4
  24.0 0.0 copy-start.5
  24.1 17.9 %all-to-all-done = f16[32,72,128]{2,1,0:T(8,128)(2,1)S(1)} async-done(((f16[32,72,128]{2,1,0:T(8,128)(2,1)}), f16[32,72,128]{2,1,0:T(8,128)(2,1)S(1)}, u32[]{:S(2)}, u32[]{:S(2)}) %all-to-all-start) | async-done | bytes 589856 | tf_op jit(solution)/shard_map/all_to_all | solution.py:666
  42.0 0.1 bitcast_convert_fusion.in_ref
  42.1 3.3 %plane_filter.1 = (f32[2304,128]{1,0:T(8,128)S(1)}, f32[8,128]{1,0:T(8,128)S(1)}) custom-call(f32[2304,128]{1,0:T(8,128)S(1)} %bitcast_convert_fusion.in_ref, f32[8,64,256]{2,1,0:T(8,128)S(1)} %hat_order.1.hat_ref, bf16[1024,256]{1,0:T(8,128)(2,1)S(1)} %copy-done.4, bf16[512,256]{1,0:T(8,128)(2,1)S(1)} %copy-done.5), custom_call_target="tpu_custom_call" | custom-call | tf_op jit(solution)/shard_map/plane_filter/pallas_call | solution.py:698
  45.4 0.1 convert.7
  45.5 0.0 copy-start.8
  45.5 0.0 copy-start.9
  45.5 0.0 copy-start.7
  45.5 0.9 %slice.5 = f16[32,64,128]{2,1,0:T(8,128)(2,1)} slice(f16[32,72,128]{2,1,0:T(8,128)(2,1)S(1)} %bitcast.20), slice={[0:32], [0:64], [0:128]} | slice | bytes 1048576 | tf_op jit(solution)/shard_map/slice | solution.py:665
  46.5 2.6 %all-to-all-start.1 = ((f16[32,64,128]{2,1,0:T(8,128)(2,1)}), f16[32,64,128]{2,1,0:T(8,128)(2,1)S(1)}, u32[]{:S(2)}, u32[]{:S(2)}) async-start(f16[32,64,128]{2,1,0:T(8,128)(2,1)} %slice.5), calls=%async_computation.1 | async-start | bytes 1048576 | tf_op jit(solution)/shard_map/all_to_all | solution.py:666
  49.1 0.0 copy-done.8
  49.1 0.0 copy-start.3
  49.1 0.2 reshape.28.table_ref
  49.3 0.2 collective-permute-start.3
  49.5 1.2 %collective-permute-done.3.there_ref = bf16[240,256]{1,0:T(8,128)(2,1)S(1)} collective-permute-done((bf16[240,256]{1,0:T(8,128)(2,1)S(1)}, bf16[240,256]{1,0:T(8,128)(2,1)S(1)}, u32[]{:S(2)}, u32[]{:S(2)}) %collective-permute-start.3) | collective-permute-done | bytes 122912 | tf_op jit(solution)/shard_map/ppermute | solution.py:591
  50.7 0.0 copy-done.7
  50.7 2.1 %near_field.1 = f32[64,256]{1,0:T(8,128)S(1)} custom-call(s32[1]{0:T(128)} %copy.25.live_ref, bf16[240,256]{1,0:T(8,128)(2,1)S(1)} %get-tuple-element.51.here_ref, bf16[240,256]{1,0:T(8,128)(2,1)S(1)} %collective-permute-done.3.there_ref, s32[8,256]{1,0:T(8,128)S(1)} %fusion.5.source_ref, s32[8,256]{1,0:T(8,128)S(1)} %bitcast.18, ...), custom_call_target="tpu_custom_call" | custom-call | tf_op jit(solution)/shard_map/near_field/pallas_call | solution.py:689
  52.9 13.1 %all-to-all-done.1 = f16[32,64,128]{2,1,0:T(8,128)(2,1)S(1)} async-done(((f16[32,64,128]{2,1,0:T(8,128)(2,1)}), f16[32,64,128]{2,1,0:T(8,128)(2,1)S(1)}, u32[]{:S(2)}, u32[]{:S(2)}) %all-to-all-start.1) | async-done | bytes 524320 | tf_op jit(solution)/shard_map/all_to_all | solution.py:666
  65.9 0.1 bitcast_convert_fusion.1.in_ref
  66.0 1.4 %z_inverse.1 = (f32[520,128]{1,0:T(8,128)S(1)}, f32[520,128]{1,0:T(8,128)S(1)}, f32[520,128]{1,0:T(8,128)S(1)}, f32[520,128]{1,0:T(8,128)S(1)}, bf16[128,128]{1,0:T(8,128)(2,1)S(1)}) custom-call(f32[2048,128]{1,0:T(8,128)S(1)} %bitcast_convert_fusion.1.in_ref, f32[8,128]{1,0:T(8,128)S(1)} %get-tuple-element.53.exponent_ref, bf16[1024,256]{1,0:T(8,128)(2,1)S(1)} %copy-done.3), custom_call_target="tpu_custom_call" | custom-call | tf_op jit(solution)/shard_map/z_inverse/pallas_call | solution.py:709
  67.4 0.1 collective-permute-start.4
  67.5 1.2 %collective-permute-done.4.edge_ref = bf16[128,128]{1,0:T(8,128)(2,1)S(1)} collective-permute-done((bf16[128,128]{1,0:T(8,128)(2,1)S(1)}, bf16[128,128]{1,0:T(8,128)(2,1)S(1)}, u32[]{:S(2)}, u32[]{:S(2)}) %collective-permute-start.4) | collective-permute-done | bytes 32800 | tf_op jit(solution)/shard_map/ppermute | solution.py:591
  68.7 3.3 %beside_sample.1 = (f32[64,256]{1,0:T(8,128)S(1)}, f32[64,256]{1,0:T(8,128)S(1)}) custom-call(s32[1]{0:T(128)} %bitcast.2.odd_ref, s32[8,512]{1,0:T(8,128)S(1)} %get-tuple-element.60.facts_ref.kinds_ref, f32[520,128]{1,0:T(8,128)S(1)} %get-tuple-element.54.p0, f32[520,128]{1,0:T(8,128)S(1)} %get-tuple-element.55.p1, f32[520,128]{1,0:T(8,128)S(1)} %get-tuple-element.56.p2, ...), custom_call_target="tpu_custom_call" | custom-call | tf_op jit(solution)/shard_map/beside_sample/pallas_call | solution.py:723
  72.0 0.1 collective-permute-start.5
  72.1 1.2 %collective-permute-start.6 = (f32[64,256]{1,0:T(8,128)S(1)}, f32[64,256]{1,0:T(8,128)S(1)}, u32[]{:S(2)}, u32[]{:S(2)}) collective-permute-start(f32[64,256]{1,0:T(8,128)S(1)} %get-tuple-element.62), channel_id=1, source_target_pairs={{0,30},{1,31},{2,4},{3,5},{4,2},{5,3},{6,8},{7,9},{8,6},{9,7},{10,... | collective-permute-start | bytes 196616 | tf_op jit(solution)/shard_map/ppermute | solution.py:591
  73.3 1.8 %own_sample.1 = f32[64,256]{1,0:T(8,128)S(1)} custom-call(s32[8,256]{1,0:T(8,128)S(1)} %get-tuple-element.34.facts_ref.kinds_ref, f32[520,128]{1,0:T(8,128)S(1)} %get-tuple-element.54.p0, f32[520,128]{1,0:T(8,128)S(1)} %get-tuple-element.55.p1, f32[520,128]{1,0:T(8,128)S(1)} %get-tuple-element.56.p2, f32[520,128]{1,0:T(8,128)S(1)} %get-tuple-element.57.p3, ...), custom_call_target="tpu_custom_call" | custom-call | tf_op jit(solution)/shard_map/own_sample/pallas_call | solution.py:734
  75.0 1.9 %collective-permute-done.5 = f32[64,256]{1,0:T(8,128)S(1)} collective-permute-done((f32[64,256]{1,0:T(8,128)S(1)}, f32[64,256]{1,0:T(8,128)S(1)}, u32[]{:S(2)}, u32[]{:S(2)}) %collective-permute-start.5) | collective-permute-done | bytes 65568 | tf_op jit(solution)/shard_map/ppermute | solution.py:591
  76.9 3.5 %collective-permute-done.6 = f32[64,256]{1,0:T(8,128)S(1)} collective-permute-done((f32[64,256]{1,0:T(8,128)S(1)}, f32[64,256]{1,0:T(8,128)S(1)}, u32[]{:S(2)}, u32[]{:S(2)}) %collective-permute-start.6) | collective-permute-done | bytes 65568 | tf_op jit(solution)/shard_map/ppermute | solution.py:591
  80.5 0.6 add_add_fusion
  (12 shorter events, 0.1 us)
Async XLA Ops:
  1.6 11.4 %collective-permute-start = (bf16[80,256]{1,0:T(8,128)(2,1)S(1)}, bf16[80,256]{1,0:T(8,128)(2,1)S(1)}, u32[]{:S(2)}, u32[]{:S(2)}) collective-permute-start(bf16[80,256]{1,0:T(8,128)(2,1)S(1)} %fusion.packed_ref.own_ref), channel_id=1, source_target_pairs={{0,2},{1,3},{2,0},{3,1},{4,6},{5,7},{6,4},{7,5},{8,10},{9,11},{10,... | collective-permute-start | bytes 122888 | tf_op jit(solution)/shard_map/ppermute | solution.py:591
  4.6 8.4 %collective-permute-start.1 = (bf16[80,256]{1,0:T(8,128)(2,1)S(1)}, bf16[80,256]{1,0:T(8,128)(2,1)S(1)}, u32[]{:S(2)}, u32[]{:S(2)}) collective-permute-start(bf16[80,256]{1,0:T(8,128)(2,1)S(1)} %fusion.packed_ref.own_ref), channel_id=1, source_target_pairs={{0,30},{1,31},{2,4},{3,5},{4,2},{5,3},{6,8},{7,9},{8,6},{9,7},{10,... | collective-permute-start | bytes 122888 | tf_op jit(solution)/shard_map/ppermute | solution.py:591
  9.1 1.2 %copy-start = (bf16[16,64,512]{2,1,0:T(8,128)(2,1)S(1)}, bf16[16,64,512]{2,1,0:T(8,128)(2,1)}, u32[]{:S(2)}) copy-start(bf16[16,64,512]{2,1,0:T(8,128)(2,1)} %param.18) | copy-start | bytes 3145732
  13.0 5.7 %copy-start.2 = (bf16[1152,256]{1,0:T(8,128)(2,1)S(1)}, bf16[1152,256]{1,0:T(8,128)(2,1)}, u32[]{:S(2)}) copy-start(bf16[1152,256]{1,0:T(8,128)(2,1)} %constant.88.clone.w_ref) | copy-start | bytes 1769476
  16.6 2.1 %collective-permute-start.2 = (f32[128,128]{1,0:T(8,128)S(1)}, f32[128,128]{1,0:T(8,128)S(1)}, u32[]{:S(2)}, u32[]{:S(2)}) collective-permute-start(f32[128,128]{1,0:T(8,128)S(1)} %get-tuple-element.45), channel_id=1, source_target_pairs={{0,1},{1,0},{2,3},{3,2},{4,5},{5,4},{6,7},{7,6},{8,9},{9,8},{10,11... | collective-permute-start | bytes 196616 | tf_op jit(solution)/shard_map/ppermute | solution.py:591
  20.1 3.7 %copy-start.1 = (f32[16,64,256]{2,1,0:T(8,128)S(1)}, f32[16,64,256]{2,1,0:T(8,128)}, u32[]{:S(2)}) copy-start(f32[16,64,256]{2,1,0:T(8,128)} %hat_ref) | copy-start | bytes 3145732
  20.1 3.7 %copy-start.6 = (bf16[128,128]{1,0:T(8,128)(2,1)S(1)}, bf16[128,128]{1,0:T(8,128)(2,1)}, u32[]{:S(2)}) copy-start(bf16[128,128]{1,0:T(8,128)(2,1)} %constant.89.clone.turn_ref) | copy-start | bytes 98308
  21.0 21.0 %all-to-all-start = ((f16[32,72,128]{2,1,0:T(8,128)(2,1)}), f16[32,72,128]{2,1,0:T(8,128)(2,1)S(1)}, u32[]{:S(2)}, u32[]{:S(2)}) async-start(f16[32,72,128]{2,1,0:T(8,128)(2,1)} %bitcast.19), calls=%async_computation | async-start | bytes 1179648 | tf_op jit(solution)/shard_map/all_to_all | solution.py:666
  24.0 18.1 %copy-start.4 = (bf16[1024,256]{1,0:T(8,128)(2,1)S(1)}, bf16[1024,256]{1,0:T(8,128)(2,1)}, u32[]{:S(2)}) copy-start(bf16[1024,256]{1,0:T(8,128)(2,1)} %constant.90.clone.y_ref) | copy-start | bytes 1572868
  24.0 18.1 %copy-start.5 = (bf16[512,256]{1,0:T(8,128)(2,1)S(1)}, bf16[512,256]{1,0:T(8,128)(2,1)}, u32[]{:S(2)}) copy-start(bf16[512,256]{1,0:T(8,128)(2,1)} %constant.91.clone.x_ref) | copy-start | bytes 786436
  45.5 3.6 %copy-start.8 = (bf16[64,16,64]{2,1,0:T(8,128)(2,1)S(1)}, bf16[64,16,64]{2,1,0:T(8,128)(2,1)}, u32[]{:S(2)}) copy-start(bf16[64,16,64]{2,1,0:T(8,128)(2,1)} %param.21) | copy-start | bytes 393220
  45.5 4.0 %copy-start.9 = (s32[256,8]{0,1:T(8,128)S(1)}, s32[256,8]{0,1:T(8,128)}, u32[]{:S(2)}) copy-start(s32[256,8]{0,1:T(8,128)} %param.19) | copy-start | bytes 24580
  45.5 5.2 %copy-start.7 = (s32[256,8]{0,1:T(8,128)S(1)}, s32[256,8]{0,1:T(8,128)}, u32[]{:S(2)}) copy-start(s32[256,8]{0,1:T(8,128)} %param.20) | copy-start | bytes 24580
  46.5 19.4 %all-to-all-start.1 = ((f16[32,64,128]{2,1,0:T(8,128)(2,1)}), f16[32,64,128]{2,1,0:T(8,128)(2,1)S(1)}, u32[]{:S(2)}, u32[]{:S(2)}) async-start(f16[32,64,128]{2,1,0:T(8,128)(2,1)} %slice.5), calls=%async_computation.1 | async-start | bytes 1048576 | tf_op jit(solution)/shard_map/all_to_all | solution.py:666
  49.1 16.9 %copy-start.3 = (bf16[1024,256]{1,0:T(8,128)(2,1)S(1)}, bf16[1024,256]{1,0:T(8,128)(2,1)}, u32[]{:S(2)}) copy-start(bf16[1024,256]{1,0:T(8,128)(2,1)} %constant.92.clone.v_ref) | copy-start | bytes 1572868
  49.3 1.4 %collective-permute-start.3 = (bf16[240,256]{1,0:T(8,128)(2,1)S(1)}, bf16[240,256]{1,0:T(8,128)(2,1)S(1)}, u32[]{:S(2)}, u32[]{:S(2)}) collective-permute-start(bf16[240,256]{1,0:T(8,128)(2,1)S(1)} %get-tuple-element.51.here_ref), channel_id=1, source_target_pairs={{0,1},{1,0},{2,3},{3,2},{4,5},{5,4},{6,7},{7,6},{8,9},{9,8},{10,11... | collective-permute-start | bytes 368648 | tf_op jit(solution)/shard_map/ppermute | solution.py:591
  67.4 1.3 %collective-permute-start.4 = (bf16[128,128]{1,0:T(8,128)(2,1)S(1)}, bf16[128,128]{1,0:T(8,128)(2,1)S(1)}, u32[]{:S(2)}, u32[]{:S(2)}) collective-permute-start(bf16[128,128]{1,0:T(8,128)(2,1)S(1)} %get-tuple-element.58), channel_id=1, source_target_pairs={{0,1},{1,0},{2,3},{3,2},{4,5},{5,4},{6,7},{7,6},{8,9},{9,8},{10,11... | collective-permute-start | bytes 98312 | tf_op jit(solution)/shard_map/ppermute | solution.py:591
  72.0 4.9 %collective-permute-start.5 = (f32[64,256]{1,0:T(8,128)S(1)}, f32[64,256]{1,0:T(8,128)S(1)}, u32[]{:S(2)}, u32[]{:S(2)}) collective-permute-start(f32[64,256]{1,0:T(8,128)S(1)} %get-tuple-element.61), channel_id=1, source_target_pairs={{0,2},{1,3},{2,0},{3,1},{4,6},{5,7},{6,4},{7,5},{8,10},{9,11},{10,... | collective-permute-start | bytes 196616 | tf_op jit(solution)/shard_map/ppermute | solution.py:591
  72.1 8.4 %collective-permute-start.6 = (f32[64,256]{1,0:T(8,128)S(1)}, f32[64,256]{1,0:T(8,128)S(1)}, u32[]{:S(2)}, u32[]{:S(2)}) collective-permute-start(f32[64,256]{1,0:T(8,128)S(1)} %get-tuple-element.62), channel_id=1, source_target_pairs={{0,30},{1,31},{2,4},{3,5},{4,2},{5,3},{6,8},{7,9},{8,6},{9,7},{10,... | collective-permute-start | bytes 196616 | tf_op jit(solution)/shard_map/ppermute | solution.py:591
